TPU v7x, 32 devices: a whole 2x2x4 slice. The times are simulated.
32 devices in a mesh: seq: 8 (over z, y), dp: 4 (over x, core).
Axes of the slice: x: 2, y: 2, z: 4, core: 2. Of those that a mesh axis runs over, the one named last changes fastest.
Arguments:
- tokens: bfloat16 [4, 4096, 1024], P('dp', 'seq'), may hold values from -6 to 6
- cotangent: bfloat16 [4, 4096, 1024], P('dp', 'seq'), may hold values from -6 to 6
- segment_ids: int32 [4, 4096], P('dp'), may hold values from 0 to 15, never falling along the last dimension, each value on 1 to 2048 neighbouring positions
- pad_mask: int32 [4, 4096], P('dp'), may hold values 0 or 1
- w_z: float32 [1024, 256], P(('seq', 'dp')), may hold values from -0.4375 to 0.4375
- w_v: float32 [1024, 2048], P(('seq', 'dp')), may hold values from -0.1875 to 0.1875
- w_r: float32 [1024, 2048], P(('seq', 'dp')), may hold values from -0.1875 to 0.1875
- w_h: float32 [2048, 1024], P(('seq', 'dp')), may hold values from -0.5 to 0.5
- w_gate: float32 [1024, 2560], P(('seq', 'dp')), may hold values from -0.1875 to 0.1875
- w_up: float32 [1024, 2560], P(('seq', 'dp')), may hold values from -0.1875 to 0.1875
- w_down: float32 [2560, 1024], P(('seq', 'dp')), may hold values from -0.25 to 0.25
- q_gain: float32 [256], P(('seq', 'dp')), may hold values from 0.5 to 1.5
- q_bias: float32 [256], P(('seq', 'dp')), may hold values from -3 to 3
- k_gain: float32 [256], P(('seq', 'dp')), may hold values from 0.5 to 1.5
- ffn_gain: float32 [1024], P(('seq', 'dp')), may hold values from 0.5 to 1.5
- norm_gain: float32 [1024], P('seq'), may hold values from 0.5 to 1.5
- ema_rate: float32 [1024, 16], P('seq'), may hold values from 1e-05 to 0.03
- ema_angle: float32 [1024, 16], P('seq'), may hold values from -3.140625 to 3.140625
- ema_input: float32 [1024, 16], P('seq'), may hold values from -4 to 4
- ema_output: float32 [1024, 16], P('seq'), may hold values from -1.5 to 1.5
- ema_skip: float32 [1024], P('seq'), may hold values from -3 to 3
Outputs:
- output: bfloat16 [4, 4096, 1024], P('dp', 'seq')
- input_grad: float32 [4, 4096, 1024], P('dp', 'seq')
- grad_w_z: float32 [1024, 256], P(('seq', 'dp'))
- grad_w_v: float32 [1024, 2048], P(('seq', 'dp'))
- grad_w_r: float32 [1024, 2048], P(('seq', 'dp'))
- grad_w_h: float32 [2048, 1024], P(('seq', 'dp'))
- grad_w_gate: float32 [1024, 2560], P(('seq', 'dp'))
- grad_w_up: float32 [1024, 2560], P(('seq', 'dp'))
- grad_w_down: float32 [2560, 1024], P(('seq', 'dp'))
- grad_q_gain: float32 [256], P(('seq', 'dp'))
- grad_q_bias: float32 [256], P(('seq', 'dp'))
- grad_k_gain: float32 [256], P(('seq', 'dp'))
- grad_ffn_gain: float32 [1024], P(('seq', 'dp'))
- grad_norm_gain: float32 [1024], P('seq')
- grad_ema_rate: float32 [1024, 16], P('seq')
- grad_ema_angle: float32 [1024, 16], P('seq')
- grad_ema_input: float32 [1024, 16], P('seq')
- grad_ema_output: float32 [1024, 16], P('seq')
- grad_ema_skip: float32 [1024], P('seq')
Inputs may be any that keep to these rules, and one draw needn't show every extreme that they name: `segment_ids`: along each group's 4096 tokens the ids never fall; each of the 16 documents covers 1 to 2048 consecutive tokens, one exactly that many.
All inputs are finite; a program needn't handle non-finite values. No bound on the sum of `pad_mask` on one device may be relied on, other than what follows from the above.
Results may differ from a plain program's by a relative error of at most 0.04.
Values may be sent and summed in bfloat16 or wider, within the bound.
No kernel may reach another device: no remote copies, remote signals or barrier semaphores. Data moves between devices by JAX's collectives and lax.ppermute only.
A program may use at most 320 MiB of HBM per device.

v0:
```python
import jax
import jax.numpy as jnp
from jax import lax
from jax.sharding import PartitionSpec as P

GROUP = 64


def silu_grad(value):
    sigma = jax.nn.sigmoid(value)
    return sigma * (1.0 + value * (1.0 - sigma))


def segment_cumsum(values, flags):

    def combine(earlier, later):
        return (later[0] + (1.0 - later[1]) * earlier[0], jnp.maximum(earlier[1], later[1]))

    return lax.associative_scan(combine, (values, flags), axis=0)[0]


def step_norm(inputs, flags, valid, gain):
    length, width = inputs.shape
    groups = width // GROUP
    grouped = inputs.reshape(length, groups, GROUP)
    totals = jnp.concatenate(
        [jnp.sum(grouped, axis=2), jnp.sum(grouped * grouped, axis=2), valid[:, None]], axis=1
    )
    running = segment_cumsum(totals, flags)
    counts = jnp.maximum(running[:, 2 * groups :], 1.0) * GROUP
    means = running[:, :groups] / counts
    variance = running[:, groups : 2 * groups] / counts - means * means
    scaled = (grouped - means[:, :, None]) * lax.rsqrt(variance + 1e-05)[:, :, None]
    return scaled.reshape(length, width) * gain[None, :]


def complex_combine(earlier, later):
    return (
        later[0] * earlier[0] - later[1] * earlier[1],
        later[0] * earlier[1] + later[1] * earlier[0],
        later[0] * earlier[2] - later[1] * earlier[3] + later[2],
        later[0] * earlier[3] + later[1] * earlier[2] + later[3],
    )


def ema_blocked(normed, rate, angle, input_w, output_w, skip_w):
    length, width = normed.shape
    highest = lax.Precision.HIGHEST
    span = 128
    count = length // span
    log_mag = jnp.log1p(-rate)
    coeff = jnp.sqrt(rate * (2.0 - rate)) * input_w
    powers = jnp.arange(span + 1).astype(jnp.float32)[:, None, None]
    radius = jnp.exp(powers * log_mag[None])
    power_re = radius * jnp.cos(powers * angle[None])
    power_im = radius * jnp.sin(powers * angle[None])
    kernel = jnp.sum(power_re[:span] * (output_w * coeff)[None], axis=2)
    places = jnp.arange(span)
    lag = places[:, None] - places[None, :]
    toeplitz = jnp.where(
        (lag >= 0)[:, :, None], jnp.take(kernel, jnp.clip(lag, 0, span - 1), axis=0), 0.0
    )
    blocks = normed.reshape(count, span, width)
    inner = jnp.einsum("ijc,bjc->bic", toeplitz, blocks, precision=highest)
    tail_re = power_re[:span][::-1] * coeff[None]
    tail_im = power_im[:span][::-1] * coeff[None]
    ends_re = jnp.einsum("jcn,bjc->bcn", tail_re, blocks, precision=highest)
    ends_im = jnp.einsum("jcn,bjc->bcn", tail_im, blocks, precision=highest)
    hop_re = jnp.broadcast_to(power_re[span][None], ends_re.shape)
    hop_im = jnp.broadcast_to(power_im[span][None], ends_re.shape)
    totals = lax.associative_scan(complex_combine, (hop_re, hop_im, ends_re, ends_im), axis=0)
    empty = jnp.zeros((1,) + ends_re.shape[1:], ends_re.dtype)
    carried_re = jnp.concatenate([empty, totals[2][:-1]], axis=0)
    carried_im = jnp.concatenate([empty, totals[3][:-1]], axis=0)
    lead_re = power_re[1:] * output_w[None]
    lead_im = power_im[1:] * output_w[None]
    outer = jnp.einsum("icn,bcn->bic", lead_re, carried_re, precision=highest) - jnp.einsum(
        "icn,bcn->bic", lead_im, carried_im, precision=highest
    )
    return (inner + outer).reshape(length, width) + skip_w[None] * normed


def score_block(queries, keys, start, span, row_segs, key_valid, scale_factor):
    scores = (
        jnp.einsum("qz,kz->qk", queries, keys, preferred_element_type=jnp.float32) * scale_factor
    )
    query_pos = start + jnp.arange(span)
    key_pos = jnp.arange(keys.shape[0])
    allowed = (
        (key_pos[None, :] <= query_pos[:, None])
        & (row_segs[None, :] == row_segs[:, None])
        & (key_valid[None, :] | (key_pos[None, :] == query_pos[:, None]))
    )
    return (jnp.where(allowed, scores, -1e30), queries)


def on_device(
    tokens,
    cotangent,
    segment_ids,
    pad_mask,
    w_z,
    w_v,
    w_r,
    w_h,
    w_gate,
    w_up,
    w_down,
    q_gain,
    q_bias,
    k_gain,
    ffn_gain,
    norm_gain,
    ema_rate,
    ema_angle,
    ema_input,
    ema_output,
    ema_skip,
):
    bf16 = jnp.bfloat16
    f32 = jnp.float32
    rows = tokens.shape[1]
    seq_index = lax.axis_index("seq")
    group_segs = segment_ids[0]
    group_valid = pad_mask[0].astype(f32)
    row_segs = lax.dynamic_slice_in_dim(group_segs, seq_index * rows, rows)
    row_valid = lax.dynamic_slice_in_dim(group_valid, seq_index * rows, rows)
    masked_in = tokens[0] * row_valid[:, None].astype(bf16)
    flags = jnp.concatenate([jnp.ones((1,), f32), (group_segs[1:] != group_segs[:-1]).astype(f32)])[
        :, None
    ]
    channel_in = lax.all_to_all(masked_in, "seq", split_axis=1, concat_axis=0, tiled=True)

    def channel_part(inputs, gain, rate, angle, input_w, output_w, skip_w):
        normed_ch = step_norm(inputs, flags, group_valid, gain)
        mixed_ch = ema_blocked(normed_ch, rate, angle, input_w, output_w, skip_w)
        return (normed_ch, jax.nn.silu(mixed_ch))

    channel_out, channel_pullback = jax.vjp(
        channel_part,
        channel_in.astype(f32),
        norm_gain,
        ema_rate,
        ema_angle,
        ema_input,
        ema_output,
        ema_skip,
    )
    sent_norm, sent_mix = (
        lax.all_to_all(channel_out[0].astype(bf16), "seq", split_axis=0, concat_axis=1, tiled=True),
        lax.all_to_all(channel_out[1].astype(bf16), "seq", split_axis=0, concat_axis=1, tiled=True),
    )
    (
        full_z,
        full_v,
        full_r,
        full_h,
        full_gate,
        full_up,
        full_down,
        full_qg,
        full_qb,
        full_kg,
        full_fg,
    ) = (
        lax.all_gather(w_z.astype(bf16), ("seq", "dp"), axis=0, tiled=True),
        lax.all_gather(w_v.astype(bf16), ("seq", "dp"), axis=0, tiled=True),
        lax.all_gather(w_r.astype(bf16), ("seq", "dp"), axis=0, tiled=True),
        lax.all_gather(w_h.astype(bf16), ("seq", "dp"), axis=0, tiled=True),
        lax.all_gather(w_gate.astype(bf16), ("seq", "dp"), axis=0, tiled=True),
        lax.all_gather(w_up.astype(bf16), ("seq", "dp"), axis=0, tiled=True),
        lax.all_gather(w_down.astype(bf16), ("seq", "dp"), axis=0, tiled=True),
        lax.all_gather(q_gain.astype(bf16), ("seq", "dp"), axis=0, tiled=True),
        lax.all_gather(q_bias.astype(bf16), ("seq", "dp"), axis=0, tiled=True),
        lax.all_gather(k_gain.astype(bf16), ("seq", "dp"), axis=0, tiled=True),
        lax.all_gather(ffn_gain.astype(bf16), ("seq", "dp"), axis=0, tiled=True),
    )
    shared = jnp.dot(sent_mix, full_z, preferred_element_type=f32)
    queries = (shared * full_qg.astype(f32)[None] + full_qb.astype(f32)[None]).astype(bf16)
    keys = (shared * full_kg.astype(f32)[None]).astype(bf16)
    value_pre = jnp.dot(sent_norm, full_v, preferred_element_type=f32)
    values = jax.nn.silu(value_pre).astype(bf16)
    gate_pre = jnp.dot(sent_mix, full_r, preferred_element_type=f32)
    reset_gate = jax.nn.silu(gate_pre)
    scale_factor = queries.shape[1] ** (-0.5)
    span = min(512, rows)
    key_valid = row_valid > 0.5
    start = 0
    masked, query_rows = score_block(queries, keys, start, span, row_segs, key_valid, scale_factor)
    top = jnp.max(masked, axis=1, keepdims=True)
    weights = jnp.exp(masked - top)
    total = jnp.sum(weights, axis=1, keepdims=True)
    probs_low = (weights / total).astype(bf16)
    attended_parts = jnp.dot(probs_low, values, preferred_element_type=f32)
    log_parts = top + jnp.log(total)
    gated = (attended_parts * reset_gate).astype(bf16)
    middle = masked_in.astype(f32) + jnp.dot(gated, full_h, preferred_element_type=f32)
    inverse = lax.rsqrt(jnp.mean(middle * middle, axis=1, keepdims=True) + 1e-05)
    normalized = middle * inverse
    ffn_in = (normalized * full_fg.astype(f32)[None]).astype(bf16)
    gate_ffn = jnp.dot(ffn_in, full_gate, preferred_element_type=f32)
    up_ffn = jnp.dot(ffn_in, full_up, preferred_element_type=f32)
    gate_act = jax.nn.silu(gate_ffn)
    hidden = (gate_act * up_ffn).astype(bf16)
    output = (middle + jnp.dot(hidden, full_down, preferred_element_type=f32)).astype(bf16)
    (
        full_z,
        full_v,
        full_r,
        full_h,
        full_gate,
        full_up,
        full_down,
        full_qg,
        full_qb,
        full_kg,
        full_fg,
    ) = (
        lax.all_gather(w_z.astype(bf16), ("seq", "dp"), axis=0, tiled=True),
        lax.all_gather(w_v.astype(bf16), ("seq", "dp"), axis=0, tiled=True),
        lax.all_gather(w_r.astype(bf16), ("seq", "dp"), axis=0, tiled=True),
        lax.all_gather(w_h.astype(bf16), ("seq", "dp"), axis=0, tiled=True),
        lax.all_gather(w_gate.astype(bf16), ("seq", "dp"), axis=0, tiled=True),
        lax.all_gather(w_up.astype(bf16), ("seq", "dp"), axis=0, tiled=True),
        lax.all_gather(w_down.astype(bf16), ("seq", "dp"), axis=0, tiled=True),
        lax.all_gather(q_gain.astype(bf16), ("seq", "dp"), axis=0, tiled=True),
        lax.all_gather(q_bias.astype(bf16), ("seq", "dp"), axis=0, tiled=True),
        lax.all_gather(k_gain.astype(bf16), ("seq", "dp"), axis=0, tiled=True),
        lax.all_gather(ffn_gain.astype(bf16), ("seq", "dp"), axis=0, tiled=True),
    )
    grad_out = cotangent[0].astype(f32)
    grad_low = grad_out.astype(bf16)
    grad_w_down = jnp.einsum("rf,rd->fd", hidden, grad_low, preferred_element_type=f32)
    grad_hidden = jnp.einsum("rd,fd->rf", grad_low, full_down, preferred_element_type=f32)
    grad_gate = (grad_hidden * up_ffn * silu_grad(gate_ffn)).astype(bf16)
    grad_upv = (grad_hidden * gate_act).astype(bf16)
    grad_w_gate = jnp.einsum("rd,rf->df", ffn_in, grad_gate, preferred_element_type=f32)
    grad_w_up = jnp.einsum("rd,rf->df", ffn_in, grad_upv, preferred_element_type=f32)
    grad_ffn_in = jnp.einsum(
        "rf,df->rd", grad_gate, full_gate, preferred_element_type=f32
    ) + jnp.einsum("rf,df->rd", grad_upv, full_up, preferred_element_type=f32)
    grad_ffn_gain = jnp.sum(grad_ffn_in * normalized, axis=0)
    grad_normal = grad_ffn_in * full_fg.astype(f32)[None]
    grad_middle = grad_out + inverse * (
        grad_normal - normalized * jnp.mean(grad_normal * normalized, axis=1, keepdims=True)
    )
    middle_low = grad_middle.astype(bf16)
    grad_w_h = jnp.einsum("re,rd->ed", gated, middle_low, preferred_element_type=f32)
    grad_gated = (
        jnp.einsum("rd,ed->re", middle_low, full_h, preferred_element_type=f32)
        .astype(bf16)
        .astype(f32)
    )
    grad_att = (grad_gated * reset_gate).astype(bf16)
    grad_gate_pre = (grad_gated * attended_parts * silu_grad(gate_pre)).astype(bf16)
    start = 0
    masked, query_rows = score_block(queries, keys, start, span, row_segs, key_valid, scale_factor)
    probs = jnp.exp(masked - log_parts)
    probs_low = probs.astype(bf16)
    grad_values = jnp.einsum("qk,qe->ke", probs_low, grad_att, preferred_element_type=f32)
    grad_probs = jnp.einsum("qe,ke->qk", grad_att, values, preferred_element_type=f32)
    grad_scores = (
        probs * (grad_probs - jnp.sum(probs * grad_probs, axis=1, keepdims=True))
    ).astype(bf16)
    query_parts = jnp.dot(grad_scores, keys, preferred_element_type=f32) * scale_factor
    grad_keys = (
        jnp.einsum("qk,qz->kz", grad_scores, query_rows, preferred_element_type=f32) * scale_factor
    )
    grad_value_pre = (grad_values * silu_grad(value_pre)).astype(bf16)
    grad_q_gain = jnp.sum(query_parts * shared, axis=0)
    grad_q_bias = jnp.sum(query_parts, axis=0)
    grad_k_gain = jnp.sum(grad_keys * shared, axis=0)
    grad_shared = (
        query_parts * full_qg.astype(f32)[None] + grad_keys * full_kg.astype(f32)[None]
    ).astype(bf16)
    grad_w_z = jnp.einsum("rd,rz->dz", sent_mix, grad_shared, preferred_element_type=f32)
    grad_w_r = jnp.einsum("rd,re->de", sent_mix, grad_gate_pre, preferred_element_type=f32)
    grad_w_v = jnp.einsum("rd,re->de", sent_norm, grad_value_pre, preferred_element_type=f32)
    grad_mix_rows = (
        jnp.einsum("rz,dz->rd", grad_shared, full_z, preferred_element_type=f32)
        + jnp.einsum("re,de->rd", grad_gate_pre, full_r, preferred_element_type=f32)
    ).astype(bf16)
    grad_norm_rows = jnp.einsum(
        "re,de->rd", grad_value_pre, full_v, preferred_element_type=f32
    ).astype(bf16)
    grad_norm_ch, grad_mix_ch = (
        lax.all_to_all(grad_norm_rows, "seq", split_axis=1, concat_axis=0, tiled=True),
        lax.all_to_all(grad_mix_rows, "seq", split_axis=1, concat_axis=0, tiled=True),
    )
    channel_grads = channel_pullback((grad_norm_ch.astype(f32), grad_mix_ch.astype(f32)))
    grad_in_rows = lax.all_to_all(channel_grads[0], "seq", split_axis=0, concat_axis=1, tiled=True)
    input_grad = (grad_middle + grad_in_rows) * row_valid[:, None]
    param_sums = lax.psum(
        (
            channel_grads[1],
            channel_grads[2],
            channel_grads[3],
            channel_grads[4],
            channel_grads[5],
            channel_grads[6],
        ),
        "dp",
    )
    (
        shard_z,
        shard_v,
        shard_r,
        shard_h,
        shard_gate,
        shard_up,
        shard_down,
        shard_qg,
        shard_qb,
        shard_kg,
        shard_fgain,
    ) = (
        lax.psum_scatter(grad_w_z, ("seq", "dp"), scatter_dimension=0, tiled=True),
        lax.psum_scatter(grad_w_v, ("seq", "dp"), scatter_dimension=0, tiled=True),
        lax.psum_scatter(grad_w_r, ("seq", "dp"), scatter_dimension=0, tiled=True),
        lax.psum_scatter(grad_w_h, ("seq", "dp"), scatter_dimension=0, tiled=True),
        lax.psum_scatter(grad_w_gate, ("seq", "dp"), scatter_dimension=0, tiled=True),
        lax.psum_scatter(grad_w_up, ("seq", "dp"), scatter_dimension=0, tiled=True),
        lax.psum_scatter(grad_w_down, ("seq", "dp"), scatter_dimension=0, tiled=True),
        lax.psum_scatter(grad_q_gain, ("seq", "dp"), scatter_dimension=0, tiled=True),
        lax.psum_scatter(grad_q_bias, ("seq", "dp"), scatter_dimension=0, tiled=True),
        lax.psum_scatter(grad_k_gain, ("seq", "dp"), scatter_dimension=0, tiled=True),
        lax.psum_scatter(grad_ffn_gain, ("seq", "dp"), scatter_dimension=0, tiled=True),
    )
    return (
        output[None],
        input_grad[None],
        shard_z,
        shard_v,
        shard_r,
        shard_h,
        shard_gate,
        shard_up,
        shard_down,
        shard_qg,
        shard_qb,
        shard_kg,
        shard_fgain,
        param_sums[0],
        param_sums[1],
        param_sums[2],
        param_sums[3],
        param_sums[4],
        param_sums[5],
    )


def solution(mesh):
    placed = (
        P("dp", "seq", None),
        P("dp", "seq", None),
        P("dp", None),
        P("dp", None),
        P(("seq", "dp"), None),
        P(("seq", "dp"), None),
        P(("seq", "dp"), None),
        P(("seq", "dp"), None),
        P(("seq", "dp"), None),
        P(("seq", "dp"), None),
        P(("seq", "dp"), None),
        P(("seq", "dp")),
        P(("seq", "dp")),
        P(("seq", "dp")),
        P(("seq", "dp")),
        P("seq"),
        P("seq", None),
        P("seq", None),
        P("seq", None),
        P("seq", None),
        P("seq"),
    )
    return jax.shard_map(
        on_device,
        mesh=mesh,
        in_specs=placed,
        out_specs=(
            P("dp", "seq", None),
            P("dp", "seq", None),
            P(("seq", "dp"), None),
            P(("seq", "dp"), None),
            P(("seq", "dp"), None),
            P(("seq", "dp"), None),
            P(("seq", "dp"), None),
            P(("seq", "dp"), None),
            P(("seq", "dp"), None),
            P(("seq", "dp")),
            P(("seq", "dp")),
            P(("seq", "dp")),
            P(("seq", "dp")),
            P("seq"),
            P("seq", None),
            P("seq", None),
            P("seq", None),
            P("seq", None),
            P("seq"),
        ),
        check_vma=False,
    )
```

profile of v0, /device:TPU:0, one launch (start us, length us, event | category | flops | bytes accessed | tf_op | source)
XLA Modules:
  0.0 1526.0 jit_solution(599466670859567393)
XLA Ops:
  16.7 7.4 all-to-all-start
  41.1 55.0 %gather_fusion = f32[16384,128]{1,0:T(8,128)} fusion(f32[128,128]{1,0:T(8,128)S(1)} %get-tuple-element.214, s32[16384]{0:T(1024)S(1)} %broadcast_clamp_fusion), kind=kCustom, calls=%fused_computation | custom fusion | bytes 16842752 | tf_op jit(solution)/shard_map/jvp(jit(_take))/gather | solution.py:61
  99.0 7.6 select_select_fusion
  118.8 9.3 copy.506
  179.3 5.8 fusion.179
  203.3 5.6 pad.1254
  209.0 5.5 pad.1016
  214.4 16.6 %fusion.177 = f32[128,32,128]{2,1,0:T(8,128)} fusion(f32[32,128,128]{1,0,2:T(8,128)S(1)} %fusion.17, f32[128,128,128]{1,0,2:T(8,128)} %copy.506), kind=kOutput, calls=%fused_computation.516 | convolution fusion | flops 805306368 | bytes 12582912 | tf_op jit(solution)/shard_map/jvp(ijc,bjc->bic)/dot_general | solution.py:64
  248.2 5.5 multiply_convert_fusion.7
  257.7 6.1 all-to-all-start.1
  264.8 51.1 %all-reduce.195 = (bf16[256]{0:T(256)(128)(2,1)S(1)}, bf16[256]{0:T(256)(128)(2,1)S(1)}, bf16[256]{0:T(256)(128)(2,1)S(1)}, bf16[1024]{0:T(1024)(128)(2,1)S(1)}) all-reduce(bf16[256]{0:T(256)(128)(2,1)S(1)} %dynamic-update-slice.2, bf16[256]{0:T(256)(128)(2,1)S(1)} %dynamic-update-slice.1, ...), channel_id=1, replica_groups=mesh['seq'=8,'dp'=4] {'seq','dp'}, use_global_device_ids=true, to_apply=%add.187 | all-reduce | flops 1792 | bytes 7168
  316.6 5.5 all-to-all-start.2
  322.2 57.5 %all_gather.43 = bf16[1024,256]{1,0:T(8,128)(2,1)S(1)} all-gather(bf16[32,256]{1,0:T(8,128)(2,1)S(1)} %convert_element_type.260), channel_id=1, replica_groups=mesh['seq'=8,'dp'=4] {'seq','dp'}, dimensions={0}, use_global_device_ids=true | all-gather | bytes 540672 | tf_op jit(solution)/shard_map/all_gather | solution.py:166
  381.4 8.8 fusion.5
  390.2 6.2 online-softmax
  396.5 9.2 multiply_convert_fusion.4
  405.6 5.6 multiply_reduce_fusion.6
  412.8 7.4 fusion.181
  420.2 7.1 fusion.182
  427.3 9.1 all-gather.17.cloned.1.call-done
  436.5 10.3 multiply_convert_fusion
  446.8 6.8 fusion.183
  460.3 5.7 fusion.1
  472.9 8.0 fusion.70
  481.0 7.5 fusion.189
  488.6 5.2 multiply_convert_fusion.3
  495.2 6.8 fusion.188
  503.2 7.4 fusion.190
  510.6 7.2 fusion.191
  517.9 5.3 fusion.184
  533.0 5.2 convolution_convert_fusion.1
  539.6 7.3 fusion.56
  546.8 9.9 all-to-all-done.4
  653.9 4.7 pad.837
  665.1 4.7 pad.838
  711.0 8.4 pad.842
  719.5 5.5 pad.834
  724.9 8.5 pad.843
  733.4 7.9 pad.841
  743.9 5.5 pad.839
  749.3 8.3 pad.781
  760.3 5.3 fusion.186
  769.3 10.7 add_bitcast_fusion
  794.0 5.2 multiply_reduce_fusion.3
  838.0 7.7 fusion.16
  845.7 6.0 all-to-all-start.5
  851.7 7.8 fusion.42
  859.6 76.5 %all-reduce.193 = (f32[256]{0:T(256)S(1)}, f32[256]{0:T(256)S(1)}, f32[256]{0:T(256)S(1)}, f32[1024]{0:T(1024)S(1)}) all-reduce(f32[256]{0:T(256)S(1)} %copy-done.215, f32[256]{0:T(256)S(1)} %copy-done.216, f32[256]{0:T(256)S(1)} %copy-done.214, f32[1024]{0:T(1024)S(1)} %copy-done.198), channel_id=9, replica_groups=mesh['seq'=8,'dp'=4] {'seq','dp'}, use_global_device_ids=true, to_apply=%region_20.21.clone | all-reduce | flops 1792 | bytes 14336
  938.4 5.6 pad.951
  944.0 5.5 pad.950
  949.5 7.9 pad.929
  957.3 8.4 pad.956
  965.8 8.5 pad.957
  974.2 8.0 pad.955
  1002.0 4.7 fusion.25
  1009.6 4.7 fusion.18
  1017.1 16.9 %select_bitcast_fusion = f32[128,128,128]{1,0,2:T(8,128)} fusion(pred[128,128]{1,0:T(8,128)(4,1)S(1)} %copy-done.119, f32[32,128,128]{1,0,2:T(8,128)S(1)} %copy-done.1, f32[32,128,128]{1,0,2:T(8,128)} %copy-done.2), kind=kOutput, calls=%fused_computation.2 | convolution fusion | flops 807403520 | bytes 12599296 | tf_op jit(solution)/shard_map/transpose(jvp(ijc,bjc->bic))/dot_general | solution.py:64
  1034.0 9.5 copy.574
  1043.5 98.4 %scatter_custom_fusion = f32[128,128]{1,0:T(8,128)S(1)} fusion(s32[16384]{0:T(1024)} %fusion.76, f32[16384,128]{1,0:T(8,128)} %bitcast.300, f32[]{:T(128)} %constant.28.clone.1), kind=kCustom, calls=%fused_computation.253 | custom fusion | flops 2097152 | bytes 66048 | tf_op jit(solution)/shard_map/transpose(jvp(jit(_take)))/scatter-add | solution.py:61
  1146.2 4.9 fusion.49
  1151.5 14.9 all-reduce.194
  1173.3 42.5 %reduce-scatter.16.cloned.1.call-done = f32[32,2560]{1,0:T(8,128)} async-done(((f32[1024,2560]{1,0:T(8,128)}), f32[32,2560]{1,0:T(8,128)}) %reduce-scatter.16.cloned.1.call-update) | async-done | bytes 327696 | tf_op jit(solution)/shard_map/reduce_scatter | solution.py:321
  1215.8 151.7 %reduce-scatter.18.cloned.1.call-done = f32[32,2560]{1,0:T(8,128)} async-done(((f32[1024,2560]{1,0:T(8,128)}), f32[32,2560]{1,0:T(8,128)}) %reduce-scatter.18.cloned.1.call-update) | async-done | bytes 327696 | tf_op jit(solution)/shard_map/reduce_scatter | solution.py:322
  1367.6 151.7 %reduce-scatter.20.cloned.1.call-done = f32[80,1024]{1,0:T(8,128)} async-done(((f32[2560,1024]{1,0:T(8,128)}), f32[80,1024]{1,0:T(8,128)}) %reduce-scatter.20.cloned.1.call-update) | async-done | bytes 327696 | tf_op jit(solution)/shard_map/reduce_scatter | solution.py:323
  (1040 shorter events, 405.2 us)
Async XLA Ops:
  7.2 374.2 %all-gather.7.cloned.1.call-start = ((), (), s32[]{:S(2)}) async-start(), calls=%async_computation.13 | async-start | bytes 4325376 | tf_op jit(solution)/shard_map/all_gather | solution.py:167
  9.0 387.5 %all-gather.9.cloned.1.call-start = ((), (), s32[]{:S(2)}) async-start(), calls=%async_computation.14 | async-start | bytes 4325376 | tf_op jit(solution)/shard_map/all_gather | solution.py:168
  10.7 394.9 %all-gather.11.cloned.1.call-start = ((), (), s32[]{:S(2)}) async-start(), calls=%async_computation.15 | async-start | bytes 4325376 | tf_op jit(solution)/shard_map/all_gather | solution.py:169
  12.4 400.4 %all-gather.13.cloned.1.call-start = ((), (), s32[]{:S(2)}) async-start(), calls=%async_computation.16 | async-start | bytes 5406720 | tf_op jit(solution)/shard_map/all_gather | solution.py:170
  14.1 406.1 %all-gather.15.cloned.1.call-start = ((), (), s32[]{:S(2)}) async-start(), calls=%async_computation.17 | async-start | bytes 5406720 | tf_op jit(solution)/shard_map/all_gather | solution.py:171
  15.6 19.1 %copy-start.132 = (f32[128,16]{0,1:T(8,128)S(1)}, f32[128,16]{0,1:T(8,128)}, u32[]{:S(2)}) copy-start(f32[128,16]{0,1:T(8,128)} %param.40) | copy-start | bytes 24580
  15.6 19.1 %copy-start.151 = (f32[128,16]{0,1:T(8,128)S(1)}, f32[128,16]{0,1:T(8,128)}, u32[]{:S(2)}) copy-start(f32[128,16]{0,1:T(8,128)} %param.37) | copy-start | bytes 24580
  15.6 19.1 %copy-start.166 = (f32[128,16]{0,1:T(8,128)S(1)}, f32[128,16]{0,1:T(8,128)}, u32[]{:S(2)}) copy-start(f32[128,16]{0,1:T(8,128)} %param.39) | copy-start | bytes 24580
  16.7 18.1 %copy-start.160 = (f32[128,16]{0,1:T(8,128)S(1)}, f32[128,16]{0,1:T(8,128)}, u32[]{:S(2)}) copy-start(f32[128,16]{0,1:T(8,128)} %param.38) | copy-start | bytes 24580
  16.7 118.4 %all-to-all-start = ((bf16[512,8,128]{0,2,1:T(8,128)(2,1)}), bf16[512,8,128]{0,2,1:T(8,128)(2,1)}, u32[]{:S(2)}, u32[]{:S(2)}) async-start(bf16[512,8,128]{0,2,1:T(8,128)(2,1)} %broadcast_multiply_fusion.1), calls=%async_computation | async-start | bytes 2097152 | tf_op jit(solution)/shard_map/all_to_all | solution.py:132
  24.1 412.4 %all-gather.17.cloned.1.call-start = ((), (), s32[]{:S(2)}) async-start(), calls=%async_computation.18 | async-start | bytes 5406720 | tf_op jit(solution)/shard_map/all_gather | solution.py:172
  25.9 118.5 %copy-start.141 = (f32[2048,1]{0,1:T(1,128)}, f32[2048,1]{0,1:T(1,128)S(1)}, u32[]{:S(2)}) copy-start(f32[2048,1]{0,1:T(1,128)S(1)} %get-tuple-element.343) | copy-start | bytes 24580
  26.4 119.5 %copy-start.158 = (f32[1024,1]{0,1:T(1,128)}, f32[1024,1]{0,1:T(1,128)S(1)}, u32[]{:S(2)}) copy-start(f32[1024,1]{0,1:T(1,128)S(1)} %get-tuple-element.378) | copy-start | bytes 12292
  26.9 120.0 %copy-start.170 = (f32[512,1]{0,1:T(1,128)}, f32[512,1]{0,1:T(1,128)S(1)}, u32[]{:S(2)}) copy-start(f32[512,1]{0,1:T(1,128)S(1)} %get-tuple-element.380) | copy-start | bytes 6148
  27.4 120.3 %copy-start.180 = (f32[256,1]{0,1:T(1,128)}, f32[256,1]{0,1:T(1,128)S(1)}, u32[]{:S(2)}) copy-start(f32[256,1]{0,1:T(1,128)S(1)} %get-tuple-element.382) | copy-start | bytes 3076
  27.8 120.3 %copy-start.184 = (f32[128]{0:T(128)}, f32[128]{0:T(128)S(1)}, u32[]{:S(2)}) copy-start(f32[128]{0:T(128)S(1)} %get-tuple-element.396) | copy-start | bytes 1540
  28.2 120.3 %copy-start.186 = (f32[64]{0:T(128)}, f32[64]{0:T(128)S(1)}, u32[]{:S(2)}) copy-start(f32[64]{0:T(128)S(1)} %get-tuple-element.394) | copy-start | bytes 772
  28.4 120.2 %copy-start.188 = (f32[32]{0:T(128)}, f32[32]{0:T(128)S(1)}, u32[]{:S(2)}) copy-start(f32[32]{0:T(128)S(1)} %get-tuple-element.392) | copy-start | bytes 388
  28.7 120.2 %copy-start.190 = (f32[16]{0:T(128)}, f32[16]{0:T(128)S(1)}, u32[]{:S(2)}) copy-start(f32[16]{0:T(128)S(1)} %get-tuple-element.390) | copy-start | bytes 196
  28.9 120.2 %copy-start.191 = (f32[8]{0:T(128)}, f32[8]{0:T(128)S(1)}, u32[]{:S(2)}) copy-start(f32[8]{0:T(128)S(1)} %get-tuple-element.388) | copy-start | bytes 100
  30.9 68.1 %copy-start.118 = (pred[128,128]{1,0:T(8,128)(4,1)}, pred[128,128]{1,0:T(8,128)(4,1)S(1)}, u32[]{:S(2)}) copy-start(pred[128,128]{1,0:T(8,128)(4,1)S(1)} %fusion.78) | copy-start | bytes 49156
  34.7 61.3 %copy-start.120 = (f32[128,16]{0,1:T(8,128)}, f32[128,16]{0,1:T(8,128)S(1)}, u32[]{:S(2)}) copy-start(f32[128,16]{0,1:T(8,128)S(1)} %get-tuple-element.201) | copy-start | bytes 24580
  38.7 94.6 %copy-start.19 = (f32[129,128,16]{1,2,0:T(8,128)}, f32[129,128,16]{1,2,0:T(8,128)S(1)}, u32[]{:S(2)}) copy-start(f32[129,128,16]{1,2,0:T(8,128)S(1)} %get-tuple-element.316) | copy-start | bytes 3170308
  38.7 152.9 %copy-start.5 = (f32[129,128,16]{1,2,0:T(8,128)}, f32[129,128,16]{1,2,0:T(8,128)S(1)}, u32[]{:S(2)}) copy-start(f32[129,128,16]{1,2,0:T(8,128)S(1)} %get-tuple-element.317) | copy-start | bytes 3170308
  133.9 61.5 %copy-start.76 = (f32[128,16]{0,1:T(8,128)}, f32[128,16]{0,1:T(8,128)S(1)}, u32[]{:S(2)}) copy-start(f32[128,16]{0,1:T(8,128)S(1)} %get-tuple-element.196) | copy-start | bytes 24580
  173.3 41.1 %copy-start = (f32[32,128,128]{1,0,2:T(8,128)}, f32[32,128,128]{1,0,2:T(8,128)S(1)}, u32[]{:S(2)}) copy-start(f32[32,128,128]{1,0,2:T(8,128)S(1)} %fusion.17) | copy-start | bytes 6291460
  179.3 29.6 %copy-start.50 = (f32[128,32,16]{0,2,1:T(8,128)}, f32[128,32,16]{0,2,1:T(8,128)S(1)}, u32[]{:S(2)}) copy-start(f32[128,32,16]{0,2,1:T(8,128)S(1)} %copy.508) | copy-start | bytes 786436
  201.4 29.7 %copy-start.59 = (f32[15,128,16]{1,2,0:T(8,128)}, f32[15,128,16]{1,2,0:T(8,128)S(1)}, u32[]{:S(2)}) copy-start(f32[15,128,16]{1,2,0:T(8,128)S(1)} %get-tuple-element.179) | copy-start | bytes 368644
  201.4 29.7 %copy-start.61 = (f32[15,128,16]{1,2,0:T(8,128)}, f32[15,128,16]{1,2,0:T(8,128)S(1)}, u32[]{:S(2)}) copy-start(f32[15,128,16]{1,2,0:T(8,128)S(1)} %get-tuple-element.180) | copy-start | bytes 368644
  241.0 290.5 %copy-start.4 = (f32[32,128,128]{1,0,2:T(8,128)}, f32[32,128,128]{1,0,2:T(8,128)S(1)}, u32[]{:S(2)}) copy-start(f32[32,128,128]{1,0,2:T(8,128)S(1)} %add_bitcast_fusion.1) | copy-start | bytes 6291460
  257.7 64.5 %copy-start.163 = (f32[1,512]{1,0:T(1,128)S(1)}, f32[1,512]{1,0:T(1,128)}, u32[]{:S(2)}) copy-start(f32[1,512]{1,0:T(1,128)} %copy-done.162) | copy-start | bytes 6148
  257.7 58.9 %all-to-all-start.1 = ((bf16[8,512,128]{1,2,0:T(8,128)(2,1)}), bf16[8,512,128]{1,2,0:T(8,128)(2,1)S(1)}, u32[]{:S(2)}, u32[]{:S(2)}) async-start(bf16[8,512,128]{1,2,0:T(8,128)(2,1)} %multiply_convert_fusion.6), calls=%async_computation.1 | async-start | bytes 2097152 | tf_op jit(solution)/shard_map/all_to_all | solution.py:151
  316.6 63.6 %copy-start.45 = (bf16[8,512,128]{1,2,0:T(8,128)(2,1)}, bf16[8,512,128]{1,2,0:T(8,128)(2,1)S(1)}, u32[]{:S(2)}) copy-start(bf16[8,512,128]{1,2,0:T(8,128)(2,1)S(1)} %all-to-all-done.1) | copy-start | bytes 3145732
  316.6 64.7 %all-to-all-start.2 = ((bf16[8,512,128]{1,2,0:T(8,128)(2,1)}), bf16[8,512,128]{1,2,0:T(8,128)(2,1)}, u32[]{:S(2)}, u32[]{:S(2)}) async-start(bf16[8,512,128]{1,2,0:T(8,128)(2,1)} %get-tuple-element.176), calls=%async_computation.2 | async-start | bytes 2097152 | tf_op jit(solution)/shard_map/all_to_all | solution.py:150
  322.1 851.2 %reduce-scatter.8.cloned.1.call-start = ((), (), s32[]{:S(2)}) async-start(), calls=%async_computation.19 | async-start | bytes 1081344 | tf_op jit(solution)/shard_map/reduce_scatter | solution.py:317
  472.9 700.4 %reduce-scatter.14.cloned.1.call-start = ((), (), s32[]{:S(2)}) async-start(), calls=%async_computation.22 | async-start | bytes 8650752 | tf_op jit(solution)/shard_map/reduce_scatter | solution.py:320
  481.0 692.3 %reduce-scatter.12.cloned.1.call-start = ((), (), s32[]{:S(2)}) async-start(), calls=%async_computation.21 | async-start | bytes 8650752 | tf_op jit(solution)/shard_map/reduce_scatter | solution.py:319
  488.6 684.7 %reduce-scatter.10.cloned.1.call-start = ((), (), s32[]{:S(2)}) async-start(), calls=%async_computation.20 | async-start | bytes 8650752 | tf_op jit(solution)/shard_map/reduce_scatter | solution.py:318
  502.0 713.9 %reduce-scatter.16.cloned.1.call-start = ((), (), s32[]{:S(2)}) async-start(), calls=%async_computation.23 | async-start | bytes 10813440 | tf_op jit(solution)/shard_map/reduce_scatter | solution.py:321
  510.6 857.0 %reduce-scatter.18.cloned.1.call-start = ((), (), s32[]{:S(2)}) async-start(), calls=%async_computation.24 | async-start | bytes 10813440 | tf_op jit(solution)/shard_map/reduce_scatter | solution.py:322
  524.9 31.8 %all-to-all-start.4 = ((bf16[512,8,128]{0,2,1:T(8,128)(2,1)}), bf16[512,8,128]{0,2,1:T(8,128)(2,1)S(1)}, u32[]{:S(2)}, u32[]{:S(2)}) async-start(bf16[512,8,128]{0,2,1:T(8,128)(2,1)} %bitcast.310), calls=%async_computation.4 | async-start | bytes 2097152 | tf_op jit(solution)/shard_map/all_to_all | solution.py:288
  529.6 989.7 %reduce-scatter.20.cloned.1.call-start = ((), (), s32[]{:S(2)}) async-start(), calls=%async_computation.25 | async-start | bytes 10813440 | tf_op jit(solution)/shard_map/reduce_scatter | solution.py:323
  557.7 230.6 %all-to-all-start.3 = ((bf16[512,8,128]{0,2,1:T(8,128)(2,1)}), bf16[512,8,128]{0,2,1:T(8,128)(2,1)S(1)}, u32[]{:S(2)}, u32[]{:S(2)}) async-start(bf16[512,8,128]{0,2,1:T(8,128)(2,1)} %bitcast.45), calls=%async_computation.3 | async-start | bytes 2097152 | tf_op jit(solution)/shard_map/all_to_all | solution.py:287
  589.1 23.1 %copy-start.70 = (f32[8,128,16]{1,2,0:T(8,128)S(1)}, f32[8,128,16]{1,2,0:T(8,128)}, u32[]{:S(2)}) copy-start(f32[8,128,16]{1,2,0:T(8,128)} %copy-done.69) | copy-start | bytes 196612
  589.1 23.1 %copy-start.72 = (f32[8,128,16]{1,2,0:T(8,128)S(1)}, f32[8,128,16]{1,2,0:T(8,128)}, u32[]{:S(2)}) copy-start(f32[8,128,16]{1,2,0:T(8,128)} %copy-done.71) | copy-start | bytes 196612
  590.1 57.2 %copy-start.56 = (f32[16,128,16]{1,2,0:T(8,128)S(1)}, f32[16,128,16]{1,2,0:T(8,128)}, u32[]{:S(2)}) copy-start(f32[16,128,16]{1,2,0:T(8,128)} %copy-done.55) | copy-start | bytes 393220
  647.3 59.2 %copy-start.51 = (f32[128,32,16]{0,2,1:T(8,128)S(1)}, f32[128,32,16]{0,2,1:T(8,128)}, u32[]{:S(2)}) copy-start(f32[128,32,16]{0,2,1:T(8,128)} %copy-done.50) | copy-start | bytes 786436
  708.8 32.5 %slice-start.1 = ((f32[16,128,16]{1,2,0:T(8,128)}), f32[1,128,16]{1,2,0:T(8,128)S(1)}, s32[]{:S(2)}) async-start(f32[16,128,16]{1,2,0:T(8,128)} %copy-done.85), calls=%async_computation.27 | async-start | bytes 16384 | tf_op jit(solution)/shard_map/transpose(jvp())/split | solution.py:71
  719.5 38.2 %slice-start = ((f32[16,128,16]{1,2,0:T(8,128)}), f32[1,128,16]{1,2,0:T(8,128)S(1)}, s32[]{:S(2)}) async-start(f32[16,128,16]{1,2,0:T(8,128)} %copy-done.84), calls=%async_computation.26 | async-start | bytes 16384 | tf_op jit(solution)/shard_map/transpose(jvp())/split | solution.py:71
  724.9 19.0 %copy-start.81 = (f32[16,128,16]{1,2,0:T(8,128)S(1)}, f32[16,128,16]{1,2,0:T(8,128)}, u32[]{:S(2)}) copy-start(f32[16,128,16]{1,2,0:T(8,128)} %get-tuple-element.231) | copy-start | bytes 393220
  799.3 17.8 %copy-start.187 = (f32[64]{0:T(128)S(1)}, f32[64]{0:T(128)}, u32[]{:S(2)}) copy-start(f32[64]{0:T(128)} %copy-done.186) | copy-start | bytes 772
  799.3 18.3 %copy-start.185 = (f32[128]{0:T(128)S(1)}, f32[128]{0:T(128)}, u32[]{:S(2)}) copy-start(f32[128]{0:T(128)} %copy-done.184) | copy-start | bytes 1540
  799.3 18.9 %copy-start.181 = (f32[256,1]{0,1:T(1,128)S(1)}, f32[256,1]{0,1:T(1,128)}, u32[]{:S(2)}) copy-start(f32[256,1]{0,1:T(1,128)} %copy-done.180) | copy-start | bytes 3076
  799.3 19.9 %copy-start.171 = (f32[512,1]{0,1:T(1,128)S(1)}, f32[512,1]{0,1:T(1,128)}, u32[]{:S(2)}) copy-start(f32[512,1]{0,1:T(1,128)} %copy-done.170) | copy-start | bytes 6148
  799.5 21.2 %copy-start.159 = (f32[1024,1]{0,1:T(1,128)S(1)}, f32[1024,1]{0,1:T(1,128)}, u32[]{:S(2)}) copy-start(f32[1024,1]{0,1:T(1,128)} %copy-done.158) | copy-start | bytes 12292
  801.6 21.7 %copy-start.142 = (f32[2048,1]{0,1:T(1,128)S(1)}, f32[2048,1]{0,1:T(1,128)}, u32[]{:S(2)}) copy-start(f32[2048,1]{0,1:T(1,128)} %copy-done.141) | copy-start | bytes 24580
  845.7 321.4 %all-to-all-start.5 = ((f32[8,512,128]{1,2,0:T(8,128)}), f32[8,512,128]{1,2,0:T(8,128)}, u32[]{:S(2)}, u32[]{:S(2)}) async-start(f32[8,512,128]{1,2,0:T(8,128)} %fusion.16), calls=%async_computation.5 | async-start | bytes 4194304 | tf_op jit(solution)/shard_map/all_to_all | solution.py:291
  851.7 92.3 %copy-start.80 = (f32[16,128,16]{1,2,0:T(8,128)S(1)}, f32[16,128,16]{1,2,0:T(8,128)}, u32[]{:S(2)}) copy-start(f32[16,128,16]{1,2,0:T(8,128)} %get-tuple-element.129) | copy-start | bytes 393220
  859.5 122.8 %copy-start.25 = (f32[128,32,16]{1,2,0:T(8,128)S(1)}, f32[128,32,16]{1,2,0:T(8,128)}, u32[]{:S(2)}) copy-start(f32[128,32,16]{1,2,0:T(8,128)} %copy.530) | copy-start | bytes 786436
  1034.0 110.2 %copy-start.20 = (f32[129,128,16]{1,2,0:T(8,128)S(1)}, f32[129,128,16]{1,2,0:T(8,128)}, u32[]{:S(2)}) copy-start(f32[129,128,16]{1,2,0:T(8,128)} %copy-done.19) | copy-start | bytes 3170308
  1034.0 110.2 %copy-start.43 = (f32[128,128,16]{0,2,1:T(8,128)S(1)}, f32[128,128,16]{0,2,1:T(8,128)}, u32[]{:S(2)}) copy-start(f32[128,128,16]{0,2,1:T(8,128)} %copy.552) | copy-start | bytes 3145732
  1034.0 110.2 %copy-start.133 = (f32[128,16]{0,1:T(8,128)S(1)}, f32[128,16]{0,1:T(8,128)}, u32[]{:S(2)}) copy-start(f32[128,16]{0,1:T(8,128)} %param.40) | copy-start | bytes 24580
  1034.0 110.2 %copy-start.154 = (f32[128,16]{0,1:T(8,128)S(1)}, f32[128,16]{0,1:T(8,128)}, u32[]{:S(2)}) copy-start(f32[128,16]{0,1:T(8,128)} %copy-done.153) | copy-start | bytes 24580
  1043.5 100.7 %copy-start.6 = (f32[129,128,16]{1,2,0:T(8,128)S(1)}, f32[129,128,16]{1,2,0:T(8,128)}, u32[]{:S(2)}) copy-start(f32[129,128,16]{1,2,0:T(8,128)} %copy-done.5) | copy-start | bytes 3170308
  (185 other events, 763.5 us)
Sparse Core Ops, SparseCore 0:
  11.5 70.4 all-gather.6
  85.4 60.5 all-gather.8
  148.9 60.6 all-gather.10
  212.8 80.3 all-gather.12
  296.5 72.2 all-gather.14
  372.1 64.3 all-gather.16
  473.0 136.3 reduce-scatter.7
  612.3 144.7 reduce-scatter.13
  760.1 154.4 reduce-scatter.11
  917.4 146.7 reduce-scatter.9
  1067.2 148.6 reduce-scatter.15
  1218.7 148.8 reduce-scatter.17
  1370.5 148.6 reduce-scatter.19
where the time goes:
time: 1550 us; the launch traced here: 1530 us
  local copies, waits for them, and re-layouts  442 us (29%)
  waiting for transfers between devices  365 us (24%)
  matrix products  234 us (15%)
  other arithmetic  224 us (14%)
  blocking collectives  200 us (13%)
  starting transfers between devices  33.9 us (2%)
  between operations  19.8 us (1%)
    pad x64, local copies, waits for them, and re-layouts, ema_blocked(): lax.associative_scan(complex_combine, (hop_re, hop_im, ends_re, ends_im),...  190 us
    reduce_scatter x1, waiting for transfers between devices, on_device(): lax.psum_scatter(grad_w_up, ('seq', 'dp'), scatter_dimension=0, tiled=True)  152 us
    reduce_scatter x1, waiting for transfers between devices, on_device(): lax.psum_scatter(grad_w_down, ('seq', 'dp'), scatter_dimension=0, tiled=T...  152 us
    unnamed x2, blocking collectives  128 us
    scatter-add x1, other arithmetic, ema_blocked(): jnp.take(kernel, jnp.clip(lag, 0, span - 1), axis=0)  98.4 us
    all_gather x1, blocking collectives, on_device(): lax.all_gather(w_z.astype(bf16), ('seq', 'dp'), axis=0, tiled=True)  57.5 us
    gather x1, local copies, waits for them, and re-layouts, ema_blocked(): jnp.take(kernel, jnp.clip(lag, 0, span - 1), axis=0)  55 us
    dot_general x3, matrix products, ema_blocked(): inner = jnp.einsum('ijc,bjc->bic', toeplitz, blocks, precision=highest)  44.2 us
  transfers between devices with their start and end apart: 19, of which 5 were waited for; matrix products, arithmetic and copies ran while one was open for 56% of the time, Pallas kernels for 0%

commit v1 on v0

v1 whole, which is shorter than its diff:
```python
import functools
import math

import jax
import jax.numpy as jnp
from jax import lax
from jax.experimental import pallas as pl
from jax.experimental.pallas import tpu as pltpu
from jax.sharding import PartitionSpec as P

GROUP = 64
DOCS = 16
LANES = 128
SUB = 8
SPAN = 32
BAND = 64
bf16 = jnp.bfloat16
f32 = jnp.float32
VMEM_LIMIT = 60 * 1024 * 1024


def split3(value):
    first = value.astype(bf16)
    rest = value - first.astype(f32)
    second = rest.astype(bf16)
    third = (rest - second.astype(f32)).astype(bf16)
    return first, second, third


def dot(left, right):
    return jnp.dot(left, right, preferred_element_type=f32)


def dot3(left, parts):
    return dot(left, parts[0]) + dot(left, parts[1]) + dot(left, parts[2])


def dot3_left(parts, right):
    return dot(parts[0], right) + dot(parts[1], right) + dot(parts[2], right)


def iota(shape, axis):
    return lax.broadcasted_iota(jnp.int32, shape, axis)


def group_pick(width, shift):
    own = lax.shift_right_logical(iota((width, LANES), 0), GROUP.bit_length() - 1)
    return (own + shift == iota((width, LANES), 1)).astype(bf16)


def group_spread(groups, width):
    own = lax.shift_right_logical(iota((groups, width), 1), GROUP.bit_length() - 1)
    return (own == iota((groups, width), 0)).astype(bf16)


ANY = pl.BlockSpec(memory_space=pl.ANY)
VM = pl.BlockSpec(memory_space=pltpu.VMEM)
SM = pl.BlockSpec(memory_space=pltpu.SMEM)


def kernel_call(body, outs, args, specs=None, scratch=(), name=None, micros=10, after=(), grid=None, out_specs=None):
    specs = [VM] * len(args) if specs is None else specs
    count = len(args)

    def run(*refs):
        body(*refs[:count], *refs[count + len(after) :])

    more = {} if grid is None else dict(grid=grid, out_specs=tuple(out_specs))
    return pl.pallas_call(
        run,
        out_shape=tuple(jax.ShapeDtypeStruct(shape, dtype) for shape, dtype in outs),
        in_specs=list(specs) + [ANY] * len(after),
        scratch_shapes=list(scratch),
        compiler_params=pltpu.CompilerParams(vmem_limit_bytes=VMEM_LIMIT),
        cost_estimate=pl.CostEstimate(
            flops=int(micros * 1.0e9), bytes_accessed=int(micros * 3.0e6), transcendentals=0
        ),
        name=name,
        **more,
    )(*args, *after)


def tie(value, *after):
    def nothing(*refs):
        return None

    return pl.pallas_call(
        nothing,
        out_shape=jax.ShapeDtypeStruct(value.shape, value.dtype),
        in_specs=[ANY] * (1 + len(after)),
        out_specs=ANY,
        input_output_aliases={0: 0},
        name="tie",
    )(value, *after)


def split_wide(value):
    return jnp.concatenate(split3(value), axis=1)


def spread_wide(groups, width, start):
    own = lax.shift_right_logical(iota((3 * groups, LANES), 1) + start, GROUP.bit_length() - 1)
    return (own == lax.rem(iota((3 * groups, LANES), 0), groups)).astype(bf16)


def moments(total, groups):
    counts = jnp.maximum(total[:, 2 * groups : 2 * groups + 1], 1.0) * float(GROUP)
    means = total[:, :groups] / counts
    variance = total[:, groups : 2 * groups] / counts - means * means
    return means, lax.rsqrt(variance + 1e-05), counts


def stats_kernel(tok_ref, valid_ref, segc_ref, segr_ref, prefix_ref, totals_ref):
    rows, width = tok_ref.shape
    groups = width // GROUP
    valid = valid_ref[...]
    masked = tok_ref[...].astype(f32) * valid
    low = masked.astype(bf16)
    square = masked * masked
    high = square.astype(bf16)
    rest = (square - high.astype(f32)).astype(bf16)
    second = group_pick(width, groups)
    sums = dot(low, group_pick(width, 0)) + dot(high, second) + dot(rest, second)
    sums = sums + jnp.where(iota((rows, LANES), 1) == 2 * groups, valid, 0.0)
    parts = split3(sums)
    earlier = (iota((rows, rows), 1) <= iota((rows, rows), 0)) & (segc_ref[...] == segr_ref[...])
    prefix_ref[...] = dot3(earlier.astype(f32).astype(bf16), parts)
    member = (iota((DOCS, rows), 0) == segr_ref[...]).astype(f32).astype(bf16)
    totals_ref[...] = dot3(member, parts)


def scan_ends(src_ref, a_ref, b_ref, end_ref, rows, ndim, reverse):
    half = ndim // 2
    for start in range(0, ndim, half):
        a = [a_ref[pl.ds((start + n) * SUB, SUB), :] for n in range(half)]
        b = [b_ref[pl.ds((start + n) * SUB, SUB), :] for n in range(half)]

        def step(i, state, a=a, b=b):
            t = rows - 1 - i if reverse else i
            x = src_ref[pl.ds(pl.multiple_of(t * SUB, SUB), SUB), :]
            fresh = []
            for n in range(half):
                re, im = state[2 * n], state[2 * n + 1]
                if reverse:
                    fresh += [a[n] * re + b[n] * im + x, a[n] * im - b[n] * re]
                else:
                    fresh += [a[n] * re - b[n] * im + x, a[n] * im + b[n] * re]
            return tuple(fresh)

        zero = jnp.zeros((SUB, LANES), f32)
        state = lax.fori_loop(0, rows, step, (zero,) * (2 * half), unroll=8)
        for n in range(half):
            end_ref[pl.ds((start + n) * SUB, SUB), :] = state[2 * n]
            end_ref[pl.ds((ndim + start + n) * SUB, SUB), :] = state[2 * n + 1]


def all_moments(prefix_ref, segc_ref, carry_ref, groups):
    total = prefix_ref[...] + jnp.where(segc_ref[...] == segc_ref[0:1, :], carry_ref[...], 0.0)
    return moments(total, groups)


def lane_rows(j, rows):
    return pl.ds(j, rows, stride=SUB)


def norm_kernel(tok_ref, valid_ref, segc_ref, prefix_ref, carry_ref, gain_ref, a_ref, b_ref,
                sent_ref, xs_ref, end_ref):
    rows, width = tok_ref.shape
    groups = width // GROUP
    ndim = a_ref.shape[0] // SUB
    means, scale, _ = all_moments(prefix_ref, segc_ref, carry_ref, groups)
    means, scale, valid = split_wide(means), split_wide(scale), valid_ref[...]
    for j in range(SUB):
        at = slice(j * LANES, (j + 1) * LANES)
        spread = spread_wide(groups, width, j * LANES)
        normed = (tok_ref[:, at].astype(f32) * valid - dot(means, spread)) * dot(scale, spread) * gain_ref[:, at]
        sent_ref[:, at] = normed.astype(bf16)
        xs_ref[lane_rows(j, rows), :] = normed
    scan_ends(xs_ref, a_ref, b_ref, end_ref, rows, ndim, False)


def mix_kernel(xs_ref, start_ref, a_ref, b_ref, g_ref, skip_ref, mixed_ref, sent_ref, keep_ref, state_ref):
    rows = xs_ref.shape[0] // SUB
    ndim = a_ref.shape[0] // SUB
    half = ndim // 2
    state_ref[...] = start_ref[...]

    def chunk(i, _):
        keep_ref[i] = state_ref[...]
        for start in range(0, ndim, half):
            re_at = [pl.ds((start + n) * SUB, SUB) for n in range(half)]
            im_at = [pl.ds((ndim + start + n) * SUB, SUB) for n in range(half)]
            a = [a_ref[at, :] for at in re_at]
            b = [b_ref[at, :] for at in re_at]
            g = [g_ref[at, :] for at in re_at]

            def step(k, state, start=start, a=a, b=b, g=g):
                at = pl.ds(pl.multiple_of((i * SPAN + k) * SUB, SUB), SUB)
                x = xs_ref[at, :]
                fresh, terms = [], []
                for n in range(half):
                    re, im = state[2 * n], state[2 * n + 1]
                    now = a[n] * re - b[n] * im + x
                    fresh += [now, a[n] * im + b[n] * re]
                    terms.append(g[n] * now)
                terms.append(skip_ref[...] * x if start == 0 else mixed_ref[at, :])
                while len(terms) > 1:
                    terms = [sum(terms[p : p + 2][1:], terms[p]) for p in range(0, len(terms), 2)]
                mixed_ref[at, :] = terms[0]
                return tuple(fresh)

            state = []
            for n in range(half):
                state += [state_ref[re_at[n], :], state_ref[im_at[n], :]]
            state = lax.fori_loop(0, SPAN, step, tuple(state), unroll=8)
            for n in range(half):
                state_ref[re_at[n], :] = state[2 * n]
                state_ref[im_at[n], :] = state[2 * n + 1]
        return 0

    lax.fori_loop(0, rows // SPAN, chunk, 0)

    def band(i, _):
        at = pl.ds(pl.multiple_of(i * BAND, BAND), BAND)
        for j in range(SUB):
            mixed = mixed_ref[pl.ds(i * (BAND * SUB) + j, BAND, stride=SUB), :]
            sent_ref[at, j * LANES : (j + 1) * LANES] = (mixed * jax.nn.sigmoid(mixed)).astype(bf16)
        return 0

    lax.fori_loop(0, rows // BAND, band, 0)


def back_ends_kernel(grad_ref, mixed_ref, a_ref, b_ref, drive_ref, end_ref):
    rows = grad_ref.shape[0]
    ndim = a_ref.shape[0] // SUB

    def band(i, _):
        at = pl.ds(pl.multiple_of(i * BAND, BAND), BAND)
        for j in range(SUB):
            where = pl.ds(i * (BAND * SUB) + j, BAND, stride=SUB)
            mixed = mixed_ref[where, :]
            sigma = jax.nn.sigmoid(mixed)
            slope = sigma * (1.0 + mixed * (1.0 - sigma))
            drive_ref[where, :] = grad_ref[at, j * LANES : (j + 1) * LANES].astype(f32) * slope
        return 0

    lax.fori_loop(0, rows // BAND, band, 0)
    scan_ends(drive_ref, a_ref, b_ref, end_ref, rows, ndim, True)


def back_scan_kernel(xs_ref, drive_ref, keep_ref, start_ref, sums_in_ref, a_ref, b_ref, g_ref, skip_ref,
                     dxs_ref, state_ref, sums_ref, hist_ref):
    ndim = a_ref.shape[0] // SUB
    rows = xs_ref.shape[0] // SUB
    part = 4
    count = rows // SPAN
    state_ref[...] = start_ref[...]
    sums_ref[...] = sums_in_ref[...]

    def chunk(c, _):
        i = count - 1 - c
        for start in range(0, ndim, part):
            re_at = [pl.ds((start + n) * SUB, SUB) for n in range(part)]
            im_at = [pl.ds((ndim + start + n) * SUB, SUB) for n in range(part)]
            last_at = [pl.ds((2 * ndim + start + n) * SUB, SUB) for n in range(part)]
            a = [a_ref[at, :] for at in re_at]
            b = [b_ref[at, :] for at in re_at]
            g = [g_ref[at, :] for at in re_at]

            def forward(k, state, a=a, b=b):
                x = xs_ref[pl.ds(pl.multiple_of((i * SPAN + k) * SUB, SUB), SUB), :]
                fresh = []
                for n in range(part):
                    re, im = state[2 * n], state[2 * n + 1]
                    hist_ref[k, pl.ds(2 * n * SUB, SUB), :] = re
                    hist_ref[k, pl.ds((2 * n + 1) * SUB, SUB), :] = im
                    fresh += [a[n] * re - b[n] * im + x, a[n] * im + b[n] * re]
                return tuple(fresh)

            state = []
            for n in range(part):
                state += [keep_ref[i, re_at[n], :], keep_ref[i, im_at[n], :]]
            lax.fori_loop(0, SPAN, forward, tuple(state), unroll=8)

            def backward(k, held, start=start, a=a, b=b, g=g):
                t = SPAN - 1 - k
                at = pl.ds(pl.multiple_of((i * SPAN + t) * SUB, SUB), SUB)
                x, drive = xs_ref[at, :], drive_ref[at, :]
                fresh, terms = [], []
                for n in range(part):
                    re, im, m_re, m_im, same = held[5 * n : 5 * n + 5]
                    now_re = a[n] * re + b[n] * im + drive
                    now_im = a[n] * im - b[n] * re
                    old_re = hist_ref[t, pl.ds(2 * n * SUB, SUB), :]
                    old_im = hist_ref[t, pl.ds((2 * n + 1) * SUB, SUB), :]
                    fresh += [
                        now_re,
                        now_im,
                        m_re + (now_re * old_re + now_im * old_im),
                        m_im + (now_im * old_re - now_re * old_im),
                        same + x * now_re,
                    ]
                    terms.append(g[n] * now_re)
                total = (terms[0] + terms[1]) + (terms[2] + terms[3])
                if start == 0:
                    dxs_ref[at, :] = total + skip_ref[...] * drive
                else:
                    dxs_ref[at, :] = total + dxs_ref[at, :]
                return tuple(fresh)

            held = []
            for n in range(part):
                held += [state_ref[re_at[n], :], state_ref[im_at[n], :]]
                held += [sums_ref[re_at[n], :], sums_ref[im_at[n], :], sums_ref[last_at[n], :]]
            held = lax.fori_loop(0, SPAN, backward, tuple(held), unroll=8)
            for n in range(part):
                state_ref[re_at[n], :] = held[5 * n]
                state_ref[im_at[n], :] = held[5 * n + 1]
                sums_ref[re_at[n], :] = held[5 * n + 2]
                sums_ref[im_at[n], :] = held[5 * n + 3]
                sums_ref[last_at[n], :] = held[5 * n + 4]
        return 0

    lax.fori_loop(0, count, chunk, 0)

    def skip_step(k, total):
        at = pl.ds(pl.multiple_of(k * SUB, SUB), SUB)
        return total + xs_ref[at, :] * drive_ref[at, :]

    last = pl.ds(3 * ndim * SUB, SUB)
    sums_ref[last, :] = lax.fori_loop(0, rows, skip_step, sums_ref[last, :], unroll=8)


def back_norm_kernel(*refs):
    dxs_refs, refs = refs[:-12], refs[-12:]
    (grad_ref, tok_ref, valid_ref, segc_ref, segr_ref, prefix_ref, carry_ref, gain_ref,
     dn_ref, dgain_ref, suffix_ref, totals_ref) = refs
    rows, width = tok_ref.shape
    groups = width // GROUP
    means, scale, counts = all_moments(prefix_ref, segc_ref, carry_ref, groups)
    wide_means, wide_scale, valid = split_wide(means), split_wide(scale), valid_ref[...]
    plain, leaning = jnp.zeros((rows, LANES), f32), jnp.zeros((rows, LANES), f32)
    for j in range(SUB):
        at = slice(j * LANES, (j + 1) * LANES)
        spread = spread_wide(groups, width, j * LANES)
        own = lax.shift_right_logical(iota((LANES, LANES), 0) + j * LANES, GROUP.bit_length() - 1)
        pick = (own == iota((LANES, LANES), 1)).astype(bf16)
        centred = tok_ref[:, at].astype(f32) * valid - dot(wide_means, spread)
        ema = [ref[lane_rows(j, ref.shape[0] // SUB), :] for ref in dxs_refs]
        dn = grad_ref[:, at].astype(f32) + jnp.concatenate(ema, axis=0)
        dgain_ref[:, at] = jnp.sum(dn * centred * dot(wide_scale, spread), axis=0, keepdims=True)
        dn = dn * gain_ref[:, at]
        dn_ref[:, at] = dn
        plain = plain + dot3_left(split3(dn), pick)
        leaning = leaning + dot3_left(split3(dn * centred), pick)
    plain, leaning = plain[:, :groups], leaning[:, :groups]
    d_variance = -0.5 * leaning * scale * scale * scale
    d_second = d_variance / counts
    d_first = (-scale * plain - 2.0 * means * d_variance) / counts
    flow = jnp.concatenate([d_first, d_second, jnp.zeros((rows, LANES - 2 * groups), f32)], axis=1)
    parts = split3(flow)
    later = (iota((rows, rows), 1) >= iota((rows, rows), 0)) & (segc_ref[...] == segr_ref[...])
    suffix_ref[...] = dot3(later.astype(f32).astype(bf16), parts)
    member = (iota((DOCS, rows), 0) == segr_ref[...]).astype(f32).astype(bf16)
    totals_ref[...] = dot3(member, parts)


def input_kernel(dn_ref, suffix_ref, back_ref, tok_ref, valid_ref, segc_ref, prefix_ref, carry_ref, middle_ref, out_ref):
    rows, width = tok_ref.shape
    groups = width // GROUP
    _, scale, _ = all_moments(prefix_ref, segc_ref, carry_ref, groups)
    flow = suffix_ref[...] + jnp.where(segc_ref[...] == segc_ref[rows - 1 : rows, :], back_ref[...], 0.0)
    scale, valid = split_wide(scale), valid_ref[...]
    first, second = split_wide(flow[:, :groups]), split_wide(flow[:, groups : 2 * groups])
    for j in range(SUB):
        at = slice(j * LANES, (j + 1) * LANES)
        spread = spread_wide(groups, width, j * LANES)
        masked = tok_ref[:, at].astype(f32) * valid
        grad = dn_ref[:, at] * dot(scale, spread) + dot(first, spread) + 2.0 * masked * dot(second, spread)
        out_ref[:, at] = valid * (middle_ref[:, at] + grad)


def swap(value, axis, bit):
    count = lax.axis_size(axis)
    return lax.ppermute(value, axis, [(i, i ^ bit) for i in range(count)])


def gather_small(value, axis):
    index, count = lax.axis_index(axis), lax.axis_size(axis)
    value, bit = value[None], 1
    while bit < count:
        other = swap(value, axis, bit)
        upper = (index & bit) != 0
        value = jnp.concatenate([jnp.where(upper, other, value), jnp.where(upper, value, other)], axis=0)
        bit *= 2
    return value


def cmul(left, right):
    return (left[0] * right[0] - left[1] * right[1], left[0] * right[1] + left[1] * right[0])


def state_before(ends, hop, axis, reverse):
    index, count = lax.axis_index(axis), lax.axis_size(axis)
    if reverse:
        index = count - 1 - index
    half = ends.shape[0] // 2
    before = (jnp.zeros_like(ends[:half]), jnp.zeros_like(ends[:half]))
    reach = (jnp.ones_like(hop[0]), jnp.zeros_like(hop[1]))
    bit = 1
    while bit < count:
        other = swap(ends, axis, bit)
        upper = (index & bit) != 0
        far, own = (other[:half], other[half:]), (ends[:half], ends[half:])
        moved = cmul(reach, far)
        before = tuple(v + jnp.where(upper, w, 0.0) for v, w in zip(before, moved))
        if bit * 2 < count:
            lower = tuple(jnp.where(upper, v, w) for v, w in zip(far, own))
            higher = tuple(jnp.where(upper, w, v) for v, w in zip(far, own))
            carried = cmul(hop, lower)
            ends = jnp.concatenate([carried[0] + higher[0], carried[1] + higher[1]], axis=0)
            longer = cmul(reach, hop)
            reach = tuple(jnp.where(upper, v, w) for v, w in zip(longer, reach))
            hop = cmul(hop, hop)
        bit *= 2
    return jnp.concatenate(before, axis=0)


def ema_params(full, ndim, rows):
    full = jnp.transpose(full, (1, 0, 2))
    full = full.reshape(full.shape[0], SUB, -1)
    rate, angle, input_w, output_w = (full[i * ndim : (i + 1) * ndim] for i in range(4))
    gain, skip = full[4 * ndim], full[4 * ndim + 1]
    base = jnp.sqrt(rate * (2.0 - rate))
    cos, sin = jnp.cos(angle), jnp.sin(angle)
    a, b = (1.0 - rate) * cos, (1.0 - rate) * sin
    hop, steps = (a, b), 1
    while steps < rows:
        hop, steps = cmul(hop, hop), steps * 2
    return dict(rate=rate, input_w=input_w, output_w=output_w, gain=gain, skip=skip, base=base,
                cos=cos, sin=sin, a=a, b=b, coeff=base * input_w, hop=hop)


def ema_param_grads(par, sums):
    ndim = par["rate"].shape[0]
    m_re, m_im, same = sums[:ndim], sums[ndim : 2 * ndim], sums[2 * ndim : 3 * ndim]
    weight = par["output_w"] * par["coeff"]
    d_a, d_b = weight * m_re, weight * m_im
    d_coeff = par["output_w"] * same
    d_output = par["coeff"] * same
    d_input = par["base"] * d_coeff
    d_rate = d_coeff * par["input_w"] * (1.0 - par["rate"]) / par["base"] - par["cos"] * d_a - par["sin"] * d_b
    d_angle = par["a"] * d_b - par["b"] * d_a
    return d_rate, d_angle, d_input, d_output


def mul_t(left, right):
    return lax.dot_general(left, right, (((1,), (1,)), ((), ())), preferred_element_type=f32)


def t_mul(left, right):
    return lax.dot_general(left, right, (((0,), (0,)), ((), ())), preferred_element_type=f32)


def silu_grad(value):
    sigma = jax.nn.sigmoid(value)
    return sigma * (1.0 + value * (1.0 - sigma))


def bits_of(count):
    return count.bit_length() - 1


class Pieces:
    def __init__(self, arrays, owners):
        self.arrays, self.owners = arrays, owners

    def copies(self, refs, where, column, me, sem):
        made = []
        for ref, owners in zip(refs, self.owners):
            block = ref.shape[1]
            for slot, owner in enumerate(owners):
                start = pl.multiple_of((me ^ owner) * block, block)
                to = where.at[pl.ds(start, block), column : column + ref.shape[2]]
                made.append(pltpu.make_async_copy(ref.at[slot], to, sem))
        return made


class Columns:
    def __init__(self, parts, starts):
        self.parts, self.starts = parts, starts
        self.arrays = [array for part in parts for array in part.arrays]

    def copies(self, refs, where, me, sem):
        made, refs = [], list(refs)
        for part, start in zip(self.parts, self.starts):
            own = [refs.pop(0) for _ in part.arrays]
            made += part.copies(own, where, start, me, sem)
        return made


class Gather:
    def __init__(self, shard, order):
        self.order = order
        if order is None:
            full = lax.all_gather(shard, ("seq", "dp"), axis=0, tiled=True)
            self.arrays, self.owners = [full[None]], [[0]]
            return
        self.arrays, self.owners, self.place = [shard[None]], [[0]], 0

    def step(self, after=()):
        if self.order is None:
            return ()
        bit = self.order[self.place]
        mine = [tie(value, *after) for value in self.arrays] if after else self.arrays
        others = [swap_bit(value, bit) for value in mine]
        moved = [[owner ^ (1 << bit) for owner in row] for row in self.owners]
        if self.place < len(self.order) - 2:
            self.arrays = [jnp.concatenate([mine[0], others[0]], axis=0)]
            self.owners = [self.owners[0] + moved[0]]
        else:
            self.arrays, self.owners = mine + others, self.owners + moved
        self.place += 1
        return (self.arrays[-1],)

    @property
    def pieces(self):
        return Pieces(self.arrays, self.owners)


def swap_bit(value, bit):
    dp_bits = bits_of(lax.axis_size("dp"))
    if bit < dp_bits:
        return swap(value, "dp", 1 << bit)
    return swap(value, "seq", 1 << (bit - dp_bits))


class Reduce:
    def __init__(self, blocks, order):
        self.keep, self.send = blocks
        self.order = order
        self.left = list(order or ())
        self.other = None
        self.begin()

    def begin(self):
        if self.left:
            self.other = swap_bit(self.send, self.left.pop(0))

    def step(self):
        if self.order is None:
            return ()
        if not self.left:
            self.keep = self.keep.astype(f32) + self.other.astype(f32)
            return (self.keep,)
        half = self.keep.shape[0] // 2
        self.send = (self.keep[half:].astype(f32) + self.other[half:].astype(f32)).astype(bf16)
        self.keep = (self.keep[:half].astype(f32) + self.other[:half].astype(f32)).astype(bf16)
        self.begin()
        return (self.send,)

    def finish(self, core, widths):
        if self.order is None:
            outs, at = [], 0
            for width in widths:
                part = self.keep[0, :, at : at + width]
                zero = jnp.zeros_like(part)
                full = jnp.concatenate([jnp.where(core == 0, part, zero), jnp.where(core == 0, zero, part)], axis=1)
                outs.append(lax.psum_scatter(full, ("seq", "dp"), scatter_dimension=0, tiled=True).astype(f32))
                at += width
            return outs
        chip_rows = self.keep[0]
        rows = chip_rows.shape[0] // 2
        lower, upper = chip_rows[:rows], chip_rows[rows:]
        own = jnp.where(core == 0, lower, upper)
        other = swap_bit(jnp.where(core == 0, upper, lower).astype(bf16), 0).astype(f32)
        outs, at = [], 0
        for width in widths:
            mine, theirs = own[:, at : at + width], other[:, at : at + width]
            outs.append(
                jnp.concatenate([jnp.where(core == 0, mine, theirs), jnp.where(core == 0, theirs, mine)], axis=1)
            )
            at += width
        return outs


def allowed_pairs(segc_ref, segr_ref, validr_ref):
    rows = segc_ref.shape[0]
    query, key = iota((rows, rows), 0), iota((rows, rows), 1)
    same = segc_ref[...] == segr_ref[...]
    usable = validr_ref[...] > 0.5
    return (key <= query) & same & (usable | (key == query))


def attention_kernel(pieces1, tile, *refs):
    n1 = len(pieces1.arrays)
    me_ref, norm_ref, mix_ref, segc_ref, segr_ref, validr_ref, qg_ref, qb_ref, kg_ref = refs[:9]
    w1_refs = refs[9 : 9 + n1]
    shared_ref, q_ref, k_ref, lse_ref, vpre_ref, values_ref, gpre_ref, att_ref, gated_ref, w1, probs_ref, sem1 = refs[9 + n1 :]
    me = me_ref[0]
    values_width = values_ref.shape[1]
    copies1 = pieces1.copies(w1_refs, w1, me, sem1)
    for copy in copies1:
        copy.start()
    for copy in copies1:
        copy.wait()
    shared = dot(mix_ref[...], w1[:, 2 * values_width :])
    shared_ref[...] = shared
    queries = (shared * qg_ref[...] + qb_ref[...]).astype(bf16)
    keys = (shared * kg_ref[...]).astype(bf16)
    q_ref[...] = queries
    k_ref[...] = keys
    scores = mul_t(queries, keys) * (queries.shape[1] ** -0.5)
    masked = jnp.where(allowed_pairs(segc_ref, segr_ref, validr_ref), scores, -1e30)
    top = jnp.max(masked, axis=1, keepdims=True)
    weights = jnp.exp(masked - top)
    total = jnp.sum(weights, axis=1, keepdims=True)
    probs_ref[...] = (weights / total).astype(bf16)
    lse_ref[...] = top + jnp.log(total)

    def columns(i, _):
        at = pl.ds(pl.multiple_of(i * tile, tile), tile)
        value_pre = dot(norm_ref[...], w1[:, at])
        vpre_ref[:, at] = value_pre.astype(bf16)
        values = (value_pre * jax.nn.sigmoid(value_pre)).astype(bf16)
        values_ref[:, at] = values
        gate_pre = dot(mix_ref[...], w1[:, pl.ds(pl.multiple_of(values_width + i * tile, tile), tile)])
        gpre_ref[:, at] = gate_pre.astype(bf16)
        attended = dot(probs_ref[...], values)
        att_ref[:, at] = attended.astype(bf16)
        gated_ref[:, at] = (attended * (gate_pre * jax.nn.sigmoid(gate_pre))).astype(bf16)
        return 0

    lax.fori_loop(0, values_width // tile, columns, 0)


def project_kernel(pieces2, tile, *refs):
    n2 = len(pieces2.arrays)
    me_ref, gated_ref, tok_ref, valid_ref, fg_ref = refs[:5]
    middle_ref, ffn_ref, inv_ref, w2, sem2 = refs[5 + n2 :]
    width = tok_ref.shape[1]
    copies2 = pieces2.copies(refs[5 : 5 + n2], w2, me_ref[0], sem2)
    for copy in copies2:
        copy.start()
    for copy in copies2:
        copy.wait()

    def out_columns(i, square):
        at = pl.ds(pl.multiple_of(i * tile, tile), tile)
        middle = tok_ref[:, at].astype(f32) * valid_ref[...] + dot(gated_ref[...], w2[:, at])
        middle_ref[:, at] = middle
        return square + jnp.sum(middle * middle, axis=1, keepdims=True)

    square = lax.fori_loop(0, width // tile, out_columns, jnp.zeros((tok_ref.shape[0], 1), f32))
    inverse = lax.rsqrt(square * (1.0 / width) + 1e-05)
    inv_ref[...] = inverse
    ffn_ref[...] = (middle_ref[...] * inverse * fg_ref[...]).astype(bf16)


def hidden_kernel(pieces3, pieces4, tile, *refs):
    n3, n4 = len(pieces3.arrays), len(pieces4.arrays)
    me_ref, ffn_ref, cot_ref = refs[:3]
    w3_refs, w4_refs = refs[3 : 3 + n3], refs[3 + n3 : 3 + n3 + n4]
    hid_ref, gg0, gu0, far_ref, w3, w4, sem3, sem4 = refs[3 + n3 + n4 :]
    me = me_ref[0]
    half = gg0.shape[1]
    copies3 = pieces3.copies(w3_refs, w3, me, sem3)
    copies4 = pieces4.copies(w4_refs, w4, me, sem4)
    for copy in copies3 + copies4:
        copy.start()
    for copy in copies3 + copies4:
        copy.wait()
    for rel in range(2):
        base = ((me_ref[1] ^ rel) * half)

        def columns(i, _, base=base, rel=rel):
            at = pl.ds(pl.multiple_of(i * tile, tile), tile)
            gate = dot(ffn_ref[...], w3[:, pl.ds(pl.multiple_of(base + i * tile, tile), tile)])
            up = dot(ffn_ref[...], w3[:, pl.ds(pl.multiple_of(2 * half + base + i * tile, tile), tile)])
            sigma = jax.nn.sigmoid(gate)
            act = gate * sigma
            hid_ref[:, pl.ds(pl.multiple_of(rel * half + i * tile, tile), tile)] = (act * up).astype(bf16)
            grad = mul_t(cot_ref[...], w4[pl.ds(pl.multiple_of(base + i * tile, tile), tile), :])
            grad_gate = (grad * up * (sigma * (1.0 + gate * (1.0 - sigma)))).astype(bf16)
            grad_up = (grad * act).astype(bf16)
            if rel == 0:
                gg0[:, at] = grad_gate
                gu0[:, at] = grad_up
            else:
                far_ref[:, at] = grad_gate
                far_ref[:, pl.ds(pl.multiple_of(half + i * tile, tile), tile)] = grad_up
            return 0

        lax.fori_loop(0, half // tile, columns, 0)


def ffn_back_kernel(pieces3, pieces4, tile, *refs):
    n3, n4 = len(pieces3.arrays), len(pieces4.arrays)
    me_ref, hid_ref, gg0, gu0, far_ref, middle_ref, inv_ref, cot_ref, fg_ref = refs[:9]
    w3_refs, w4_refs = refs[9 : 9 + n3], refs[9 + n3 : 9 + n3 + n4]
    out_ref, gmid_ref, low_own, low_oth, low_ref, dfg_ref, w3, w4, gin_ref, sem3, sem4 = refs[9 + n3 + n4 :]
    me, core = me_ref[0], me_ref[1]
    half = gg0.shape[1]
    rows, width = middle_ref.shape
    copies3 = pieces3.copies(w3_refs, w3, me, sem3)
    copies4 = pieces4.copies(w4_refs, w4, me, sem4)
    for copy in copies3 + copies4:
        copy.start()
    for copy in copies3:
        copy.wait()
    starts = [pl.multiple_of((core ^ rel) * half, half) for rel in range(2)]

    def grad_columns(i, carry):
        lean = carry
        at = pl.ds(pl.multiple_of(i * tile, tile), tile)
        grad = jnp.zeros((rows, tile), f32)
        for rel, (gg, gu) in enumerate(((gg0[...], gu0[...]), (far_ref[:, :half], far_ref[:, half:]))):
            grad = grad + mul_t(gg, w3[at, pl.ds(starts[rel], half)])
            up_start = pl.multiple_of(starts[rel] + 2 * half, half)
            grad = grad + mul_t(gu, w3[at, pl.ds(up_start, half)])
        normal = middle_ref[:, at] * inv_ref[...]
        dfg_ref[:, at] = jnp.sum(grad * normal, axis=0, keepdims=True)
        grad = grad * fg_ref[:, at]
        gin_ref[:, at] = grad
        return lean + jnp.sum(grad * normal, axis=1, keepdims=True)

    lean = lax.fori_loop(0, width // tile, grad_columns, jnp.zeros((rows, 1), f32)) * (1.0 / width)
    inverse = inv_ref[...]
    grad_middle = cot_ref[...].astype(f32) + inverse * (gin_ref[...] - middle_ref[...] * inverse * lean)
    gmid_ref[...] = grad_middle
    low_ref[...] = grad_middle.astype(bf16)
    part = width // 2
    low_own[...] = low_ref[:, pl.ds(pl.multiple_of(core * part, part), part)]
    low_oth[...] = low_ref[:, pl.ds(pl.multiple_of((1 - core) * part, part), part)]
    for copy in copies4:
        copy.wait()

    def out_columns(i, _):
        at = pl.ds(pl.multiple_of(i * tile, tile), tile)
        total = middle_ref[:, at]
        for rel in range(2):
            total = total + dot(hid_ref[:, rel * half : (rel + 1) * half], w4[pl.ds(starts[rel], half), at])
        out_ref[:, at] = total.astype(bf16)
        return 0

    lax.fori_loop(0, width // tile, out_columns, 0)


def attention_back_kernel(pieces1, pieces2, tile, *refs):
    n1, n2 = len(pieces1.arrays), len(pieces2.arrays)
    (me_ref, low_ref, q_ref, k_ref, lse_ref, shared_ref, vpre_ref, values_ref, gpre_ref, att_ref, segc_ref, segr_ref,
     validr_ref, qg_ref, kg_ref) = refs[:15]
    w1_refs, w2_refs = refs[15 : 15 + n1], refs[15 + n1 : 15 + n1 + n2]
    (gmix_ref, gnorm_ref, gv_own, gv_oth, gr_own, gr_oth, dgain_ref,
     w1, w2, probs_ref, low_probs_ref, gprobs_ref, ggp_ref, gvp_ref, gsh_ref, sem1, sem2) = refs[15 + n1 + n2 :]
    me, core = me_ref[0], me_ref[1]
    rows, width = low_ref.shape
    values_width = values_ref.shape[1]
    copies1 = pieces1.copies(w1_refs, w1, me, sem1)
    copies2 = pieces2.copies(w2_refs, w2, me, sem2)
    for copy in copies2 + copies1:
        copy.start()
    queries, keys = q_ref[...], k_ref[...]
    factor = queries.shape[1] ** -0.5
    scores = mul_t(queries, keys) * factor
    masked = jnp.where(allowed_pairs(segc_ref, segr_ref, validr_ref), scores, -1e30)
    probs = jnp.exp(masked - lse_ref[...])
    probs_ref[...] = probs
    low_probs_ref[...] = probs.astype(bf16)
    gprobs_ref[...] = jnp.zeros((rows, rows), f32)
    for copy in copies2:
        copy.wait()

    def columns(i, _):
        at = pl.ds(pl.multiple_of(i * tile, tile), tile)
        grad = mul_t(low_ref[...], w2[at, :]).astype(bf16).astype(f32)
        gate_pre = gpre_ref[:, at].astype(f32)
        sigma = jax.nn.sigmoid(gate_pre)
        grad_att = (grad * (gate_pre * sigma)).astype(bf16)
        slope = sigma * (1.0 + gate_pre * (1.0 - sigma))
        ggp_ref[:, at] = (grad * att_ref[:, at].astype(f32) * slope).astype(bf16)
        gprobs_ref[...] += mul_t(grad_att, values_ref[:, at])
        grad_values = t_mul(low_probs_ref[...], grad_att)
        gvp_ref[:, at] = (grad_values * silu_grad(vpre_ref[:, at].astype(f32))).astype(bf16)
        return 0

    lax.fori_loop(0, values_width // tile, columns, 0)
    probs, grad_probs = probs_ref[...], gprobs_ref[...]
    grad_scores = (probs * (grad_probs - jnp.sum(probs * grad_probs, axis=1, keepdims=True))).astype(bf16)
    grad_queries = dot(grad_scores, keys) * factor
    grad_keys = t_mul(grad_scores, queries) * factor
    shared = shared_ref[...]
    dgain_ref[0:1, :] = jnp.sum(grad_queries * shared, axis=0, keepdims=True)
    dgain_ref[1:2, :] = jnp.sum(grad_queries, axis=0, keepdims=True)
    dgain_ref[2:3, :] = jnp.sum(grad_keys * shared, axis=0, keepdims=True)
    gsh_ref[...] = (grad_queries * qg_ref[...] + grad_keys * kg_ref[...]).astype(bf16)
    for source, own, other, start in (
        (gvp_ref, gv_own, gv_oth, 0), (ggp_ref, gr_own, gr_oth, 0), (gsh_ref, gr_own, gr_oth, values_width // 2)
    ):
        part = source.shape[1] // 2
        own[:, start : start + part] = source[:, pl.ds(pl.multiple_of(core * part, part), part)]
        other[:, start : start + part] = source[:, pl.ds(pl.multiple_of((1 - core) * part, part), part)]
    for copy in copies1:
        copy.wait()

    def in_columns(i, _):
        at = pl.ds(pl.multiple_of(i * tile, tile), tile)
        gmix_ref[:, at] = (
            mul_t(gsh_ref[...], w1[at, 2 * values_width :])
            + mul_t(ggp_ref[...], w1[at, values_width : 2 * values_width])
        ).astype(bf16)
        gnorm_ref[:, at] = mul_t(gvp_ref[...], w1[at, :values_width]).astype(bf16)
        return 0

    lax.fori_loop(0, width // tile, in_columns, 0)


def weight_grad_kernel(halves, offset, order, blocks, me_ref, own, other, mine, theirs, *outs):
    chip, core = lax.shift_right_logical(me_ref[0], 1), me_ref[1]
    keep, send = outs if order is not None else (outs[0], None)
    block = keep.shape[1]
    half = own.shape[1] // halves
    span = mine.shape[1]
    if order is None:
        tile = math.gcd(half, 512)
    else:
        tile = math.lcm(block, LANES)
        while tile < 256 and half % (2 * tile) == 0:
            tile *= 2
    step = span if span <= 640 else math.gcd(span, 640) if math.gcd(span, 640) >= 256 else math.gcd(span, 512)
    if step < 256:
        step = 384 if span % 384 == 0 else step
    for rel in range(halves):
        base = (core ^ rel) * half if halves == 2 else 0

        def strip(i, _, base=base, rel=rel):
            left = own[:, pl.ds(pl.multiple_of(rel * half + i * tile, tile), tile)]
            far = rel if halves == 1 else 1 - rel
            right = other[:, pl.ds(pl.multiple_of(far * half + i * tile, tile), tile)]
            for c in range(0, span, step):
                cols = slice(c, c + step)
                out = t_mul(left, mine[:, cols]) + t_mul(right, theirs[:, offset + c : offset + c + step])
                out = out.astype(keep.dtype)
                if order is None:
                    keep[0, pl.ds(pl.multiple_of(base + i * tile, tile), tile), cols] = out
                    continue
                for s in range(tile // block):
                    rel_chip = (lax.div(base + i * tile, block) + s) ^ chip
                    slot = 0
                    for p, bit in enumerate(order):
                        up = len(order) - 1 - p
                        slot = slot | ((lax.shift_right_logical(rel_chip, bit - 1) & 1) << up)
                    piece = out[s * block : (s + 1) * block, :]
                    lower = slot < blocks // 2
                    index = slot & (blocks // 2 - 1)

                    @pl.when(lower)
                    def _():
                        keep[index, :, cols] = piece

                    @pl.when(jnp.logical_not(lower))
                    def _():
                        send[index, :, cols] = piece

            return 0

        lax.fori_loop(0, half // tile, strip, 0)


def weight_grad(left, right, order, me, chips, name, halves=1, offset=0, micros=8, after=()):
    total, span = left[0].shape[1], right[0].shape[1]
    if order is None:
        outs = [((1, total, span), bf16)]
    else:
        outs = [((chips // 2, total // chips, span), bf16)] * 2
    body = functools.partial(weight_grad_kernel, halves, offset, order, chips)
    given = kernel_call(body, outs, [me, *left, *right], [SM] + [VM] * 4, name=name, micros=micros, after=after)
    return (given[0], None) if order is None else tuple(given)


def exchange_start(pack, totals, axis):
    index, count = lax.axis_index(axis), lax.axis_size(axis)
    lanes = pack.shape[1]
    rows = pack.shape[0]
    full, totals_shape = pack, totals.shape
    totals = totals.reshape(-1, lanes)
    before, bit = jnp.zeros_like(totals), 1
    while bit < count:
        other = swap(jnp.concatenate([totals, full], axis=0), axis, bit)
        upper = (index & bit) != 0
        far_totals, far = other[: totals.shape[0]], other[totals.shape[0] :]
        before = before + jnp.where(upper, far_totals, 0.0)
        totals = totals + far_totals
        full = jnp.concatenate([jnp.where(upper, far, full), jnp.where(upper, full, far)], axis=0)
        bit *= 2
    return full.reshape(count, rows, lanes), before.reshape(totals_shape)


def exchange_end(pack, totals, axis):
    index, count = lax.axis_index(axis), lax.axis_size(axis)
    lanes = pack.shape[2]
    totals_shape = totals.shape
    totals = totals.reshape(-1, lanes)
    rows = totals.shape[0]
    after, bit = jnp.zeros_like(totals), 1
    while bit < count:
        upper = (index & bit) != 0
        pairs = pack.reshape((pack.shape[0] // 2, 2) + pack.shape[1:])
        goes = jnp.where(upper, pairs[:, 0], pairs[:, 1])
        stays = jnp.where(upper, pairs[:, 1], pairs[:, 0])
        other = swap(jnp.concatenate([totals, goes.reshape(-1, lanes)], axis=0), axis, bit)
        after = after + jnp.where(upper, 0.0, other[:rows])
        totals = totals + other[:rows]
        pack = stays + other[rows:].reshape(stays.shape)
        bit *= 2
    return pack[0], after.reshape(totals_shape)


def sum_over(value, axis):
    bit = 1
    while bit < lax.axis_size(axis):
        value = value + swap(value, axis, bit)
        bit *= 2
    return value


def on_device(tokens, cotangent, segment_ids, pad_mask, w_z, w_v, w_r, w_h, w_gate, w_up, w_down, q_gain, q_bias,
              k_gain, ffn_gain, norm_gain, ema_rate, ema_angle, ema_input, ema_output, ema_skip):
    rows, width = tokens.shape[1:]
    seq_count, dp_count = lax.axis_size("seq"), lax.axis_size("dp")
    seq_index, dp_index = lax.axis_index("seq"), lax.axis_index("dp")
    devices = seq_count * dp_count
    chips = devices // 2
    core = dp_index & 1
    fits = all(value.shape[0] % 16 == 0 for value in (w_z, w_h, w_down))
    dp_bits, all_bits = bits_of(dp_count), bits_of(devices)
    inner = list(range(1, dp_bits))
    first_seq, rest_seq = [dp_bits], list(range(all_bits - 1, dp_bits, -1))
    if fits:
        gather_a = rest_seq + first_seq + inner + [0]
        gather_b = rest_seq + inner + first_seq + [0]
        gather_c = inner + first_seq + rest_seq + [0]
        reduce_a, reduce_b = gather_a[-2::-1], gather_b[-2::-1]
        me = jnp.stack([seq_index * dp_count + dp_index, core]).astype(jnp.int32)
    else:
        gather_a = gather_b = gather_c = reduce_a = reduce_b = None
        me = jnp.stack([core * 0, core]).astype(jnp.int32)
    values_width, hidden_width = w_v.shape[1], w_gate.shape[1]
    z_width = w_z.shape[1]
    get_v = Gather(w_v.astype(bf16), gather_a)
    get_r = Gather(jnp.concatenate([w_r, w_z], axis=1).astype(bf16), gather_b)
    get_down = Gather(w_down.astype(bf16), gather_c)
    get_h = Gather(w_h.astype(bf16), gather_a)
    get_gate = Gather(w_gate.astype(bf16), gather_a)
    get_up = Gather(w_up.astype(bf16), gather_b)
    first_v, first_r, first_down = get_v.step(), get_r.step(), get_down.step()
    first_h = get_h.step(first_v)

    row_segs = lax.dynamic_slice_in_dim(segment_ids[0], seq_index * rows, rows)
    row_valid = lax.dynamic_slice_in_dim(pad_mask[0], seq_index * rows, rows).astype(f32)
    valid_col, seg_col, seg_row, valid_row = row_valid[:, None], row_segs[:, None], row_segs[None], row_valid[None]
    prefix, totals = kernel_call(
        stats_kernel, [((rows, LANES), f32), ((DOCS, LANES), f32)], [tokens[0], valid_col, seg_col, seg_row],
        name="stats", micros=5,
    )

    ndim, lanes = ema_rate.shape[1], norm_gain.shape[0]
    gains = jnp.concatenate([q_gain, q_bias, k_gain, ffn_gain])[None].astype(bf16).astype(f32)
    gains = gather_small(gains, "dp").reshape(-1)
    size = gains.shape[0]
    extra = -(-size // lanes)
    gains = jnp.pad(gains, (0, extra * lanes - size)).reshape(extra, lanes)
    pack = jnp.concatenate(
        [ema_rate.T, ema_angle.T, ema_input.T, ema_output.T, norm_gain[None], ema_skip[None], gains], axis=0
    )
    full, before = exchange_start(pack, totals, "seq")
    carry = lax.dynamic_slice_in_dim(before, row_segs[0], 1)
    gains = full[:, 4 * ndim + 2 :].reshape(seq_count, -1)[:, :size].reshape(devices, -1)
    zs, fs = q_gain.shape[0], ffn_gain.shape[0]
    full_qg = gains[:, :zs].reshape(1, -1)
    full_qb = gains[:, zs : 2 * zs].reshape(1, -1)
    full_kg = gains[:, 2 * zs : 3 * zs].reshape(1, -1)
    full_fg = gains[:, 3 * zs :].reshape(1, -1)
    par = ema_params(full[:, : 4 * ndim + 2], ndim, rows)
    flat = lambda value: value.reshape(-1, LANES)
    a_flat, b_flat, g_flat = flat(par["a"]), flat(par["b"]), flat(par["output_w"] * par["coeff"])
    gain_row = par["gain"].reshape(1, width)
    sent_norm, xs, ends = kernel_call(
        norm_kernel,
        [((rows, width), bf16), ((rows * SUB, LANES), f32), ((2 * ndim * SUB, LANES), f32)],
        [tokens[0], valid_col, seg_col, prefix, carry, gain_row, a_flat, b_flat],
        name="norm", micros=13, after=first_v + first_r + first_down,
    )
    seq_steps = len(rest_seq)
    for _ in range(seq_steps - 1):
        deep_v, deep_r = get_v.step(), get_r.step()
    first_gate, first_up = get_gate.step(deep_v), get_up.step(deep_r)
    middle_v, middle_r, second_down = get_v.step(), get_r.step(), get_down.step()
    start_state = state_before(ends.reshape(2 * ndim, SUB, LANES), par["hop"], "seq", False)
    mixed, sent_mix, kept = kernel_call(
        mix_kernel,
        [((rows * SUB, LANES), f32), ((rows, width), bf16), ((rows // SPAN, 2 * ndim * SUB, LANES), f32)],
        [xs, flat(start_state), a_flat, b_flat, g_flat, par["skip"]],
        scratch=[pltpu.VMEM((2 * ndim * SUB, LANES), f32)],
        name="mix", micros=16, after=middle_v + middle_r + first_h + second_down,
    )
    for getter in (get_v, get_r):
        while getter.order is not None and getter.place < all_bits:
            getter.step()
    for _ in range(seq_steps - 1):
        get_h.step()
        deep_gate, deep_up = get_gate.step(), get_up.step()
    third_h = get_h.step((mixed,))
    third_gate, third_up = get_gate.step((mixed,)), get_up.step((mixed,))
    third_down = get_down.step(deep_gate + deep_up)
    while get_h.order is not None and get_h.place < all_bits:
        get_h.step()
    pieces1 = Columns((get_v.pieces, get_r.pieces), (0, values_width))
    pieces2 = Columns((get_h.pieces,), (0,))

    tile = 256
    w1_shape, w2_shape = (width, 2 * values_width + z_width), (values_width, width)
    w3_shape, w4_shape = (width, 2 * hidden_width), (hidden_width, width)
    dma = pltpu.SemaphoreType.DMA
    wide = ((rows, values_width), bf16)

    def any_of(*groups):
        return [ANY] * sum(len(group.arrays) for group in groups)

    shared, queries, keys, log_total, value_pre, values, gate_pre, attended, gated = kernel_call(
        functools.partial(attention_kernel, pieces1, tile),
        [((rows, z_width), f32), ((rows, z_width), bf16), ((rows, z_width), bf16), ((rows, 1), f32), wide, wide, wide,
         wide, wide],
        [me, sent_norm, sent_mix, seg_col, seg_row, valid_row, full_qg, full_qb, full_kg, *pieces1.arrays],
        [SM] + [VM] * 8 + any_of(pieces1),
        scratch=[pltpu.VMEM(w1_shape, bf16), pltpu.VMEM((rows, rows), bf16), dma],
        name="attention", micros=20, after=third_h + third_gate + third_up,
    )
    for getter in (get_gate, get_up, get_down):
        while getter.order is not None and getter.place < all_bits - 1:
            getter.step()
        getter.step((gated,))
    pieces3 = Columns((get_gate.pieces, get_up.pieces), (0, hidden_width))
    pieces4 = Columns((get_down.pieces,), (0,))
    middle, ffn_in, inverse = kernel_call(
        functools.partial(project_kernel, pieces2, tile),
        [((rows, width), f32), ((rows, width), bf16), ((rows, 1), f32)],
        [me, gated, tokens[0], valid_col, full_fg, *pieces2.arrays],
        [SM] + [VM] * 4 + any_of(pieces2),
        scratch=[pltpu.VMEM(w2_shape, bf16), dma],
        name="project", micros=6,
    )

    def other_core(value):
        return swap_bit(value, 0)

    grad_low = cotangent[0]
    part = width // 2
    cot_own = lax.dynamic_slice_in_dim(grad_low, core * part, part, axis=1)
    cot_oth = other_core(lax.dynamic_slice_in_dim(grad_low, (1 - core) * part, part, axis=1))
    half_hidden = ((rows, hidden_width // 2), bf16)
    hid, gg_own, gu_own, far = kernel_call(
        functools.partial(hidden_kernel, pieces3, pieces4, tile),
        [((rows, hidden_width), bf16), half_hidden, half_hidden, ((rows, hidden_width), bf16)],
        [me, ffn_in, grad_low, *pieces3.arrays, *pieces4.arrays],
        [SM, VM, VM] + any_of(pieces3, pieces4),
        scratch=[pltpu.VMEM(w3_shape, bf16), pltpu.VMEM(w4_shape, bf16), dma, dma],
        name="hidden", micros=20, after=(cot_oth,),
    )
    output, grad_middle, low_own, low_oth, middle_low, dfg = kernel_call(
        functools.partial(ffn_back_kernel, pieces3, pieces4, tile),
        [((rows, width), bf16), ((rows, width), f32), ((rows, part), bf16), ((rows, part), bf16), ((rows, width), bf16),
         ((1, width), f32)],
        [me, hid, gg_own, gu_own, far, middle, inverse, grad_low, full_fg, *pieces3.arrays, *pieces4.arrays],
        [SM] + [VM] * 8 + any_of(pieces3, pieces4),
        scratch=[pltpu.VMEM(w3_shape, bf16), pltpu.VMEM(w4_shape, bf16), pltpu.VMEM((rows, width), f32), dma, dma],
        name="ffn_back", micros=22,
    )
    hid_pair, ffn_pair = (hid, other_core(hid)), (ffn_in, other_core(ffn_in))
    far_other = other_core(far)
    down = Reduce(
        weight_grad(hid_pair, (cot_own, cot_oth), reduce_a, me, chips, "grad_down", halves=2, after=(output,)), reduce_a
    )
    gate = Reduce(
        weight_grad(ffn_pair, (gg_own, far_other), reduce_b, me, chips, "grad_gate", after=(down.keep,)), reduce_b
    )
    up = Reduce(
        weight_grad(ffn_pair, (gu_own, far_other), reduce_a, me, chips, "grad_up", offset=hidden_width // 2,
                    after=(gate.keep,)),
        reduce_a,
    )
    gated_pair, mix_pair, norm_pair = ((value, other_core(value)) for value in (gated, sent_mix, sent_norm))
    half_values = ((rows, values_width // 2), bf16)
    half_mixed = ((rows, (values_width + z_width) // 2), bf16)
    grad_mix_rows, grad_norm_rows, gv_own, gv_oth, gr_own, gr_oth, dgains = kernel_call(
        functools.partial(attention_back_kernel, pieces1, pieces2, tile),
        [((rows, width), bf16)] * 2 + [half_values] * 2 + [half_mixed] * 2 + [((3, z_width), f32)],
        [me, middle_low, queries, keys, log_total, shared, value_pre, values, gate_pre, attended, seg_col, seg_row,
         valid_row, full_qg, full_kg, *pieces1.arrays, *pieces2.arrays],
        [SM] + [VM] * 14 + any_of(pieces1, pieces2),
        scratch=[pltpu.VMEM(w1_shape, bf16), pltpu.VMEM(w2_shape, bf16), pltpu.VMEM((rows, rows), f32),
                 pltpu.VMEM((rows, rows), bf16), pltpu.VMEM((rows, rows), f32), pltpu.VMEM((rows, values_width), bf16),
                 pltpu.VMEM((rows, values_width), bf16), pltpu.VMEM((rows, z_width), bf16), dma, dma],
        name="attention_back", micros=28,
        after=(up.keep, gated_pair[1], mix_pair[1], norm_pair[1]),
    )
    pins = down.step() + gate.step()
    drive, back_ends = kernel_call(
        back_ends_kernel, [((rows * SUB, LANES), f32), ((2 * ndim * SUB, LANES), f32)],
        [grad_mix_rows, mixed, a_flat, b_flat], name="back_ends", micros=12, after=pins,
    )
    heads = Reduce(
        weight_grad(gated_pair, (low_own, other_core(low_oth)), reduce_b, me, chips, "grad_h", after=(back_ends,)), reduce_b
    )
    pins = up.step() + down.step()
    value = Reduce(
        weight_grad(norm_pair, (gv_own, other_core(gv_oth)), reduce_a, me, chips, "grad_v", after=(heads.keep,) + pins),
        reduce_a,
    )
    pins = gate.step()
    reset = Reduce(
        weight_grad(mix_pair, (gr_own, other_core(gr_oth)), reduce_b, me, chips, "grad_r", after=(value.keep,) + pins),
        reduce_b,
    )
    hop_back = (par["hop"][0], -par["hop"][1])
    back_state = flat(state_before(back_ends.reshape(2 * ndim, SUB, LANES), hop_back, "seq", True))
    sums = jnp.zeros(((3 * ndim + 1) * SUB, LANES), f32)
    cuts = 4
    plan = [
        lambda: (reset.keep,) + down.step() + up.step(),
        lambda: down.step() + gate.step(),
        lambda: heads.step() + value.step() + up.step(),
        lambda: gate.step() + up.step(),
    ]
    long = rows * SUB // cuts
    pieces_dx = []
    for cut in range(cuts - 1, -1, -1):
        block = pl.BlockSpec((long, LANES), lambda i, cut=cut: (cut, 0))
        keep_block = pl.BlockSpec((rows // SPAN // cuts, 2 * ndim * SUB, LANES), lambda i, cut=cut: (cut, 0, 0))
        dxs, back_state, sums = kernel_call(
            back_scan_kernel,
            [((long, LANES), f32), ((2 * ndim * SUB, LANES), f32), (((3 * ndim + 1) * SUB, LANES), f32)],
            [xs, drive, kept, back_state, sums, a_flat, b_flat, g_flat, par["skip"]],
            [block, block, keep_block] + [VM] * 6,
            scratch=[pltpu.VMEM((SPAN, 8 * SUB, LANES), f32)],
            name="back", micros=10, after=plan.pop(0)(), grid=(1,), out_specs=[VM] * 3,
        )
        pieces_dx.insert(0, dxs)
    pins = heads.step() + reset.step()
    dn, dgain, suffix, back_totals = kernel_call(
        back_norm_kernel,
        [((rows, width), f32), ((1, width), f32), ((rows, LANES), f32), ((DOCS, LANES), f32)],
        [*pieces_dx, grad_norm_rows, tokens[0], valid_col, seg_col, seg_row, prefix, carry, gain_row],
        name="back_norm", micros=6, after=pins,
    )
    sums = sums.reshape(3 * ndim + 1, SUB, LANES)
    d_params = ema_param_grads(par, sums)
    d_pack = jnp.concatenate(list(d_params) + [dgain.reshape(1, SUB, LANES), sums[3 * ndim :]], axis=0)
    d_pack = jnp.transpose(d_pack.reshape(4 * ndim + 2, seq_count, lanes), (1, 0, 2))
    owned = [dgains[i].reshape(devices, zs) for i in range(3)] + [dfg.reshape(devices, fs)]
    owned = jnp.concatenate(owned, axis=1).reshape(seq_count, -1)
    owned = jnp.pad(owned, ((0, 0), (0, extra * lanes - size))).reshape(seq_count, extra, lanes)
    own_pack, after_totals = exchange_end(jnp.concatenate([d_pack, owned], axis=1), back_totals, "seq")
    back_carry = lax.dynamic_slice_in_dim(after_totals, row_segs[rows - 1], 1)
    (input_grad,) = kernel_call(
        input_kernel, [((rows, width), f32)],
        [dn, suffix, back_carry, tokens[0], valid_col, seg_col, prefix, carry, grad_middle], name="input", micros=6,
        after=value.step(),
    )
    total = sum_over(own_pack, "dp")
    mine = lax.dynamic_index_in_dim(total[4 * ndim + 2 :].reshape(-1)[:size].reshape(dp_count, -1), dp_index, 0, keepdims=False)
    while any(message.left or message.keep.dtype == bf16 for message in (heads, value, reset)) and fits:
        for message in (heads, value, reset):
            if message.left or message.keep.dtype == bf16:
                message.step()
    (shard_down,) = down.finish(core, [part])
    (shard_gate,) = gate.finish(core, [hidden_width // 2])
    (shard_up,) = up.finish(core, [hidden_width // 2])
    (shard_h,) = heads.finish(core, [part])
    (shard_v,) = value.finish(core, [values_width // 2])
    shard_r, shard_z = reset.finish(core, [values_width // 2, z_width // 2])
    return (
        output[None], input_grad[None], shard_z, shard_v, shard_r, shard_h, shard_gate, shard_up, shard_down,
        mine[:zs], mine[zs : 2 * zs], mine[2 * zs : 3 * zs], mine[3 * zs :],
        total[4 * ndim], total[:ndim].T, total[ndim : 2 * ndim].T, total[2 * ndim : 3 * ndim].T,
        total[3 * ndim : 4 * ndim].T, total[4 * ndim + 1],
    )


def solution(mesh):
    by_token, by_group = P("dp", "seq", None), P("dp", None)
    by_row, by_owner = P(("seq", "dp"), None), P(("seq", "dp"))
    params = (by_row,) * 7 + (by_owner,) * 4 + (P("seq"),) + (P("seq", None),) * 4 + (P("seq"),)
    return jax.shard_map(
        on_device,
        mesh=mesh,
        in_specs=(by_token, by_token, by_group, by_group) + params,
        out_specs=(by_token, by_token) + params,
        check_vma=False,
    )
```

time: 1550 us -> 596 us (0.38); the launches traced: 1530 us -> 590 us
  local copies, waits for them, and re-layouts: 442 us -> 19.7 us
  Pallas kernels: 6.22 us -> 248 us
  matrix products: 234 us -> 0 us
  blocking collectives: 200 us -> 0 us
  waiting for transfers between devices: 365 us -> 173 us
  other arithmetic: 224 us -> 66.3 us
  starting transfers between devices: 33.9 us -> 76.6 us
    reduce_scatter x7 -> x0, waiting for transfers between devices: 346 us -> none  [the longest x1 152 us: on_device(): lax.psum_scatter(grad_w_up, ('seq', 'dp'), scatter_dimension=0, tiled=True)]
    pallas_call x0 -> x34, Pallas kernels: none -> 248 us  [the longest x21 248 us: kernel_call(): pl.pallas_call(run, out_shape=tuple((jax.ShapeDtypeStruct(shape, dtype) f...]
    dot_general x41 -> x0, matrix products: 234 us -> none  [the longest x3 44.2 us: ema_blocked(): inner = jnp.einsum('ijc,bjc->bic', toeplitz, blocks, precision=highest)]
    pad x129 -> x1, local copies, waits for them, and re-layouts: 211 us -> 0.01 us  [on_device(): jnp.pad(owned, ((0, 0), (0, extra * lanes - size)))]
    ppermute x0 -> x92, waiting for transfers between devices: none -> 173 us  [swap(): return lax.ppermute(value, axis, [(i, i ^ bit) for i in range(count)])]
    unnamed x2 -> x0, blocking collectives: 128 us -> none
    scatter-add x1 -> x0, other arithmetic: 98.4 us -> none  [ema_blocked(): jnp.take(kernel, jnp.clip(lag, 0, span - 1), axis=0)]
    ppermute x0 -> x92, starting transfers between devices: none -> 76.6 us  [swap(): return lax.ppermute(value, axis, [(i, i ^ bit) for i in range(count)])]
  transfers between devices with their start and end apart: 19 -> 92, of which waited for: 5 -> 28; matrix products, arithmetic and copies ran while one was open for 56% -> 13% of each run, Pallas kernels for 0% -> 39%
where the time goes in v1:
time: 596 us; the launch traced here: 590 us
  Pallas kernels  248 us (42%)
  waiting for transfers between devices  173 us (29%)
  starting transfers between devices  76.6 us (13%)
  other arithmetic  66.3 us (11%)
  local copies, waits for them, and re-layouts  19.7 us (3%)
  between operations  6.08 us (1%)
    pallas_call x21, Pallas kernels, kernel_call(): pl.pallas_call(run, out_shape=tuple((jax.ShapeDtypeStruct(shape, dtype) f...  248 us
    ppermute x92, waiting for transfers between devices, swap(): return lax.ppermute(value, axis, [(i, i ^ bit) for i in range(count)])  173 us
    ppermute x92, starting transfers between devices, swap(): return lax.ppermute(value, axis, [(i, i ^ bit) for i in range(count)])  76.6 us
    convert_element_type x12, other arithmetic, step(): (self.keep[:half].astype(f32) + self.other[:half].astype(f32)).astype(bf16)  17.7 us
    concatenate x18, other arithmetic, step(): self.arrays = [jnp.concatenate([mine[0], others[0]], axis=0)]  15.7 us
  transfers between devices with their start and end apart: 92, of which 28 were waited for; matrix products, arithmetic and copies ran while one was open for 13% of the time, Pallas kernels for 39%

profile of v1, /device:TPU:0, one launch (start us, length us, event | category | flops | bytes accessed | tf_op | source)
XLA Modules:
  0.0 590.0 jit_solution(17734099004789098645)
XLA Ops:
  5.0 3.7 collective-permute-start.6
  9.8 1.9 collective-permute-start.7
  17.0 4.5 stats.1
  22.4 1.9 collective-permute-start.2
  27.2 2.0 collective-permute-start.3
  33.1 2.7 collective-permute-start.4
  41.3 7.3 %collective-permute-done.15 = bf16[1,64,1024]{2,1,0:T(8,128)(2,1)S(1)} collective-permute-done((bf16[1,64,1024]{2,1,0:T(8,128)(2,1)}, bf16[1,64,1024]{2,1,0:T(8,128)(2,1)S(1)}, u32[]{:S(2)}, u32[]{:S(2)}) %collective-permute-start.15) | collective-permute-done | bytes 131104 | tf_op jit(solution)/shard_map/ppermute | solution.py:385
  52.9 12.6 %norm.1 = (bf16[512,1024]{1,0:T(8,128)(2,1)}, f32[4096,128]{1,0:T(8,128)}, f32[256,128]{1,0:T(8,128)}) custom-call(bf16[512,1024]{1,0:T(8,128)(2,1)} %bitcast.243, f32[512,1]{1,0:T(8,128)} %copy.59.refs_1_.refs_3_.refs_6_.refs_4_, s32[512,1]{1,0:T(8,128)} %copy.60.refs_2_.refs_3_.refs_10_.refs_7_.refs_5_, ...), custom_call_target="tpu_custom_call" | custom-call | flops 12999999488 | bytes 39000000 | tf_op jit(solution)/shard_map/norm/pallas_call | solution.py:69
  67.9 2.8 collective-permute-done.8
  70.7 2.3 collective-permute-start.25
  73.2 1.9 collective-permute-start.9
  77.5 1.9 pad_maximum_fusion.6.refs_9_.refs_0_
  79.4 2.4 collective-permute-start.28
  83.4 3.4 collective-permute-done.28
  86.9 2.3 collective-permute-start.26
  92.7 5.0 collective-permute-done.26
  98.7 2.2 pad_maximum_fusion.4.refs_6_.refs_9_.refs_15_
  105.1 15.5 %mix.1 = (f32[4096,128]{1,0:T(8,128)}, bf16[512,1024]{1,0:T(8,128)(2,1)}, f32[16,256,128]{2,1,0:T(8,128)}) custom-call(f32[4096,128]{1,0:T(8,128)} %get-tuple-element.88.refs_0_, f32[256,128]{1,0:T(8,128)} %maximum_bitcast_fusion.refs_1_, f32[128,128]{1,0:T(8,128)} %bitcast.211, f32[128,128]{1,0:T(8,128)} %bitcast.204, f32[128,128]{1,0:T(8,128)} %bitcast.217, ...), custom_call_target="tpu_custom_call" | custom-call | flops 16000000000 | bytes 48000000 | tf_op jit(solution)/shard_map/mix/pallas_call | solution.py:69
  121.9 1.8 pad_maximum_fusion.11.refs_0_
  127.2 12.3 %collective-permute-done.24 = bf16[4,64,1024]{2,1,0:T(8,128)(2,1)S(1)} collective-permute-done((bf16[4,64,1024]{2,1,0:T(8,128)(2,1)}, bf16[4,64,1024]{2,1,0:T(8,128)(2,1)S(1)}, u32[]{:S(2)}, u32[]{:S(2)}) %collective-permute-start.24) | collective-permute-done | bytes 524320 | tf_op jit(solution)/shard_map/ppermute | solution.py:385
  142.6 8.3 %collective-permute-done.40 = bf16[4,80,1024]{2,1,0:T(8,128)(2,1)S(1)} collective-permute-done((bf16[4,80,1024]{2,1,0:T(8,128)(2,1)S(1)}, bf16[4,80,1024]{2,1,0:T(8,128)(2,1)S(1)}, u32[]{:S(2)}, u32[]{:S(2)}) %collective-permute-start.40) | collective-permute-done | bytes 655392 | tf_op jit(solution)/shard_map/ppermute | solution.py:385
  154.2 13.5 %collective-permute-done.27 = bf16[4,32,2560]{2,1,0:T(8,128)(2,1)S(1)} collective-permute-done((bf16[4,32,2560]{2,1,0:T(8,128)(2,1)}, bf16[4,32,2560]{2,1,0:T(8,128)(2,1)S(1)}, u32[]{:S(2)}, u32[]{:S(2)}) %collective-permute-start.27) | collective-permute-done | bytes 655392 | tf_op jit(solution)/shard_map/ppermute | solution.py:385
  171.7 17.4 %attention.1 = (f32[512,256]{1,0:T(8,128)}, bf16[512,256]{1,0:T(8,128)(2,1)}, bf16[512,256]{1,0:T(8,128)(2,1)}, f32[512,1]{1,0:T(8,128)}, bf16[512,2048]{1,0:T(8...) custom-call(s32[2]{0:T(128)} %pad_add_fusion.refs_0_, ...), custom_call_target="tpu_custom_call" | custom-call | flops 20000000000 | bytes 60000000 | tf_op jit(solution)/shard_map/attention/pallas_call | solution.py:69
  189.1 11.2 %collective-permute-done.41.refs_0_ = bf16[8,80,1024]{2,1,0:T(8,128)(2,1)} collective-permute-done((bf16[8,80,1024]{2,1,0:T(8,128)(2,1)S(1)}, bf16[8,80,1024]{2,1,0:T(8,128)(2,1)}, u32[]{:S(2)}, u32[]{:S(2)}) %collective-permute-start.41) | collective-permute-done | bytes 1310752 | tf_op jit(solution)/shard_map/ppermute | solution.py:385
  202.5 17.9 %collective-permute-done.34.refs_0_ = bf16[8,32,2560]{2,1,0:T(8,128)(2,1)} collective-permute-done((bf16[8,32,2560]{2,1,0:T(8,128)(2,1)}, bf16[8,32,2560]{2,1,0:T(8,128)(2,1)}, u32[]{:S(2)}, u32[]{:S(2)}) %collective-permute-start.34) | collective-permute-done | bytes 1310752 | tf_op jit(solution)/shard_map/ppermute | solution.py:385
  223.4 9.1 %project.1 = (f32[512,1024]{1,0:T(8,128)}, bf16[512,1024]{1,0:T(8,128)(2,1)}, f32[512,1]{1,0:T(8,128)}) custom-call(s32[2]{0:T(128)} %pad_add_fusion.refs_0_, bf16[512,2048]{1,0:T(8,128)(2,1)} %get-tuple-element.92.refs_1_, bf16[512,1024]{1,0:T(8,128)(2,1)} %bitcast.244, f32[512,1]{1,0:T(8,128)} %copy.59.refs_1_.refs_3_.refs_6_.refs_4_, ...), custom_call_target="tpu_custom_call" | custom-call | flops 6000000000 | bytes 18000000 | tf_op jit(solution)/shard_map/project/pallas_call | solution.py:69
  232.6 20.0 %hidden.1 = (bf16[512,2560]{1,0:T(8,128)(2,1)}, bf16[512,1280]{1,0:T(8,128)(2,1)}, bf16[512,1280]{1,0:T(8,128)(2,1)}, bf16[512,2560]{1,0:T(8,128)(2,1)}) custom-call(s32[2]{0:T(128)} %pad_add_fusion.refs_0_, bf16[512,1024]{1,0:T(8,128)(2,1)} %get-tuple-element.93.refs_1_, bf16[512,1024]{1,0:T(8,128)(2,1)} %bitcast.200, ...), custom_call_target="tpu_custom_call" | custom-call | flops 20000000000 | bytes 60000000 | tf_op jit(solution)/shard_map/hidden/pallas_call | solution.py:69
  255.8 22.4 %ffn_back.1 = (bf16[512,1024]{1,0:T(8,128)(2,1)}, f32[512,1024]{1,0:T(8,128)}, bf16[512,512]{1,0:T(8,128)(2,1)}, bf16[512,512]{1,0:T(8,128)(2,1)}, bf16[512,1024]{1,0:T(8,128)(2,1)}, /*index=5*/f32[1,1024]{1,0:T(1,128)}) custom-call(s32[2]{0:T(128)} %pad_add_fusion.refs_0_, bf16[512,2560]{1,0:T(8,128)(2,1)} %get-tuple-element.94.refs_1_, ...), custom_call_target="tpu_custom_call" | custom-call | flops 22000001024 | bytes 66000000 | tf_op jit(solution)/shard_map/ffn_back/pallas_call | solution.py:69
  280.6 8.2 %grad_down.1 = (bf16[8,160,512]{2,1,0:T(8,128)(2,1)}, bf16[8,160,512]{2,1,0:T(8,128)(2,1)}) custom-call(s32[2]{0:T(128)} %pad_add_fusion.refs_0_, bf16[512,2560]{1,0:T(8,128)(2,1)} %get-tuple-element.94.refs_1_, bf16[512,2560]{1,0:T(8,128)(2,1)} %collective-permute-done.47.refs_2_, bf16[512,512]{1,0:T(8,128)(2,1)} %get-tuple-element.189.refs_3_, ...), custom_call_target="tpu_custom_call" | custom-call | flops 8000000000 | bytes 24000000 | tf_op jit(solution)/shard_map/grad_down/pallas_call | solution.py:69
  288.8 9.5 %grad_gate.1 = (bf16[8,64,1280]{2,1,0:T(8,128)(2,1)}, bf16[8,64,1280]{2,1,0:T(8,128)(2,1)}) custom-call(s32[2]{0:T(128)} %pad_add_fusion.refs_0_, bf16[512,1024]{1,0:T(8,128)(2,1)} %get-tuple-element.93.refs_1_, bf16[512,1024]{1,0:T(8,128)(2,1)} %collective-permute-done.45.refs_2_, bf16[512,1280]{1,0:T(8,128)(2,1)} %get-tuple-element.95.refs_2_.refs_3_, ...), custom_call_target="tpu_custom_call" | custom-call | flops 8000000000 | bytes 24000000 | tf_op jit(solution)/shard_map/grad_gate/pallas_call | solution.py:69
  298.3 9.5 %grad_up.1 = (bf16[8,64,1280]{2,1,0:T(8,128)(2,1)}, bf16[8,64,1280]{2,1,0:T(8,128)(2,1)}) custom-call(s32[2]{0:T(128)} %pad_add_fusion.refs_0_, bf16[512,1024]{1,0:T(8,128)(2,1)} %get-tuple-element.93.refs_1_, bf16[512,1024]{1,0:T(8,128)(2,1)} %collective-permute-done.45.refs_2_, bf16[512,1280]{1,0:T(8,128)(2,1)} %get-tuple-element.96.refs_3_, ...), custom_call_target="tpu_custom_call" | custom-call | flops 8000000000 | bytes 24000000 | tf_op jit(solution)/shard_map/grad_up/pallas_call | solution.py:69
  310.6 27.8 %attention_back.1 = (bf16[512,1024]{1,0:T(8,128)(2,1)}, bf16[512,1024]{1,0:T(8,128)(2,1)}, bf16[512,1024]{1,0:T(8,128)(2,1)}, bf16[512,1024]{1,0:T(8,128)(2,1)},...) custom-call(s32[2]{0:T(128)} %pad_add_fusion.refs_0_, ...), custom_call_target="tpu_custom_call" | custom-call | flops 28000000000 | bytes 84000000 | tf_op jit(solution)/shard_map/attention_back/pallas_call | solution.py:69
  338.4 2.3 collective-permute-done.52
  340.7 2.4 add_convert_fusion.1
  343.2 24.2 %collective-permute-done.51 = bf16[8,160,512]{2,1,0:T(8,128)(2,1)} collective-permute-done((bf16[8,160,512]{2,1,0:T(8,128)(2,1)}, bf16[8,160,512]{2,1,0:T(8,128)(2,1)}, u32[]{:S(2)}, u32[]{:S(2)}) %collective-permute-start.51) | collective-permute-done | bytes 1310752 | tf_op jit(solution)/shard_map/ppermute | solution.py:385
  367.3 2.6 add_convert_fusion.2
  369.9 12.1 %back_ends.1 = (f32[4096,128]{1,0:T(8,128)}, f32[256,128]{1,0:T(8,128)}) custom-call(bf16[512,1024]{1,0:T(8,128)(2,1)} %get-tuple-element.113.refs_0_, f32[4096,128]{1,0:T(8,128)} %get-tuple-element.91.refs_1_, f32[128,128]{1,0:T(8,128)} %bitcast.212, f32[128,128]{1,0:T(8,128)} %bitcast.205, bf16[4,160,512]{2,1,0:T(8,128)(2,1)} %get-tuple-element.170.refs_4_, ...), custom_call_target="tpu_custom_call" | custom-call | flops 12000000000 | bytes 36000000 | tf_op jit(solution)/shard_map/back_ends/pallas_call | solution.py:69
  383.8 3.5 collective-permute-done.53
  390.1 2.4 add_convert_fusion
  392.5 2.5 collective-permute-done.54
  395.9 8.0 %grad_h.1 = (bf16[8,128,512]{2,1,0:T(8,128)(2,1)}, bf16[8,128,512]{2,1,0:T(8,128)(2,1)}) custom-call(s32[2]{0:T(128)} %pad_add_fusion.refs_0_, bf16[512,2048]{1,0:T(8,128)(2,1)} %get-tuple-element.92.refs_1_, bf16[512,2048]{1,0:T(8,128)(2,1)} %collective-permute-done.48.refs_28_.refs_2_, bf16[512,512]{1,0:T(8,128)(2,1)} %get-tuple-element.123.refs_3_, ...), custom_call_target="tpu_custom_call" | custom-call | flops 8000000000 | bytes 24000000 | tf_op jit(solution)/shard_map/grad_h/pallas_call | solution.py:69
  406.1 6.8 %collective-permute-done.63 = bf16[4,64,1280]{2,1,0:T(8,128)(2,1)S(1)} collective-permute-done((bf16[4,64,1280]{2,1,0:T(8,128)(2,1)}, bf16[4,64,1280]{2,1,0:T(8,128)(2,1)S(1)}, u32[]{:S(2)}, u32[]{:S(2)}) %collective-permute-start.63) | collective-permute-done | bytes 655392 | tf_op jit(solution)/shard_map/ppermute | solution.py:385
  415.7 11.3 %collective-permute-done.60 = bf16[4,160,512]{2,1,0:T(8,128)(2,1)S(1)} collective-permute-done((bf16[4,160,512]{2,1,0:T(8,128)(2,1)S(1)}, bf16[4,160,512]{2,1,0:T(8,128)(2,1)S(1)}, u32[]{:S(2)}, u32[]{:S(2)}) %collective-permute-start.60) | collective-permute-done | bytes 655392 | tf_op jit(solution)/shard_map/ppermute | solution.py:385
  427.9 2.0 collective-permute-start.62
  429.9 7.6 %grad_v.1 = (bf16[8,64,1024]{2,1,0:T(8,128)(2,1)}, bf16[8,64,1024]{2,1,0:T(8,128)(2,1)}) custom-call(s32[2]{0:T(128)} %pad_add_fusion.refs_0_, bf16[512,1024]{1,0:T(8,128)(2,1)} %get-tuple-element.87.refs_1_, bf16[512,1024]{1,0:T(8,128)(2,1)} %collective-permute-done.50.refs_30_.refs_2_, bf16[512,1024]{1,0:T(8,128)(2,1)} %get-tuple-element.121.refs_3_, ...), custom_call_target="tpu_custom_call" | custom-call | flops 8000000000 | bytes 24000000 | tf_op jit(solution)/shard_map/grad_v/pallas_call | solution.py:69
  437.8 9.6 %grad_r.1 = (bf16[8,64,1152]{2,1,0:T(8,128)(2,1)}, bf16[8,64,1152]{2,1,0:T(8,128)(2,1)}) custom-call(s32[2]{0:T(128)} %pad_add_fusion.refs_0_, bf16[512,1024]{1,0:T(8,128)(2,1)} %get-tuple-element.90.refs_2_.refs_1_, bf16[512,1024]{1,0:T(8,128)(2,1)} %collective-permute-done.49.refs_29_.refs_2_, bf16[512,1152]{1,0:T(8,128)(2,1)} %get-tuple-element.119.refs_3_, ...), custom_call_target="tpu_custom_call" | custom-call | flops 8000000000 | bytes 24000000 | tf_op jit(solution)/shard_map/grad_r/pallas_call | solution.py:69
  449.0 2.9 collective-permute-start.64
  452.7 10.5 %back.4 = (f32[1024,128]{1,0:T(8,128)}, f32[256,128]{1,0:T(8,128)}, f32[392,128]{1,0:T(8,128)}) custom-call(f32[4096,128]{1,0:T(8,128)} %get-tuple-element.88.refs_0_, f32[4096,128]{1,0:T(8,128)} %get-tuple-element.116.refs_1_, f32[16,256,128]{2,1,0:T(8,128)} %get-tuple-element.117.refs_2_, f32[256,128]{1,0:T(8,128)} %maximum_bitcast_fusion.1.refs_3_, ...), custom_call_target="tpu_custom_call" | custom-call | flops 10000000000 | bytes 30000000 | tf_op jit(solution)/shard_map/back/pallas_call | solution.py:69
  463.9 2.3 add_convert_fusion.9
  466.2 1.8 collective-permute-start.71
  469.7 10.4 %back.5 = (f32[1024,128]{1,0:T(8,128)}, f32[256,128]{1,0:T(8,128)}, f32[392,128]{1,0:T(8,128)}) custom-call(f32[4096,128]{1,0:T(8,128)} %get-tuple-element.88.refs_0_, f32[4096,128]{1,0:T(8,128)} %get-tuple-element.116.refs_1_, f32[16,256,128]{2,1,0:T(8,128)} %get-tuple-element.117.refs_2_, f32[256,128]{1,0:T(8,128)} %get-tuple-element.129.refs_3_, ...), custom_call_target="tpu_custom_call" | custom-call | flops 10000000000 | bytes 30000000 | tf_op jit(solution)/shard_map/back/pallas_call | solution.py:69
  490.0 10.4 %back.6 = (f32[1024,128]{1,0:T(8,128)}, f32[256,128]{1,0:T(8,128)}, f32[392,128]{1,0:T(8,128)}) custom-call(f32[4096,128]{1,0:T(8,128)} %get-tuple-element.88.refs_0_, f32[4096,128]{1,0:T(8,128)} %get-tuple-element.116.refs_1_, f32[16,256,128]{2,1,0:T(8,128)} %get-tuple-element.117.refs_2_, f32[256,128]{1,0:T(8,128)} %get-tuple-element.131.refs_3_, ...), custom_call_target="tpu_custom_call" | custom-call | flops 10000000000 | bytes 30000000 | tf_op jit(solution)/shard_map/back/pallas_call | solution.py:69
  500.4 10.4 %back.7 = (f32[1024,128]{1,0:T(8,128)}, f32[256,128]{1,0:T(8,128)}, f32[392,128]{1,0:T(8,128)}) custom-call(f32[4096,128]{1,0:T(8,128)} %get-tuple-element.88.refs_0_, f32[4096,128]{1,0:T(8,128)} %get-tuple-element.116.refs_1_, f32[16,256,128]{2,1,0:T(8,128)} %get-tuple-element.117.refs_2_, f32[256,128]{1,0:T(8,128)} %get-tuple-element.135.refs_3_, ...), custom_call_target="tpu_custom_call" | custom-call | flops 10000000000 | bytes 30000000 | tf_op jit(solution)/shard_map/back/pallas_call | solution.py:69
  517.1 7.0 %back_norm.1 = (f32[512,1024]{1,0:T(8,128)}, f32[1,1024]{1,0:T(1,128)}, f32[512,128]{1,0:T(8,128)}, f32[16,128]{1,0:T(8,128)}) custom-call(f32[1024,128]{1,0:T(8,128)} %get-tuple-element.137.refs_0_, f32[1024,128]{1,0:T(8,128)} %get-tuple-element.138.refs_1_, f32[1024,128]{1,0:T(8,128)} %get-tuple-element.139.refs_2_, ...), custom_call_target="tpu_custom_call" | custom-call | flops 6000000000 | bytes 18000000 | tf_op jit(solution)/shard_map/back_norm/pallas_call | solution.py:69
  526.3 2.3 collective-permute-start.85
  529.4 6.2 %collective-permute-done.85 = bf16[1,128,512]{2,1,0:T(8,128)(2,1)} collective-permute-done((bf16[1,128,512]{2,1,0:T(8,128)(2,1)}, bf16[1,128,512]{2,1,0:T(8,128)(2,1)}, u32[]{:S(2)}, u32[]{:S(2)}) %collective-permute-start.85) | collective-permute-done | bytes 131104 | tf_op jit(solution)/shard_map/ppermute | solution.py:385
  538.6 3.9 collective-permute-done.74
  542.6 2.0 collective-permute-start.75
  544.6 3.5 collective-permute-done.75
  550.9 2.4 collective-permute-done.91
  557.5 5.6 collective-permute-done.81
  566.8 3.7 collective-permute-done.82
  570.6 5.9 input.1
  579.1 7.9 %collective-permute-done.79 = bf16[1,64,1152]{2,1,0:T(8,128)(2,1)S(1)} collective-permute-done((bf16[1,64,1152]{2,1,0:T(8,128)(2,1)S(1)}, bf16[1,64,1152]{2,1,0:T(8,128)(2,1)S(1)}, u32[]{:S(2)}, u32[]{:S(2)}) %collective-permute-start.79) | collective-permute-done | bytes 147488 | tf_op jit(solution)/shard_map/ppermute | solution.py:385
  (462 shorter events, 122.6 us)
Async XLA Ops:
  2.8 13.8 %collective-permute-start = (f32[1,1,56]{2,1,0:T(1,128)S(1)}, f32[1,1,56]{2,1,0:T(1,128)S(1)}, u32[]{:S(2)}, u32[]{:S(2)}) collective-permute-start(f32[1,1,56]{2,1,0:T(1,128)S(1)} %maximum_convert_fusion), channel_id=1, source_target_pairs={{0,1},{1,0},{2,3},{3,2},{4,5},{5,4},{6,7},{7,6},{8,9},{9,8},{10,11... | collective-permute-start | bytes 680 | tf_op jit(solution)/shard_map/ppermute | solution.py:385
  5.0 31.8 %collective-permute-start.6 = (bf16[1,32,2304]{2,1,0:T(8,128)(2,1)S(1)}, bf16[1,32,2304]{2,1,0:T(8,128)(2,1)S(1)}, u32[]{:S(2)}, u32[]{:S(2)}) collective-permute-start(bf16[1,32,2304]{2,1,0:T(8,128)(2,1)S(1)} %pad_maximum_fusion.27), channel_id=1, source_target_pairs={{0,16},{4,20},{8,24},{12,28},{16,0},{20,4},{24,8},{28,12},{1,17},{... | collective-permute-start | bytes 442376 | tf_op jit(solution)/shard_map/ppermute | solution.py:385
  9.6 26.1 %collective-permute-start.5 = (bf16[1,32,2048]{2,1,0:T(8,128)(2,1)S(1)}, bf16[1,32,2048]{2,1,0:T(8,128)(2,1)S(1)}, u32[]{:S(2)}, u32[]{:S(2)}) collective-permute-start(bf16[1,32,2048]{2,1,0:T(8,128)(2,1)S(1)} %convert_bitcast_fusion.5), channel_id=1, source_target_pairs={{0,16},{4,20},{8,24},{12,28},{16,0},{20,4},{24,8},{28,12},{1,17},{... | collective-permute-start | bytes 393224 | tf_op jit(solution)/shard_map/ppermute | solution.py:385
  9.8 29.2 %collective-permute-start.7 = (bf16[1,80,1024]{2,1,0:T(8,128)(2,1)S(1)}, bf16[1,80,1024]{2,1,0:T(8,128)(2,1)S(1)}, u32[]{:S(2)}, u32[]{:S(2)}) collective-permute-start(bf16[1,80,1024]{2,1,0:T(8,128)(2,1)S(1)} %convert_bitcast_fusion.2), channel_id=1, source_target_pairs={{0,2},{1,3},{2,0},{3,1},{4,6},{5,7},{6,4},{7,5},{8,10},{9,11},{10,... | collective-permute-start | bytes 491528 | tf_op jit(solution)/shard_map/ppermute | solution.py:385
  33.1 17.4 %collective-permute-start.4 = (f32[288,128]{1,0:T(8,128)S(1)}, f32[288,128]{1,0:T(8,128)S(1)}, u32[]{:S(2)}, u32[]{:S(2)}) collective-permute-start(f32[288,128]{1,0:T(8,128)S(1)} %pad_maximum_fusion.26), channel_id=1, source_target_pairs={{0,16},{4,20},{8,24},{12,28},{16,0},{20,4},{24,8},{28,12},{1,17},{... | collective-permute-start | bytes 442376 | tf_op jit(solution)/shard_map/ppermute | solution.py:385
  35.8 31.2 %collective-permute-start.11 = (bf16[2,32,2048]{2,1,0:T(8,128)(2,1)S(1)}, bf16[2,32,2048]{2,1,0:T(8,128)(2,1)S(1)}, u32[]{:S(2)}, u32[]{:S(2)}) collective-permute-start(bf16[2,32,2048]{2,1,0:T(8,128)(2,1)S(1)} %pad_maximum_fusion.20.refs_8_.refs_1_), channel_id=1, source_target_pairs={{0,8},{4,12},{8,0},{12,4},{16,24},{20,28},{24,16},{28,20},{1,9},{5... | collective-permute-start | bytes 786440 | tf_op jit(solution)/shard_map/ppermute | solution.py:385
  36.5 12.1 %collective-permute-start.15 = (bf16[1,64,1024]{2,1,0:T(8,128)(2,1)}, bf16[1,64,1024]{2,1,0:T(8,128)(2,1)S(1)}, u32[]{:S(2)}, u32[]{:S(2)}) collective-permute-start(bf16[1,64,1024]{2,1,0:T(8,128)(2,1)} %tie.13), channel_id=1, source_target_pairs={{0,16},{4,20},{8,24},{12,28},{16,0},{20,4},{24,8},{28,12},{1,17},{... | collective-permute-start | bytes 393224 | tf_op jit(solution)/shard_map/ppermute | solution.py:385
  37.6 35.6 %collective-permute-start.13 = (bf16[2,32,2304]{2,1,0:T(8,128)(2,1)}, bf16[2,32,2304]{2,1,0:T(8,128)(2,1)S(1)}, u32[]{:S(2)}, u32[]{:S(2)}) collective-permute-start(bf16[2,32,2304]{2,1,0:T(8,128)(2,1)} %pad_maximum_fusion.18.refs_9_), channel_id=1, source_target_pairs={{0,8},{4,12},{8,0},{12,4},{16,24},{20,28},{24,16},{28,20},{1,9},{5... | collective-permute-start | bytes 884744 | tf_op jit(solution)/shard_map/ppermute | solution.py:385
  39.7 36.2 %collective-permute-start.16 = (bf16[2,80,1024]{2,1,0:T(8,128)(2,1)}, bf16[2,80,1024]{2,1,0:T(8,128)(2,1)}, u32[]{:S(2)}, u32[]{:S(2)}) collective-permute-start(bf16[2,80,1024]{2,1,0:T(8,128)(2,1)} %pad_maximum_fusion.12.refs_10_), channel_id=1, source_target_pairs={{0,4},{4,0},{8,12},{12,8},{16,20},{20,16},{24,28},{28,24},{1,5},{5... | collective-permute-start | bytes 983048 | tf_op jit(solution)/shard_map/ppermute | solution.py:385
  49.3 72.6 %collective-permute-start.23 = (bf16[2,64,1024]{2,1,0:T(8,128)(2,1)}, bf16[2,64,1024]{2,1,0:T(8,128)(2,1)}, u32[]{:S(2)}, u32[]{:S(2)}) collective-permute-start(bf16[2,64,1024]{2,1,0:T(8,128)(2,1)} %pad_maximum_fusion.21.refs_8_), channel_id=1, source_target_pairs={{0,8},{4,12},{8,0},{12,4},{16,24},{20,28},{24,16},{28,20},{1,9},{5... | collective-permute-start | bytes 786440 | tf_op jit(solution)/shard_map/ppermute | solution.py:385
  67.1 31.6 %collective-permute-start.12 = (bf16[4,32,2048]{2,1,0:T(8,128)(2,1)S(1)}, bf16[4,32,2048]{2,1,0:T(8,128)(2,1)}, u32[]{:S(2)}, u32[]{:S(2)}) collective-permute-start(bf16[4,32,2048]{2,1,0:T(8,128)(2,1)S(1)} %pad_maximum_fusion.10.refs_1_), channel_id=1, source_target_pairs={{0,4},{4,0},{8,12},{12,8},{16,20},{20,16},{24,28},{28,24},{1,5},{5... | collective-permute-start | bytes 1572872 | tf_op jit(solution)/shard_map/ppermute | solution.py:385
  70.7 12.7 %collective-permute-start.25 = (bf16[1,32,2560]{2,1,0:T(8,128)(2,1)}, bf16[1,32,2560]{2,1,0:T(8,128)(2,1)S(1)}, u32[]{:S(2)}, u32[]{:S(2)}) collective-permute-start(bf16[1,32,2560]{2,1,0:T(8,128)(2,1)} %tie.15), channel_id=1, source_target_pairs={{0,16},{4,20},{8,24},{12,28},{16,0},{20,4},{24,8},{28,12},{1,17},{... | collective-permute-start | bytes 491528 | tf_op jit(solution)/shard_map/ppermute | solution.py:385
  76.0 26.5 %collective-permute-start.14 = (bf16[4,32,2304]{2,1,0:T(8,128)(2,1)}, bf16[4,32,2304]{2,1,0:T(8,128)(2,1)S(1)}, u32[]{:S(2)}, u32[]{:S(2)}) collective-permute-start(bf16[4,32,2304]{2,1,0:T(8,128)(2,1)} %pad_maximum_fusion.9.refs_1_), channel_id=1, source_target_pairs={{0,2},{1,3},{2,0},{3,1},{4,6},{5,7},{6,4},{7,5},{8,10},{9,11},{10,... | collective-permute-start | bytes 1769480 | tf_op jit(solution)/shard_map/ppermute | solution.py:385
  90.7 10.9 %collective-permute-start.29 = (bf16[2,32,2560]{2,1,0:T(8,128)(2,1)S(1)}, bf16[2,32,2560]{2,1,0:T(8,128)(2,1)S(1)}, u32[]{:S(2)}, u32[]{:S(2)}) collective-permute-start(bf16[2,32,2560]{2,1,0:T(8,128)(2,1)S(1)} %pad_maximum_fusion.14), channel_id=1, source_target_pairs={{0,8},{4,12},{8,0},{12,4},{16,24},{20,28},{24,16},{28,20},{1,9},{5... | collective-permute-start | bytes 983048 | tf_op jit(solution)/shard_map/ppermute | solution.py:385
  100.9 39.1 %collective-permute-start.17 = (bf16[8,32,2048]{2,1,0:T(8,128)(2,1)}, bf16[8,32,2048]{2,1,0:T(8,128)(2,1)}, u32[]{:S(2)}, u32[]{:S(2)}) collective-permute-start(bf16[8,32,2048]{2,1,0:T(8,128)(2,1)} %pad_maximum_fusion.4.refs_6_.refs_9_.refs_15_), channel_id=1, source_target_pairs={{0,2},{1,3},{2,0},{3,1},{4,6},{5,7},{6,4},{7,5},{8,10},{9,11},{10,... | collective-permute-start | bytes 3145736 | tf_op jit(solution)/shard_map/ppermute | solution.py:385
  103.6 36.5 %collective-permute-start.20 = (bf16[8,32,2304]{2,1,0:T(8,128)(2,1)}, bf16[8,32,2304]{2,1,0:T(8,128)(2,1)}, u32[]{:S(2)}, u32[]{:S(2)}) collective-permute-start(bf16[8,32,2304]{2,1,0:T(8,128)(2,1)} %pad_maximum_fusion.3.refs_7_.refs_13_.refs_19_), channel_id=1, source_target_pairs={{0,4},{4,0},{8,12},{12,8},{16,20},{20,16},{24,28},{28,24},{1,5},{5... | collective-permute-start | bytes 3538952 | tf_op jit(solution)/shard_map/ppermute | solution.py:385
  120.6 18.9 %collective-permute-start.30 = (bf16[4,32,2560]{2,1,0:T(8,128)(2,1)}, bf16[4,32,2560]{2,1,0:T(8,128)(2,1)S(1)}, u32[]{:S(2)}, u32[]{:S(2)}) collective-permute-start(bf16[4,32,2560]{2,1,0:T(8,128)(2,1)} %tie.18), channel_id=1, source_target_pairs={{0,2},{1,3},{2,0},{3,1},{4,6},{5,7},{6,4},{7,5},{8,10},{9,11},{10,... | collective-permute-start | bytes 1966088 | tf_op jit(solution)/shard_map/ppermute | solution.py:385
  123.7 15.7 %collective-permute-start.24 = (bf16[4,64,1024]{2,1,0:T(8,128)(2,1)}, bf16[4,64,1024]{2,1,0:T(8,128)(2,1)S(1)}, u32[]{:S(2)}, u32[]{:S(2)}) collective-permute-start(bf16[4,64,1024]{2,1,0:T(8,128)(2,1)} %tie.14), channel_id=1, source_target_pairs={{0,4},{4,0},{8,12},{12,8},{16,20},{20,16},{24,28},{28,24},{1,5},{5... | collective-permute-start | bytes 1572872 | tf_op jit(solution)/shard_map/ppermute | solution.py:385
  124.8 26.0 %collective-permute-start.40 = (bf16[4,80,1024]{2,1,0:T(8,128)(2,1)S(1)}, bf16[4,80,1024]{2,1,0:T(8,128)(2,1)S(1)}, u32[]{:S(2)}, u32[]{:S(2)}) collective-permute-start(bf16[4,80,1024]{2,1,0:T(8,128)(2,1)S(1)} %copy-done.3), channel_id=1, source_target_pairs={{0,16},{4,20},{8,24},{12,28},{16,0},{20,4},{24,8},{28,12},{1,17},{... | collective-permute-start | bytes 1966088 | tf_op jit(solution)/shard_map/ppermute | solution.py:385
  139.5 31.1 %collective-permute-start.18 = (bf16[8,32,2048]{2,1,0:T(8,128)(2,1)}, bf16[8,32,2048]{2,1,0:T(8,128)(2,1)}, u32[]{:S(2)}, u32[]{:S(2)}) collective-permute-start(bf16[8,32,2048]{2,1,0:T(8,128)(2,1)} %pad_maximum_fusion.4.refs_6_.refs_9_.refs_15_), channel_id=1, source_target_pairs={{0,1},{1,0},{2,3},{3,2},{4,5},{5,4},{6,7},{7,6},{8,9},{9,8},{10,11... | collective-permute-start | bytes 3145736 | tf_op jit(solution)/shard_map/ppermute | solution.py:385
  139.5 31.2 %collective-permute-start.21 = (bf16[8,32,2304]{2,1,0:T(8,128)(2,1)}, bf16[8,32,2304]{2,1,0:T(8,128)(2,1)}, u32[]{:S(2)}, u32[]{:S(2)}) collective-permute-start(bf16[8,32,2304]{2,1,0:T(8,128)(2,1)} %pad_maximum_fusion.3.refs_7_.refs_13_.refs_19_), channel_id=1, source_target_pairs={{0,1},{1,0},{2,3},{3,2},{4,5},{5,4},{6,7},{7,6},{8,9},{9,8},{10,11... | collective-permute-start | bytes 3538952 | tf_op jit(solution)/shard_map/ppermute | solution.py:385
  140.0 31.4 %collective-permute-start.19 = (bf16[8,32,2048]{2,1,0:T(8,128)(2,1)}, bf16[8,32,2048]{2,1,0:T(8,128)(2,1)}, u32[]{:S(2)}, u32[]{:S(2)}) collective-permute-start(bf16[8,32,2048]{2,1,0:T(8,128)(2,1)} %collective-permute-done.17.refs_10_.refs_16_), channel_id=1, source_target_pairs={{0,1},{1,0},{2,3},{3,2},{4,5},{5,4},{6,7},{7,6},{8,9},{9,8},{10,11... | collective-permute-start | bytes 3145736 | tf_op jit(solution)/shard_map/ppermute | solution.py:385
  140.1 31.6 %collective-permute-start.22 = (bf16[8,32,2304]{2,1,0:T(8,128)(2,1)}, bf16[8,32,2304]{2,1,0:T(8,128)(2,1)}, u32[]{:S(2)}, u32[]{:S(2)}) collective-permute-start(bf16[8,32,2304]{2,1,0:T(8,128)(2,1)} %collective-permute-done.20.refs_14_.refs_20_), channel_id=1, source_target_pairs={{0,1},{1,0},{2,3},{3,2},{4,5},{5,4},{6,7},{7,6},{8,9},{9,8},{10,11... | collective-permute-start | bytes 3538952 | tf_op jit(solution)/shard_map/ppermute | solution.py:385
  150.8 16.9 %collective-permute-start.27 = (bf16[4,32,2560]{2,1,0:T(8,128)(2,1)}, bf16[4,32,2560]{2,1,0:T(8,128)(2,1)S(1)}, u32[]{:S(2)}, u32[]{:S(2)}) collective-permute-start(bf16[4,32,2560]{2,1,0:T(8,128)(2,1)} %tie.16), channel_id=1, source_target_pairs={{0,4},{4,0},{8,12},{12,8},{16,20},{20,16},{24,28},{28,24},{1,5},{5... | collective-permute-start | bytes 1966088 | tf_op jit(solution)/shard_map/ppermute | solution.py:385
  167.7 33.1 %collective-permute-start.31 = (bf16[8,64,1024]{2,1,0:T(8,128)(2,1)}, bf16[8,64,1024]{2,1,0:T(8,128)(2,1)}, u32[]{:S(2)}, u32[]{:S(2)}) collective-permute-start(bf16[8,64,1024]{2,1,0:T(8,128)(2,1)} %pad_maximum_fusion.5.refs_17_.refs_5_.refs_23_), channel_id=1, source_target_pairs={{0,2},{1,3},{2,0},{3,1},{4,6},{5,7},{6,4},{7,5},{8,10},{9,11},{10,... | collective-permute-start | bytes 3145736 | tf_op jit(solution)/shard_map/ppermute | solution.py:385
  170.6 29.7 %collective-permute-start.41 = (bf16[8,80,1024]{2,1,0:T(8,128)(2,1)S(1)}, bf16[8,80,1024]{2,1,0:T(8,128)(2,1)}, u32[]{:S(2)}, u32[]{:S(2)}) collective-permute-start(bf16[8,80,1024]{2,1,0:T(8,128)(2,1)S(1)} %pad_maximum_fusion.2.refs_0_), channel_id=1, source_target_pairs={{0,8},{4,12},{8,0},{12,4},{16,24},{20,28},{24,16},{28,20},{1,9},{5... | collective-permute-start | bytes 3932168 | tf_op jit(solution)/shard_map/ppermute | solution.py:385
  170.6 31.8 %collective-permute-start.37 = (bf16[8,32,2560]{2,1,0:T(8,128)(2,1)S(1)}, bf16[8,32,2560]{2,1,0:T(8,128)(2,1)}, u32[]{:S(2)}, u32[]{:S(2)}) collective-permute-start(bf16[8,32,2560]{2,1,0:T(8,128)(2,1)S(1)} %pad_maximum_fusion.1.refs_19_.refs_0_), channel_id=1, source_target_pairs={{0,4},{4,0},{8,12},{12,8},{16,20},{20,16},{24,28},{28,24},{1,5},{5... | collective-permute-start | bytes 3932168 | tf_op jit(solution)/shard_map/ppermute | solution.py:385
  171.4 49.0 %collective-permute-start.34 = (bf16[8,32,2560]{2,1,0:T(8,128)(2,1)}, bf16[8,32,2560]{2,1,0:T(8,128)(2,1)}, u32[]{:S(2)}, u32[]{:S(2)}) collective-permute-start(bf16[8,32,2560]{2,1,0:T(8,128)(2,1)} %pad_maximum_fusion.refs_18_.refs_0_), channel_id=1, source_target_pairs={{0,2},{1,3},{2,0},{3,1},{4,6},{5,7},{6,4},{7,5},{8,10},{9,11},{10,... | collective-permute-start | bytes 3932168 | tf_op jit(solution)/shard_map/ppermute | solution.py:385
  200.3 21.9 %collective-permute-start.43 = (bf16[8,80,1024]{2,1,0:T(8,128)(2,1)}, bf16[8,80,1024]{2,1,0:T(8,128)(2,1)}, u32[]{:S(2)}, u32[]{:S(2)}) collective-permute-start(bf16[8,80,1024]{2,1,0:T(8,128)(2,1)} %tie.25.refs_12_.refs_18_), channel_id=1, source_target_pairs={{0,1},{1,0},{2,3},{3,2},{4,5},{5,4},{6,7},{7,6},{8,9},{9,8},{10,11... | collective-permute-start | bytes 3932168 | tf_op jit(solution)/shard_map/ppermute | solution.py:385
  200.3 20.6 %collective-permute-start.32 = (bf16[8,64,1024]{2,1,0:T(8,128)(2,1)}, bf16[8,64,1024]{2,1,0:T(8,128)(2,1)}, u32[]{:S(2)}, u32[]{:S(2)}) collective-permute-start(bf16[8,64,1024]{2,1,0:T(8,128)(2,1)} %pad_maximum_fusion.5.refs_17_.refs_5_.refs_23_), channel_id=1, source_target_pairs={{0,1},{1,0},{2,3},{3,2},{4,5},{5,4},{6,7},{7,6},{8,9},{9,8},{10,11... | collective-permute-start | bytes 3145736 | tf_op jit(solution)/shard_map/ppermute | solution.py:385
  200.8 21.4 %collective-permute-start.33 = (bf16[8,64,1024]{2,1,0:T(8,128)(2,1)}, bf16[8,64,1024]{2,1,0:T(8,128)(2,1)}, u32[]{:S(2)}, u32[]{:S(2)}) collective-permute-start(bf16[8,64,1024]{2,1,0:T(8,128)(2,1)} %collective-permute-done.31.refs_6_.refs_24_), channel_id=1, source_target_pairs={{0,1},{1,0},{2,3},{3,2},{4,5},{5,4},{6,7},{7,6},{8,9},{9,8},{10,11... | collective-permute-start | bytes 3145736 | tf_op jit(solution)/shard_map/ppermute | solution.py:385
  202.4 17.9 %collective-permute-start.44 = (bf16[512,512]{1,0:T(8,128)(2,1)S(1)}, bf16[512,512]{1,0:T(8,128)(2,1)}, u32[]{:S(2)}, u32[]{:S(2)}) collective-permute-start(bf16[512,512]{1,0:T(8,128)(2,1)S(1)} %get-tuple-element.190), channel_id=1, source_target_pairs={{0,1},{1,0},{2,3},{3,2},{4,5},{5,4},{6,7},{7,6},{8,9},{9,8},{10,11... | collective-permute-start | bytes 1572872 | tf_op jit(solution)/shard_map/ppermute | solution.py:385
  220.3 12.2 %collective-permute-start.42 = (bf16[8,80,1024]{2,1,0:T(8,128)(2,1)S(1)}, bf16[8,80,1024]{2,1,0:T(8,128)(2,1)}, u32[]{:S(2)}, u32[]{:S(2)}) collective-permute-start(bf16[8,80,1024]{2,1,0:T(8,128)(2,1)S(1)} %copy-done.5), channel_id=1, source_target_pairs={{0,1},{1,0},{2,3},{3,2},{4,5},{5,4},{6,7},{7,6},{8,9},{9,8},{10,11... | collective-permute-start | bytes 3932168 | tf_op jit(solution)/shard_map/ppermute | solution.py:385
  220.4 12.2 %collective-permute-start.39 = (bf16[8,32,2560]{2,1,0:T(8,128)(2,1)}, bf16[8,32,2560]{2,1,0:T(8,128)(2,1)}, u32[]{:S(2)}, u32[]{:S(2)}) collective-permute-start(bf16[8,32,2560]{2,1,0:T(8,128)(2,1)} %tie.22.refs_8_.refs_14_), channel_id=1, source_target_pairs={{0,1},{1,0},{2,3},{3,2},{4,5},{5,4},{6,7},{7,6},{8,9},{9,8},{10,11... | collective-permute-start | bytes 3932168 | tf_op jit(solution)/shard_map/ppermute | solution.py:385
  221.7 10.9 %collective-permute-start.38 = (bf16[8,32,2560]{2,1,0:T(8,128)(2,1)S(1)}, bf16[8,32,2560]{2,1,0:T(8,128)(2,1)}, u32[]{:S(2)}, u32[]{:S(2)}) collective-permute-start(bf16[8,32,2560]{2,1,0:T(8,128)(2,1)S(1)} %copy-done.7), channel_id=1, source_target_pairs={{0,1},{1,0},{2,3},{3,2},{4,5},{5,4},{6,7},{7,6},{8,9},{9,8},{10,11... | collective-permute-start | bytes 3932168 | tf_op jit(solution)/shard_map/ppermute | solution.py:385
  252.6 27.5 %collective-permute-start.47 = (bf16[512,2560]{1,0:T(8,128)(2,1)}, bf16[512,2560]{1,0:T(8,128)(2,1)}, u32[]{:S(2)}, u32[]{:S(2)}) collective-permute-start(bf16[512,2560]{1,0:T(8,128)(2,1)} %get-tuple-element.94.refs_1_), channel_id=1, source_target_pairs={{0,1},{1,0},{2,3},{3,2},{4,5},{5,4},{6,7},{7,6},{8,9},{9,8},{10,11... | collective-permute-start | bytes 7864328 | tf_op jit(solution)/shard_map/ppermute | solution.py:385
  254.7 54.9 %collective-permute-start.50 = (bf16[512,1024]{1,0:T(8,128)(2,1)}, bf16[512,1024]{1,0:T(8,128)(2,1)}, u32[]{:S(2)}, u32[]{:S(2)}) collective-permute-start(bf16[512,1024]{1,0:T(8,128)(2,1)} %get-tuple-element.87.refs_1_), channel_id=1, source_target_pairs={{0,1},{1,0},{2,3},{3,2},{4,5},{5,4},{6,7},{7,6},{8,9},{9,8},{10,11... | collective-permute-start | bytes 3145736 | tf_op jit(solution)/shard_map/ppermute | solution.py:385
  255.2 55.1 %collective-permute-start.49 = (bf16[512,1024]{1,0:T(8,128)(2,1)}, bf16[512,1024]{1,0:T(8,128)(2,1)}, u32[]{:S(2)}, u32[]{:S(2)}) collective-permute-start(bf16[512,1024]{1,0:T(8,128)(2,1)} %get-tuple-element.90.refs_2_.refs_1_), channel_id=1, source_target_pairs={{0,1},{1,0},{2,3},{3,2},{4,5},{5,4},{6,7},{7,6},{8,9},{9,8},{10,11... | collective-permute-start | bytes 3145736 | tf_op jit(solution)/shard_map/ppermute | solution.py:385
  255.3 33.5 %collective-permute-start.45 = (bf16[512,1024]{1,0:T(8,128)(2,1)}, bf16[512,1024]{1,0:T(8,128)(2,1)}, u32[]{:S(2)}, u32[]{:S(2)}) collective-permute-start(bf16[512,1024]{1,0:T(8,128)(2,1)} %get-tuple-element.93.refs_1_), channel_id=1, source_target_pairs={{0,1},{1,0},{2,3},{3,2},{4,5},{5,4},{6,7},{7,6},{8,9},{9,8},{10,11... | collective-permute-start | bytes 3145736 | tf_op jit(solution)/shard_map/ppermute | solution.py:385
  255.7 33.1 %collective-permute-start.46 = (bf16[512,2560]{1,0:T(8,128)(2,1)}, bf16[512,2560]{1,0:T(8,128)(2,1)}, u32[]{:S(2)}, u32[]{:S(2)}) collective-permute-start(bf16[512,2560]{1,0:T(8,128)(2,1)} %get-tuple-element.97.refs_4_), channel_id=1, source_target_pairs={{0,1},{1,0},{2,3},{3,2},{4,5},{5,4},{6,7},{7,6},{8,9},{9,8},{10,11... | collective-permute-start | bytes 7864328 | tf_op jit(solution)/shard_map/ppermute | solution.py:385
  280.1 30.4 %collective-permute-start.48 = (bf16[512,2048]{1,0:T(8,128)(2,1)S(1)}, bf16[512,2048]{1,0:T(8,128)(2,1)}, u32[]{:S(2)}, u32[]{:S(2)}) collective-permute-start(bf16[512,2048]{1,0:T(8,128)(2,1)S(1)} %copy-done), channel_id=1, source_target_pairs={{0,1},{1,0},{2,3},{3,2},{4,5},{5,4},{6,7},{7,6},{8,9},{9,8},{10,11... | collective-permute-start | bytes 6291464 | tf_op jit(solution)/shard_map/ppermute | solution.py:385
  288.7 107.1 %collective-permute-start.58 = (bf16[512,512]{1,0:T(8,128)(2,1)}, bf16[512,512]{1,0:T(8,128)(2,1)}, u32[]{:S(2)}, u32[]{:S(2)}) collective-permute-start(bf16[512,512]{1,0:T(8,128)(2,1)} %get-tuple-element.124), channel_id=1, source_target_pairs={{0,1},{1,0},{2,3},{3,2},{4,5},{5,4},{6,7},{7,6},{8,9},{9,8},{10,11... | collective-permute-start | bytes 1572872 | tf_op jit(solution)/shard_map/ppermute | solution.py:385
  307.8 82.2 %collective-permute-start.59 = (bf16[8,64,1280]{2,1,0:T(8,128)(2,1)}, bf16[8,64,1280]{2,1,0:T(8,128)(2,1)}, u32[]{:S(2)}, u32[]{:S(2)}) collective-permute-start(bf16[8,64,1280]{2,1,0:T(8,128)(2,1)} %get-tuple-element.126), channel_id=1, source_target_pairs={{0,2},{1,3},{2,0},{3,1},{4,6},{5,7},{6,4},{7,5},{8,10},{9,11},{10,... | collective-permute-start | bytes 3932168 | tf_op jit(solution)/shard_map/ppermute | solution.py:385
  309.6 31.1 %collective-permute-start.52 = (bf16[8,64,1280]{2,1,0:T(8,128)(2,1)}, bf16[8,64,1280]{2,1,0:T(8,128)(2,1)}, u32[]{:S(2)}, u32[]{:S(2)}) collective-permute-start(bf16[8,64,1280]{2,1,0:T(8,128)(2,1)} %get-tuple-element.115), channel_id=1, source_target_pairs={{0,4},{4,0},{8,12},{12,8},{16,20},{20,16},{24,28},{28,24},{1,5},{5... | collective-permute-start | bytes 3932168 | tf_op jit(solution)/shard_map/ppermute | solution.py:385
  310.2 57.1 %collective-permute-start.51 = (bf16[8,160,512]{2,1,0:T(8,128)(2,1)}, bf16[8,160,512]{2,1,0:T(8,128)(2,1)}, u32[]{:S(2)}, u32[]{:S(2)}) collective-permute-start(bf16[8,160,512]{2,1,0:T(8,128)(2,1)} %get-tuple-element.114), channel_id=1, source_target_pairs={{0,2},{1,3},{2,0},{3,1},{4,6},{5,7},{6,4},{7,5},{8,10},{9,11},{10,... | collective-permute-start | bytes 3932168 | tf_op jit(solution)/shard_map/ppermute | solution.py:385
  383.2 44.7 %collective-permute-start.57 = (bf16[512,1024]{1,0:T(8,128)(2,1)}, bf16[512,1024]{1,0:T(8,128)(2,1)}, u32[]{:S(2)}, u32[]{:S(2)}) collective-permute-start(bf16[512,1024]{1,0:T(8,128)(2,1)} %get-tuple-element.122), channel_id=1, source_target_pairs={{0,1},{1,0},{2,3},{3,2},{4,5},{5,4},{6,7},{7,6},{8,9},{9,8},{10,11... | collective-permute-start | bytes 3145736 | tf_op jit(solution)/shard_map/ppermute | solution.py:385
  383.3 54.3 %collective-permute-start.56 = (bf16[512,1152]{1,0:T(8,128)(2,1)}, bf16[512,1152]{1,0:T(8,128)(2,1)}, u32[]{:S(2)}, u32[]{:S(2)}) collective-permute-start(bf16[512,1152]{1,0:T(8,128)(2,1)} %get-tuple-element.120), channel_id=1, source_target_pairs={{0,1},{1,0},{2,3},{3,2},{4,5},{5,4},{6,7},{7,6},{8,9},{9,8},{10,11... | collective-permute-start | bytes 3538952 | tf_op jit(solution)/shard_map/ppermute | solution.py:385
  387.3 27.2 %collective-permute-start.61 = (bf16[4,64,1280]{2,1,0:T(8,128)(2,1)}, bf16[4,64,1280]{2,1,0:T(8,128)(2,1)}, u32[]{:S(2)}, u32[]{:S(2)}) collective-permute-start(bf16[4,64,1280]{2,1,0:T(8,128)(2,1)} %get-tuple-element.168.refs_5_), channel_id=1, source_target_pairs={{0,2},{1,3},{2,0},{3,1},{4,6},{5,7},{6,4},{7,5},{8,10},{9,11},{10,... | collective-permute-start | bytes 1966088 | tf_op jit(solution)/shard_map/ppermute | solution.py:385
  395.0 17.9 %collective-permute-start.63 = (bf16[4,64,1280]{2,1,0:T(8,128)(2,1)}, bf16[4,64,1280]{2,1,0:T(8,128)(2,1)S(1)}, u32[]{:S(2)}, u32[]{:S(2)}) collective-permute-start(bf16[4,64,1280]{2,1,0:T(8,128)(2,1)} %get-tuple-element.166.refs_6_), channel_id=1, source_target_pairs={{0,4},{4,0},{8,12},{12,8},{16,20},{20,16},{24,28},{28,24},{1,5},{5... | collective-permute-start | bytes 1966088 | tf_op jit(solution)/shard_map/ppermute | solution.py:385
  403.9 23.0 %collective-permute-start.60 = (bf16[4,160,512]{2,1,0:T(8,128)(2,1)S(1)}, bf16[4,160,512]{2,1,0:T(8,128)(2,1)S(1)}, u32[]{:S(2)}, u32[]{:S(2)}) collective-permute-start(bf16[4,160,512]{2,1,0:T(8,128)(2,1)S(1)} %copy-done.33), channel_id=1, source_target_pairs={{0,4},{4,0},{8,12},{12,8},{16,20},{20,16},{24,28},{28,24},{1,5},{5... | collective-permute-start | bytes 1966088 | tf_op jit(solution)/shard_map/ppermute | solution.py:385
  412.9 50.2 %collective-permute-start.66 = (bf16[8,128,512]{2,1,0:T(8,128)(2,1)}, bf16[8,128,512]{2,1,0:T(8,128)(2,1)}, u32[]{:S(2)}, u32[]{:S(2)}) collective-permute-start(bf16[8,128,512]{2,1,0:T(8,128)(2,1)} %get-tuple-element.133), channel_id=1, source_target_pairs={{0,4},{4,0},{8,12},{12,8},{16,20},{20,16},{24,28},{28,24},{1,5},{5... | collective-permute-start | bytes 3145736 | tf_op jit(solution)/shard_map/ppermute | solution.py:385
  414.5 33.0 %collective-permute-start.68 = (bf16[2,64,1280]{2,1,0:T(8,128)(2,1)}, bf16[2,64,1280]{2,1,0:T(8,128)(2,1)S(1)}, u32[]{:S(2)}, u32[]{:S(2)}) collective-permute-start(bf16[2,64,1280]{2,1,0:T(8,128)(2,1)} %get-tuple-element.178.refs_11_), channel_id=1, source_target_pairs={{0,8},{4,12},{8,0},{12,4},{16,24},{20,28},{24,16},{28,20},{1,9},{5... | collective-permute-start | bytes 983048 | tf_op jit(solution)/shard_map/ppermute | solution.py:385
  427.0 22.0 %collective-permute-start.65 = (bf16[2,64,1280]{2,1,0:T(8,128)(2,1)S(1)}, bf16[2,64,1280]{2,1,0:T(8,128)(2,1)S(1)}, u32[]{:S(2)}, u32[]{:S(2)}) collective-permute-start(bf16[2,64,1280]{2,1,0:T(8,128)(2,1)S(1)} %get-tuple-element.180.refs_6_), channel_id=1, source_target_pairs={{0,8},{4,12},{8,0},{12,4},{16,24},{20,28},{24,16},{28,20},{1,9},{5... | collective-permute-start | bytes 983048 | tf_op jit(solution)/shard_map/ppermute | solution.py:385
  427.9 20.3 %collective-permute-start.62 = (bf16[2,160,512]{2,1,0:T(8,128)(2,1)}, bf16[2,160,512]{2,1,0:T(8,128)(2,1)S(1)}, u32[]{:S(2)}, u32[]{:S(2)}) collective-permute-start(bf16[2,160,512]{2,1,0:T(8,128)(2,1)} %get-tuple-element.182.refs_7_), channel_id=1, source_target_pairs={{0,8},{4,12},{8,0},{12,4},{16,24},{20,28},{24,16},{28,20},{1,9},{5... | collective-permute-start | bytes 983048 | tf_op jit(solution)/shard_map/ppermute | solution.py:385
  437.5 49.9 %collective-permute-start.67 = (bf16[8,64,1024]{2,1,0:T(8,128)(2,1)}, bf16[8,64,1024]{2,1,0:T(8,128)(2,1)S(1)}, u32[]{:S(2)}, u32[]{:S(2)}) collective-permute-start(bf16[8,64,1024]{2,1,0:T(8,128)(2,1)} %get-tuple-element.134), channel_id=1, source_target_pairs={{0,2},{1,3},{2,0},{3,1},{4,6},{5,7},{6,4},{7,5},{8,10},{9,11},{10,... | collective-permute-start | bytes 3145736 | tf_op jit(solution)/shard_map/ppermute | solution.py:385
  447.4 67.3 %collective-permute-start.72 = (bf16[8,64,1152]{2,1,0:T(8,128)(2,1)}, bf16[8,64,1152]{2,1,0:T(8,128)(2,1)}, u32[]{:S(2)}, u32[]{:S(2)}) collective-permute-start(bf16[8,64,1152]{2,1,0:T(8,128)(2,1)} %get-tuple-element.142), channel_id=1, source_target_pairs={{0,4},{4,0},{8,12},{12,8},{16,20},{20,16},{24,28},{28,24},{1,5},{5... | collective-permute-start | bytes 3538952 | tf_op jit(solution)/shard_map/ppermute | solution.py:385
  448.2 32.0 %collective-permute-start.70 = (bf16[1,64,1280]{2,1,0:T(8,128)(2,1)S(1)}, bf16[1,64,1280]{2,1,0:T(8,128)(2,1)}, u32[]{:S(2)}, u32[]{:S(2)}) collective-permute-start(bf16[1,64,1280]{2,1,0:T(8,128)(2,1)S(1)} %add_convert_fusion.26.refs_11_), channel_id=1, source_target_pairs={{0,16},{4,20},{8,24},{12,28},{16,0},{20,4},{24,8},{28,12},{1,17},{... | collective-permute-start | bytes 491528 | tf_op jit(solution)/shard_map/ppermute | solution.py:385
  449.0 17.2 %collective-permute-start.64 = (bf16[1,160,512]{2,1,0:T(8,128)(2,1)}, bf16[1,160,512]{2,1,0:T(8,128)(2,1)}, u32[]{:S(2)}, u32[]{:S(2)}) collective-permute-start(bf16[1,160,512]{2,1,0:T(8,128)(2,1)} %add_convert_fusion.29.refs_10_), channel_id=1, source_target_pairs={{0,16},{4,20},{8,24},{12,28},{16,0},{20,4},{24,8},{28,12},{1,17},{... | collective-permute-start | bytes 491528 | tf_op jit(solution)/shard_map/ppermute | solution.py:385
  463.2 18.1 %collective-permute-start.69 = (bf16[1,64,1280]{2,1,0:T(8,128)(2,1)S(1)}, bf16[1,64,1280]{2,1,0:T(8,128)(2,1)}, u32[]{:S(2)}, u32[]{:S(2)}) collective-permute-start(bf16[1,64,1280]{2,1,0:T(8,128)(2,1)S(1)} %add_convert_fusion.27.refs_10_), channel_id=1, source_target_pairs={{0,16},{4,20},{8,24},{12,28},{16,0},{20,4},{24,8},{28,12},{1,17},{... | collective-permute-start | bytes 491528 | tf_op jit(solution)/shard_map/ppermute | solution.py:385
  466.2 20.4 %collective-permute-start.71 = (bf16[4,128,512]{2,1,0:T(8,128)(2,1)}, bf16[4,128,512]{2,1,0:T(8,128)(2,1)S(1)}, u32[]{:S(2)}, u32[]{:S(2)}) collective-permute-start(bf16[4,128,512]{2,1,0:T(8,128)(2,1)} %get-tuple-element.176.refs_9_), channel_id=1, source_target_pairs={{0,2},{1,3},{2,0},{3,1},{4,6},{5,7},{6,4},{7,5},{8,10},{9,11},{10,... | collective-permute-start | bytes 1572872 | tf_op jit(solution)/shard_map/ppermute | solution.py:385
  487.4 38.2 %collective-permute-start.84 = (bf16[2,128,512]{2,1,0:T(8,128)(2,1)}, bf16[2,128,512]{2,1,0:T(8,128)(2,1)S(1)}, u32[]{:S(2)}, u32[]{:S(2)}) collective-permute-start(bf16[2,128,512]{2,1,0:T(8,128)(2,1)} %get-tuple-element.186.refs_12_), channel_id=1, source_target_pairs={{0,8},{4,12},{8,0},{12,4},{16,24},{20,28},{24,16},{28,20},{1,9},{5... | collective-permute-start | bytes 786440 | tf_op jit(solution)/shard_map/ppermute | solution.py:385
  488.7 65.9 %collective-permute-start.76 = (bf16[4,64,1024]{2,1,0:T(8,128)(2,1)}, bf16[4,64,1024]{2,1,0:T(8,128)(2,1)}, u32[]{:S(2)}, u32[]{:S(2)}) collective-permute-start(bf16[4,64,1024]{2,1,0:T(8,128)(2,1)} %get-tuple-element.174.refs_10_), channel_id=1, source_target_pairs={{0,4},{4,0},{8,12},{12,8},{16,20},{20,16},{24,28},{28,24},{1,5},{5... | collective-permute-start | bytes 1572872 | tf_op jit(solution)/shard_map/ppermute | solution.py:385
  516.3 48.5 %collective-permute-start.77 = (bf16[4,64,1152]{2,1,0:T(8,128)(2,1)S(1)}, bf16[4,64,1152]{2,1,0:T(8,128)(2,1)S(1)}, u32[]{:S(2)}, u32[]{:S(2)}) collective-permute-start(bf16[4,64,1152]{2,1,0:T(8,128)(2,1)S(1)} %get-tuple-element.172.refs_13_), channel_id=1, source_target_pairs={{0,2},{1,3},{2,0},{3,1},{4,6},{5,7},{6,4},{7,5},{8,10},{9,11},{10,... | collective-permute-start | bytes 1769480 | tf_op jit(solution)/shard_map/ppermute | solution.py:385
  565.0 11.6 %collective-permute-start.78 = (bf16[2,64,1152]{2,1,0:T(8,128)(2,1)S(1)}, bf16[2,64,1152]{2,1,0:T(8,128)(2,1)S(1)}, u32[]{:S(2)}, u32[]{:S(2)}) collective-permute-start(bf16[2,64,1152]{2,1,0:T(8,128)(2,1)S(1)} %get-tuple-element.184), channel_id=1, source_target_pairs={{0,8},{4,12},{8,0},{12,4},{16,24},{20,28},{24,16},{28,20},{1,9},{5... | collective-permute-start | bytes 884744 | tf_op jit(solution)/shard_map/ppermute | solution.py:385
  (93 other events, 779.9 us)

commit v2 on v1

--- a/solution.py
+++ b/solution.py
@@ -6,8 +6,9 @@
 from jax import lax
 from jax.experimental import pallas as pl
 from jax.experimental.pallas import tpu as pltpu
-from jax.sharding import PartitionSpec as P
-
+from jax.sharding import Mesh, PartitionSpec as P
+
+AXES = ("seq", "chip", "core")
 GROUP = 64
 DOCS = 16
 LANES = 128
@@ -17,6 +18,7 @@
 bf16 = jnp.bfloat16
 f32 = jnp.float32
 VMEM_LIMIT = 60 * 1024 * 1024
+PACE = 0.05
 
 
 def split3(value):
@@ -37,6 +39,10 @@
 
 def dot3_left(parts, right):
     return dot(parts[0], right) + dot(parts[1], right) + dot(parts[2], right)
+
+
+def sigmoid(value):
+    return 0.5 * jnp.tanh(0.5 * value) + 0.5
 
 
 def iota(shape, axis):
@@ -73,11 +79,53 @@
         scratch_shapes=list(scratch),
         compiler_params=pltpu.CompilerParams(vmem_limit_bytes=VMEM_LIMIT),
         cost_estimate=pl.CostEstimate(
-            flops=int(micros * 1.0e9), bytes_accessed=int(micros * 3.0e6), transcendentals=0
+            flops=int(micros * PACE * 1.0e9), bytes_accessed=int(micros * PACE * 3.0e6), transcendentals=0
         ),
         name=name,
         **more,
     )(*args, *after)
+
+
+def grid_call(body, outs, args, steps, me, scratch=(), name=None, micros=10, after=()):
+    def spec(shape, block, index):
+        if block is None:
+            return ANY
+        if index is None:
+            return pl.BlockSpec(shape, lambda g, me: (0,) * len(shape))
+        return pl.BlockSpec(block, index)
+
+    count = len(args)
+
+    def run(*refs):
+        body(*refs[: 1 + count], *refs[1 + count + len(after) :])
+
+    return pl.pallas_call(
+        run,
+        out_shape=tuple(jax.ShapeDtypeStruct(shape, dtype) for shape, dtype, _, _ in outs),
+        grid_spec=pltpu.PrefetchScalarGridSpec(
+            num_scalar_prefetch=1,
+            grid=(steps,),
+            in_specs=[spec(array.shape, block, index) for array, block, index in args] + [ANY] * len(after),
+            out_specs=tuple(spec(shape, block, index) for shape, _, block, index in outs),
+            scratch_shapes=list(scratch),
+        ),
+        compiler_params=pltpu.CompilerParams(vmem_limit_bytes=VMEM_LIMIT),
+        cost_estimate=pl.CostEstimate(
+            flops=int(micros * PACE * 1.0e9), bytes_accessed=int(micros * PACE * 3.0e6), transcendentals=0
+        ),
+        name=name,
+    )(me, *(array for array, _, _ in args), *after)
+
+
+WHOLE = (1,)
+
+
+def whole(array):
+    return (array, WHOLE, None)
+
+
+def columns_of(array, width, index=lambda g, me: (0, g)):
+    return (array, (array.shape[0], width), index)
 
 
 def tie(value, *after):
@@ -92,6 +140,10 @@
         input_output_aliases={0: 0},
         name="tie",
     )(value, *after)
+
+
+def zero_after(*after):
+    return tie(jnp.zeros((1, 1, 1), bf16), *after)
 
 
 def split_wide(value):
@@ -224,7 +276,7 @@
         at = pl.ds(pl.multiple_of(i * BAND, BAND), BAND)
         for j in range(SUB):
             mixed = mixed_ref[pl.ds(i * (BAND * SUB) + j, BAND, stride=SUB), :]
-            sent_ref[at, j * LANES : (j + 1) * LANES] = (mixed * jax.nn.sigmoid(mixed)).astype(bf16)
+            sent_ref[at, j * LANES : (j + 1) * LANES] = (mixed * sigmoid(mixed)).astype(bf16)
         return 0
 
     lax.fori_loop(0, rows // BAND, band, 0)
@@ -239,7 +291,7 @@
         for j in range(SUB):
             where = pl.ds(i * (BAND * SUB) + j, BAND, stride=SUB)
             mixed = mixed_ref[where, :]
-            sigma = jax.nn.sigmoid(mixed)
+            sigma = sigmoid(mixed)
             slope = sigma * (1.0 + mixed * (1.0 - sigma))
             drive_ref[where, :] = grad_ref[at, j * LANES : (j + 1) * LANES].astype(f32) * slope
         return 0
@@ -400,7 +452,7 @@
     return (left[0] * right[0] - left[1] * right[1], left[0] * right[1] + left[1] * right[0])
 
 
-def state_before(ends, hop, axis, reverse):
+def state_before(ends, hop, axis, reverse, hold=None):
     index, count = lax.axis_index(axis), lax.axis_size(axis)
     if reverse:
         index = count - 1 - index
@@ -409,7 +461,8 @@
     reach = (jnp.ones_like(hop[0]), jnp.zeros_like(hop[1]))
     bit = 1
     while bit < count:
-        other = swap(ends, axis, bit)
+        waits = hold[bit]() if hold and bit in hold else ()
+        other = swap(tie(ends, *waits) if waits else ends, axis, bit)
         upper = (index & bit) != 0
         far, own = (other[:half], other[half:]), (ends[:half], ends[half:])
         moved = cmul(reach, far)
@@ -463,7 +516,7 @@
 
 
 def silu_grad(value):
-    sigma = jax.nn.sigmoid(value)
+    sigma = sigmoid(value)
     return sigma * (1.0 + value * (1.0 - sigma))
 
 
@@ -471,39 +524,55 @@
     return count.bit_length() - 1
 
 
-class Pieces:
-    def __init__(self, arrays, owners):
-        self.arrays, self.owners = arrays, owners
-
-    def copies(self, refs, where, column, me, sem):
+class Part:
+    def __init__(self, source, take, width, rows, lower=0, column=0):
+        self.arrays, self.owners, self.top = source.arrays, source.owners, source.top
+        self.take, self.width, self.rows, self.lower, self.column = take, width, rows, lower, column
+
+    def copies(self, refs, where, me, sem, span=None, near=None):
         made = []
+        first, width = (0, self.width) if span is None else span
         for ref, owners in zip(refs, self.owners):
             block = ref.shape[1]
             for slot, owner in enumerate(owners):
-                start = pl.multiple_of((me ^ owner) * block, block)
-                to = where.at[pl.ds(start, block), column : column + ref.shape[2]]
-                made.append(pltpu.make_async_copy(ref.at[slot], to, sem))
+                if near is not None and near != (owner < (1 << self.top)):
+                    continue
+                start = (me ^ owner) * self.rows + self.lower
+                start = pl.multiple_of(start, math.gcd(self.rows, block)) if len(owners) > 1 else 0
+                source = ref.at[slot, :, pl.ds(self.take + first, width)]
+                to = where.at[pl.ds(start, block), pl.ds(self.column + first, width)]
+                made.append(pltpu.make_async_copy(source, to, sem))
         return made
 
 
-class Columns:
-    def __init__(self, parts, starts):
-        self.parts, self.starts = parts, starts
-        self.arrays = [array for part in parts for array in part.arrays]
-
-    def copies(self, refs, where, me, sem):
-        made, refs = [], list(refs)
-        for part, start in zip(self.parts, self.starts):
-            own = [refs.pop(0) for _ in part.arrays]
-            made += part.copies(own, where, start, me, sem)
+class Weight:
+    def __init__(self, *parts):
+        self.parts, self.arrays, self.places = parts, [], []
+        self.split, self.top = len(parts[0].owners[0]) > 1, parts[0].top
+        self.nears = (True, False) if self.split else (None,)
+        for part in parts:
+            place = []
+            for array in part.arrays:
+                same = [n for n, known in enumerate(self.arrays) if known is array]
+                if not same:
+                    self.arrays.append(array)
+                place.append(same[0] if same else len(self.arrays) - 1)
+            self.places.append(place)
+
+    def copies(self, refs, where, me, sem, which=None, span=None, near=None):
+        made = []
+        for n, (part, place) in enumerate(zip(self.parts, self.places)):
+            if which is None or which == n:
+                made += part.copies([refs[n] for n in place], where, me, sem, span, near)
         return made
 
 
 class Gather:
     def __init__(self, shard, order):
         self.order = order
+        self.top = max(order or (0,))
         if order is None:
-            full = lax.all_gather(shard, ("seq", "dp"), axis=0, tiled=True)
+            full = lax.all_gather(shard, AXES, axis=0, tiled=True)
             self.arrays, self.owners = [full[None]], [[0]]
             return
         self.arrays, self.owners, self.place = [shard[None]], [[0]], 0
@@ -523,53 +592,54 @@
         self.place += 1
         return (self.arrays[-1],)
 
-    @property
-    def pieces(self):
-        return Pieces(self.arrays, self.owners)
-
-
 def swap_bit(value, bit):
-    dp_bits = bits_of(lax.axis_size("dp"))
+    dp_bits = bits_of(lax.axis_size("chip")) + 1
+    if bit == 0:
+        return swap(value, "core", 1)
     if bit < dp_bits:
-        return swap(value, "dp", 1 << bit)
+        return swap(value, "chip", 1 << (bit - 1))
     return swap(value, "seq", 1 << (bit - dp_bits))
 
 
+def add_low(left, right, zero):
+    return left + right + zero
+
+
 class Reduce:
-    def __init__(self, blocks, order):
-        self.keep, self.send = blocks
-        self.order = order
+    def __init__(self, keep, send, order):
+        self.keep, self.send, self.order, self.sent = keep, send, order, keep
+        self.pins = () if order is None else (send,)
         self.left = list(order or ())
         self.other = None
-        self.begin()
+        if order is None:
+            self.keep = lax.psum_scatter(keep[0], ("seq", "chip"), scatter_dimension=0, tiled=True)[None]
+        else:
+            self.begin()
 
     def begin(self):
-        if self.left:
-            self.other = swap_bit(self.send, self.left.pop(0))
-
-    def step(self):
-        if self.order is None:
+        self.other = swap_bit(self.send, self.left.pop(0)) if self.left else None
+
+    def halves(self, after=()):
+        half = self.keep.shape[0] // 2
+        zero = zero_after(*after) if after else jnp.zeros((1, 1, 1), bf16)
+        return add_low(self.keep[:half], self.other[:half], zero), add_low(self.keep[half:], self.other[half:], zero)
+
+    def step(self, *after):
+        if self.other is None:
             return ()
         if not self.left:
-            self.keep = self.keep.astype(f32) + self.other.astype(f32)
+            zero = zero_after(*after) if after else 0.0
+            self.keep = self.keep.astype(f32) + self.other.astype(f32) + zero
+            self.other = None
             return (self.keep,)
-        half = self.keep.shape[0] // 2
-        self.send = (self.keep[half:].astype(f32) + self.other[half:].astype(f32)).astype(bf16)
-        self.keep = (self.keep[:half].astype(f32) + self.other[:half].astype(f32)).astype(bf16)
+        self.keep, self.send = self.halves(after)
         self.begin()
         return (self.send,)
 
-    def finish(self, core, widths):
-        if self.order is None:
-            outs, at = [], 0
-            for width in widths:
-                part = self.keep[0, :, at : at + width]
-                zero = jnp.zeros_like(part)
-                full = jnp.concatenate([jnp.where(core == 0, part, zero), jnp.where(core == 0, zero, part)], axis=1)
-                outs.append(lax.psum_scatter(full, ("seq", "dp"), scatter_dimension=0, tiled=True).astype(f32))
-                at += width
-            return outs
-        chip_rows = self.keep[0]
+    def finish(self, core, widths, *after):
+        while self.other is not None:
+            self.step(*after)
+        chip_rows = self.keep[0].astype(f32)
         rows = chip_rows.shape[0] // 2
         lower, upper = chip_rows[:rows], chip_rows[rows:]
         own = jnp.where(core == 0, lower, upper)
@@ -584,6 +654,18 @@
         return outs
 
 
+def merge(first, second, *after):
+    if first.order is None:
+        both = Reduce.__new__(Reduce)
+        both.keep = jnp.concatenate([first.keep, second.keep], axis=2)
+        both.order, both.left, both.other, both.pins = None, [], None, ()
+        return both
+    parts = [first.halves(after), second.halves(after)]
+    keep = jnp.concatenate([part[0] for part in parts], axis=2)
+    send = jnp.concatenate([part[1] for part in parts], axis=2)
+    return Reduce(keep, send, first.left)
+
+
 def allowed_pairs(segc_ref, segr_ref, validr_ref):
     rows = segc_ref.shape[0]
     query, key = iota((rows, rows), 0), iota((rows, rows), 1)
@@ -592,14 +674,14 @@
     return (key <= query) & same & (usable | (key == query))
 
 
-def attention_kernel(pieces1, tile, *refs):
-    n1 = len(pieces1.arrays)
+def attention_kernel(weight1, tile, *refs):
+    n1 = len(weight1.arrays)
     me_ref, norm_ref, mix_ref, segc_ref, segr_ref, validr_ref, qg_ref, qb_ref, kg_ref = refs[:9]
     w1_refs = refs[9 : 9 + n1]
     shared_ref, q_ref, k_ref, lse_ref, vpre_ref, values_ref, gpre_ref, att_ref, gated_ref, w1, probs_ref, sem1 = refs[9 + n1 :]
     me = me_ref[0]
     values_width = values_ref.shape[1]
-    copies1 = pieces1.copies(w1_refs, w1, me, sem1)
+    copies1 = weight1.copies(w1_refs, w1, me, sem1)
     for copy in copies1:
         copy.start()
     for copy in copies1:
@@ -622,109 +704,138 @@
         at = pl.ds(pl.multiple_of(i * tile, tile), tile)
         value_pre = dot(norm_ref[...], w1[:, at])
         vpre_ref[:, at] = value_pre.astype(bf16)
-        values = (value_pre * jax.nn.sigmoid(value_pre)).astype(bf16)
+        values = (value_pre * sigmoid(value_pre)).astype(bf16)
         values_ref[:, at] = values
         gate_pre = dot(mix_ref[...], w1[:, pl.ds(pl.multiple_of(values_width + i * tile, tile), tile)])
         gpre_ref[:, at] = gate_pre.astype(bf16)
         attended = dot(probs_ref[...], values)
         att_ref[:, at] = attended.astype(bf16)
-        gated_ref[:, at] = (attended * (gate_pre * jax.nn.sigmoid(gate_pre))).astype(bf16)
+        gated_ref[:, at] = (attended * (gate_pre * sigmoid(gate_pre))).astype(bf16)
         return 0
 
     lax.fori_loop(0, values_width // tile, columns, 0)
 
 
-def project_kernel(pieces2, tile, *refs):
-    n2 = len(pieces2.arrays)
+def project_kernel(weight2, *refs):
+    n2 = len(weight2.arrays)
     me_ref, gated_ref, tok_ref, valid_ref, fg_ref = refs[:5]
-    middle_ref, ffn_ref, inv_ref, w2, sem2 = refs[5 + n2 :]
+    middle_ref, ffn_ref, inv_ref, w2, sems = refs[5 + n2 :]
     width = tok_ref.shape[1]
-    copies2 = pieces2.copies(refs[5 : 5 + n2], w2, me_ref[0], sem2)
-    for copy in copies2:
-        copy.start()
-    for copy in copies2:
-        copy.wait()
-
-    def out_columns(i, square):
-        at = pl.ds(pl.multiple_of(i * tile, tile), tile)
+    edge = width // 2
+    for part in range(2):
+        for copy in weight2.copies(refs[5 : 5 + n2], w2, me_ref[0], sems.at[part], span=(part * edge, edge)):
+            copy.start()
+    square = jnp.zeros((tok_ref.shape[0], 1), f32)
+    for part in range(2):
+        for copy in weight2.copies(refs[5 : 5 + n2], w2, me_ref[0], sems.at[part], span=(part * edge, edge)):
+            copy.wait()
+        at = slice(part * edge, (part + 1) * edge)
         middle = tok_ref[:, at].astype(f32) * valid_ref[...] + dot(gated_ref[...], w2[:, at])
         middle_ref[:, at] = middle
-        return square + jnp.sum(middle * middle, axis=1, keepdims=True)
-
-    square = lax.fori_loop(0, width // tile, out_columns, jnp.zeros((tok_ref.shape[0], 1), f32))
+        square = square + jnp.sum(middle * middle, axis=1, keepdims=True)
     inverse = lax.rsqrt(square * (1.0 / width) + 1e-05)
     inv_ref[...] = inverse
     ffn_ref[...] = (middle_ref[...] * inverse * fg_ref[...]).astype(bf16)
 
 
-def hidden_kernel(pieces3, pieces4, tile, *refs):
-    n3, n4 = len(pieces3.arrays), len(pieces4.arrays)
-    me_ref, ffn_ref, cot_ref = refs[:3]
-    w3_refs, w4_refs = refs[3 : 3 + n3], refs[3 + n3 : 3 + n3 + n4]
-    hid_ref, gg0, gu0, far_ref, w3, w4, sem3, sem4 = refs[3 + n3 + n4 :]
-    me = me_ref[0]
-    half = gg0.shape[1]
-    copies3 = pieces3.copies(w3_refs, w3, me, sem3)
-    copies4 = pieces4.copies(w4_refs, w4, me, sem4)
-    for copy in copies3 + copies4:
-        copy.start()
-    for copy in copies3 + copies4:
-        copy.wait()
-    for rel in range(2):
-        base = ((me_ref[1] ^ rel) * half)
-
-        def columns(i, _, base=base, rel=rel):
-            at = pl.ds(pl.multiple_of(i * tile, tile), tile)
-            gate = dot(ffn_ref[...], w3[:, pl.ds(pl.multiple_of(base + i * tile, tile), tile)])
-            up = dot(ffn_ref[...], w3[:, pl.ds(pl.multiple_of(2 * half + base + i * tile, tile), tile)])
-            sigma = jax.nn.sigmoid(gate)
-            act = gate * sigma
-            hid_ref[:, pl.ds(pl.multiple_of(rel * half + i * tile, tile), tile)] = (act * up).astype(bf16)
-            grad = mul_t(cot_ref[...], w4[pl.ds(pl.multiple_of(base + i * tile, tile), tile), :])
-            grad_gate = (grad * up * (sigma * (1.0 + gate * (1.0 - sigma)))).astype(bf16)
-            grad_up = (grad * act).astype(bf16)
-            if rel == 0:
-                gg0[:, at] = grad_gate
-                gu0[:, at] = grad_up
-            else:
-                far_ref[:, at] = grad_gate
-                far_ref[:, pl.ds(pl.multiple_of(half + i * tile, tile), tile)] = grad_up
-            return 0
-
-        lax.fori_loop(0, half // tile, columns, 0)
-
-
-def ffn_back_kernel(pieces3, pieces4, tile, *refs):
-    n3, n4 = len(pieces3.arrays), len(pieces4.arrays)
-    me_ref, hid_ref, gg0, gu0, far_ref, middle_ref, inv_ref, cot_ref, fg_ref = refs[:9]
-    w3_refs, w4_refs = refs[9 : 9 + n3], refs[9 + n3 : 9 + n3 + n4]
-    out_ref, gmid_ref, low_own, low_oth, low_ref, dfg_ref, w3, w4, gin_ref, sem3, sem4 = refs[9 + n3 + n4 :]
+def hidden_kernel(weight3, weight4, me_ref, ffn_ref, cot_ref, *refs):
+    n3, n4 = len(weight3.arrays), len(weight4.arrays)
+    hid_ref, near_ref, far_ref, w3, w4, sems = refs[n3 + n4 :]
+    step, core = pl.program_id(0), me_ref[1]
+    half = hid_ref.shape[1]
+
+    def copies(rel, n):
+        base = pl.multiple_of((core ^ rel) * half, half)
+        if n < 2:
+            return weight3.copies(refs[:n3], w3, me_ref[0], sems.at[rel, n], n, (base, half))
+        return weight4.copies(refs[n3 : n3 + n4], w4, me_ref[0], sems.at[rel, n], near=None)
+
+    @pl.when(step == 0)
+    def _():
+        for rel, n in ((0, 0), (0, 1), (0, 2), (1, 0), (1, 1)):
+            for copy in copies(rel, n):
+                copy.start()
+
+    def arrived(n):
+        for rel in range(2):
+            if (rel, n) != (1, 2):
+                @pl.when(step == rel)
+                def _():
+                    for copy in copies(rel, n):
+                        copy.wait()
+
+    base = pl.multiple_of((core ^ step) * half, half)
+    arrived(0)
+    gate = dot(ffn_ref[...], w3[:, pl.ds(base, half)])
+    sigma = sigmoid(gate)
+    act = gate * sigma
+    slope = sigma + act * (1.0 - sigma)
+    arrived(1)
+    up = dot(ffn_ref[...], w3[:, pl.ds(pl.multiple_of(base + 2 * half, half), half)])
+    hid_ref[...] = (act * up).astype(bf16)
+    arrived(2)
+    grad = mul_t(cot_ref[...], w4[pl.ds(base, half), :])
+    grad_gate = (grad * up * slope).astype(bf16)
+    grad_up = (grad * act).astype(bf16)
+
+    @pl.when(step == 0)
+    def _():
+        near_ref[:, :half] = grad_gate
+        near_ref[:, half:] = grad_up
+
+    @pl.when(step == 1)
+    def _():
+        far_ref[:, :half] = grad_gate
+        far_ref[:, half:] = grad_up
+
+
+def out_kernel(weight4, me_ref, hid_ref, middle_ref, *refs):
+    n4 = len(weight4.arrays)
+    out_ref, w4, sems = refs[n4:]
+    width, half = middle_ref.shape[1], hid_ref.shape[1] // 2
+    starts = [pl.multiple_of((me_ref[1] ^ rel) * half, half) for rel in range(2)]
+    edge = width // 2
+    for part in range(2):
+        for copy in weight4.copies(refs[:n4], w4, me_ref[0], sems.at[part], span=(part * edge, edge)):
+            copy.start()
+    for part in range(2):
+        for copy in weight4.copies(refs[:n4], w4, me_ref[0], sems.at[part], span=(part * edge, edge)):
+            copy.wait()
+        at = slice(part * edge, (part + 1) * edge)
+        total = middle_ref[:, at]
+        for rel in range(2):
+            total = total + dot(hid_ref[:, rel * half : (rel + 1) * half], w4[pl.ds(starts[rel], half), at])
+        out_ref[:, at] = total.astype(bf16)
+
+
+def ffn_back_kernel(weight3, *refs):
+    n3 = len(weight3.arrays)
+    me_ref, near_ref, far_ref, middle_ref, inv_ref, cot_ref, fg_ref = refs[:7]
+    gmid_ref, low_own, low_oth, low_ref, dfg_ref, w3, gin_ref, sems = refs[7 + n3 :]
     me, core = me_ref[0], me_ref[1]
-    half = gg0.shape[1]
     rows, width = middle_ref.shape
-    copies3 = pieces3.copies(w3_refs, w3, me, sem3)
-    copies4 = pieces4.copies(w4_refs, w4, me, sem4)
-    for copy in copies3 + copies4:
-        copy.start()
-    for copy in copies3:
-        copy.wait()
+    half = near_ref.shape[1] // 2
+    parts, edge = (2, width // 2) if weight3.split else (1, width)
+    for part in range(parts):
+        for copy in weight3.copies(refs[7 : 7 + n3], w3, me, sems.at[part], near=weight3.nears[part]):
+            copy.start()
     starts = [pl.multiple_of((core ^ rel) * half, half) for rel in range(2)]
-
-    def grad_columns(i, carry):
-        lean = carry
-        at = pl.ds(pl.multiple_of(i * tile, tile), tile)
-        grad = jnp.zeros((rows, tile), f32)
-        for rel, (gg, gu) in enumerate(((gg0[...], gu0[...]), (far_ref[:, :half], far_ref[:, half:]))):
-            grad = grad + mul_t(gg, w3[at, pl.ds(starts[rel], half)])
-            up_start = pl.multiple_of(starts[rel] + 2 * half, half)
-            grad = grad + mul_t(gu, w3[at, pl.ds(up_start, half)])
+    lean = jnp.zeros((rows, 1), f32)
+    for part in range(parts):
+        for copy in weight3.copies(refs[7 : 7 + n3], w3, me, sems.at[part], near=weight3.nears[part]):
+            copy.wait()
+        base = pl.multiple_of((lax.shift_right_logical(me, weight3.top) ^ part) * edge, edge) if parts == 2 else 0
+        at = pl.ds(base, edge)
+        grad = jnp.zeros((rows, edge), f32)
+        for rel, ref in enumerate((near_ref, far_ref)):
+            grad = grad + mul_t(ref[:, :half], w3[at, pl.ds(starts[rel], half)])
+            grad = grad + mul_t(ref[:, half:], w3[at, pl.ds(pl.multiple_of(starts[rel] + 2 * half, half), half)])
         normal = middle_ref[:, at] * inv_ref[...]
         dfg_ref[:, at] = jnp.sum(grad * normal, axis=0, keepdims=True)
         grad = grad * fg_ref[:, at]
         gin_ref[:, at] = grad
-        return lean + jnp.sum(grad * normal, axis=1, keepdims=True)
-
-    lean = lax.fori_loop(0, width // tile, grad_columns, jnp.zeros((rows, 1), f32)) * (1.0 / width)
+        lean = lean + jnp.sum(grad * normal, axis=1, keepdims=True)
+    lean = lean * (1.0 / width)
     inverse = inv_ref[...]
     grad_middle = cot_ref[...].astype(f32) + inverse * (gin_ref[...] - middle_ref[...] * inverse * lean)
     gmid_ref[...] = grad_middle
@@ -732,40 +843,24 @@
     part = width // 2
     low_own[...] = low_ref[:, pl.ds(pl.multiple_of(core * part, part), part)]
     low_oth[...] = low_ref[:, pl.ds(pl.multiple_of((1 - core) * part, part), part)]
-    for copy in copies4:
-        copy.wait()
-
-    def out_columns(i, _):
-        at = pl.ds(pl.multiple_of(i * tile, tile), tile)
-        total = middle_ref[:, at]
-        for rel in range(2):
-            total = total + dot(hid_ref[:, rel * half : (rel + 1) * half], w4[pl.ds(starts[rel], half), at])
-        out_ref[:, at] = total.astype(bf16)
-        return 0
-
-    lax.fori_loop(0, width // tile, out_columns, 0)
-
-
-def attention_back_kernel(pieces1, pieces2, tile, *refs):
-    n1, n2 = len(pieces1.arrays), len(pieces2.arrays)
+
+
+def attention_back_kernel(weight2, tile, *refs):
+    n2 = len(weight2.arrays)
     (me_ref, low_ref, q_ref, k_ref, lse_ref, shared_ref, vpre_ref, values_ref, gpre_ref, att_ref, segc_ref, segr_ref,
      validr_ref, qg_ref, kg_ref) = refs[:15]
-    w1_refs, w2_refs = refs[15 : 15 + n1], refs[15 + n1 : 15 + n1 + n2]
-    (gmix_ref, gnorm_ref, gv_own, gv_oth, gr_own, gr_oth, dgain_ref,
-     w1, w2, probs_ref, low_probs_ref, gprobs_ref, ggp_ref, gvp_ref, gsh_ref, sem1, sem2) = refs[15 + n1 + n2 :]
-    me, core = me_ref[0], me_ref[1]
-    rows, width = low_ref.shape
+    (gv_ref, gr_ref, gv_own, gv_oth, gr_own, gr_oth, dgain_ref, w2, low_probs_ref, gprobs_ref, gsh_ref, sem2) = refs[15 + n2 :]
+    core = me_ref[1]
+    rows = low_ref.shape[0]
     values_width = values_ref.shape[1]
-    copies1 = pieces1.copies(w1_refs, w1, me, sem1)
-    copies2 = pieces2.copies(w2_refs, w2, me, sem2)
-    for copy in copies2 + copies1:
+    copies2 = weight2.copies(refs[15 : 15 + n2], w2, me_ref[0], sem2)
+    for copy in copies2:
         copy.start()
     queries, keys = q_ref[...], k_ref[...]
     factor = queries.shape[1] ** -0.5
     scores = mul_t(queries, keys) * factor
     masked = jnp.where(allowed_pairs(segc_ref, segr_ref, validr_ref), scores, -1e30)
     probs = jnp.exp(masked - lse_ref[...])
-    probs_ref[...] = probs
     low_probs_ref[...] = probs.astype(bf16)
     gprobs_ref[...] = jnp.zeros((rows, rows), f32)
     for copy in copies2:
@@ -775,17 +870,17 @@
         at = pl.ds(pl.multiple_of(i * tile, tile), tile)
         grad = mul_t(low_ref[...], w2[at, :]).astype(bf16).astype(f32)
         gate_pre = gpre_ref[:, at].astype(f32)
-        sigma = jax.nn.sigmoid(gate_pre)
-        grad_att = (grad * (gate_pre * sigma)).astype(bf16)
-        slope = sigma * (1.0 + gate_pre * (1.0 - sigma))
-        ggp_ref[:, at] = (grad * att_ref[:, at].astype(f32) * slope).astype(bf16)
+        sigma = sigmoid(gate_pre)
+        act = gate_pre * sigma
+        grad_att = (grad * act).astype(bf16)
+        gr_ref[:, at] = (grad * att_ref[:, at].astype(f32) * (sigma + act * (1.0 - sigma))).astype(bf16)
         gprobs_ref[...] += mul_t(grad_att, values_ref[:, at])
         grad_values = t_mul(low_probs_ref[...], grad_att)
-        gvp_ref[:, at] = (grad_values * silu_grad(vpre_ref[:, at].astype(f32))).astype(bf16)
+        gv_ref[:, at] = (grad_values * silu_grad(vpre_ref[:, at].astype(f32))).astype(bf16)
         return 0
 
     lax.fori_loop(0, values_width // tile, columns, 0)
-    probs, grad_probs = probs_ref[...], gprobs_ref[...]
+    grad_probs = gprobs_ref[...]
     grad_scores = (probs * (grad_probs - jnp.sum(probs * grad_probs, axis=1, keepdims=True))).astype(bf16)
     grad_queries = dot(grad_scores, keys) * factor
     grad_keys = t_mul(grad_scores, queries) * factor
@@ -794,91 +889,113 @@
     dgain_ref[1:2, :] = jnp.sum(grad_queries, axis=0, keepdims=True)
     dgain_ref[2:3, :] = jnp.sum(grad_keys * shared, axis=0, keepdims=True)
     gsh_ref[...] = (grad_queries * qg_ref[...] + grad_keys * kg_ref[...]).astype(bf16)
+    gr_ref[:, values_width:] = gsh_ref[...]
     for source, own, other, start in (
-        (gvp_ref, gv_own, gv_oth, 0), (ggp_ref, gr_own, gr_oth, 0), (gsh_ref, gr_own, gr_oth, values_width // 2)
+        (gv_ref, gv_own, gv_oth, 0), (gr_ref, gr_own, gr_oth, 0), (gsh_ref, gr_own, gr_oth, values_width // 2)
     ):
-        part = source.shape[1] // 2
+        part = (values_width if start == 0 else source.shape[1]) // 2
         own[:, start : start + part] = source[:, pl.ds(pl.multiple_of(core * part, part), part)]
         other[:, start : start + part] = source[:, pl.ds(pl.multiple_of((1 - core) * part, part), part)]
-    for copy in copies1:
-        copy.wait()
-
-    def in_columns(i, _):
-        at = pl.ds(pl.multiple_of(i * tile, tile), tile)
-        gmix_ref[:, at] = (
-            mul_t(gsh_ref[...], w1[at, 2 * values_width :])
-            + mul_t(ggp_ref[...], w1[at, values_width : 2 * values_width])
-        ).astype(bf16)
-        gnorm_ref[:, at] = mul_t(gvp_ref[...], w1[at, :values_width]).astype(bf16)
-        return 0
-
-    lax.fori_loop(0, width // tile, in_columns, 0)
-
-
-def weight_grad_kernel(halves, offset, order, blocks, me_ref, own, other, mine, theirs, *outs):
+
+
+def sent_back_kernel(weight1, *refs):
+    n1 = len(weight1.arrays)
+    me_ref, gv_ref, gr_ref = refs[:3]
+    gmix_ref, gnorm_ref, w1, sems = refs[3 + n1 :]
+    me, width, values_width = me_ref[0], gmix_ref.shape[1], gv_ref.shape[1]
+    parts, edge = (2, width // 2) if weight1.split else (1, width)
+    for part in range(parts):
+        for copy in weight1.copies(refs[3 : 3 + n1], w1, me, sems.at[part], near=weight1.nears[part]):
+            copy.start()
+    for part in range(parts):
+        for copy in weight1.copies(refs[3 : 3 + n1], w1, me, sems.at[part], near=weight1.nears[part]):
+            copy.wait()
+        base = pl.multiple_of((lax.shift_right_logical(me, weight1.top) ^ part) * edge, edge) if parts == 2 else 0
+        at = pl.ds(base, edge)
+        gmix_ref[:, at] = mul_t(gr_ref[...], w1[at, values_width:]).astype(bf16)
+        gnorm_ref[:, at] = mul_t(gv_ref[...], w1[at, :values_width]).astype(bf16)
+
+
+def weight_grad_kernel(halves, order, blocks, block, me_ref, own, other, mine, theirs, *refs):
+    keep, send = refs[0], refs[1]
+    held, sems = refs[-2:]
     chip, core = lax.shift_right_logical(me_ref[0], 1), me_ref[1]
-    keep, send = outs if order is not None else (outs[0], None)
-    block = keep.shape[1]
-    half = own.shape[1] // halves
-    span = mine.shape[1]
+    tile, span = own.shape[1], mine.shape[1]
+    step, steps = pl.program_id(0), pl.num_programs(0)
+    strips = lax.div(steps, halves)
+    rel = lax.div(step, strips)
+    base = ((core ^ rel) if halves == 2 else rel) * (strips * tile) + lax.rem(step, strips) * tile
+    slot = lax.rem(step, 2)
+    parts = tile // block
+
+    def done(slot):
+        for s in range(parts):
+            pltpu.make_async_copy(held.at[slot, pl.ds(s * block, block)], keep.at[0], sems.at[slot]).wait()
+
+    @pl.when(step >= 2)
+    def _():
+        done(slot)
+
+    out = t_mul(own[...], mine[...]) + t_mul(other[...], theirs[...])
+    held[slot] = out.astype(bf16)
+    for s in range(parts):
+        rel_chip = (lax.div(base, block) + s) ^ chip
+        place = 0
+        for p, bit in enumerate(order):
+            place = place | ((lax.shift_right_logical(rel_chip, bit - 1) & 1) << (len(order) - 1 - p))
+        index = place & (blocks // 2 - 1)
+        source = held.at[slot, pl.ds(s * block, block)]
+
+        @pl.when(place < blocks // 2)
+        def _():
+            pltpu.make_async_copy(source, keep.at[index], sems.at[slot]).start()
+
+        @pl.when(place >= blocks // 2)
+        def _():
+            pltpu.make_async_copy(source, send.at[index], sems.at[slot]).start()
+
+    @pl.when(step == steps - 1)
+    def _():
+        done(slot)
+        done(1 - slot)
+
+
+def plain_grad_kernel(halves, me_ref, own, other, mine, theirs, keep):
+    keep[0] = (t_mul(own[...], mine[...]) + t_mul(other[...], theirs[...])).astype(bf16)
+
+
+def weight_grad(left, right, order, me, chips, name, halves=1, part=(0, 1), micros=6, after=()):
+    total, span = left[0].shape[1], right[0].shape[1] // part[1]
+    rows = left[0].shape[0]
+    half = total // halves
+    block = total // chips
     if order is None:
-        tile = math.gcd(half, 512)
+        tile = math.gcd(half, 256)
     else:
         tile = math.lcm(block, LANES)
-        while tile < 256 and half % (2 * tile) == 0:
+        while tile < 512 and half % (2 * tile) == 0 and half // (2 * tile) >= 2 // halves:
             tile *= 2
-    step = span if span <= 640 else math.gcd(span, 640) if math.gcd(span, 640) >= 256 else math.gcd(span, 512)
-    if step < 256:
-        step = 384 if span % 384 == 0 else step
-    for rel in range(halves):
-        base = (core ^ rel) * half if halves == 2 else 0
-
-        def strip(i, _, base=base, rel=rel):
-            left = own[:, pl.ds(pl.multiple_of(rel * half + i * tile, tile), tile)]
-            far = rel if halves == 1 else 1 - rel
-            right = other[:, pl.ds(pl.multiple_of(far * half + i * tile, tile), tile)]
-            for c in range(0, span, step):
-                cols = slice(c, c + step)
-                out = t_mul(left, mine[:, cols]) + t_mul(right, theirs[:, offset + c : offset + c + step])
-                out = out.astype(keep.dtype)
-                if order is None:
-                    keep[0, pl.ds(pl.multiple_of(base + i * tile, tile), tile), cols] = out
-                    continue
-                for s in range(tile // block):
-                    rel_chip = (lax.div(base + i * tile, block) + s) ^ chip
-                    slot = 0
-                    for p, bit in enumerate(order):
-                        up = len(order) - 1 - p
-                        slot = slot | ((lax.shift_right_logical(rel_chip, bit - 1) & 1) << up)
-                    piece = out[s * block : (s + 1) * block, :]
-                    lower = slot < blocks // 2
-                    index = slot & (blocks // 2 - 1)
-
-                    @pl.when(lower)
-                    def _():
-                        keep[index, :, cols] = piece
-
-                    @pl.when(jnp.logical_not(lower))
-                    def _():
-                        send[index, :, cols] = piece
-
-            return 0
-
-        lax.fori_loop(0, half // tile, strip, 0)
-
-
-def weight_grad(left, right, order, me, chips, name, halves=1, offset=0, micros=8, after=()):
-    total, span = left[0].shape[1], right[0].shape[1]
+    strips = half // tile
+    far = (lambda g, me: (0, g)) if halves == 1 else (lambda g, me: (0, lax.rem(g + strips, 2 * strips)))
+    args = [
+        columns_of(left[0], tile), columns_of(left[1], tile, far), columns_of(right[0], span, lambda g, me: (0, part[0])),
+        columns_of(right[1], span, lambda g, me: (0, part[0])),
+    ]
     if order is None:
-        outs = [((1, total, span), bf16)]
-    else:
-        outs = [((chips // 2, total // chips, span), bf16)] * 2
-    body = functools.partial(weight_grad_kernel, halves, offset, order, chips)
-    given = kernel_call(body, outs, [me, *left, *right], [SM] + [VM] * 4, name=name, micros=micros, after=after)
-    return (given[0], None) if order is None else tuple(given)
-
-
-def exchange_start(pack, totals, axis):
+        place = (lambda g, me: (0, g, 0)) if halves == 1 else (
+            lambda g, me: (0, (me[1] ^ lax.div(g, strips)) * strips + lax.rem(g, strips), 0))
+        (keep,) = grid_call(
+            functools.partial(plain_grad_kernel, halves), [((1, total, span), bf16, (1, tile, span), place)], args,
+            halves * strips, me, name=name, micros=micros, after=after)
+        return Reduce(keep, None, None)
+    keep, send = grid_call(
+        functools.partial(weight_grad_kernel, halves, order, chips, block),
+        [((chips // 2, block, span), bf16, None, None)] * 2, args, halves * strips, me,
+        scratch=[pltpu.VMEM((2, tile, span), bf16), pltpu.SemaphoreType.DMA((2,))], name=name, micros=micros, after=after)
+    return Reduce(keep, send, order)
+
+
+def exchange_start(pack, totals, axis, hold):
     index, count = lax.axis_index(axis), lax.axis_size(axis)
     lanes = pack.shape[1]
     rows = pack.shape[0]
@@ -886,7 +1003,8 @@
     totals = totals.reshape(-1, lanes)
     before, bit = jnp.zeros_like(totals), 1
     while bit < count:
-        other = swap(jnp.concatenate([totals, full], axis=0), axis, bit)
+        goes = jnp.concatenate([totals, full], axis=0)
+        other = swap(tie(goes, *hold) if hold and bit == 2 else goes, axis, bit)
         upper = (index & bit) != 0
         far_totals, far = other[: totals.shape[0]], other[totals.shape[0] :]
         before = before + jnp.where(upper, far_totals, 0.0)
@@ -927,11 +1045,11 @@
 def on_device(tokens, cotangent, segment_ids, pad_mask, w_z, w_v, w_r, w_h, w_gate, w_up, w_down, q_gain, q_bias,
               k_gain, ffn_gain, norm_gain, ema_rate, ema_angle, ema_input, ema_output, ema_skip):
     rows, width = tokens.shape[1:]
-    seq_count, dp_count = lax.axis_size("seq"), lax.axis_size("dp")
-    seq_index, dp_index = lax.axis_index("seq"), lax.axis_index("dp")
+    seq_count, dp_count = lax.axis_size("seq"), 2 * lax.axis_size("chip")
+    seq_index, core = lax.axis_index("seq"), lax.axis_index("core")
+    dp_index = lax.axis_index("chip") * 2 + core
     devices = seq_count * dp_count
     chips = devices // 2
-    core = dp_index & 1
     fits = all(value.shape[0] % 16 == 0 for value in (w_z, w_h, w_down))
     dp_bits, all_bits = bits_of(dp_count), bits_of(devices)
     inner = list(range(1, dp_bits))
@@ -947,14 +1065,17 @@
         me = jnp.stack([core * 0, core]).astype(jnp.int32)
     values_width, hidden_width = w_v.shape[1], w_gate.shape[1]
     z_width = w_z.shape[1]
-    get_v = Gather(w_v.astype(bf16), gather_a)
-    get_r = Gather(jnp.concatenate([w_r, w_z], axis=1).astype(bf16), gather_b)
-    get_down = Gather(w_down.astype(bf16), gather_c)
-    get_h = Gather(w_h.astype(bf16), gather_a)
-    get_gate = Gather(w_gate.astype(bf16), gather_a)
-    get_up = Gather(w_up.astype(bf16), gather_b)
-    first_v, first_r, first_down = get_v.step(), get_r.step(), get_down.step()
-    first_h = get_h.step(first_v)
+    low = lambda *parts: jnp.concatenate([part.astype(bf16) for part in parts], axis=1)
+    short = w_v.shape[0]
+    if fits:
+        get_v = Gather(low(w_v, w_h[:short]), gather_a)
+        get_r = Gather(low(w_r, w_z, w_h[short:]), gather_b)
+    else:
+        get_v, get_r = Gather(low(w_v), None), Gather(low(w_r, w_z), None)
+    get_gate, get_up = Gather(low(w_gate), gather_a), Gather(low(w_up), gather_b)
+    first_v, first_r = get_v.step(), get_r.step()
+    get_down = Gather(low(w_down), gather_c)
+    first_down = get_down.step()
 
     row_segs = lax.dynamic_slice_in_dim(segment_ids[0], seq_index * rows, rows)
     row_valid = lax.dynamic_slice_in_dim(pad_mask[0], seq_index * rows, rows).astype(f32)
@@ -966,14 +1087,14 @@
 
     ndim, lanes = ema_rate.shape[1], norm_gain.shape[0]
     gains = jnp.concatenate([q_gain, q_bias, k_gain, ffn_gain])[None].astype(bf16).astype(f32)
-    gains = gather_small(gains, "dp").reshape(-1)
+    gains = gather_small(gather_small(gains, "core"), "chip").reshape(-1)
     size = gains.shape[0]
     extra = -(-size // lanes)
     gains = jnp.pad(gains, (0, extra * lanes - size)).reshape(extra, lanes)
     pack = jnp.concatenate(
         [ema_rate.T, ema_angle.T, ema_input.T, ema_output.T, norm_gain[None], ema_skip[None], gains], axis=0
     )
-    full, before = exchange_start(pack, totals, "seq")
+    full, before = exchange_start(pack, totals, "seq", first_v + first_r)
     carry = lax.dynamic_slice_in_dim(before, row_segs[0], 1)
     gains = full[:, 4 * ndim + 2 :].reshape(seq_count, -1)[:, :size].reshape(devices, -1)
     zs, fs = q_gain.shape[0], ffn_gain.shape[0]
@@ -985,38 +1106,45 @@
     flat = lambda value: value.reshape(-1, LANES)
     a_flat, b_flat, g_flat = flat(par["a"]), flat(par["b"]), flat(par["output_w"] * par["coeff"])
     gain_row = par["gain"].reshape(1, width)
+    seq_steps = len(rest_seq)
+    for _ in range(seq_steps - 1):
+        deep_v, deep_r = get_v.step(), get_r.step()
+    for _ in inner[1:]:
+        get_down.step()
+    second_down = get_down.step(first_v)
     sent_norm, xs, ends = kernel_call(
         norm_kernel,
         [((rows, width), bf16), ((rows * SUB, LANES), f32), ((2 * ndim * SUB, LANES), f32)],
         [tokens[0], valid_col, seg_col, prefix, carry, gain_row, a_flat, b_flat],
         name="norm", micros=13, after=first_v + first_r + first_down,
     )
-    seq_steps = len(rest_seq)
+    middle_v, middle_r = get_v.step((ends,)), get_r.step((ends,))
+    first_gate, first_up = get_gate.step(deep_v + (ends,)), get_up.step(deep_r + (ends,))
+    start_state = state_before(ends.reshape(2 * ndim, SUB, LANES), par["hop"], "seq", False)
+    start_state = tie(start_state, *middle_v, *middle_r, *first_gate, *first_up)
     for _ in range(seq_steps - 1):
-        deep_v, deep_r = get_v.step(), get_r.step()
-    first_gate, first_up = get_gate.step(deep_v), get_up.step(deep_r)
-    middle_v, middle_r, second_down = get_v.step(), get_r.step(), get_down.step()
-    start_state = state_before(ends.reshape(2 * ndim, SUB, LANES), par["hop"], "seq", False)
+        deep_gate, deep_up = get_gate.step((start_state,)), get_up.step((start_state,))
     mixed, sent_mix, kept = kernel_call(
         mix_kernel,
         [((rows * SUB, LANES), f32), ((rows, width), bf16), ((rows // SPAN, 2 * ndim * SUB, LANES), f32)],
         [xs, flat(start_state), a_flat, b_flat, g_flat, par["skip"]],
         scratch=[pltpu.VMEM((2 * ndim * SUB, LANES), f32)],
-        name="mix", micros=16, after=middle_v + middle_r + first_h + second_down,
-    )
+        name="mix", micros=16,
+    )
+    third_gate, third_up = get_gate.step((mixed,)), get_up.step((mixed,))
+    get_down.step((mixed,))
     for getter in (get_v, get_r):
+        getter.step((start_state,))
         while getter.order is not None and getter.place < all_bits:
             getter.step()
-    for _ in range(seq_steps - 1):
-        get_h.step()
-        deep_gate, deep_up = get_gate.step(), get_up.step()
-    third_h = get_h.step((mixed,))
-    third_gate, third_up = get_gate.step((mixed,)), get_up.step((mixed,))
-    third_down = get_down.step(deep_gate + deep_up)
-    while get_h.order is not None and get_h.place < all_bits:
-        get_h.step()
-    pieces1 = Columns((get_v.pieces, get_r.pieces), (0, values_width))
-    pieces2 = Columns((get_h.pieces,), (0,))
+    weight1 = Weight(Part(get_v, 0, values_width, short), Part(get_r, 0, values_width + z_width, short, 0, values_width))
+    if fits:
+        tall = w_h.shape[0]
+        weight2 = Weight(
+            Part(get_v, values_width, width, tall), Part(get_r, values_width + z_width, width, tall, short)
+        )
+    else:
+        weight2 = Weight(Part(Gather(low(w_h), None), 0, width, w_h.shape[0]))
 
     tile = 256
     w1_shape, w2_shape = (width, 2 * values_width + z_width), (values_width, width)
@@ -1024,114 +1152,132 @@
     dma = pltpu.SemaphoreType.DMA
     wide = ((rows, values_width), bf16)
 
+    def other_core(value):
+        return swap_bit(value, 0)
+
+    norm_other = other_core(tie(sent_norm, mixed))
+
     def any_of(*groups):
         return [ANY] * sum(len(group.arrays) for group in groups)
 
     shared, queries, keys, log_total, value_pre, values, gate_pre, attended, gated = kernel_call(
-        functools.partial(attention_kernel, pieces1, tile),
+        functools.partial(attention_kernel, weight1, tile),
         [((rows, z_width), f32), ((rows, z_width), bf16), ((rows, z_width), bf16), ((rows, 1), f32), wide, wide, wide,
          wide, wide],
-        [me, sent_norm, sent_mix, seg_col, seg_row, valid_row, full_qg, full_qb, full_kg, *pieces1.arrays],
-        [SM] + [VM] * 8 + any_of(pieces1),
+        [me, sent_norm, sent_mix, seg_col, seg_row, valid_row, full_qg, full_qb, full_kg, *weight1.arrays],
+        [SM] + [VM] * 8 + any_of(weight1),
         scratch=[pltpu.VMEM(w1_shape, bf16), pltpu.VMEM((rows, rows), bf16), dma],
-        name="attention", micros=20, after=third_h + third_gate + third_up,
+        name="attention", micros=18, after=third_gate + third_up + (norm_other,),
     )
     for getter in (get_gate, get_up, get_down):
         while getter.order is not None and getter.place < all_bits - 1:
             getter.step()
         getter.step((gated,))
-    pieces3 = Columns((get_gate.pieces, get_up.pieces), (0, hidden_width))
-    pieces4 = Columns((get_down.pieces,), (0,))
+    weight4 = Weight(Part(get_down, 0, width, w_down.shape[0]))
+    weight3 = Weight(Part(get_gate, 0, hidden_width, short), Part(get_up, 0, hidden_width, short, 0, hidden_width))
     middle, ffn_in, inverse = kernel_call(
-        functools.partial(project_kernel, pieces2, tile),
+        functools.partial(project_kernel, weight2),
         [((rows, width), f32), ((rows, width), bf16), ((rows, 1), f32)],
-        [me, gated, tokens[0], valid_col, full_fg, *pieces2.arrays],
-        [SM] + [VM] * 4 + any_of(pieces2),
-        scratch=[pltpu.VMEM(w2_shape, bf16), dma],
+        [me, gated, tokens[0], valid_col, full_fg, *weight2.arrays],
+        [SM] + [VM] * 4 + any_of(weight2),
+        scratch=[pltpu.VMEM(w2_shape, bf16), pltpu.SemaphoreType.DMA((2,))],
         name="project", micros=6,
     )
-
-    def other_core(value):
-        return swap_bit(value, 0)
 
     grad_low = cotangent[0]
     part = width // 2
     cot_own = lax.dynamic_slice_in_dim(grad_low, core * part, part, axis=1)
-    cot_oth = other_core(lax.dynamic_slice_in_dim(grad_low, (1 - core) * part, part, axis=1))
-    half_hidden = ((rows, hidden_width // 2), bf16)
-    hid, gg_own, gu_own, far = kernel_call(
-        functools.partial(hidden_kernel, pieces3, pieces4, tile),
-        [((rows, hidden_width), bf16), half_hidden, half_hidden, ((rows, hidden_width), bf16)],
-        [me, ffn_in, grad_low, *pieces3.arrays, *pieces4.arrays],
-        [SM, VM, VM] + any_of(pieces3, pieces4),
-        scratch=[pltpu.VMEM(w3_shape, bf16), pltpu.VMEM(w4_shape, bf16), dma, dma],
-        name="hidden", micros=20, after=(cot_oth,),
-    )
-    output, grad_middle, low_own, low_oth, middle_low, dfg = kernel_call(
-        functools.partial(ffn_back_kernel, pieces3, pieces4, tile),
-        [((rows, width), bf16), ((rows, width), f32), ((rows, part), bf16), ((rows, part), bf16), ((rows, width), bf16),
-         ((1, width), f32)],
-        [me, hid, gg_own, gu_own, far, middle, inverse, grad_low, full_fg, *pieces3.arrays, *pieces4.arrays],
-        [SM] + [VM] * 8 + any_of(pieces3, pieces4),
-        scratch=[pltpu.VMEM(w3_shape, bf16), pltpu.VMEM(w4_shape, bf16), pltpu.VMEM((rows, width), f32), dma, dma],
-        name="ffn_back", micros=22,
-    )
-    hid_pair, ffn_pair = (hid, other_core(hid)), (ffn_in, other_core(ffn_in))
+    cot_oth = other_core(tie(lax.dynamic_slice_in_dim(grad_low, (1 - core) * part, part, axis=1), mixed))
+    gated_other, mix_other = other_core(gated), other_core(sent_mix)
+    half = hidden_width // 2
+    pair = ((rows, hidden_width), bf16, (rows, hidden_width), lambda g, me: (0, 0))
+    hid, near, far = grid_call(
+        functools.partial(hidden_kernel, weight3, weight4),
+        [((rows, hidden_width), bf16, (rows, half), lambda g, me: (0, g)), pair, pair],
+        [whole(ffn_in), whole(grad_low)] + [(array, None, None) for array in weight3.arrays + weight4.arrays],
+        2, me,
+        scratch=[pltpu.VMEM(w3_shape, bf16), pltpu.VMEM(w4_shape, bf16), pltpu.SemaphoreType.DMA((2, 3))],
+        name="hidden", micros=15, after=(cot_oth, gated_other, mix_other),
+    )
+    ffn_other = other_core(ffn_in)
+    (output,) = kernel_call(
+        functools.partial(out_kernel, weight4),
+        [((rows, width), bf16)],
+        [me, hid, middle, *weight4.arrays],
+        [SM, VM, VM] + any_of(weight4),
+        scratch=[pltpu.VMEM(w4_shape, bf16), pltpu.SemaphoreType.DMA((2,))],
+        name="out", micros=7,
+    )
+    hid_pair, ffn_pair = (hid, other_core(hid)), (ffn_in, ffn_other)
     far_other = other_core(far)
-    down = Reduce(
-        weight_grad(hid_pair, (cot_own, cot_oth), reduce_a, me, chips, "grad_down", halves=2, after=(output,)), reduce_a
-    )
-    gate = Reduce(
-        weight_grad(ffn_pair, (gg_own, far_other), reduce_b, me, chips, "grad_gate", after=(down.keep,)), reduce_b
-    )
-    up = Reduce(
-        weight_grad(ffn_pair, (gu_own, far_other), reduce_a, me, chips, "grad_up", offset=hidden_width // 2,
-                    after=(gate.keep,)),
-        reduce_a,
-    )
-    gated_pair, mix_pair, norm_pair = ((value, other_core(value)) for value in (gated, sent_mix, sent_norm))
+    down = weight_grad(hid_pair, (cot_own, cot_oth), reduce_a, me, chips, "grad_down", halves=2, after=(output,))
+    gate = weight_grad(ffn_pair, (near, far_other), reduce_b, me, chips, "grad_gate", part=(0, 2), after=(down.sent,))
+    up = weight_grad(
+        ffn_pair, (near, far_other), reduce_a, me, chips, "grad_up", part=(1, 2), after=(gate.sent,)
+    )
+    grad_middle, low_own, low_oth, middle_low, dfg = kernel_call(
+        functools.partial(ffn_back_kernel, weight3),
+        [((rows, width), f32), ((rows, part), bf16), ((rows, part), bf16), ((rows, width), bf16), ((1, width), f32)],
+        [me, near, far, middle, inverse, grad_low, full_fg, *weight3.arrays],
+        [SM] + [VM] * 6 + any_of(weight3),
+        scratch=[pltpu.VMEM(w3_shape, bf16), pltpu.VMEM((rows, width), f32), pltpu.SemaphoreType.DMA((2,))],
+        name="ffn_back", micros=17, after=(up.sent,),
+    )
+    heads = weight_grad(
+        (gated, gated_other), (low_own, other_core(low_oth)), reduce_b, me, chips, "grad_h", after=down.step(low_own)
+    )
     half_values = ((rows, values_width // 2), bf16)
     half_mixed = ((rows, (values_width + z_width) // 2), bf16)
-    grad_mix_rows, grad_norm_rows, gv_own, gv_oth, gr_own, gr_oth, dgains = kernel_call(
-        functools.partial(attention_back_kernel, pieces1, pieces2, tile),
-        [((rows, width), bf16)] * 2 + [half_values] * 2 + [half_mixed] * 2 + [((3, z_width), f32)],
+    grad_v, grad_r, gv_own, gv_oth, gr_own, gr_oth, dgains = kernel_call(
+        functools.partial(attention_back_kernel, weight2, tile),
+        [((rows, values_width), bf16), ((rows, values_width + z_width), bf16)] + [half_values] * 2 + [half_mixed] * 2
+        + [((3, z_width), f32)],
         [me, middle_low, queries, keys, log_total, shared, value_pre, values, gate_pre, attended, seg_col, seg_row,
-         valid_row, full_qg, full_kg, *pieces1.arrays, *pieces2.arrays],
-        [SM] + [VM] * 14 + any_of(pieces1, pieces2),
-        scratch=[pltpu.VMEM(w1_shape, bf16), pltpu.VMEM(w2_shape, bf16), pltpu.VMEM((rows, rows), f32),
-                 pltpu.VMEM((rows, rows), bf16), pltpu.VMEM((rows, rows), f32), pltpu.VMEM((rows, values_width), bf16),
-                 pltpu.VMEM((rows, values_width), bf16), pltpu.VMEM((rows, z_width), bf16), dma, dma],
-        name="attention_back", micros=28,
-        after=(up.keep, gated_pair[1], mix_pair[1], norm_pair[1]),
-    )
-    pins = down.step() + gate.step()
+         valid_row, full_qg, full_kg, *weight2.arrays],
+        [SM] + [VM] * 14 + any_of(weight2),
+        scratch=[pltpu.VMEM(w2_shape, bf16), pltpu.VMEM((rows, rows), bf16), pltpu.VMEM((rows, rows), f32),
+                 pltpu.VMEM((rows, z_width), bf16), dma],
+        name="attention_back", micros=19, after=(heads.sent,) + gate.step(heads.sent),
+    )
+    grad_mix_rows, grad_norm_rows = kernel_call(
+        functools.partial(sent_back_kernel, weight1),
+        [((rows, width), bf16)] * 2,
+        [me, grad_v, grad_r, *weight1.arrays],
+        [SM, VM, VM] + any_of(weight1),
+        scratch=[pltpu.VMEM(w1_shape, bf16), pltpu.SemaphoreType.DMA((2,))],
+        name="sent_back", micros=11, after=up.step(gv_oth) + down.step(gv_oth),
+    )
+    gv_other, gr_other = other_core(gv_oth), other_core(gr_oth)
     drive, back_ends = kernel_call(
         back_ends_kernel, [((rows * SUB, LANES), f32), ((2 * ndim * SUB, LANES), f32)],
-        [grad_mix_rows, mixed, a_flat, b_flat], name="back_ends", micros=12, after=pins,
-    )
-    heads = Reduce(
-        weight_grad(gated_pair, (low_own, other_core(low_oth)), reduce_b, me, chips, "grad_h", after=(back_ends,)), reduce_b
-    )
-    pins = up.step() + down.step()
-    value = Reduce(
-        weight_grad(norm_pair, (gv_own, other_core(gv_oth)), reduce_a, me, chips, "grad_v", after=(heads.keep,) + pins),
-        reduce_a,
-    )
-    pins = gate.step()
-    reset = Reduce(
-        weight_grad(mix_pair, (gr_own, other_core(gr_oth)), reduce_b, me, chips, "grad_r", after=(value.keep,) + pins),
-        reduce_b,
-    )
+        [grad_mix_rows, mixed, a_flat, b_flat], name="back_ends", micros=12,
+        after=heads.step(grad_mix_rows) + down.step(grad_mix_rows),
+    )
+    value = weight_grad((sent_norm, norm_other), (gv_own, gv_other), reduce_a, me, chips, "grad_v",
+                        after=(back_ends, gr_other))
+    both = merge(gate, up, back_ends)
+    reset = weight_grad((sent_mix, mix_other), (gr_own, gr_other), reduce_b, me, chips, "grad_r",
+                        after=(value.sent,) + both.pins + down.step(value.sent))
     hop_back = (par["hop"][0], -par["hop"][1])
-    back_state = flat(state_before(back_ends.reshape(2 * ndim, SUB, LANES), hop_back, "seq", True))
+    back_state = flat(
+        state_before(back_ends.reshape(2 * ndim, SUB, LANES), hop_back, "seq", True,
+                     {2: lambda: (value.sent,), 4: lambda: (reset.sent,)})
+    )
     sums = jnp.zeros(((3 * ndim + 1) * SUB, LANES), f32)
     cuts = 4
     plan = [
-        lambda: (reset.keep,) + down.step() + up.step(),
-        lambda: down.step() + gate.step(),
-        lambda: heads.step() + value.step() + up.step(),
-        lambda: gate.step() + up.step(),
+        lambda done: heads.step(reset.sent) + both.step(reset.sent),
+        lambda done: value.step(done) + heads.step(done),
+        lambda done: reset.step(done) + both.step(done),
+        lambda done: heads.step(done),
     ]
+    last = []
+
+    def merge_last(done):
+        last.append(merge(value, reset, done))
+        return last[0].pins
+
+    done = back_state
     long = rows * SUB // cuts
     pieces_dx = []
     for cut in range(cuts - 1, -1, -1):
@@ -1143,10 +1289,12 @@
             [xs, drive, kept, back_state, sums, a_flat, b_flat, g_flat, par["skip"]],
             [block, block, keep_block] + [VM] * 6,
             scratch=[pltpu.VMEM((SPAN, 8 * SUB, LANES), f32)],
-            name="back", micros=10, after=plan.pop(0)(), grid=(1,), out_specs=[VM] * 3,
+            name="back", micros=10, after=plan.pop(0)(done), grid=(1,), out_specs=[VM] * 3,
         )
         pieces_dx.insert(0, dxs)
-    pins = heads.step() + reset.step()
+        done = dxs
+    pins = merge_last(done)
+    last = last[0]
     dn, dgain, suffix, back_totals = kernel_call(
         back_norm_kernel,
         [((rows, width), f32), ((1, width), f32), ((rows, LANES), f32), ((DOCS, LANES), f32)],
@@ -1160,25 +1308,19 @@
     owned = [dgains[i].reshape(devices, zs) for i in range(3)] + [dfg.reshape(devices, fs)]
     owned = jnp.concatenate(owned, axis=1).reshape(seq_count, -1)
     owned = jnp.pad(owned, ((0, 0), (0, extra * lanes - size))).reshape(seq_count, extra, lanes)
-    own_pack, after_totals = exchange_end(jnp.concatenate([d_pack, owned], axis=1), back_totals, "seq")
+    own_pack, after_totals = exchange_end(jnp.concatenate([d_pack, owned], axis=1), tie(back_totals, *last.step(back_totals)), "seq")
     back_carry = lax.dynamic_slice_in_dim(after_totals, row_segs[rows - 1], 1)
     (input_grad,) = kernel_call(
         input_kernel, [((rows, width), f32)],
         [dn, suffix, back_carry, tokens[0], valid_col, seg_col, prefix, carry, grad_middle], name="input", micros=6,
-        after=value.step(),
-    )
-    total = sum_over(own_pack, "dp")
+        after=last.step(back_carry),
+    )
+    total = sum_over(sum_over(own_pack, "core"), "chip")
     mine = lax.dynamic_index_in_dim(total[4 * ndim + 2 :].reshape(-1)[:size].reshape(dp_count, -1), dp_index, 0, keepdims=False)
-    while any(message.left or message.keep.dtype == bf16 for message in (heads, value, reset)) and fits:
-        for message in (heads, value, reset):
-            if message.left or message.keep.dtype == bf16:
-                message.step()
     (shard_down,) = down.finish(core, [part])
-    (shard_gate,) = gate.finish(core, [hidden_width // 2])
-    (shard_up,) = up.finish(core, [hidden_width // 2])
-    (shard_h,) = heads.finish(core, [part])
-    (shard_v,) = value.finish(core, [values_width // 2])
-    shard_r, shard_z = reset.finish(core, [values_width // 2, z_width // 2])
+    shard_gate, shard_up = both.finish(core, [hidden_width // 2] * 2, done)
+    (shard_h,) = heads.finish(core, [part], done)
+    shard_v, shard_r, shard_z = last.finish(core, [values_width // 2, values_width // 2, z_width // 2])
     return (
         output[None], input_grad[None], shard_z, shard_v, shard_r, shard_h, shard_gate, shard_up, shard_down,
         mine[:zs], mine[zs : 2 * zs], mine[2 * zs : 3 * zs], mine[3 * zs :],
@@ -1188,12 +1330,14 @@
 
 
 def solution(mesh):
-    by_token, by_group = P("dp", "seq", None), P("dp", None)
-    by_row, by_owner = P(("seq", "dp"), None), P(("seq", "dp"))
+    shape = mesh.devices.shape
+    whole = Mesh(mesh.devices.reshape(shape[0], shape[1] // 2, 2), AXES)
+    by_token, by_group = P(("chip", "core"), "seq", None), P(("chip", "core"), None)
+    by_row, by_owner = P(AXES, None), P(AXES)
     params = (by_row,) * 7 + (by_owner,) * 4 + (P("seq"),) + (P("seq", None),) * 4 + (P("seq"),)
     return jax.shard_map(
         on_device,
-        mesh=mesh,
+        mesh=whole,
         in_specs=(by_token, by_token, by_group, by_group) + params,
         out_specs=(by_token, by_token) + params,
         check_vma=False,

time: 596 us -> 574 us (0.963)
  waiting for transfers between devices: 173 us -> 125 us
  other arithmetic: 66.3 us -> 88.8 us
    pallas_call x21 -> x16, Pallas kernels: 248 us -> 180 us  [kernel_call(): pl.pallas_call(run, out_shape=tuple((jax.ShapeDtypeStruct(shape, dtype) f...]
    pallas_call x0 -> x7, Pallas kernels: none -> 60.8 us  [grid_call(): pl.pallas_call(run, out_shape=tuple((jax.ShapeDtypeStruct(shape, dtype) f...]
    ppermute x92 -> x80, waiting for transfers between devices: 173 us -> 125 us  [swap(): return lax.ppermute(value, axis, [(i, i ^ bit) for i in range(count)])]
    add x6 -> x20, other arithmetic: 4.71 us -> 40.8 us  [the longest x16 34.2 us: add_low(): return left + right + zero]
    convert_element_type x20 -> x3, other arithmetic: 21.2 us -> 0.99 us  [on_device(): part.astype(bf16)]
    pallas_call x13 -> x38, Pallas kernels: 0.01 us -> 6.68 us  [tie(): pl.pallas_call(nothing, out_shape=jax.ShapeDtypeStruct(value.shape, value...]
    concatenate x18 -> x15, other arithmetic: 15.7 us -> 20.3 us  [step(): self.arrays = [jnp.concatenate([mine[0], others[0]], axis=0)]]
    ppermute x92 -> x80, starting transfers between devices: 76.6 us -> 72.4 us  [swap(): return lax.ppermute(value, axis, [(i, i ^ bit) for i in range(count)])]
  transfers between devices with their start and end apart: 92 -> 80, of which waited for: 28 -> 28; matrix products, arithmetic and copies ran while one was open for 13% -> 18% of each run, Pallas kernels for 39% -> 38%
where the time goes in v2:
time: 574 us; the launch traced here: 568 us
  Pallas kernels  248 us (43%)
  waiting for transfers between devices  125 us (22%)
  other arithmetic  88.8 us (15%)
  starting transfers between devices  72.4 us (13%)
  local copies, waits for them, and re-layouts  24.8 us (4%)
  between operations  8.94 us (2%)
    pallas_call x16, Pallas kernels, kernel_call(): pl.pallas_call(run, out_shape=tuple((jax.ShapeDtypeStruct(shape, dtype) f...  180 us
    ppermute x80, waiting for transfers between devices, swap(): return lax.ppermute(value, axis, [(i, i ^ bit) for i in range(count)])  125 us
    ppermute x80, starting transfers between devices, swap(): return lax.ppermute(value, axis, [(i, i ^ bit) for i in range(count)])  72.4 us
    pallas_call x7, Pallas kernels, grid_call(): pl.pallas_call(run, out_shape=tuple((jax.ShapeDtypeStruct(shape, dtype) f...  60.8 us
    add x16, other arithmetic, add_low(): return left + right + zero  34.2 us
    concatenate x15, other arithmetic, step(): self.arrays = [jnp.concatenate([mine[0], others[0]], axis=0)]  20.3 us
  transfers between devices with their start and end apart: 80, of which 28 were waited for; matrix products, arithmetic and copies ran while one was open for 18% of the time, Pallas kernels for 38%

profile of v2, /device:TPU:0, one launch (start us, length us, event | category | flops | bytes accessed | tf_op | source)
XLA Modules:
  0.0 568.0 jit_solution(8214103382840417267)
XLA Ops:
  5.2 3.7 collective-permute-start.3
  11.4 4.4 stats.1
  17.4 2.0 collective-permute-done.1
  22.3 2.1 collective-permute-done.2
  26.6 7.1 %collective-permute-done.4 = bf16[1,32,3328]{2,1,0:T(8,128)(2,1)S(1)} collective-permute-done((bf16[1,32,3328]{2,1,0:T(8,128)(2,1)S(1)}, bf16[1,32,3328]{2,1,0:T(8,128)(2,1)S(1)}, u32[]{:S(2)}, u32[]{:S(2)}) %collective-permute-start.4) | collective-permute-done | bytes 213024 | tf_op jit(solution)/shard_map/ppermute | solution.py:437
  36.1 3.0 collective-permute-done.5
  43.9 2.9 collective-permute-done.6
  49.1 12.8 %norm.1 = (bf16[512,1024]{1,0:T(8,128)(2,1)}, f32[4096,128]{1,0:T(8,128)}, f32[256,128]{1,0:T(8,128)}) custom-call(bf16[512,1024]{1,0:T(8,128)(2,1)} %bitcast.196, f32[512,1]{1,0:T(8,128)} %copy.84.refs_1_.refs_3_.refs_6_.refs_4_, s32[512,1]{1,0:T(8,128)} %copy.85.refs_2_.refs_3_.refs_10_.refs_7_.refs_5_, ...), custom_call_target="tpu_custom_call" | custom-call | flops 650000000 | bytes 1950000 | tf_op jit(solution)/shard_map/norm/pallas_call | solution.py:75
  68.6 6.5 %collective-permute-done.11 = bf16[2,32,3072]{2,1,0:T(8,128)(2,1)S(1)} collective-permute-done((bf16[2,32,3072]{2,1,0:T(8,128)(2,1)S(1)}, bf16[2,32,3072]{2,1,0:T(8,128)(2,1)S(1)}, u32[]{:S(2)}, u32[]{:S(2)}) %collective-permute-start.11) | collective-permute-done | bytes 393248 | tf_op jit(solution)/shard_map/ppermute | solution.py:437
  78.4 8.3 %collective-permute-done.13 = bf16[2,32,3328]{2,1,0:T(8,128)(2,1)S(1)} collective-permute-done((bf16[2,32,3328]{2,1,0:T(8,128)(2,1)S(1)}, bf16[2,32,3328]{2,1,0:T(8,128)(2,1)S(1)}, u32[]{:S(2)}, u32[]{:S(2)}) %collective-permute-start.13) | collective-permute-done | bytes 426016 | tf_op jit(solution)/shard_map/ppermute | solution.py:437
  93.2 7.3 %collective-permute-done.16 = bf16[1,32,2560]{2,1,0:T(8,128)(2,1)S(1)} collective-permute-done((bf16[1,32,2560]{2,1,0:T(8,128)(2,1)}, bf16[1,32,2560]{2,1,0:T(8,128)(2,1)S(1)}, u32[]{:S(2)}, u32[]{:S(2)}) %collective-permute-start.16) | collective-permute-done | bytes 163872 | tf_op jit(solution)/shard_map/ppermute | solution.py:437
  104.3 2.7 collective-permute-done.14
  108.3 2.5 collective-permute-start.25
  112.7 15.6 %mix.1 = (f32[4096,128]{1,0:T(8,128)}, bf16[512,1024]{1,0:T(8,128)(2,1)}, f32[16,256,128]{2,1,0:T(8,128)}) custom-call(f32[4096,128]{1,0:T(8,128)} %get-tuple-element.88.refs_0_, f32[256,128]{1,0:T(8,128)} %bitcast.216, f32[128,128]{1,0:T(8,128)} %bitcast.210, f32[128,128]{1,0:T(8,128)} %bitcast.203, f32[128,128]{1,0:T(8,128)} %bitcast.224, ...), custom_call_target="tpu_custom_call" | custom-call | flops 800000000 | bytes 2400000 | tf_op jit(solution)/shard_map/mix/pallas_call | solution.py:75
  128.3 2.2 collective-permute-start.35
  137.0 12.4 %collective-permute-done.23 = bf16[2,32,2560]{2,1,0:T(8,128)(2,1)} collective-permute-done((bf16[2,32,2560]{2,1,0:T(8,128)(2,1)}, bf16[2,32,2560]{2,1,0:T(8,128)(2,1)}, u32[]{:S(2)}, u32[]{:S(2)}) %collective-permute-start.23) | collective-permute-done | bytes 327712 | tf_op jit(solution)/shard_map/ppermute | solution.py:437
  152.9 4.2 collective-permute-done.35
  157.1 2.3 copy.119.refs_0_
  159.3 20.9 %collective-permute-done.26 = bf16[4,32,2560]{2,1,0:T(8,128)(2,1)} collective-permute-done((bf16[4,32,2560]{2,1,0:T(8,128)(2,1)}, bf16[4,32,2560]{2,1,0:T(8,128)(2,1)}, u32[]{:S(2)}, u32[]{:S(2)}) %collective-permute-start.26) | collective-permute-done | bytes 655392 | tf_op jit(solution)/shard_map/ppermute | solution.py:437
  182.3 2.5 pad_maximum_fusion.4.refs_0_
  186.2 2.3 pad_maximum_fusion.3.refs_18_.refs_0_
  195.9 17.5 %attention.1 = (f32[512,256]{1,0:T(8,128)}, bf16[512,256]{1,0:T(8,128)(2,1)}, bf16[512,256]{1,0:T(8,128)(2,1)}, f32[512,1]{1,0:T(8,128)}, bf16[512,2048]{1,0:T(8...) custom-call(s32[2]{0:T(128)} %pad_add_fusion.refs_0_, ...), custom_call_target="tpu_custom_call" | custom-call | flops 900000000 | bytes 2700000 | tf_op jit(solution)/shard_map/attention/pallas_call | solution.py:75
  213.4 2.9 collective-permute-done.36.refs_0_
  216.9 2.8 collective-permute-done.31.refs_0_
  219.7 2.2 dynamic-slice_bitcast_fusion
  222.5 3.6 collective-permute-done.39.refs_15_.refs_4_
  227.8 7.9 %project.1 = (f32[512,1024]{1,0:T(8,128)}, bf16[512,1024]{1,0:T(8,128)(2,1)}, f32[512,1]{1,0:T(8,128)}) custom-call(s32[2]{0:T(128)} %pad_add_fusion.refs_0_, bf16[512,2048]{1,0:T(8,128)(2,1)} %get-tuple-element.92.refs_1_, bf16[512,1024]{1,0:T(8,128)(2,1)} %bitcast.197, f32[512,1]{1,0:T(8,128)} %copy.84.refs_1_.refs_3_.refs_6_.refs_4_, ...), custom_call_target="tpu_custom_call" | custom-call | flops 300000000 | bytes 900000 | tf_op jit(solution)/shard_map/project/pallas_call | solution.py:75
  235.8 19.1 %hidden.1 = (bf16[512,2560]{1,0:T(8,128)(2,1)}, bf16[512,2560]{1,0:T(8,128)(2,1)}, bf16[512,2560]{1,0:T(8,128)(2,1)}) custom-call(s32[2]{0:T(128)} %pad_add_fusion.refs_0_, bf16[512,1024]{1,0:T(8,128)(2,1)} %get-tuple-element.93.refs_1_, bf16[512,1024]{1,0:T(8,128)(2,1)} %bitcast.200, bf16[8,32,2560]{2,1,0:T(8,128)(2,1)} %tie.51.refs_3_.refs_7_, ...), custom_call_target="tpu_custom_call" | custom-call | flops 750000000 | bytes 2250000 | tf_op jit(solution)/shard_map/hidden/pallas_call | solution.py:102
  255.6 8.2 %out.1.refs_5_ = bf16[512,1024]{1,0:T(8,128)(2,1)} custom-call(s32[2]{0:T(128)} %pad_add_fusion.refs_0_, bf16[512,2560]{1,0:T(8,128)(2,1)} %get-tuple-element.94.refs_1_, f32[512,1024]{1,0:T(8,128)} %get-tuple-element.95.refs_2_.refs_3_, bf16[8,80,1024]{2,1,0:T(8,128)(2,1)} %tie.57.refs_11_.refs_3_, bf16[8,80,1024]{2,1,0:T(8,128)(2,1)} %tie.58.refs_12_.refs_4_, ...), custom_call_target="tpu_custom_call" | custom-call | flops 350000000 | bytes 1050000 | tf_op jit(solution)/shard_map/out/pallas_call | solution.py:75
  263.8 7.5 %grad_down.1 = (bf16[8,160,512]{2,1,0:T(8,128)(2,1)}, bf16[8,160,512]{2,1,0:T(8,128)(2,1)}) custom-call(s32[2]{0:T(128)} %pad_add_fusion.refs_0_, bf16[512,2560]{1,0:T(8,128)(2,1)} %get-tuple-element.94.refs_1_, bf16[512,2560]{1,0:T(8,128)(2,1)} %collective-permute-done.44.refs_2_, bf16[512,512]{1,0:T(8,128)(2,1)} %get-tuple-element.189.refs_3_, ...), custom_call_target="tpu_custom_call" | custom-call | flops 300000000 | bytes 900000 | tf_op jit(solution)/shard_map/grad_down/pallas_call | solution.py:102
  274.5 7.0 %grad_gate.1 = (bf16[8,64,1280]{2,1,0:T(8,128)(2,1)}, bf16[8,64,1280]{2,1,0:T(8,128)(2,1)}) custom-call(s32[2]{0:T(128)} %pad_add_fusion.refs_0_, bf16[512,1024]{1,0:T(8,128)(2,1)} %get-tuple-element.93.refs_1_, bf16[512,1024]{1,0:T(8,128)(2,1)} %collective-permute-done.42.refs_2_, bf16[512,2560]{1,0:T(8,128)(2,1)} %get-tuple-element.96.refs_3_.refs_1_, ...), custom_call_target="tpu_custom_call" | custom-call | flops 300000000 | bytes 900000 | tf_op jit(solution)/shard_map/grad_gate/pallas_call | solution.py:102
  283.1 7.1 %grad_up.1 = (bf16[8,64,1280]{2,1,0:T(8,128)(2,1)}, bf16[8,64,1280]{2,1,0:T(8,128)(2,1)}) custom-call(s32[2]{0:T(128)} %pad_add_fusion.refs_0_, bf16[512,1024]{1,0:T(8,128)(2,1)} %get-tuple-element.93.refs_1_, bf16[512,1024]{1,0:T(8,128)(2,1)} %collective-permute-done.42.refs_2_, bf16[512,2560]{1,0:T(8,128)(2,1)} %get-tuple-element.96.refs_3_.refs_1_, ...), custom_call_target="tpu_custom_call" | custom-call | flops 300000000 | bytes 900000 | tf_op jit(solution)/shard_map/grad_up/pallas_call | solution.py:102
  290.3 14.9 %ffn_back.1 = (f32[512,1024]{1,0:T(8,128)}, bf16[512,512]{1,0:T(8,128)(2,1)}, bf16[512,512]{1,0:T(8,128)(2,1)}, bf16[512,1024]{1,0:T(8,128)(2,1)}, f32[1,1024]{1,0:T(1,128)}) custom-call(s32[2]{0:T(128)} %pad_add_fusion.refs_0_, bf16[512,2560]{1,0:T(8,128)(2,1)} %get-tuple-element.96.refs_3_.refs_1_, bf16[512,2560]{1,0:T(8,128)(2,1)} %get-tuple-element.97.refs_2_, ...), custom_call_target="tpu_custom_call" | custom-call | flops 850000000 | bytes 2550000 | tf_op jit(solution)/shard_map/ffn_back/pallas_call | solution.py:75
  310.3 2.1 fusion.2
  314.0 6.9 %grad_h.1 = (bf16[8,128,512]{2,1,0:T(8,128)(2,1)}, bf16[8,128,512]{2,1,0:T(8,128)(2,1)}) custom-call(s32[2]{0:T(128)} %pad_add_fusion.refs_0_, bf16[512,2048]{1,0:T(8,128)(2,1)} %get-tuple-element.92.refs_1_, bf16[512,2048]{1,0:T(8,128)(2,1)} %collective-permute-done.40.refs_16_.refs_2_, bf16[512,512]{1,0:T(8,128)(2,1)} %get-tuple-element.111.refs_1_.refs_3_, ...), custom_call_target="tpu_custom_call" | custom-call | flops 300000000 | bytes 900000 | tf_op jit(solution)/shard_map/grad_h/pallas_call | solution.py:102
  321.4 3.2 fusion.1
  324.6 21.2 %attention_back.1 = (bf16[512,2048]{1,0:T(8,128)(2,1)}, bf16[512,2304]{1,0:T(8,128)(2,1)}, bf16[512,1024]{1,0:T(8,128)(2,1)}, bf16[512,1024]{1,0:T(8,128)(2,1)},...) custom-call(s32[2]{0:T(128)} %pad_add_fusion.refs_0_, ...), custom_call_target="tpu_custom_call" | custom-call | flops 950000000 | bytes 2850000 | tf_op jit(solution)/shard_map/attention_back/pallas_call | solution.py:75
  349.2 2.5 fusion.20
  353.3 2.9 fusion
  357.6 10.7 %sent_back.1 = (bf16[512,1024]{1,0:T(8,128)(2,1)}, bf16[512,1024]{1,0:T(8,128)(2,1)}) custom-call(s32[2]{0:T(128)} %pad_add_fusion.refs_0_, bf16[512,2048]{1,0:T(8,128)(2,1)} %get-tuple-element.116.refs_1_, bf16[512,2304]{1,0:T(8,128)(2,1)} %get-tuple-element.117.refs_2_, bf16[8,32,3072]{2,1,0:T(8,128)(2,1)} %tie.44.refs_9_.refs_5_.refs_15_.refs_3_, ...), custom_call_target="tpu_custom_call" | custom-call | flops 550000000 | bytes 1650000 | tf_op jit(solution)/shard_map/sent_back/pallas_call | solution.py:75
  369.5 2.3 fusion.34.refs_5_
  371.8 2.6 collective-permute-done.50
  375.8 2.9 fusion.10
  378.7 12.2 %back_ends.1 = (f32[4096,128]{1,0:T(8,128)}, f32[256,128]{1,0:T(8,128)}) custom-call(bf16[512,1024]{1,0:T(8,128)(2,1)} %get-tuple-element.120.refs_1_.refs_0_, f32[4096,128]{1,0:T(8,128)} %get-tuple-element.91.refs_1_, f32[128,128]{1,0:T(8,128)} %bitcast.211, f32[128,128]{1,0:T(8,128)} %bitcast.204, bf16[4,128,512]{2,1,0:T(8,128)(2,1)} %get-tuple-element.176.refs_4_, ...), custom_call_target="tpu_custom_call" | custom-call | flops 600000000 | bytes 1800000 | tf_op jit(solution)/shard_map/back_ends/pallas_call | solution.py:75
  398.5 6.3 %grad_v.1 = (bf16[8,64,1024]{2,1,0:T(8,128)(2,1)}, bf16[8,64,1024]{2,1,0:T(8,128)(2,1)}) custom-call(s32[2]{0:T(128)} %pad_add_fusion.refs_0_, bf16[512,1024]{1,0:T(8,128)(2,1)} %get-tuple-element.87.refs_1_, bf16[512,1024]{1,0:T(8,128)(2,1)} %collective-permute-done.27.refs_19_.refs_2_, bf16[512,1024]{1,0:T(8,128)(2,1)} %get-tuple-element.125.refs_3_, ...), custom_call_target="tpu_custom_call" | custom-call | flops 300000000 | bytes 900000 | tf_op jit(solution)/shard_map/grad_v/pallas_call | solution.py:102
  406.0 2.3 add_add_fusion.2.refs_7_
  408.4 7.0 %grad_r.1 = (bf16[8,64,1152]{2,1,0:T(8,128)(2,1)}, bf16[8,64,1152]{2,1,0:T(8,128)(2,1)}) custom-call(s32[2]{0:T(128)} %pad_add_fusion.refs_0_, bf16[512,1024]{1,0:T(8,128)(2,1)} %get-tuple-element.90.refs_2_.refs_1_, bf16[512,1024]{1,0:T(8,128)(2,1)} %collective-permute-done.41.refs_17_.refs_2_, bf16[512,1152]{1,0:T(8,128)(2,1)} %get-tuple-element.128.refs_3_, ...), custom_call_target="tpu_custom_call" | custom-call | flops 300000000 | bytes 900000 | tf_op jit(solution)/shard_map/grad_r/pallas_call | solution.py:102
  424.0 2.6 collective-permute-start.59
  427.4 6.1 %collective-permute-done.59 = f32[32,8,128]{2,1,0:T(8,128)S(1)} collective-permute-done((f32[32,8,128]{2,1,0:T(8,128)}, f32[32,8,128]{2,1,0:T(8,128)S(1)}, u32[]{:S(2)}, u32[]{:S(2)}) %collective-permute-start.59) | collective-permute-done | bytes 131104 | tf_op jit(solution)/shard_map/ppermute | solution.py:437
  438.0 3.1 collective-permute-start.65
  441.8 10.5 %back.4 = (f32[1024,128]{1,0:T(8,128)}, f32[256,128]{1,0:T(8,128)}, f32[392,128]{1,0:T(8,128)}) custom-call(f32[4096,128]{1,0:T(8,128)} %get-tuple-element.88.refs_0_, f32[4096,128]{1,0:T(8,128)} %get-tuple-element.122.refs_1_, f32[16,256,128]{2,1,0:T(8,128)} %get-tuple-element.123.refs_2_, f32[256,128]{1,0:T(8,128)} %maximum_bitcast_fusion.2.refs_3_, ...), custom_call_target="tpu_custom_call" | custom-call | flops 500000000 | bytes 1500000 | tf_op jit(solution)/shard_map/back/pallas_call | solution.py:75
  454.4 2.7 fusion.8
  457.9 10.3 %back.5 = (f32[1024,128]{1,0:T(8,128)}, f32[256,128]{1,0:T(8,128)}, f32[392,128]{1,0:T(8,128)}) custom-call(f32[4096,128]{1,0:T(8,128)} %get-tuple-element.88.refs_0_, f32[4096,128]{1,0:T(8,128)} %get-tuple-element.122.refs_1_, f32[16,256,128]{2,1,0:T(8,128)} %get-tuple-element.123.refs_2_, f32[256,128]{1,0:T(8,128)} %get-tuple-element.130.refs_3_, ...), custom_call_target="tpu_custom_call" | custom-call | flops 500000000 | bytes 1500000 | tf_op jit(solution)/shard_map/back/pallas_call | solution.py:75
  472.3 2.1 fusion.6
  475.9 10.7 %back.6 = (f32[1024,128]{1,0:T(8,128)}, f32[256,128]{1,0:T(8,128)}, f32[392,128]{1,0:T(8,128)}) custom-call(f32[4096,128]{1,0:T(8,128)} %get-tuple-element.88.refs_0_, f32[4096,128]{1,0:T(8,128)} %get-tuple-element.122.refs_1_, f32[16,256,128]{2,1,0:T(8,128)} %get-tuple-element.123.refs_2_, f32[256,128]{1,0:T(8,128)} %get-tuple-element.134.refs_3_, ...), custom_call_target="tpu_custom_call" | custom-call | flops 500000000 | bytes 1500000 | tf_op jit(solution)/shard_map/back/pallas_call | solution.py:75
  490.0 10.4 %back.7 = (f32[1024,128]{1,0:T(8,128)}, f32[256,128]{1,0:T(8,128)}, f32[392,128]{1,0:T(8,128)}) custom-call(f32[4096,128]{1,0:T(8,128)} %get-tuple-element.88.refs_0_, f32[4096,128]{1,0:T(8,128)} %get-tuple-element.122.refs_1_, f32[16,256,128]{2,1,0:T(8,128)} %get-tuple-element.123.refs_2_, f32[256,128]{1,0:T(8,128)} %get-tuple-element.138.refs_3_, ...), custom_call_target="tpu_custom_call" | custom-call | flops 500000000 | bytes 1500000 | tf_op jit(solution)/shard_map/back/pallas_call | solution.py:75
  513.2 7.0 %back_norm.1 = (f32[512,1024]{1,0:T(8,128)}, f32[1,1024]{1,0:T(1,128)}, f32[512,128]{1,0:T(8,128)}, f32[16,128]{1,0:T(8,128)}) custom-call(f32[1024,128]{1,0:T(8,128)} %get-tuple-element.141.refs_1_.refs_0_, f32[1024,128]{1,0:T(8,128)} %get-tuple-element.140.refs_1_, f32[1024,128]{1,0:T(8,128)} %get-tuple-element.137.refs_1_.refs_2_, ...), custom_call_target="tpu_custom_call" | custom-call | flops 300000000 | bytes 900000 | tf_op jit(solution)/shard_map/back_norm/pallas_call | solution.py:75
  522.2 4.1 collective-permute-done.69
  530.5 3.5 collective-permute-done.70
  535.9 2.8 collective-permute-done.71
  538.7 2.7 collective-permute-start.72
  542.4 8.1 %collective-permute-done.72 = f32[84,128]{1,0:T(8,128)S(1)} collective-permute-done((f32[84,128]{1,0:T(8,128)S(1)}, f32[84,128]{1,0:T(8,128)S(1)}, u32[]{:S(2)}, u32[]{:S(2)}) %collective-permute-start.72) | collective-permute-done | bytes 43040 | tf_op jit(solution)/shard_map/ppermute | solution.py:437
  552.4 3.3 collective-permute-done.73
  557.3 5.9 %input.1 = f32[512,1024]{1,0:T(8,128)} custom-call(f32[512,1024]{1,0:T(8,128)} %get-tuple-element.143.refs_0_, f32[512,128]{1,0:T(8,128)} %get-tuple-element.144.refs_1_, f32[1,128]{1,0:T(1,128)} %fusion.53.refs_1_.refs_2_, bf16[512,1024]{1,0:T(8,128)(2,1)} %bitcast.199, f32[512,1]{1,0:T(8,128)} %copy.84.refs_1_.refs_3_.refs_6_.refs_4_, ...), custom_call_target="tpu_custom_call" | custom-call | flops 300000000 | bytes 900000 | tf_op jit(solution)/shard_map/input/pallas_call | solution.py:75
  (500 shorter events, 149.9 us)
Async XLA Ops:
  2.7 13.0 %collective-permute-start = (f32[1,1,56]{2,1,0:T(1,128)S(1)}, f32[1,1,56]{2,1,0:T(1,128)S(1)}, u32[]{:S(2)}, u32[]{:S(2)}) collective-permute-start(f32[1,1,56]{2,1,0:T(1,128)S(1)} %maximum_convert_fusion), channel_id=1, source_target_pairs={{0,1},{1,0},{2,3},{3,2},{4,5},{5,4},{6,7},{7,6},{8,9},{9,8},{10,11... | collective-permute-start | bytes 680 | tf_op jit(solution)/shard_map/ppermute | solution.py:437
  5.2 20.6 %collective-permute-start.3 = (bf16[1,32,3072]{2,1,0:T(8,128)(2,1)S(1)}, bf16[1,32,3072]{2,1,0:T(8,128)(2,1)S(1)}, u32[]{:S(2)}, u32[]{:S(2)}) collective-permute-start(bf16[1,32,3072]{2,1,0:T(8,128)(2,1)S(1)} %maximum_bitcast_fusion.1), channel_id=1, source_target_pairs={{0,16},{4,20},{8,24},{12,28},{16,0},{20,4},{24,8},{28,12},{1,17},{... | collective-permute-start | bytes 589832 | tf_op jit(solution)/shard_map/ppermute | solution.py:437
  21.9 11.8 %collective-permute-start.4 = (bf16[1,32,3328]{2,1,0:T(8,128)(2,1)S(1)}, bf16[1,32,3328]{2,1,0:T(8,128)(2,1)S(1)}, u32[]{:S(2)}, u32[]{:S(2)}) collective-permute-start(bf16[1,32,3328]{2,1,0:T(8,128)(2,1)S(1)} %maximum_bitcast_fusion), channel_id=1, source_target_pairs={{0,16},{4,20},{8,24},{12,28},{16,0},{20,4},{24,8},{28,12},{1,17},{... | collective-permute-start | bytes 638984 | tf_op jit(solution)/shard_map/ppermute | solution.py:437
  63.1 12.1 %collective-permute-start.11 = (bf16[2,32,3072]{2,1,0:T(8,128)(2,1)S(1)}, bf16[2,32,3072]{2,1,0:T(8,128)(2,1)S(1)}, u32[]{:S(2)}, u32[]{:S(2)}) collective-permute-start(bf16[2,32,3072]{2,1,0:T(8,128)(2,1)S(1)} %copy-done.14), channel_id=1, source_target_pairs={{0,8},{4,12},{8,0},{12,4},{16,24},{20,28},{24,16},{28,20},{1,9},{5... | collective-permute-start | bytes 1179656 | tf_op jit(solution)/shard_map/ppermute | solution.py:437
  63.1 23.7 %collective-permute-start.13 = (bf16[2,32,3328]{2,1,0:T(8,128)(2,1)S(1)}, bf16[2,32,3328]{2,1,0:T(8,128)(2,1)S(1)}, u32[]{:S(2)}, u32[]{:S(2)}) collective-permute-start(bf16[2,32,3328]{2,1,0:T(8,128)(2,1)S(1)} %copy-done.30), channel_id=1, source_target_pairs={{0,8},{4,12},{8,0},{12,4},{16,24},{20,28},{24,16},{28,20},{1,9},{5... | collective-permute-start | bytes 1277960 | tf_op jit(solution)/shard_map/ppermute | solution.py:437
  65.1 45.7 %collective-permute-start.34 = (bf16[2,80,1024]{2,1,0:T(8,128)(2,1)}, bf16[2,80,1024]{2,1,0:T(8,128)(2,1)}, u32[]{:S(2)}, u32[]{:S(2)}) collective-permute-start(bf16[2,80,1024]{2,1,0:T(8,128)(2,1)} %tie.55), channel_id=1, source_target_pairs={{0,4},{4,0},{8,12},{12,8},{16,20},{20,16},{24,28},{28,24},{1,5},{5... | collective-permute-start | bytes 983048 | tf_op jit(solution)/shard_map/ppermute | solution.py:437
  68.5 20.5 %collective-permute-start.9 = (f32[32,8,128]{2,1,0:T(8,128)S(1)}, f32[32,8,128]{2,1,0:T(8,128)S(1)}, u32[]{:S(2)}, u32[]{:S(2)}) collective-permute-start(f32[32,8,128]{2,1,0:T(8,128)S(1)} %pad_maximum_fusion.30), channel_id=1, source_target_pairs={{0,8},{4,12},{8,0},{12,4},{16,24},{20,28},{24,16},{28,20},{1,9},{5... | collective-permute-start | bytes 393224 | tf_op jit(solution)/shard_map/ppermute | solution.py:437
  76.1 14.6 %collective-permute-start.15 = (bf16[1,32,2560]{2,1,0:T(8,128)(2,1)}, bf16[1,32,2560]{2,1,0:T(8,128)(2,1)S(1)}, u32[]{:S(2)}, u32[]{:S(2)}) collective-permute-start(bf16[1,32,2560]{2,1,0:T(8,128)(2,1)} %tie.41), channel_id=1, source_target_pairs={{0,16},{4,20},{8,24},{12,28},{16,0},{20,4},{24,8},{28,12},{1,17},{... | collective-permute-start | bytes 491528 | tf_op jit(solution)/shard_map/ppermute | solution.py:437
  76.9 26.1 %collective-permute-start.12 = (bf16[4,32,3072]{2,1,0:T(8,128)(2,1)}, bf16[4,32,3072]{2,1,0:T(8,128)(2,1)S(1)}, u32[]{:S(2)}, u32[]{:S(2)}) collective-permute-start(bf16[4,32,3072]{2,1,0:T(8,128)(2,1)} %tie.39), channel_id=1, source_target_pairs={{0,4},{4,0},{8,12},{12,8},{16,20},{20,16},{24,28},{28,24},{1,5},{5... | collective-permute-start | bytes 2359304 | tf_op jit(solution)/shard_map/ppermute | solution.py:437
  87.7 12.8 %collective-permute-start.16 = (bf16[1,32,2560]{2,1,0:T(8,128)(2,1)}, bf16[1,32,2560]{2,1,0:T(8,128)(2,1)S(1)}, u32[]{:S(2)}, u32[]{:S(2)}) collective-permute-start(bf16[1,32,2560]{2,1,0:T(8,128)(2,1)} %tie.42), channel_id=1, source_target_pairs={{0,16},{4,20},{8,24},{12,28},{16,0},{20,4},{24,8},{28,12},{1,17},{... | collective-permute-start | bytes 491528 | tf_op jit(solution)/shard_map/ppermute | solution.py:437
  89.0 18.0 %collective-permute-start.14 = (bf16[4,32,3328]{2,1,0:T(8,128)(2,1)}, bf16[4,32,3328]{2,1,0:T(8,128)(2,1)S(1)}, u32[]{:S(2)}, u32[]{:S(2)}) collective-permute-start(bf16[4,32,3328]{2,1,0:T(8,128)(2,1)} %tie.40), channel_id=1, source_target_pairs={{0,2},{2,0},{1,3},{3,1},{4,6},{6,4},{5,7},{7,5},{8,10},{10,8},{9,1... | collective-permute-start | bytes 2555912 | tf_op jit(solution)/shard_map/ppermute | solution.py:437
  90.7 11.6 %collective-permute-start.10 = (f32[32,8,128]{2,1,0:T(8,128)S(1)}, f32[32,8,128]{2,1,0:T(8,128)S(1)}, u32[]{:S(2)}, u32[]{:S(2)}) collective-permute-start(f32[32,8,128]{2,1,0:T(8,128)S(1)} %pad_maximum_fusion.31), channel_id=1, source_target_pairs={{0,16},{4,20},{8,24},{12,28},{16,0},{20,4},{24,8},{28,12},{1,17},{... | collective-permute-start | bytes 393224 | tf_op jit(solution)/shard_map/ppermute | solution.py:437
  108.3 26.1 %collective-permute-start.25 = (bf16[2,32,2560]{2,1,0:T(8,128)(2,1)}, bf16[2,32,2560]{2,1,0:T(8,128)(2,1)}, u32[]{:S(2)}, u32[]{:S(2)}) collective-permute-start(bf16[2,32,2560]{2,1,0:T(8,128)(2,1)} %tie.48), channel_id=1, source_target_pairs={{0,8},{4,12},{8,0},{12,4},{16,24},{20,28},{24,16},{28,20},{1,9},{5... | collective-permute-start | bytes 983048 | tf_op jit(solution)/shard_map/ppermute | solution.py:437
  128.3 28.8 %collective-permute-start.35 = (bf16[4,80,1024]{2,1,0:T(8,128)(2,1)}, bf16[4,80,1024]{2,1,0:T(8,128)(2,1)}, u32[]{:S(2)}, u32[]{:S(2)}) collective-permute-start(bf16[4,80,1024]{2,1,0:T(8,128)(2,1)} %tie.56), channel_id=1, source_target_pairs={{0,16},{4,20},{8,24},{12,28},{16,0},{20,4},{24,8},{28,12},{1,17},{... | collective-permute-start | bytes 1966088 | tf_op jit(solution)/shard_map/ppermute | solution.py:437
  130.4 18.9 %collective-permute-start.23 = (bf16[2,32,2560]{2,1,0:T(8,128)(2,1)}, bf16[2,32,2560]{2,1,0:T(8,128)(2,1)}, u32[]{:S(2)}, u32[]{:S(2)}) collective-permute-start(bf16[2,32,2560]{2,1,0:T(8,128)(2,1)} %tie.46), channel_id=1, source_target_pairs={{0,8},{4,12},{8,0},{12,4},{16,24},{20,28},{24,16},{28,20},{1,9},{5... | collective-permute-start | bytes 983048 | tf_op jit(solution)/shard_map/ppermute | solution.py:437
  131.4 50.4 %collective-permute-start.20 = (bf16[8,32,3328]{2,1,0:T(8,128)(2,1)S(1)}, bf16[8,32,3328]{2,1,0:T(8,128)(2,1)}, u32[]{:S(2)}, u32[]{:S(2)}) collective-permute-start(bf16[8,32,3328]{2,1,0:T(8,128)(2,1)S(1)} %copy-done.1), channel_id=1, source_target_pairs={{0,4},{4,0},{8,12},{12,8},{16,20},{20,16},{24,28},{28,24},{1,5},{5... | collective-permute-start | bytes 5111816 | tf_op jit(solution)/shard_map/ppermute | solution.py:437
  133.0 49.3 %collective-permute-start.17 = (bf16[8,32,3072]{2,1,0:T(8,128)(2,1)S(1)}, bf16[8,32,3072]{2,1,0:T(8,128)(2,1)}, u32[]{:S(2)}, u32[]{:S(2)}) collective-permute-start(bf16[8,32,3072]{2,1,0:T(8,128)(2,1)S(1)} %copy-done.2), channel_id=1, source_target_pairs={{0,2},{2,0},{1,3},{3,1},{4,6},{6,4},{5,7},{7,5},{8,10},{10,8},{9,1... | collective-permute-start | bytes 4718600 | tf_op jit(solution)/shard_map/ppermute | solution.py:437
  136.4 43.8 %collective-permute-start.26 = (bf16[4,32,2560]{2,1,0:T(8,128)(2,1)}, bf16[4,32,2560]{2,1,0:T(8,128)(2,1)}, u32[]{:S(2)}, u32[]{:S(2)}) collective-permute-start(bf16[4,32,2560]{2,1,0:T(8,128)(2,1)} %tie.49), channel_id=1, source_target_pairs={{0,2},{2,0},{1,3},{3,1},{4,6},{6,4},{5,7},{7,5},{8,10},{10,8},{9,1... | collective-permute-start | bytes 1966088 | tf_op jit(solution)/shard_map/ppermute | solution.py:437
  151.3 30.4 %collective-permute-start.24 = (bf16[4,32,2560]{2,1,0:T(8,128)(2,1)}, bf16[4,32,2560]{2,1,0:T(8,128)(2,1)}, u32[]{:S(2)}, u32[]{:S(2)}) collective-permute-start(bf16[4,32,2560]{2,1,0:T(8,128)(2,1)} %tie.47), channel_id=1, source_target_pairs={{0,4},{4,0},{8,12},{12,8},{16,20},{20,16},{24,28},{28,24},{1,5},{5... | collective-permute-start | bytes 1966088 | tf_op jit(solution)/shard_map/ppermute | solution.py:437
  157.1 31.5 %collective-permute-start.18 = (bf16[8,32,3072]{2,1,0:T(8,128)(2,1)S(1)}, bf16[8,32,3072]{2,1,0:T(8,128)(2,1)}, u32[]{:S(2)}, u32[]{:S(2)}) collective-permute-start(bf16[8,32,3072]{2,1,0:T(8,128)(2,1)S(1)} %copy-done.2), channel_id=1, source_target_pairs={{0,1},{1,0},{2,3},{3,2},{4,5},{5,4},{6,7},{7,6},{8,9},{9,8},{10,11... | collective-permute-start | bytes 4718600 | tf_op jit(solution)/shard_map/ppermute | solution.py:437
  181.7 9.6 %collective-permute-start.21 = (bf16[8,32,3328]{2,1,0:T(8,128)(2,1)S(1)}, bf16[8,32,3328]{2,1,0:T(8,128)(2,1)}, u32[]{:S(2)}, u32[]{:S(2)}) collective-permute-start(bf16[8,32,3328]{2,1,0:T(8,128)(2,1)S(1)} %copy-done.1), channel_id=1, source_target_pairs={{0,1},{1,0},{2,3},{3,2},{4,5},{5,4},{6,7},{7,6},{8,9},{9,8},{10,11... | collective-permute-start | bytes 5111816 | tf_op jit(solution)/shard_map/ppermute | solution.py:437
  181.8 14.1 %collective-permute-start.22 = (bf16[8,32,3328]{2,1,0:T(8,128)(2,1)}, bf16[8,32,3328]{2,1,0:T(8,128)(2,1)}, u32[]{:S(2)}, u32[]{:S(2)}) collective-permute-start(bf16[8,32,3328]{2,1,0:T(8,128)(2,1)} %collective-permute-done.20.refs_14_.refs_10_.refs_20_.refs_8_), channel_id=1, source_target_pairs={{0,1},{1,0},{2,3},{3,2},{4,5},{5,4},{6,7},{7,6},{8,9},{9,8},{10,11... | collective-permute-start | bytes 5111816 | tf_op jit(solution)/shard_map/ppermute | solution.py:437
  182.3 13.6 %collective-permute-start.19 = (bf16[8,32,3072]{2,1,0:T(8,128)(2,1)}, bf16[8,32,3072]{2,1,0:T(8,128)(2,1)}, u32[]{:S(2)}, u32[]{:S(2)}) collective-permute-start(bf16[8,32,3072]{2,1,0:T(8,128)(2,1)} %collective-permute-done.17.refs_10_.refs_6_.refs_16_.refs_4_), channel_id=1, source_target_pairs={{0,1},{1,0},{2,3},{3,2},{4,5},{5,4},{6,7},{7,6},{8,9},{9,8},{10,11... | collective-permute-start | bytes 4718600 | tf_op jit(solution)/shard_map/ppermute | solution.py:437
  184.9 31.4 %collective-permute-start.36 = (bf16[8,80,1024]{2,1,0:T(8,128)(2,1)}, bf16[8,80,1024]{2,1,0:T(8,128)(2,1)}, u32[]{:S(2)}, u32[]{:S(2)}) collective-permute-start(bf16[8,80,1024]{2,1,0:T(8,128)(2,1)} %pad_maximum_fusion.4.refs_0_), channel_id=1, source_target_pairs={{0,8},{4,12},{8,0},{12,4},{16,24},{20,28},{24,16},{28,20},{1,9},{5... | collective-permute-start | bytes 3932168 | tf_op jit(solution)/shard_map/ppermute | solution.py:437
  188.6 31.2 %collective-permute-start.31 = (bf16[8,32,2560]{2,1,0:T(8,128)(2,1)}, bf16[8,32,2560]{2,1,0:T(8,128)(2,1)}, u32[]{:S(2)}, u32[]{:S(2)}) collective-permute-start(bf16[8,32,2560]{2,1,0:T(8,128)(2,1)} %pad_maximum_fusion.3.refs_18_.refs_0_), channel_id=1, source_target_pairs={{0,4},{4,0},{8,12},{12,8},{16,20},{20,16},{24,28},{28,24},{1,5},{5... | collective-permute-start | bytes 3932168 | tf_op jit(solution)/shard_map/ppermute | solution.py:437
  191.4 30.7 %collective-permute-start.28 = (bf16[8,32,2560]{2,1,0:T(8,128)(2,1)S(1)}, bf16[8,32,2560]{2,1,0:T(8,128)(2,1)}, u32[]{:S(2)}, u32[]{:S(2)}) collective-permute-start(bf16[8,32,2560]{2,1,0:T(8,128)(2,1)S(1)} %pad_maximum_fusion.2.refs_17_.refs_0_), channel_id=1, source_target_pairs={{0,2},{2,0},{1,3},{3,1},{4,6},{6,4},{5,7},{7,5},{8,10},{10,8},{9,1... | collective-permute-start | bytes 3932168 | tf_op jit(solution)/shard_map/ppermute | solution.py:437
  216.3 10.3 %collective-permute-start.38 = (bf16[8,80,1024]{2,1,0:T(8,128)(2,1)}, bf16[8,80,1024]{2,1,0:T(8,128)(2,1)}, u32[]{:S(2)}, u32[]{:S(2)}) collective-permute-start(bf16[8,80,1024]{2,1,0:T(8,128)(2,1)} %tie.58.refs_12_.refs_4_), channel_id=1, source_target_pairs={{0,1},{1,0},{2,3},{3,2},{4,5},{5,4},{6,7},{7,6},{8,9},{9,8},{10,11... | collective-permute-start | bytes 3932168 | tf_op jit(solution)/shard_map/ppermute | solution.py:437
  216.3 10.4 %collective-permute-start.37 = (bf16[8,80,1024]{2,1,0:T(8,128)(2,1)}, bf16[8,80,1024]{2,1,0:T(8,128)(2,1)}, u32[]{:S(2)}, u32[]{:S(2)}) collective-permute-start(bf16[8,80,1024]{2,1,0:T(8,128)(2,1)} %tie.57.refs_11_.refs_3_), channel_id=1, source_target_pairs={{0,1},{1,0},{2,3},{3,2},{4,5},{5,4},{6,7},{7,6},{8,9},{9,8},{10,11... | collective-permute-start | bytes 3932168 | tf_op jit(solution)/shard_map/ppermute | solution.py:437
  216.8 9.4 %collective-permute-start.41 = (bf16[512,1024]{1,0:T(8,128)(2,1)}, bf16[512,1024]{1,0:T(8,128)(2,1)}, u32[]{:S(2)}, u32[]{:S(2)}) collective-permute-start(bf16[512,1024]{1,0:T(8,128)(2,1)} %get-tuple-element.90.refs_2_.refs_1_), channel_id=1, source_target_pairs={{0,1},{1,0},{2,3},{3,2},{4,5},{5,4},{6,7},{7,6},{8,9},{9,8},{10,11... | collective-permute-start | bytes 3145736 | tf_op jit(solution)/shard_map/ppermute | solution.py:437
  219.7 16.0 %collective-permute-start.40 = (bf16[512,2048]{1,0:T(8,128)(2,1)S(1)}, bf16[512,2048]{1,0:T(8,128)(2,1)}, u32[]{:S(2)}, u32[]{:S(2)}) collective-permute-start(bf16[512,2048]{1,0:T(8,128)(2,1)S(1)} %copy-done), channel_id=1, source_target_pairs={{0,1},{1,0},{2,3},{3,2},{4,5},{5,4},{6,7},{7,6},{8,9},{9,8},{10,11... | collective-permute-start | bytes 6291464 | tf_op jit(solution)/shard_map/ppermute | solution.py:437
  226.1 9.7 %collective-permute-start.33 = (bf16[8,32,2560]{2,1,0:T(8,128)(2,1)}, bf16[8,32,2560]{2,1,0:T(8,128)(2,1)}, u32[]{:S(2)}, u32[]{:S(2)}) collective-permute-start(bf16[8,32,2560]{2,1,0:T(8,128)(2,1)} %tie.54.refs_8_.refs_12_), channel_id=1, source_target_pairs={{0,1},{1,0},{2,3},{3,2},{4,5},{5,4},{6,7},{7,6},{8,9},{9,8},{10,11... | collective-permute-start | bytes 3932168 | tf_op jit(solution)/shard_map/ppermute | solution.py:437
  226.2 9.5 %collective-permute-start.32 = (bf16[8,32,2560]{2,1,0:T(8,128)(2,1)}, bf16[8,32,2560]{2,1,0:T(8,128)(2,1)}, u32[]{:S(2)}, u32[]{:S(2)}) collective-permute-start(bf16[8,32,2560]{2,1,0:T(8,128)(2,1)} %tie.53.refs_7_.refs_11_), channel_id=1, source_target_pairs={{0,1},{1,0},{2,3},{3,2},{4,5},{5,4},{6,7},{7,6},{8,9},{9,8},{10,11... | collective-permute-start | bytes 3932168 | tf_op jit(solution)/shard_map/ppermute | solution.py:437
  226.6 9.2 %collective-permute-start.30 = (bf16[8,32,2560]{2,1,0:T(8,128)(2,1)}, bf16[8,32,2560]{2,1,0:T(8,128)(2,1)}, u32[]{:S(2)}, u32[]{:S(2)}) collective-permute-start(bf16[8,32,2560]{2,1,0:T(8,128)(2,1)} %tie.52.refs_4_.refs_8_), channel_id=1, source_target_pairs={{0,1},{1,0},{2,3},{3,2},{4,5},{5,4},{6,7},{7,6},{8,9},{9,8},{10,11... | collective-permute-start | bytes 3932168 | tf_op jit(solution)/shard_map/ppermute | solution.py:437
  226.7 9.0 %collective-permute-start.29 = (bf16[8,32,2560]{2,1,0:T(8,128)(2,1)S(1)}, bf16[8,32,2560]{2,1,0:T(8,128)(2,1)}, u32[]{:S(2)}, u32[]{:S(2)}) collective-permute-start(bf16[8,32,2560]{2,1,0:T(8,128)(2,1)S(1)} %copy-done.4), channel_id=1, source_target_pairs={{0,1},{1,0},{2,3},{3,2},{4,5},{5,4},{6,7},{7,6},{8,9},{9,8},{10,11... | collective-permute-start | bytes 3932168 | tf_op jit(solution)/shard_map/ppermute | solution.py:437
  254.9 8.9 %collective-permute-start.44 = (bf16[512,2560]{1,0:T(8,128)(2,1)}, bf16[512,2560]{1,0:T(8,128)(2,1)}, u32[]{:S(2)}, u32[]{:S(2)}) collective-permute-start(bf16[512,2560]{1,0:T(8,128)(2,1)} %get-tuple-element.94.refs_1_), channel_id=1, source_target_pairs={{0,1},{1,0},{2,3},{3,2},{4,5},{5,4},{6,7},{7,6},{8,9},{9,8},{10,11... | collective-permute-start | bytes 7864328 | tf_op jit(solution)/shard_map/ppermute | solution.py:437
  255.1 17.8 %collective-permute-start.43 = (bf16[512,2560]{1,0:T(8,128)(2,1)}, bf16[512,2560]{1,0:T(8,128)(2,1)S(1)}, u32[]{:S(2)}, u32[]{:S(2)}) collective-permute-start(bf16[512,2560]{1,0:T(8,128)(2,1)} %get-tuple-element.97.refs_2_), channel_id=1, source_target_pairs={{0,1},{1,0},{2,3},{3,2},{4,5},{5,4},{6,7},{7,6},{8,9},{9,8},{10,11... | collective-permute-start | bytes 7864328 | tf_op jit(solution)/shard_map/ppermute | solution.py:437
  255.5 17.5 %collective-permute-start.42 = (bf16[512,1024]{1,0:T(8,128)(2,1)S(1)}, bf16[512,1024]{1,0:T(8,128)(2,1)}, u32[]{:S(2)}, u32[]{:S(2)}) collective-permute-start(bf16[512,1024]{1,0:T(8,128)(2,1)S(1)} %copy-done.10), channel_id=1, source_target_pairs={{0,1},{1,0},{2,3},{3,2},{4,5},{5,4},{6,7},{7,6},{8,9},{9,8},{10,11... | collective-permute-start | bytes 3145736 | tf_op jit(solution)/shard_map/ppermute | solution.py:437
  271.3 38.9 %collective-permute-start.46 = (bf16[8,160,512]{2,1,0:T(8,128)(2,1)}, bf16[8,160,512]{2,1,0:T(8,128)(2,1)}, u32[]{:S(2)}, u32[]{:S(2)}) collective-permute-start(bf16[8,160,512]{2,1,0:T(8,128)(2,1)} %get-tuple-element.113), channel_id=1, source_target_pairs={{0,2},{2,0},{1,3},{3,1},{4,6},{6,4},{5,7},{7,5},{8,10},{10,8},{9,1... | collective-permute-start | bytes 3932168 | tf_op jit(solution)/shard_map/ppermute | solution.py:437
  281.6 39.8 %collective-permute-start.47 = (bf16[8,64,1280]{2,1,0:T(8,128)(2,1)}, bf16[8,64,1280]{2,1,0:T(8,128)(2,1)}, u32[]{:S(2)}, u32[]{:S(2)}) collective-permute-start(bf16[8,64,1280]{2,1,0:T(8,128)(2,1)} %get-tuple-element.115), channel_id=1, source_target_pairs={{0,4},{4,0},{8,12},{12,8},{16,20},{20,16},{24,28},{28,24},{1,5},{5... | collective-permute-start | bytes 3932168 | tf_op jit(solution)/shard_map/ppermute | solution.py:437
  305.2 48.1 %collective-permute-start.48 = (bf16[8,64,1280]{2,1,0:T(8,128)(2,1)}, bf16[8,64,1280]{2,1,0:T(8,128)(2,1)}, u32[]{:S(2)}, u32[]{:S(2)}) collective-permute-start(bf16[8,64,1280]{2,1,0:T(8,128)(2,1)} %get-tuple-element.118), channel_id=1, source_target_pairs={{0,2},{2,0},{1,3},{3,1},{4,6},{6,4},{5,7},{7,5},{8,10},{10,8},{9,1... | collective-permute-start | bytes 3932168 | tf_op jit(solution)/shard_map/ppermute | solution.py:437
  312.4 36.9 %collective-permute-start.49 = (bf16[4,160,512]{2,1,0:T(8,128)(2,1)S(1)}, bf16[4,160,512]{2,1,0:T(8,128)(2,1)}, u32[]{:S(2)}, u32[]{:S(2)}) collective-permute-start(bf16[4,160,512]{2,1,0:T(8,128)(2,1)S(1)} %get-tuple-element.170.refs_5_), channel_id=1, source_target_pairs={{0,4},{4,0},{8,12},{12,8},{16,20},{20,16},{24,28},{28,24},{1,5},{5... | collective-permute-start | bytes 1966088 | tf_op jit(solution)/shard_map/ppermute | solution.py:437
  346.3 50.0 %collective-permute-start.53 = (bf16[512,1024]{1,0:T(8,128)(2,1)}, bf16[512,1024]{1,0:T(8,128)(2,1)}, u32[]{:S(2)}, u32[]{:S(2)}) collective-permute-start(bf16[512,1024]{1,0:T(8,128)(2,1)} %get-tuple-element.119.refs_1_), channel_id=1, source_target_pairs={{0,1},{1,0},{2,3},{3,2},{4,5},{5,4},{6,7},{7,6},{8,9},{9,8},{10,11... | collective-permute-start | bytes 3145736 | tf_op jit(solution)/shard_map/ppermute | solution.py:437
  346.6 44.9 %collective-permute-start.56 = (bf16[4,64,1280]{2,1,0:T(8,128)(2,1)S(1)}, bf16[4,64,1280]{2,1,0:T(8,128)(2,1)}, u32[]{:S(2)}, u32[]{:S(2)}) collective-permute-start(bf16[4,64,1280]{2,1,0:T(8,128)(2,1)S(1)} %copy-done.38), channel_id=1, source_target_pairs={{0,2},{2,0},{1,3},{3,1},{4,6},{6,4},{5,7},{7,5},{8,10},{10,8},{9,1... | collective-permute-start | bytes 1966088 | tf_op jit(solution)/shard_map/ppermute | solution.py:437
  348.1 26.3 %collective-permute-start.50 = (bf16[8,128,512]{2,1,0:T(8,128)(2,1)}, bf16[8,128,512]{2,1,0:T(8,128)(2,1)}, u32[]{:S(2)}, u32[]{:S(2)}) collective-permute-start(bf16[8,128,512]{2,1,0:T(8,128)(2,1)} %get-tuple-element.121), channel_id=1, source_target_pairs={{0,4},{4,0},{8,12},{12,8},{16,20},{20,16},{24,28},{28,24},{1,5},{5... | collective-permute-start | bytes 3145736 | tf_op jit(solution)/shard_map/ppermute | solution.py:437
  351.8 17.0 %collective-permute-start.51 = (bf16[2,160,512]{2,1,0:T(8,128)(2,1)S(1)}, bf16[2,160,512]{2,1,0:T(8,128)(2,1)S(1)}, u32[]{:S(2)}, u32[]{:S(2)}) collective-permute-start(bf16[2,160,512]{2,1,0:T(8,128)(2,1)S(1)} %get-tuple-element.182.refs_12_), channel_id=1, source_target_pairs={{0,8},{4,12},{8,0},{12,4},{16,24},{20,28},{24,16},{28,20},{1,9},{5... | collective-permute-start | bytes 983048 | tf_op jit(solution)/shard_map/ppermute | solution.py:437
  356.2 37.6 %collective-permute-start.57 = (bf16[4,64,1280]{2,1,0:T(8,128)(2,1)S(1)}, bf16[4,64,1280]{2,1,0:T(8,128)(2,1)}, u32[]{:S(2)}, u32[]{:S(2)}) collective-permute-start(bf16[4,64,1280]{2,1,0:T(8,128)(2,1)S(1)} %get-tuple-element.168.refs_11_), channel_id=1, source_target_pairs={{0,4},{4,0},{8,12},{12,8},{16,20},{20,16},{24,28},{28,24},{1,5},{5... | collective-permute-start | bytes 1966088 | tf_op jit(solution)/shard_map/ppermute | solution.py:437
  369.5 28.0 %collective-permute-start.54 = (bf16[512,1152]{1,0:T(8,128)(2,1)}, bf16[512,1152]{1,0:T(8,128)(2,1)S(1)}, u32[]{:S(2)}, u32[]{:S(2)}) collective-permute-start(bf16[512,1152]{1,0:T(8,128)(2,1)} %get-tuple-element.126), channel_id=1, source_target_pairs={{0,1},{1,0},{2,3},{3,2},{4,5},{5,4},{6,7},{7,6},{8,9},{9,8},{10,11... | collective-permute-start | bytes 3538952 | tf_op jit(solution)/shard_map/ppermute | solution.py:437
  374.4 31.6 %collective-permute-start.58 = (bf16[1,160,512]{2,1,0:T(8,128)(2,1)}, bf16[1,160,512]{2,1,0:T(8,128)(2,1)}, u32[]{:S(2)}, u32[]{:S(2)}) collective-permute-start(bf16[1,160,512]{2,1,0:T(8,128)(2,1)} %fusion.34.refs_5_), channel_id=1, source_target_pairs={{0,16},{4,20},{8,24},{12,28},{16,0},{20,4},{24,8},{28,12},{1,17},{... | collective-permute-start | bytes 491528 | tf_op jit(solution)/shard_map/ppermute | solution.py:437
  391.5 42.8 %collective-permute-start.60 = (bf16[4,128,512]{2,1,0:T(8,128)(2,1)}, bf16[4,128,512]{2,1,0:T(8,128)(2,1)}, u32[]{:S(2)}, u32[]{:S(2)}) collective-permute-start(bf16[4,128,512]{2,1,0:T(8,128)(2,1)} %get-tuple-element.176.refs_4_), channel_id=1, source_target_pairs={{0,2},{2,0},{1,3},{3,1},{4,6},{6,4},{5,7},{7,5},{8,10},{10,8},{9,1... | collective-permute-start | bytes 1572872 | tf_op jit(solution)/shard_map/ppermute | solution.py:437
  395.7 40.4 %collective-permute-start.61 = (bf16[2,64,2560]{2,1,0:T(8,128)(2,1)S(1)}, bf16[2,64,2560]{2,1,0:T(8,128)(2,1)}, u32[]{:S(2)}, u32[]{:S(2)}) collective-permute-start(bf16[2,64,2560]{2,1,0:T(8,128)(2,1)S(1)} %pad_maximum_fusion.10.refs_6_), channel_id=1, source_target_pairs={{0,8},{4,12},{8,0},{12,4},{16,24},{20,28},{24,16},{28,20},{1,9},{5... | collective-permute-start | bytes 1966088 | tf_op jit(solution)/shard_map/ppermute | solution.py:437
  396.3 19.6 %collective-permute-start.52 = (f32[32,8,128]{2,1,0:T(8,128)}, f32[32,8,128]{2,1,0:T(8,128)S(1)}, u32[]{:S(2)}, u32[]{:S(2)}) collective-permute-start(f32[32,8,128]{2,1,0:T(8,128)} %bitcast.41), channel_id=1, source_target_pairs={{0,4},{4,0},{8,12},{12,8},{16,20},{20,16},{24,28},{28,24},{1,5},{5... | collective-permute-start | bytes 393224 | tf_op jit(solution)/shard_map/ppermute | solution.py:437
  419.1 35.3 %collective-permute-start.62 = (bf16[8,64,1024]{2,1,0:T(8,128)(2,1)}, bf16[8,64,1024]{2,1,0:T(8,128)(2,1)}, u32[]{:S(2)}, u32[]{:S(2)}) collective-permute-start(bf16[8,64,1024]{2,1,0:T(8,128)(2,1)} %get-tuple-element.132), channel_id=1, source_target_pairs={{0,2},{2,0},{1,3},{3,1},{4,6},{6,4},{5,7},{7,5},{8,10},{10,8},{9,1... | collective-permute-start | bytes 3145736 | tf_op jit(solution)/shard_map/ppermute | solution.py:437
  420.5 51.7 %collective-permute-start.64 = (bf16[8,64,1152]{2,1,0:T(8,128)(2,1)}, bf16[8,64,1152]{2,1,0:T(8,128)(2,1)}, u32[]{:S(2)}, u32[]{:S(2)}) collective-permute-start(bf16[8,64,1152]{2,1,0:T(8,128)(2,1)} %get-tuple-element.136), channel_id=1, source_target_pairs={{0,4},{4,0},{8,12},{12,8},{16,20},{20,16},{24,28},{28,24},{1,5},{5... | collective-permute-start | bytes 3538952 | tf_op jit(solution)/shard_map/ppermute | solution.py:437
  424.0 9.5 %collective-permute-start.59 = (f32[32,8,128]{2,1,0:T(8,128)}, f32[32,8,128]{2,1,0:T(8,128)S(1)}, u32[]{:S(2)}, u32[]{:S(2)}) collective-permute-start(f32[32,8,128]{2,1,0:T(8,128)} %tie.67), channel_id=1, source_target_pairs={{0,16},{4,20},{8,24},{12,28},{16,0},{20,4},{24,8},{28,12},{1,17},{... | collective-permute-start | bytes 393224 | tf_op jit(solution)/shard_map/ppermute | solution.py:437
  436.1 16.7 %collective-permute-start.63 = (bf16[2,128,512]{2,1,0:T(8,128)(2,1)S(1)}, bf16[2,128,512]{2,1,0:T(8,128)(2,1)}, u32[]{:S(2)}, u32[]{:S(2)}) collective-permute-start(bf16[2,128,512]{2,1,0:T(8,128)(2,1)S(1)} %get-tuple-element.188.refs_9_), channel_id=1, source_target_pairs={{0,8},{4,12},{8,0},{12,4},{16,24},{20,28},{24,16},{28,20},{1,9},{5... | collective-permute-start | bytes 786440 | tf_op jit(solution)/shard_map/ppermute | solution.py:437
  438.0 31.5 %collective-permute-start.65 = (bf16[1,64,2560]{2,1,0:T(8,128)(2,1)S(1)}, bf16[1,64,2560]{2,1,0:T(8,128)(2,1)S(1)}, u32[]{:S(2)}, u32[]{:S(2)}) collective-permute-start(bf16[1,64,2560]{2,1,0:T(8,128)(2,1)S(1)} %fusion.14.refs_10_), channel_id=1, source_target_pairs={{0,16},{4,20},{8,24},{12,28},{16,0},{20,4},{24,8},{28,12},{1,17},{... | collective-permute-start | bytes 983048 | tf_op jit(solution)/shard_map/ppermute | solution.py:437
  454.3 33.4 %collective-permute-start.66 = (bf16[1,128,512]{2,1,0:T(8,128)(2,1)S(1)}, bf16[1,128,512]{2,1,0:T(8,128)(2,1)}, u32[]{:S(2)}, u32[]{:S(2)}) collective-permute-start(bf16[1,128,512]{2,1,0:T(8,128)(2,1)S(1)} %fusion.38.refs_10_), channel_id=1, source_target_pairs={{0,16},{4,20},{8,24},{12,28},{16,0},{20,4},{24,8},{28,12},{1,17},{... | collective-permute-start | bytes 393224 | tf_op jit(solution)/shard_map/ppermute | solution.py:437
  457.1 50.4 %collective-permute-start.67 = (bf16[4,64,1024]{2,1,0:T(8,128)(2,1)S(1)}, bf16[4,64,1024]{2,1,0:T(8,128)(2,1)}, u32[]{:S(2)}, u32[]{:S(2)}) collective-permute-start(bf16[4,64,1024]{2,1,0:T(8,128)(2,1)S(1)} %get-tuple-element.174.refs_9_), channel_id=1, source_target_pairs={{0,4},{4,0},{8,12},{12,8},{16,20},{20,16},{24,28},{28,24},{1,5},{5... | collective-permute-start | bytes 1572872 | tf_op jit(solution)/shard_map/ppermute | solution.py:437
  471.4 32.0 %collective-permute-start.76 = (bf16[32,2560]{1,0:T(8,128)(2,1)S(1)}, bf16[32,2560]{1,0:T(8,128)(2,1)}, u32[]{:S(2)}, u32[]{:S(2)}) collective-permute-start(bf16[32,2560]{1,0:T(8,128)(2,1)S(1)} %fusion.32), channel_id=1, source_target_pairs={{0,1},{1,0},{2,3},{3,2},{4,5},{5,4},{6,7},{7,6},{8,9},{9,8},{10,11... | collective-permute-start | bytes 491528 | tf_op jit(solution)/shard_map/ppermute | solution.py:437
  474.4 34.9 %collective-permute-start.68 = (bf16[4,64,1152]{2,1,0:T(8,128)(2,1)S(1)}, bf16[4,64,1152]{2,1,0:T(8,128)(2,1)}, u32[]{:S(2)}, u32[]{:S(2)}) collective-permute-start(bf16[4,64,1152]{2,1,0:T(8,128)(2,1)S(1)} %get-tuple-element.172.refs_9_), channel_id=1, source_target_pairs={{0,2},{2,0},{1,3},{3,1},{4,6},{6,4},{5,7},{7,5},{8,10},{10,8},{9,1... | collective-permute-start | bytes 1769480 | tf_op jit(solution)/shard_map/ppermute | solution.py:437
  503.2 32.7 %collective-permute-start.75 = (bf16[64,512]{1,0:T(8,128)(2,1)S(1)}, bf16[64,512]{1,0:T(8,128)(2,1)S(1)}, u32[]{:S(2)}, u32[]{:S(2)}) collective-permute-start(bf16[64,512]{1,0:T(8,128)(2,1)S(1)} %fusion.41), channel_id=1, source_target_pairs={{0,1},{1,0},{2,3},{3,2},{4,5},{5,4},{6,7},{7,6},{8,9},{9,8},{10,11... | collective-permute-start | bytes 196616 | tf_op jit(solution)/shard_map/ppermute | solution.py:437
  511.2 15.1 %collective-permute-start.69 = (bf16[2,64,2176]{2,1,0:T(8,128)(2,1)S(1)}, bf16[2,64,2176]{2,1,0:T(8,128)(2,1)S(1)}, u32[]{:S(2)}, u32[]{:S(2)}) collective-permute-start(bf16[2,64,2176]{2,1,0:T(8,128)(2,1)S(1)} %pad_maximum_fusion.11.refs_12_), channel_id=1, source_target_pairs={{0,8},{4,12},{8,0},{12,4},{16,24},{20,28},{24,16},{28,20},{1,9},{5... | collective-permute-start | bytes 1671176 | tf_op jit(solution)/shard_map/ppermute | solution.py:437
  538.7 11.8 %collective-permute-start.72 = (f32[84,128]{1,0:T(8,128)S(1)}, f32[84,128]{1,0:T(8,128)S(1)}, u32[]{:S(2)}, u32[]{:S(2)}) collective-permute-start(f32[84,128]{1,0:T(8,128)S(1)} %pad_maximum_fusion.38), channel_id=1, source_target_pairs={{0,16},{4,20},{8,24},{12,28},{16,0},{20,4},{24,8},{28,12},{1,17},{... | collective-permute-start | bytes 129032 | tf_op jit(solution)/shard_map/ppermute | solution.py:437
  542.1 13.6 %collective-permute-start.73 = (bf16[1,64,2176]{2,1,0:T(8,128)(2,1)S(1)}, bf16[1,64,2176]{2,1,0:T(8,128)(2,1)S(1)}, u32[]{:S(2)}, u32[]{:S(2)}) collective-permute-start(bf16[1,64,2176]{2,1,0:T(8,128)(2,1)S(1)} %copy-done.57), channel_id=1, source_target_pairs={{0,16},{4,20},{8,24},{12,28},{16,0},{20,4},{24,8},{28,12},{1,17},{... | collective-permute-start | bytes 835592 | tf_op jit(solution)/shard_map/ppermute | solution.py:437
  (102 other events, 774.6 us)

commit v3 on v2

--- a/solution.py
+++ b/solution.py
@@ -1120,21 +1120,23 @@
     )
     middle_v, middle_r = get_v.step((ends,)), get_r.step((ends,))
     first_gate, first_up = get_gate.step(deep_v + (ends,)), get_up.step(deep_r + (ends,))
-    start_state = state_before(ends.reshape(2 * ndim, SUB, LANES), par["hop"], "seq", False)
+    start_state = state_before(
+        tie(ends, *deep_v, *deep_r, *second_down).reshape(2 * ndim, SUB, LANES), par["hop"], "seq", False
+    )
     start_state = tie(start_state, *middle_v, *middle_r, *first_gate, *first_up)
     for _ in range(seq_steps - 1):
         deep_gate, deep_up = get_gate.step((start_state,)), get_up.step((start_state,))
+    get_down.step(deep_gate + deep_up)
     mixed, sent_mix, kept = kernel_call(
         mix_kernel,
         [((rows * SUB, LANES), f32), ((rows, width), bf16), ((rows // SPAN, 2 * ndim * SUB, LANES), f32)],
         [xs, flat(start_state), a_flat, b_flat, g_flat, par["skip"]],
         scratch=[pltpu.VMEM((2 * ndim * SUB, LANES), f32)],
-        name="mix", micros=16,
-    )
-    third_gate, third_up = get_gate.step((mixed,)), get_up.step((mixed,))
-    get_down.step((mixed,))
+        name="mix", micros=16, after=deep_gate + deep_up,
+    )
+    near_last = get_v.step((start_state,)) + get_r.step((start_state,))
+    third_gate, third_up = get_gate.step((mixed,) + near_last), get_up.step((mixed,) + near_last)
     for getter in (get_v, get_r):
-        getter.step((start_state,))
         while getter.order is not None and getter.place < all_bits:
             getter.step()
     weight1 = Weight(Part(get_v, 0, values_width, short), Part(get_r, 0, values_width + z_width, short, 0, values_width))
@@ -1169,12 +1171,6 @@
         scratch=[pltpu.VMEM(w1_shape, bf16), pltpu.VMEM((rows, rows), bf16), dma],
         name="attention", micros=18, after=third_gate + third_up + (norm_other,),
     )
-    for getter in (get_gate, get_up, get_down):
-        while getter.order is not None and getter.place < all_bits - 1:
-            getter.step()
-        getter.step((gated,))
-    weight4 = Weight(Part(get_down, 0, width, w_down.shape[0]))
-    weight3 = Weight(Part(get_gate, 0, hidden_width, short), Part(get_up, 0, hidden_width, short, 0, hidden_width))
     middle, ffn_in, inverse = kernel_call(
         functools.partial(project_kernel, weight2),
         [((rows, width), f32), ((rows, width), bf16), ((rows, 1), f32)],
@@ -1184,6 +1180,13 @@
         name="project", micros=6,
     )
 
+    get_down.step(third_gate + third_up)
+    for getter in (get_gate, get_up, get_down):
+        while getter.order is not None and getter.place < all_bits - 1:
+            getter.step()
+        getter.step((ffn_in,))
+    weight4 = Weight(Part(get_down, 0, width, w_down.shape[0]))
+    weight3 = Weight(Part(get_gate, 0, hidden_width, short), Part(get_up, 0, hidden_width, short, 0, hidden_width))
     grad_low = cotangent[0]
     part = width // 2
     cot_own = lax.dynamic_slice_in_dim(grad_low, core * part, part, axis=1)

time: 574 us -> 542 us (0.944)
  waiting for transfers between devices: 125 us -> 90.8 us
    ppermute x80, waiting for transfers between devices: 125 us -> 90.8 us  [swap(): return lax.ppermute(value, axis, [(i, i ^ bit) for i in range(count)])]
    unnamed x177 -> x185, local copies, waits for them, and re-layouts: 10.4 us -> 13.5 us
  transfers between devices with their start and end apart: 80 -> 80, of which waited for: 28 -> 26; matrix products, arithmetic and copies ran while one was open for 18% -> 18% of each run, Pallas kernels for 38% -> 43%
where the time goes in v3:
time: 542 us; the launch traced here: 535 us
  Pallas kernels  247 us (46%)
  waiting for transfers between devices  90.8 us (17%)
  other arithmetic  85.9 us (16%)
  starting transfers between devices  74.5 us (14%)
  local copies, waits for them, and re-layouts  27.9 us (5%)
  between operations  8.93 us (2%)
    pallas_call x16, Pallas kernels, kernel_call(): pl.pallas_call(run, out_shape=tuple((jax.ShapeDtypeStruct(shape, dtype) f...  180 us
    ppermute x80, waiting for transfers between devices, swap(): return lax.ppermute(value, axis, [(i, i ^ bit) for i in range(count)])  90.8 us
    ppermute x80, starting transfers between devices, swap(): return lax.ppermute(value, axis, [(i, i ^ bit) for i in range(count)])  74.5 us
    pallas_call x7, Pallas kernels, grid_call(): pl.pallas_call(run, out_shape=tuple((jax.ShapeDtypeStruct(shape, dtype) f...  60.7 us
    add x16, other arithmetic, add_low(): return left + right + zero  32.5 us
    concatenate x15, other arithmetic, step(): self.arrays = [jnp.concatenate([mine[0], others[0]], axis=0)]  17.3 us
    unnamed x185, local copies, waits for them, and re-layouts  13.5 us
  transfers between devices with their start and end apart: 80, of which 26 were waited for; matrix products, arithmetic and copies ran while one was open for 18% of the time, Pallas kernels for 43%

profile of v3, /device:TPU:0, one launch (start us, length us, event | category | flops | bytes accessed | tf_op | source)
XLA Modules:
  0.0 535.4 jit_solution(16821924890695072226)
XLA Ops:
  5.2 3.7 collective-permute-start.3
  13.4 4.4 stats.1
  24.9 2.8 collective-permute-done.4
  30.0 3.2 collective-permute-done.5
  33.2 2.4 collective-permute-start.6
  44.7 12.7 %norm.1 = (bf16[512,1024]{1,0:T(8,128)(2,1)}, f32[4096,128]{1,0:T(8,128)}, f32[256,128]{1,0:T(8,128)}) custom-call(bf16[512,1024]{1,0:T(8,128)(2,1)} %bitcast.198, f32[512,1]{1,0:T(8,128)} %copy.86.refs_1_.refs_3_.refs_6_.refs_4_, s32[512,1]{1,0:T(8,128)} %copy.87.refs_2_.refs_3_.refs_10_.refs_7_.refs_5_, ...), custom_call_target="tpu_custom_call" | custom-call | flops 650000000 | bytes 1950000 | tf_op jit(solution)/shard_map/norm/pallas_call | solution.py:75
  61.5 5.1 collective-permute-done.10
  72.8 2.6 collective-permute-start.17
  79.0 4.8 collective-permute-done.16
  86.2 2.5 collective-permute-done.17
  89.4 2.6 collective-permute-done.13
  96.5 2.6 collective-permute-start.20
  99.1 2.0 collective-permute-start.18
  101.1 6.4 %collective-permute-done.19 = bf16[2,32,2560]{2,1,0:T(8,128)(2,1)S(1)} collective-permute-done((bf16[2,32,2560]{2,1,0:T(8,128)(2,1)}, bf16[2,32,2560]{2,1,0:T(8,128)(2,1)S(1)}, u32[]{:S(2)}, u32[]{:S(2)}) %collective-permute-start.19) | collective-permute-done | bytes 327712 | tf_op jit(solution)/shard_map/ppermute | solution.py:437
  109.3 3.3 collective-permute-done.18
  114.0 15.6 %mix.1 = (f32[4096,128]{1,0:T(8,128)}, bf16[512,1024]{1,0:T(8,128)(2,1)}, f32[16,256,128]{2,1,0:T(8,128)}) custom-call(f32[4096,128]{1,0:T(8,128)} %get-tuple-element.88.refs_0_, f32[256,128]{1,0:T(8,128)} %bitcast.218, f32[128,128]{1,0:T(8,128)} %bitcast.212, f32[128,128]{1,0:T(8,128)} %bitcast.205, f32[128,128]{1,0:T(8,128)} %bitcast.225, ...), custom_call_target="tpu_custom_call" | custom-call | flops 800000000 | bytes 2400000 | tf_op jit(solution)/shard_map/mix/pallas_call | solution.py:75
  138.0 2.5 pad_maximum_fusion.4.refs_0_
  140.5 3.8 collective-permute-done.27
  144.2 2.3 pad_maximum_fusion.3.refs_18_.refs_0_.refs_2_
  146.6 6.2 %collective-permute-done.26 = bf16[4,32,2560]{2,1,0:T(8,128)(2,1)S(1)} collective-permute-done((bf16[4,32,2560]{2,1,0:T(8,128)(2,1)}, bf16[4,32,2560]{2,1,0:T(8,128)(2,1)S(1)}, u32[]{:S(2)}, u32[]{:S(2)}) %collective-permute-start.26) | collective-permute-done | bytes 655392 | tf_op jit(solution)/shard_map/ppermute | solution.py:437
  160.7 17.5 %attention.1 = (f32[512,256]{1,0:T(8,128)}, bf16[512,256]{1,0:T(8,128)(2,1)}, bf16[512,256]{1,0:T(8,128)(2,1)}, f32[512,1]{1,0:T(8,128)}, bf16[512,2048]{1,0:T(8...) custom-call(s32[2]{0:T(128)} %pad_add_fusion.refs_0_, ...), custom_call_target="tpu_custom_call" | custom-call | flops 900000000 | bytes 2700000 | tf_op jit(solution)/shard_map/attention/pallas_call | solution.py:75
  178.2 7.9 %project.1 = (f32[512,1024]{1,0:T(8,128)}, bf16[512,1024]{1,0:T(8,128)(2,1)}, f32[512,1]{1,0:T(8,128)}) custom-call(s32[2]{0:T(128)} %pad_add_fusion.refs_0_, bf16[512,2048]{1,0:T(8,128)(2,1)} %get-tuple-element.92.refs_1_, bf16[512,1024]{1,0:T(8,128)(2,1)} %bitcast.199, f32[512,1]{1,0:T(8,128)} %copy.86.refs_1_.refs_3_.refs_6_.refs_4_, ...), custom_call_target="tpu_custom_call" | custom-call | flops 300000000 | bytes 900000 | tf_op jit(solution)/shard_map/project/pallas_call | solution.py:75
  187.2 2.3 dynamic-slice_bitcast_fusion
  190.5 3.4 collective-permute-done.39.refs_15_.refs_4_
  194.9 5.3 collective-permute-done.34.refs_10_.refs_14_
  200.3 3.7 collective-permute-done.31.refs_6_.refs_10_
  205.5 19.1 %hidden.1 = (bf16[512,2560]{1,0:T(8,128)(2,1)}, bf16[512,2560]{1,0:T(8,128)(2,1)}, bf16[512,2560]{1,0:T(8,128)(2,1)}) custom-call(s32[2]{0:T(128)} %pad_add_fusion.refs_0_, bf16[512,1024]{1,0:T(8,128)(2,1)} %get-tuple-element.93.refs_1_, bf16[512,1024]{1,0:T(8,128)(2,1)} %bitcast.202, bf16[8,32,2560]{2,1,0:T(8,128)(2,1)} %tie.55.refs_3_.refs_7_, ...), custom_call_target="tpu_custom_call" | custom-call | flops 750000000 | bytes 2250000 | tf_op jit(solution)/shard_map/hidden/pallas_call | solution.py:102
  225.3 8.2 %out.1.refs_5_ = bf16[512,1024]{1,0:T(8,128)(2,1)} custom-call(s32[2]{0:T(128)} %pad_add_fusion.refs_0_, bf16[512,2560]{1,0:T(8,128)(2,1)} %get-tuple-element.94.refs_1_, f32[512,1024]{1,0:T(8,128)} %get-tuple-element.95.refs_2_.refs_3_, bf16[8,80,1024]{2,1,0:T(8,128)(2,1)} %tie.61.refs_11_.refs_3_, bf16[8,80,1024]{2,1,0:T(8,128)(2,1)} %tie.62.refs_12_.refs_4_, ...), custom_call_target="tpu_custom_call" | custom-call | flops 350000000 | bytes 1050000 | tf_op jit(solution)/shard_map/out/pallas_call | solution.py:75
  233.5 7.5 %grad_down.1 = (bf16[8,160,512]{2,1,0:T(8,128)(2,1)}, bf16[8,160,512]{2,1,0:T(8,128)(2,1)}) custom-call(s32[2]{0:T(128)} %pad_add_fusion.refs_0_, bf16[512,2560]{1,0:T(8,128)(2,1)} %get-tuple-element.94.refs_1_, bf16[512,2560]{1,0:T(8,128)(2,1)} %collective-permute-done.44.refs_2_, bf16[512,512]{1,0:T(8,128)(2,1)} %get-tuple-element.189.refs_3_, ...), custom_call_target="tpu_custom_call" | custom-call | flops 300000000 | bytes 900000 | tf_op jit(solution)/shard_map/grad_down/pallas_call | solution.py:102
  243.5 7.0 %grad_gate.1 = (bf16[8,64,1280]{2,1,0:T(8,128)(2,1)}, bf16[8,64,1280]{2,1,0:T(8,128)(2,1)}) custom-call(s32[2]{0:T(128)} %pad_add_fusion.refs_0_, bf16[512,1024]{1,0:T(8,128)(2,1)} %get-tuple-element.93.refs_1_, bf16[512,1024]{1,0:T(8,128)(2,1)} %collective-permute-done.42.refs_2_, bf16[512,2560]{1,0:T(8,128)(2,1)} %get-tuple-element.96.refs_3_.refs_1_, ...), custom_call_target="tpu_custom_call" | custom-call | flops 300000000 | bytes 900000 | tf_op jit(solution)/shard_map/grad_gate/pallas_call | solution.py:102
  251.9 7.1 %grad_up.1 = (bf16[8,64,1280]{2,1,0:T(8,128)(2,1)}, bf16[8,64,1280]{2,1,0:T(8,128)(2,1)}) custom-call(s32[2]{0:T(128)} %pad_add_fusion.refs_0_, bf16[512,1024]{1,0:T(8,128)(2,1)} %get-tuple-element.93.refs_1_, bf16[512,1024]{1,0:T(8,128)(2,1)} %collective-permute-done.42.refs_2_, bf16[512,2560]{1,0:T(8,128)(2,1)} %get-tuple-element.96.refs_3_.refs_1_, ...), custom_call_target="tpu_custom_call" | custom-call | flops 300000000 | bytes 900000 | tf_op jit(solution)/shard_map/grad_up/pallas_call | solution.py:102
  259.0 14.9 %ffn_back.1 = (f32[512,1024]{1,0:T(8,128)}, bf16[512,512]{1,0:T(8,128)(2,1)}, bf16[512,512]{1,0:T(8,128)(2,1)}, bf16[512,1024]{1,0:T(8,128)(2,1)}, f32[1,1024]{1,0:T(1,128)}) custom-call(s32[2]{0:T(128)} %pad_add_fusion.refs_0_, bf16[512,2560]{1,0:T(8,128)(2,1)} %get-tuple-element.96.refs_3_.refs_1_, bf16[512,2560]{1,0:T(8,128)(2,1)} %get-tuple-element.97.refs_2_, ...), custom_call_target="tpu_custom_call" | custom-call | flops 850000000 | bytes 2550000 | tf_op jit(solution)/shard_map/ffn_back/pallas_call | solution.py:75
  279.7 2.9 fusion.2
  283.5 6.9 %grad_h.1 = (bf16[8,128,512]{2,1,0:T(8,128)(2,1)}, bf16[8,128,512]{2,1,0:T(8,128)(2,1)}) custom-call(s32[2]{0:T(128)} %pad_add_fusion.refs_0_, bf16[512,2048]{1,0:T(8,128)(2,1)} %get-tuple-element.92.refs_1_, bf16[512,2048]{1,0:T(8,128)(2,1)} %collective-permute-done.40.refs_16_.refs_2_, bf16[512,512]{1,0:T(8,128)(2,1)} %get-tuple-element.111.refs_1_.refs_3_, ...), custom_call_target="tpu_custom_call" | custom-call | flops 300000000 | bytes 900000 | tf_op jit(solution)/shard_map/grad_h/pallas_call | solution.py:102
  292.8 21.2 %attention_back.1 = (bf16[512,2048]{1,0:T(8,128)(2,1)}, bf16[512,2304]{1,0:T(8,128)(2,1)}, bf16[512,1024]{1,0:T(8,128)(2,1)}, bf16[512,1024]{1,0:T(8,128)(2,1)},...) custom-call(s32[2]{0:T(128)} %pad_add_fusion.refs_0_, ...), custom_call_target="tpu_custom_call" | custom-call | flops 950000000 | bytes 2850000 | tf_op jit(solution)/shard_map/attention_back/pallas_call | solution.py:75
  316.7 2.0 fusion.20
  320.2 3.2 fusion
  325.0 10.6 %sent_back.1 = (bf16[512,1024]{1,0:T(8,128)(2,1)}, bf16[512,1024]{1,0:T(8,128)(2,1)}) custom-call(s32[2]{0:T(128)} %pad_add_fusion.refs_0_, bf16[512,2048]{1,0:T(8,128)(2,1)} %get-tuple-element.116.refs_1_, bf16[512,2304]{1,0:T(8,128)(2,1)} %get-tuple-element.117.refs_2_, bf16[8,32,3072]{2,1,0:T(8,128)(2,1)} %tie.50.refs_9_.refs_5_.refs_15_.refs_3_, ...), custom_call_target="tpu_custom_call" | custom-call | flops 550000000 | bytes 1650000 | tf_op jit(solution)/shard_map/sent_back/pallas_call | solution.py:75
  336.9 2.2 fusion.34.refs_5_
  339.1 2.9 collective-permute-done.50
  342.0 2.2 collective-permute-start.58
  344.2 2.9 fusion.10
  347.1 12.2 %back_ends.1 = (f32[4096,128]{1,0:T(8,128)}, f32[256,128]{1,0:T(8,128)}) custom-call(bf16[512,1024]{1,0:T(8,128)(2,1)} %get-tuple-element.120.refs_1_.refs_0_, f32[4096,128]{1,0:T(8,128)} %get-tuple-element.91.refs_1_, f32[128,128]{1,0:T(8,128)} %bitcast.213, f32[128,128]{1,0:T(8,128)} %bitcast.206, bf16[4,128,512]{2,1,0:T(8,128)(2,1)} %get-tuple-element.176.refs_4_, ...), custom_call_target="tpu_custom_call" | custom-call | flops 600000000 | bytes 1800000 | tf_op jit(solution)/shard_map/back_ends/pallas_call | solution.py:75
  367.2 6.3 %grad_v.1 = (bf16[8,64,1024]{2,1,0:T(8,128)(2,1)}, bf16[8,64,1024]{2,1,0:T(8,128)(2,1)}) custom-call(s32[2]{0:T(128)} %pad_add_fusion.refs_0_, bf16[512,1024]{1,0:T(8,128)(2,1)} %get-tuple-element.87.refs_1_, bf16[512,1024]{1,0:T(8,128)(2,1)} %collective-permute-done.28.refs_19_.refs_2_, bf16[512,1024]{1,0:T(8,128)(2,1)} %get-tuple-element.125.refs_3_, ...), custom_call_target="tpu_custom_call" | custom-call | flops 300000000 | bytes 900000 | tf_op jit(solution)/shard_map/grad_v/pallas_call | solution.py:102
  374.6 2.4 add_add_fusion.2.refs_7_
  377.0 6.8 %grad_r.1 = (bf16[8,64,1152]{2,1,0:T(8,128)(2,1)}, bf16[8,64,1152]{2,1,0:T(8,128)(2,1)}) custom-call(s32[2]{0:T(128)} %pad_add_fusion.refs_0_, bf16[512,1024]{1,0:T(8,128)(2,1)} %get-tuple-element.90.refs_2_.refs_1_, bf16[512,1024]{1,0:T(8,128)(2,1)} %collective-permute-done.41.refs_17_.refs_2_, bf16[512,1152]{1,0:T(8,128)(2,1)} %get-tuple-element.128.refs_3_, ...), custom_call_target="tpu_custom_call" | custom-call | flops 300000000 | bytes 900000 | tf_op jit(solution)/shard_map/grad_r/pallas_call | solution.py:102
  392.5 2.1 collective-permute-start.59
  395.4 6.6 %collective-permute-done.59 = f32[32,8,128]{2,1,0:T(8,128)S(1)} collective-permute-done((f32[32,8,128]{2,1,0:T(8,128)}, f32[32,8,128]{2,1,0:T(8,128)S(1)}, u32[]{:S(2)}, u32[]{:S(2)}) %collective-permute-start.59) | collective-permute-done | bytes 131104 | tf_op jit(solution)/shard_map/ppermute | solution.py:437
  406.2 2.8 collective-permute-start.65
  409.8 10.5 %back.4 = (f32[1024,128]{1,0:T(8,128)}, f32[256,128]{1,0:T(8,128)}, f32[392,128]{1,0:T(8,128)}) custom-call(f32[4096,128]{1,0:T(8,128)} %get-tuple-element.88.refs_0_, f32[4096,128]{1,0:T(8,128)} %get-tuple-element.122.refs_1_, f32[16,256,128]{2,1,0:T(8,128)} %get-tuple-element.123.refs_2_, f32[256,128]{1,0:T(8,128)} %maximum_bitcast_fusion.2.refs_3_, ...), custom_call_target="tpu_custom_call" | custom-call | flops 500000000 | bytes 1500000 | tf_op jit(solution)/shard_map/back/pallas_call | solution.py:75
  421.7 2.7 fusion.8
  425.6 10.4 %back.5 = (f32[1024,128]{1,0:T(8,128)}, f32[256,128]{1,0:T(8,128)}, f32[392,128]{1,0:T(8,128)}) custom-call(f32[4096,128]{1,0:T(8,128)} %get-tuple-element.88.refs_0_, f32[4096,128]{1,0:T(8,128)} %get-tuple-element.122.refs_1_, f32[16,256,128]{2,1,0:T(8,128)} %get-tuple-element.123.refs_2_, f32[256,128]{1,0:T(8,128)} %get-tuple-element.130.refs_3_, ...), custom_call_target="tpu_custom_call" | custom-call | flops 500000000 | bytes 1500000 | tf_op jit(solution)/shard_map/back/pallas_call | solution.py:75
  440.0 2.1 fusion.6
  443.0 10.7 %back.6 = (f32[1024,128]{1,0:T(8,128)}, f32[256,128]{1,0:T(8,128)}, f32[392,128]{1,0:T(8,128)}) custom-call(f32[4096,128]{1,0:T(8,128)} %get-tuple-element.88.refs_0_, f32[4096,128]{1,0:T(8,128)} %get-tuple-element.122.refs_1_, f32[16,256,128]{2,1,0:T(8,128)} %get-tuple-element.123.refs_2_, f32[256,128]{1,0:T(8,128)} %get-tuple-element.134.refs_3_, ...), custom_call_target="tpu_custom_call" | custom-call | flops 500000000 | bytes 1500000 | tf_op jit(solution)/shard_map/back/pallas_call | solution.py:75
  457.2 10.4 %back.7 = (f32[1024,128]{1,0:T(8,128)}, f32[256,128]{1,0:T(8,128)}, f32[392,128]{1,0:T(8,128)}) custom-call(f32[4096,128]{1,0:T(8,128)} %get-tuple-element.88.refs_0_, f32[4096,128]{1,0:T(8,128)} %get-tuple-element.122.refs_1_, f32[16,256,128]{2,1,0:T(8,128)} %get-tuple-element.123.refs_2_, f32[256,128]{1,0:T(8,128)} %get-tuple-element.138.refs_3_, ...), custom_call_target="tpu_custom_call" | custom-call | flops 500000000 | bytes 1500000 | tf_op jit(solution)/shard_map/back/pallas_call | solution.py:75
  478.5 2.1 collective-permute-start.69
  480.5 7.0 %back_norm.1 = (f32[512,1024]{1,0:T(8,128)}, f32[1,1024]{1,0:T(1,128)}, f32[512,128]{1,0:T(8,128)}, f32[16,128]{1,0:T(8,128)}) custom-call(f32[1024,128]{1,0:T(8,128)} %get-tuple-element.141.refs_1_.refs_0_, f32[1024,128]{1,0:T(8,128)} %get-tuple-element.140.refs_1_, f32[1024,128]{1,0:T(8,128)} %get-tuple-element.137.refs_1_.refs_2_, ...), custom_call_target="tpu_custom_call" | custom-call | flops 300000000 | bytes 900000 | tf_op jit(solution)/shard_map/back_norm/pallas_call | solution.py:75
  489.5 3.9 collective-permute-done.69
  497.4 3.5 collective-permute-done.70
  502.8 2.7 collective-permute-done.71
  505.6 2.4 collective-permute-start.72
  509.3 7.5 %collective-permute-done.72 = f32[84,128]{1,0:T(8,128)S(1)} collective-permute-done((f32[84,128]{1,0:T(8,128)S(1)}, f32[84,128]{1,0:T(8,128)S(1)}, u32[]{:S(2)}, u32[]{:S(2)}) %collective-permute-start.72) | collective-permute-done | bytes 43040 | tf_op jit(solution)/shard_map/ppermute | solution.py:437
  518.5 3.2 collective-permute-done.73
  524.6 5.9 %input.1 = f32[512,1024]{1,0:T(8,128)} custom-call(f32[512,1024]{1,0:T(8,128)} %get-tuple-element.143.refs_0_, f32[512,128]{1,0:T(8,128)} %get-tuple-element.144.refs_1_, f32[1,128]{1,0:T(1,128)} %fusion.53.refs_1_.refs_2_, bf16[512,1024]{1,0:T(8,128)(2,1)} %bitcast.201, f32[512,1]{1,0:T(8,128)} %copy.86.refs_1_.refs_3_.refs_6_.refs_4_, ...), custom_call_target="tpu_custom_call" | custom-call | flops 300000000 | bytes 900000 | tf_op jit(solution)/shard_map/input/pallas_call | solution.py:75
  (510 shorter events, 150.0 us)
Async XLA Ops:
  2.8 8.8 %collective-permute-start = (f32[1,1,56]{2,1,0:T(1,128)S(1)}, f32[1,1,56]{2,1,0:T(1,128)S(1)}, u32[]{:S(2)}, u32[]{:S(2)}) collective-permute-start(f32[1,1,56]{2,1,0:T(1,128)S(1)} %maximum_convert_fusion), channel_id=1, source_target_pairs={{0,1},{1,0},{2,3},{3,2},{4,5},{5,4},{6,7},{7,6},{8,9},{9,8},{10,11... | collective-permute-start | bytes 680 | tf_op jit(solution)/shard_map/ppermute | solution.py:437
  5.2 19.0 %collective-permute-start.3 = (bf16[1,32,3072]{2,1,0:T(8,128)(2,1)S(1)}, bf16[1,32,3072]{2,1,0:T(8,128)(2,1)S(1)}, u32[]{:S(2)}, u32[]{:S(2)}) collective-permute-start(bf16[1,32,3072]{2,1,0:T(8,128)(2,1)S(1)} %maximum_bitcast_fusion.1), channel_id=1, source_target_pairs={{0,16},{4,20},{8,24},{12,28},{16,0},{20,4},{24,8},{28,12},{1,17},{... | collective-permute-start | bytes 589832 | tf_op jit(solution)/shard_map/ppermute | solution.py:437
  9.0 18.8 %collective-permute-start.4 = (bf16[1,32,3328]{2,1,0:T(8,128)(2,1)S(1)}, bf16[1,32,3328]{2,1,0:T(8,128)(2,1)S(1)}, u32[]{:S(2)}, u32[]{:S(2)}) collective-permute-start(bf16[1,32,3328]{2,1,0:T(8,128)(2,1)S(1)} %maximum_bitcast_fusion), channel_id=1, source_target_pairs={{0,16},{4,20},{8,24},{12,28},{16,0},{20,4},{24,8},{28,12},{1,17},{... | collective-permute-start | bytes 638984 | tf_op jit(solution)/shard_map/ppermute | solution.py:437
  20.3 19.2 %collective-permute-start.7 = (bf16[1,80,1024]{2,1,0:T(8,128)(2,1)S(1)}, bf16[1,80,1024]{2,1,0:T(8,128)(2,1)S(1)}, u32[]{:S(2)}, u32[]{:S(2)}) collective-permute-start(bf16[1,80,1024]{2,1,0:T(8,128)(2,1)S(1)} %convert_bitcast_fusion.2), channel_id=1, source_target_pairs={{0,2},{2,0},{1,3},{3,1},{4,6},{6,4},{5,7},{7,5},{8,10},{10,8},{9,1... | collective-permute-start | bytes 491528 | tf_op jit(solution)/shard_map/ppermute | solution.py:437
  33.2 9.1 %collective-permute-start.6 = (f32[288,128]{1,0:T(8,128)S(1)}, f32[288,128]{1,0:T(8,128)S(1)}, u32[]{:S(2)}, u32[]{:S(2)}) collective-permute-start(f32[288,128]{1,0:T(8,128)S(1)} %pad_maximum_fusion.27), channel_id=1, source_target_pairs={{0,16},{4,20},{8,24},{12,28},{16,0},{20,4},{24,8},{28,12},{1,17},{... | collective-permute-start | bytes 442376 | tf_op jit(solution)/shard_map/ppermute | solution.py:437
  40.3 18.7 %collective-permute-start.8 = (bf16[2,32,3072]{2,1,0:T(8,128)(2,1)S(1)}, bf16[2,32,3072]{2,1,0:T(8,128)(2,1)S(1)}, u32[]{:S(2)}, u32[]{:S(2)}) collective-permute-start(bf16[2,32,3072]{2,1,0:T(8,128)(2,1)S(1)} %copy-done.24), channel_id=1, source_target_pairs={{0,8},{4,12},{8,0},{12,4},{16,24},{20,28},{24,16},{28,20},{1,9},{5... | collective-permute-start | bytes 1179656 | tf_op jit(solution)/shard_map/ppermute | solution.py:437
  42.1 18.2 %collective-permute-start.9 = (bf16[2,32,3328]{2,1,0:T(8,128)(2,1)S(1)}, bf16[2,32,3328]{2,1,0:T(8,128)(2,1)S(1)}, u32[]{:S(2)}, u32[]{:S(2)}) collective-permute-start(bf16[2,32,3328]{2,1,0:T(8,128)(2,1)S(1)} %copy-done.39), channel_id=1, source_target_pairs={{0,8},{4,12},{8,0},{12,4},{16,24},{20,28},{24,16},{28,20},{1,9},{5... | collective-permute-start | bytes 1277960 | tf_op jit(solution)/shard_map/ppermute | solution.py:437
  57.3 9.3 %collective-permute-start.10 = (bf16[2,80,1024]{2,1,0:T(8,128)(2,1)}, bf16[2,80,1024]{2,1,0:T(8,128)(2,1)}, u32[]{:S(2)}, u32[]{:S(2)}) collective-permute-start(bf16[2,80,1024]{2,1,0:T(8,128)(2,1)} %tie.41), channel_id=1, source_target_pairs={{0,4},{4,0},{8,12},{12,8},{16,20},{20,16},{24,28},{28,24},{1,5},{5... | collective-permute-start | bytes 983048 | tf_op jit(solution)/shard_map/ppermute | solution.py:437
  70.2 13.6 %collective-permute-start.16 = (bf16[1,32,2560]{2,1,0:T(8,128)(2,1)S(1)}, bf16[1,32,2560]{2,1,0:T(8,128)(2,1)S(1)}, u32[]{:S(2)}, u32[]{:S(2)}) collective-permute-start(bf16[1,32,2560]{2,1,0:T(8,128)(2,1)S(1)} %copy-done.52), channel_id=1, source_target_pairs={{0,16},{4,20},{8,24},{12,28},{16,0},{20,4},{24,8},{28,12},{1,17},{... | collective-permute-start | bytes 491528 | tf_op jit(solution)/shard_map/ppermute | solution.py:437
  70.2 22.5 %collective-permute-start.14 = (bf16[4,32,3072]{2,1,0:T(8,128)(2,1)S(1)}, bf16[4,32,3072]{2,1,0:T(8,128)(2,1)S(1)}, u32[]{:S(2)}, u32[]{:S(2)}) collective-permute-start(bf16[4,32,3072]{2,1,0:T(8,128)(2,1)S(1)} %copy-done.18), channel_id=1, source_target_pairs={{0,4},{4,0},{8,12},{12,8},{16,20},{20,16},{24,28},{28,24},{1,5},{5... | collective-permute-start | bytes 2359304 | tf_op jit(solution)/shard_map/ppermute | solution.py:437
  71.3 22.7 %collective-permute-start.15 = (bf16[4,32,3328]{2,1,0:T(8,128)(2,1)S(1)}, bf16[4,32,3328]{2,1,0:T(8,128)(2,1)S(1)}, u32[]{:S(2)}, u32[]{:S(2)}) collective-permute-start(bf16[4,32,3328]{2,1,0:T(8,128)(2,1)S(1)} %copy-done.17), channel_id=1, source_target_pairs={{0,2},{2,0},{1,3},{3,1},{4,6},{6,4},{5,7},{7,5},{8,10},{10,8},{9,1... | collective-permute-start | bytes 2555912 | tf_op jit(solution)/shard_map/ppermute | solution.py:437
  72.8 15.9 %collective-permute-start.17 = (bf16[1,32,2560]{2,1,0:T(8,128)(2,1)S(1)}, bf16[1,32,2560]{2,1,0:T(8,128)(2,1)S(1)}, u32[]{:S(2)}, u32[]{:S(2)}) collective-permute-start(bf16[1,32,2560]{2,1,0:T(8,128)(2,1)S(1)} %copy-done.53), channel_id=1, source_target_pairs={{0,16},{4,20},{8,24},{12,28},{16,0},{20,4},{24,8},{28,12},{1,17},{... | collective-permute-start | bytes 491528 | tf_op jit(solution)/shard_map/ppermute | solution.py:437
  95.3 36.2 %collective-permute-start.23 = (bf16[8,32,3328]{2,1,0:T(8,128)(2,1)}, bf16[8,32,3328]{2,1,0:T(8,128)(2,1)}, u32[]{:S(2)}, u32[]{:S(2)}) collective-permute-start(bf16[8,32,3328]{2,1,0:T(8,128)(2,1)} %tie.51.refs_13_.refs_9_.refs_19_.refs_7_), channel_id=1, source_target_pairs={{0,4},{4,0},{8,12},{12,8},{16,20},{20,16},{24,28},{28,24},{1,5},{5... | collective-permute-start | bytes 5111816 | tf_op jit(solution)/shard_map/ppermute | solution.py:437
  96.5 33.1 %collective-permute-start.20 = (bf16[8,32,3072]{2,1,0:T(8,128)(2,1)}, bf16[8,32,3072]{2,1,0:T(8,128)(2,1)}, u32[]{:S(2)}, u32[]{:S(2)}) collective-permute-start(bf16[8,32,3072]{2,1,0:T(8,128)(2,1)} %tie.50.refs_9_.refs_5_.refs_15_.refs_3_), channel_id=1, source_target_pairs={{0,2},{2,0},{1,3},{3,1},{4,6},{6,4},{5,7},{7,5},{8,10},{10,8},{9,1... | collective-permute-start | bytes 4718600 | tf_op jit(solution)/shard_map/ppermute | solution.py:437
  99.1 8.4 %collective-permute-start.19 = (bf16[2,32,2560]{2,1,0:T(8,128)(2,1)}, bf16[2,32,2560]{2,1,0:T(8,128)(2,1)S(1)}, u32[]{:S(2)}, u32[]{:S(2)}) collective-permute-start(bf16[2,32,2560]{2,1,0:T(8,128)(2,1)} %tie.49), channel_id=1, source_target_pairs={{0,8},{4,12},{8,0},{12,4},{16,24},{20,28},{24,16},{28,20},{1,9},{5... | collective-permute-start | bytes 983048 | tf_op jit(solution)/shard_map/ppermute | solution.py:437
  99.1 13.6 %collective-permute-start.18 = (bf16[2,32,2560]{2,1,0:T(8,128)(2,1)}, bf16[2,32,2560]{2,1,0:T(8,128)(2,1)S(1)}, u32[]{:S(2)}, u32[]{:S(2)}) collective-permute-start(bf16[2,32,2560]{2,1,0:T(8,128)(2,1)} %tie.48), channel_id=1, source_target_pairs={{0,8},{4,12},{8,0},{12,4},{16,24},{20,28},{24,16},{28,20},{1,9},{5... | collective-permute-start | bytes 983048 | tf_op jit(solution)/shard_map/ppermute | solution.py:437
  113.6 24.4 %collective-permute-start.35 = (bf16[4,80,1024]{2,1,0:T(8,128)(2,1)}, bf16[4,80,1024]{2,1,0:T(8,128)(2,1)}, u32[]{:S(2)}, u32[]{:S(2)}) collective-permute-start(bf16[4,80,1024]{2,1,0:T(8,128)(2,1)} %tie.59), channel_id=1, source_target_pairs={{0,16},{4,20},{8,24},{12,28},{16,0},{20,4},{24,8},{28,12},{1,17},{... | collective-permute-start | bytes 1966088 | tf_op jit(solution)/shard_map/ppermute | solution.py:437
  131.5 12.8 %collective-permute-start.27 = (bf16[4,32,2560]{2,1,0:T(8,128)(2,1)}, bf16[4,32,2560]{2,1,0:T(8,128)(2,1)}, u32[]{:S(2)}, u32[]{:S(2)}) collective-permute-start(bf16[4,32,2560]{2,1,0:T(8,128)(2,1)} %tie.53), channel_id=1, source_target_pairs={{0,2},{2,0},{1,3},{3,1},{4,6},{6,4},{5,7},{7,5},{8,10},{10,8},{9,1... | collective-permute-start | bytes 1966088 | tf_op jit(solution)/shard_map/ppermute | solution.py:437
  134.0 20.0 %collective-permute-start.28 = (bf16[512,1024]{1,0:T(8,128)(2,1)}, bf16[512,1024]{1,0:T(8,128)(2,1)}, u32[]{:S(2)}, u32[]{:S(2)}) collective-permute-start(bf16[512,1024]{1,0:T(8,128)(2,1)} %tie.54), channel_id=1, source_target_pairs={{0,1},{1,0},{2,3},{3,2},{4,5},{5,4},{6,7},{7,6},{8,9},{9,8},{10,11... | collective-permute-start | bytes 3145736 | tf_op jit(solution)/shard_map/ppermute | solution.py:437
  135.4 19.2 %collective-permute-start.21 = (bf16[8,32,3072]{2,1,0:T(8,128)(2,1)S(1)}, bf16[8,32,3072]{2,1,0:T(8,128)(2,1)}, u32[]{:S(2)}, u32[]{:S(2)}) collective-permute-start(bf16[8,32,3072]{2,1,0:T(8,128)(2,1)S(1)} %copy-done.2), channel_id=1, source_target_pairs={{0,1},{1,0},{2,3},{3,2},{4,5},{5,4},{6,7},{7,6},{8,9},{9,8},{10,11... | collective-permute-start | bytes 4718600 | tf_op jit(solution)/shard_map/ppermute | solution.py:437
  135.4 17.4 %collective-permute-start.26 = (bf16[4,32,2560]{2,1,0:T(8,128)(2,1)}, bf16[4,32,2560]{2,1,0:T(8,128)(2,1)S(1)}, u32[]{:S(2)}, u32[]{:S(2)}) collective-permute-start(bf16[4,32,2560]{2,1,0:T(8,128)(2,1)} %tie.52), channel_id=1, source_target_pairs={{0,4},{4,0},{8,12},{12,8},{16,20},{20,16},{24,28},{28,24},{1,5},{5... | collective-permute-start | bytes 1966088 | tf_op jit(solution)/shard_map/ppermute | solution.py:437
  138.0 17.9 %collective-permute-start.24 = (bf16[8,32,3328]{2,1,0:T(8,128)(2,1)S(1)}, bf16[8,32,3328]{2,1,0:T(8,128)(2,1)}, u32[]{:S(2)}, u32[]{:S(2)}) collective-permute-start(bf16[8,32,3328]{2,1,0:T(8,128)(2,1)S(1)} %copy-done.1), channel_id=1, source_target_pairs={{0,1},{1,0},{2,3},{3,2},{4,5},{5,4},{6,7},{7,6},{8,9},{9,8},{10,11... | collective-permute-start | bytes 5111816 | tf_op jit(solution)/shard_map/ppermute | solution.py:437
  144.2 16.4 %collective-permute-start.25 = (bf16[8,32,3328]{2,1,0:T(8,128)(2,1)}, bf16[8,32,3328]{2,1,0:T(8,128)(2,1)}, u32[]{:S(2)}, u32[]{:S(2)}) collective-permute-start(bf16[8,32,3328]{2,1,0:T(8,128)(2,1)} %collective-permute-done.23.refs_3_.refs_14_.refs_10_.refs_20_.refs_8_), channel_id=1, source_target_pairs={{0,1},{1,0},{2,3},{3,2},{4,5},{5,4},{6,7},{7,6},{8,9},{9,8},{10,11... | collective-permute-start | bytes 5111816 | tf_op jit(solution)/shard_map/ppermute | solution.py:437
  152.8 7.9 %collective-permute-start.22 = (bf16[8,32,3072]{2,1,0:T(8,128)(2,1)}, bf16[8,32,3072]{2,1,0:T(8,128)(2,1)}, u32[]{:S(2)}, u32[]{:S(2)}) collective-permute-start(bf16[8,32,3072]{2,1,0:T(8,128)(2,1)} %collective-permute-done.20.refs_2_.refs_10_.refs_6_.refs_16_.refs_4_), channel_id=1, source_target_pairs={{0,1},{1,0},{2,3},{3,2},{4,5},{5,4},{6,7},{7,6},{8,9},{9,8},{10,11... | collective-permute-start | bytes 4718600 | tf_op jit(solution)/shard_map/ppermute | solution.py:437
  153.9 32.1 %collective-permute-start.36 = (bf16[8,80,1024]{2,1,0:T(8,128)(2,1)}, bf16[8,80,1024]{2,1,0:T(8,128)(2,1)}, u32[]{:S(2)}, u32[]{:S(2)}) collective-permute-start(bf16[8,80,1024]{2,1,0:T(8,128)(2,1)} %tie.60.refs_0_), channel_id=1, source_target_pairs={{0,8},{4,12},{8,0},{12,4},{16,24},{20,28},{24,16},{28,20},{1,9},{5... | collective-permute-start | bytes 3932168 | tf_op jit(solution)/shard_map/ppermute | solution.py:437
  154.6 32.2 %collective-permute-start.32 = (bf16[8,32,2560]{2,1,0:T(8,128)(2,1)}, bf16[8,32,2560]{2,1,0:T(8,128)(2,1)S(1)}, u32[]{:S(2)}, u32[]{:S(2)}) collective-permute-start(bf16[8,32,2560]{2,1,0:T(8,128)(2,1)} %pad_maximum_fusion.3.refs_18_.refs_0_.refs_2_), channel_id=1, source_target_pairs={{0,4},{4,0},{8,12},{12,8},{16,20},{20,16},{24,28},{28,24},{1,5},{5... | collective-permute-start | bytes 3932168 | tf_op jit(solution)/shard_map/ppermute | solution.py:437
  155.8 33.6 %collective-permute-start.29 = (bf16[8,32,2560]{2,1,0:T(8,128)(2,1)}, bf16[8,32,2560]{2,1,0:T(8,128)(2,1)S(1)}, u32[]{:S(2)}, u32[]{:S(2)}) collective-permute-start(bf16[8,32,2560]{2,1,0:T(8,128)(2,1)} %pad_maximum_fusion.2.refs_17_.refs_0_.refs_1_), channel_id=1, source_target_pairs={{0,2},{2,0},{1,3},{3,1},{4,6},{6,4},{5,7},{7,5},{8,10},{10,8},{9,1... | collective-permute-start | bytes 3932168 | tf_op jit(solution)/shard_map/ppermute | solution.py:437
  186.1 8.3 %collective-permute-start.38 = (bf16[8,80,1024]{2,1,0:T(8,128)(2,1)}, bf16[8,80,1024]{2,1,0:T(8,128)(2,1)}, u32[]{:S(2)}, u32[]{:S(2)}) collective-permute-start(bf16[8,80,1024]{2,1,0:T(8,128)(2,1)} %tie.62.refs_12_.refs_4_), channel_id=1, source_target_pairs={{0,1},{1,0},{2,3},{3,2},{4,5},{5,4},{6,7},{7,6},{8,9},{9,8},{10,11... | collective-permute-start | bytes 3932168 | tf_op jit(solution)/shard_map/ppermute | solution.py:437
  186.1 8.6 %collective-permute-start.37 = (bf16[8,80,1024]{2,1,0:T(8,128)(2,1)}, bf16[8,80,1024]{2,1,0:T(8,128)(2,1)}, u32[]{:S(2)}, u32[]{:S(2)}) collective-permute-start(bf16[8,80,1024]{2,1,0:T(8,128)(2,1)} %tie.61.refs_11_.refs_3_), channel_id=1, source_target_pairs={{0,1},{1,0},{2,3},{3,2},{4,5},{5,4},{6,7},{7,6},{8,9},{9,8},{10,11... | collective-permute-start | bytes 3932168 | tf_op jit(solution)/shard_map/ppermute | solution.py:437
  186.7 17.3 %collective-permute-start.40 = (bf16[512,2048]{1,0:T(8,128)(2,1)}, bf16[512,2048]{1,0:T(8,128)(2,1)}, u32[]{:S(2)}, u32[]{:S(2)}) collective-permute-start(bf16[512,2048]{1,0:T(8,128)(2,1)} %get-tuple-element.92.refs_1_), channel_id=1, source_target_pairs={{0,1},{1,0},{2,3},{3,2},{4,5},{5,4},{6,7},{7,6},{8,9},{9,8},{10,11... | collective-permute-start | bytes 6291464 | tf_op jit(solution)/shard_map/ppermute | solution.py:437
  194.4 9.6 %collective-permute-start.31 = (bf16[8,32,2560]{2,1,0:T(8,128)(2,1)}, bf16[8,32,2560]{2,1,0:T(8,128)(2,1)S(1)}, u32[]{:S(2)}, u32[]{:S(2)}) collective-permute-start(bf16[8,32,2560]{2,1,0:T(8,128)(2,1)} %tie.56.refs_4_.refs_8_), channel_id=1, source_target_pairs={{0,1},{1,0},{2,3},{3,2},{4,5},{5,4},{6,7},{7,6},{8,9},{9,8},{10,11... | collective-permute-start | bytes 3932168 | tf_op jit(solution)/shard_map/ppermute | solution.py:437
  194.8 9.2 %collective-permute-start.30 = (bf16[8,32,2560]{2,1,0:T(8,128)(2,1)S(1)}, bf16[8,32,2560]{2,1,0:T(8,128)(2,1)S(1)}, u32[]{:S(2)}, u32[]{:S(2)}) collective-permute-start(bf16[8,32,2560]{2,1,0:T(8,128)(2,1)S(1)} %copy-done.4), channel_id=1, source_target_pairs={{0,1},{1,0},{2,3},{3,2},{4,5},{5,4},{6,7},{7,6},{8,9},{9,8},{10,11... | collective-permute-start | bytes 3932168 | tf_op jit(solution)/shard_map/ppermute | solution.py:437
  224.6 8.9 %collective-permute-start.44 = (bf16[512,2560]{1,0:T(8,128)(2,1)}, bf16[512,2560]{1,0:T(8,128)(2,1)}, u32[]{:S(2)}, u32[]{:S(2)}) collective-permute-start(bf16[512,2560]{1,0:T(8,128)(2,1)} %get-tuple-element.94.refs_1_), channel_id=1, source_target_pairs={{0,1},{1,0},{2,3},{3,2},{4,5},{5,4},{6,7},{7,6},{8,9},{9,8},{10,11... | collective-permute-start | bytes 7864328 | tf_op jit(solution)/shard_map/ppermute | solution.py:437
  224.8 17.1 %collective-permute-start.43 = (bf16[512,2560]{1,0:T(8,128)(2,1)}, bf16[512,2560]{1,0:T(8,128)(2,1)S(1)}, u32[]{:S(2)}, u32[]{:S(2)}) collective-permute-start(bf16[512,2560]{1,0:T(8,128)(2,1)} %get-tuple-element.97.refs_2_), channel_id=1, source_target_pairs={{0,1},{1,0},{2,3},{3,2},{4,5},{5,4},{6,7},{7,6},{8,9},{9,8},{10,11... | collective-permute-start | bytes 7864328 | tf_op jit(solution)/shard_map/ppermute | solution.py:437
  225.2 16.7 %collective-permute-start.42 = (bf16[512,1024]{1,0:T(8,128)(2,1)S(1)}, bf16[512,1024]{1,0:T(8,128)(2,1)}, u32[]{:S(2)}, u32[]{:S(2)}) collective-permute-start(bf16[512,1024]{1,0:T(8,128)(2,1)S(1)} %copy-done), channel_id=1, source_target_pairs={{0,1},{1,0},{2,3},{3,2},{4,5},{5,4},{6,7},{7,6},{8,9},{9,8},{10,11... | collective-permute-start | bytes 3145736 | tf_op jit(solution)/shard_map/ppermute | solution.py:437
  241.0 38.7 %collective-permute-start.46 = (bf16[8,160,512]{2,1,0:T(8,128)(2,1)}, bf16[8,160,512]{2,1,0:T(8,128)(2,1)}, u32[]{:S(2)}, u32[]{:S(2)}) collective-permute-start(bf16[8,160,512]{2,1,0:T(8,128)(2,1)} %get-tuple-element.113), channel_id=1, source_target_pairs={{0,2},{2,0},{1,3},{3,1},{4,6},{6,4},{5,7},{7,5},{8,10},{10,8},{9,1... | collective-permute-start | bytes 3932168 | tf_op jit(solution)/shard_map/ppermute | solution.py:437
  250.5 40.4 %collective-permute-start.47 = (bf16[8,64,1280]{2,1,0:T(8,128)(2,1)}, bf16[8,64,1280]{2,1,0:T(8,128)(2,1)S(1)}, u32[]{:S(2)}, u32[]{:S(2)}) collective-permute-start(bf16[8,64,1280]{2,1,0:T(8,128)(2,1)} %get-tuple-element.115), channel_id=1, source_target_pairs={{0,4},{4,0},{8,12},{12,8},{16,20},{20,16},{24,28},{28,24},{1,5},{5... | collective-permute-start | bytes 3932168 | tf_op jit(solution)/shard_map/ppermute | solution.py:437
  273.9 9.4 %collective-permute-start.45 = (bf16[512,512]{1,0:T(8,128)(2,1)}, bf16[512,512]{1,0:T(8,128)(2,1)}, u32[]{:S(2)}, u32[]{:S(2)}) collective-permute-start(bf16[512,512]{1,0:T(8,128)(2,1)} %get-tuple-element.112), channel_id=1, source_target_pairs={{0,1},{1,0},{2,3},{3,2},{4,5},{5,4},{6,7},{7,6},{8,9},{9,8},{10,11... | collective-permute-start | bytes 1572872 | tf_op jit(solution)/shard_map/ppermute | solution.py:437
  274.0 46.2 %collective-permute-start.48 = (bf16[8,64,1280]{2,1,0:T(8,128)(2,1)}, bf16[8,64,1280]{2,1,0:T(8,128)(2,1)}, u32[]{:S(2)}, u32[]{:S(2)}) collective-permute-start(bf16[8,64,1280]{2,1,0:T(8,128)(2,1)} %get-tuple-element.118), channel_id=1, source_target_pairs={{0,2},{2,0},{1,3},{3,1},{4,6},{6,4},{5,7},{7,5},{8,10},{10,8},{9,1... | collective-permute-start | bytes 3932168 | tf_op jit(solution)/shard_map/ppermute | solution.py:437
  282.6 34.1 %collective-permute-start.49 = (bf16[4,160,512]{2,1,0:T(8,128)(2,1)S(1)}, bf16[4,160,512]{2,1,0:T(8,128)(2,1)}, u32[]{:S(2)}, u32[]{:S(2)}) collective-permute-start(bf16[4,160,512]{2,1,0:T(8,128)(2,1)S(1)} %get-tuple-element.170.refs_5_), channel_id=1, source_target_pairs={{0,4},{4,0},{8,12},{12,8},{16,20},{20,16},{24,28},{28,24},{1,5},{5... | collective-permute-start | bytes 1966088 | tf_op jit(solution)/shard_map/ppermute | solution.py:437
  314.6 50.6 %collective-permute-start.53 = (bf16[512,1024]{1,0:T(8,128)(2,1)}, bf16[512,1024]{1,0:T(8,128)(2,1)}, u32[]{:S(2)}, u32[]{:S(2)}) collective-permute-start(bf16[512,1024]{1,0:T(8,128)(2,1)} %get-tuple-element.119.refs_1_), channel_id=1, source_target_pairs={{0,1},{1,0},{2,3},{3,2},{4,5},{5,4},{6,7},{7,6},{8,9},{9,8},{10,11... | collective-permute-start | bytes 3145736 | tf_op jit(solution)/shard_map/ppermute | solution.py:437
  314.8 45.0 %collective-permute-start.56 = (bf16[4,64,1280]{2,1,0:T(8,128)(2,1)S(1)}, bf16[4,64,1280]{2,1,0:T(8,128)(2,1)}, u32[]{:S(2)}, u32[]{:S(2)}) collective-permute-start(bf16[4,64,1280]{2,1,0:T(8,128)(2,1)S(1)} %copy-done.42), channel_id=1, source_target_pairs={{0,2},{2,0},{1,3},{3,1},{4,6},{6,4},{5,7},{7,5},{8,10},{10,8},{9,1... | collective-permute-start | bytes 1966088 | tf_op jit(solution)/shard_map/ppermute | solution.py:437
  315.6 26.3 %collective-permute-start.50 = (bf16[8,128,512]{2,1,0:T(8,128)(2,1)}, bf16[8,128,512]{2,1,0:T(8,128)(2,1)}, u32[]{:S(2)}, u32[]{:S(2)}) collective-permute-start(bf16[8,128,512]{2,1,0:T(8,128)(2,1)} %get-tuple-element.121), channel_id=1, source_target_pairs={{0,4},{4,0},{8,12},{12,8},{16,20},{20,16},{24,28},{28,24},{1,5},{5... | collective-permute-start | bytes 3145736 | tf_op jit(solution)/shard_map/ppermute | solution.py:437
  318.8 17.4 %collective-permute-start.51 = (bf16[2,160,512]{2,1,0:T(8,128)(2,1)S(1)}, bf16[2,160,512]{2,1,0:T(8,128)(2,1)S(1)}, u32[]{:S(2)}, u32[]{:S(2)}) collective-permute-start(bf16[2,160,512]{2,1,0:T(8,128)(2,1)S(1)} %get-tuple-element.182.refs_12_), channel_id=1, source_target_pairs={{0,8},{4,12},{8,0},{12,4},{16,24},{20,28},{24,16},{28,20},{1,9},{5... | collective-permute-start | bytes 983048 | tf_op jit(solution)/shard_map/ppermute | solution.py:437
  323.4 39.6 %collective-permute-start.57 = (bf16[4,64,1280]{2,1,0:T(8,128)(2,1)}, bf16[4,64,1280]{2,1,0:T(8,128)(2,1)}, u32[]{:S(2)}, u32[]{:S(2)}) collective-permute-start(bf16[4,64,1280]{2,1,0:T(8,128)(2,1)} %get-tuple-element.168.refs_11_), channel_id=1, source_target_pairs={{0,4},{4,0},{8,12},{12,8},{16,20},{20,16},{24,28},{28,24},{1,5},{5... | collective-permute-start | bytes 1966088 | tf_op jit(solution)/shard_map/ppermute | solution.py:437
  336.9 29.3 %collective-permute-start.54 = (bf16[512,1152]{1,0:T(8,128)(2,1)}, bf16[512,1152]{1,0:T(8,128)(2,1)S(1)}, u32[]{:S(2)}, u32[]{:S(2)}) collective-permute-start(bf16[512,1152]{1,0:T(8,128)(2,1)} %get-tuple-element.126), channel_id=1, source_target_pairs={{0,1},{1,0},{2,3},{3,2},{4,5},{5,4},{6,7},{7,6},{8,9},{9,8},{10,11... | collective-permute-start | bytes 3538952 | tf_op jit(solution)/shard_map/ppermute | solution.py:437
  342.0 32.6 %collective-permute-start.58 = (bf16[1,160,512]{2,1,0:T(8,128)(2,1)}, bf16[1,160,512]{2,1,0:T(8,128)(2,1)}, u32[]{:S(2)}, u32[]{:S(2)}) collective-permute-start(bf16[1,160,512]{2,1,0:T(8,128)(2,1)} %fusion.34.refs_5_), channel_id=1, source_target_pairs={{0,16},{4,20},{8,24},{12,28},{16,0},{20,4},{24,8},{28,12},{1,17},{... | collective-permute-start | bytes 491528 | tf_op jit(solution)/shard_map/ppermute | solution.py:437
  359.8 42.9 %collective-permute-start.60 = (bf16[4,128,512]{2,1,0:T(8,128)(2,1)}, bf16[4,128,512]{2,1,0:T(8,128)(2,1)}, u32[]{:S(2)}, u32[]{:S(2)}) collective-permute-start(bf16[4,128,512]{2,1,0:T(8,128)(2,1)} %get-tuple-element.176.refs_4_), channel_id=1, source_target_pairs={{0,2},{2,0},{1,3},{3,1},{4,6},{6,4},{5,7},{7,5},{8,10},{10,8},{9,1... | collective-permute-start | bytes 1572872 | tf_op jit(solution)/shard_map/ppermute | solution.py:437
  365.0 39.5 %collective-permute-start.61 = (bf16[2,64,2560]{2,1,0:T(8,128)(2,1)S(1)}, bf16[2,64,2560]{2,1,0:T(8,128)(2,1)}, u32[]{:S(2)}, u32[]{:S(2)}) collective-permute-start(bf16[2,64,2560]{2,1,0:T(8,128)(2,1)S(1)} %pad_maximum_fusion.10.refs_6_), channel_id=1, source_target_pairs={{0,8},{4,12},{8,0},{12,4},{16,24},{20,28},{24,16},{28,20},{1,9},{5... | collective-permute-start | bytes 1966088 | tf_op jit(solution)/shard_map/ppermute | solution.py:437
  365.2 19.2 %collective-permute-start.52 = (f32[32,8,128]{2,1,0:T(8,128)}, f32[32,8,128]{2,1,0:T(8,128)S(1)}, u32[]{:S(2)}, u32[]{:S(2)}) collective-permute-start(f32[32,8,128]{2,1,0:T(8,128)} %bitcast.41), channel_id=1, source_target_pairs={{0,4},{4,0},{8,12},{12,8},{16,20},{20,16},{24,28},{28,24},{1,5},{5... | collective-permute-start | bytes 393224 | tf_op jit(solution)/shard_map/ppermute | solution.py:437
  388.0 33.7 %collective-permute-start.62 = (bf16[8,64,1024]{2,1,0:T(8,128)(2,1)}, bf16[8,64,1024]{2,1,0:T(8,128)(2,1)}, u32[]{:S(2)}, u32[]{:S(2)}) collective-permute-start(bf16[8,64,1024]{2,1,0:T(8,128)(2,1)} %get-tuple-element.132), channel_id=1, source_target_pairs={{0,2},{2,0},{1,3},{3,1},{4,6},{6,4},{5,7},{7,5},{8,10},{10,8},{9,1... | collective-permute-start | bytes 3145736 | tf_op jit(solution)/shard_map/ppermute | solution.py:437
  388.7 51.3 %collective-permute-start.64 = (bf16[8,64,1152]{2,1,0:T(8,128)(2,1)}, bf16[8,64,1152]{2,1,0:T(8,128)(2,1)}, u32[]{:S(2)}, u32[]{:S(2)}) collective-permute-start(bf16[8,64,1152]{2,1,0:T(8,128)(2,1)} %get-tuple-element.136), channel_id=1, source_target_pairs={{0,4},{4,0},{8,12},{12,8},{16,20},{20,16},{24,28},{28,24},{1,5},{5... | collective-permute-start | bytes 3538952 | tf_op jit(solution)/shard_map/ppermute | solution.py:437
  392.5 9.5 %collective-permute-start.59 = (f32[32,8,128]{2,1,0:T(8,128)}, f32[32,8,128]{2,1,0:T(8,128)S(1)}, u32[]{:S(2)}, u32[]{:S(2)}) collective-permute-start(f32[32,8,128]{2,1,0:T(8,128)} %tie.71), channel_id=1, source_target_pairs={{0,16},{4,20},{8,24},{12,28},{16,0},{20,4},{24,8},{28,12},{1,17},{... | collective-permute-start | bytes 393224 | tf_op jit(solution)/shard_map/ppermute | solution.py:437
  404.5 16.3 %collective-permute-start.63 = (bf16[2,128,512]{2,1,0:T(8,128)(2,1)S(1)}, bf16[2,128,512]{2,1,0:T(8,128)(2,1)S(1)}, u32[]{:S(2)}, u32[]{:S(2)}) collective-permute-start(bf16[2,128,512]{2,1,0:T(8,128)(2,1)S(1)} %get-tuple-element.188.refs_9_), channel_id=1, source_target_pairs={{0,8},{4,12},{8,0},{12,4},{16,24},{20,28},{24,16},{28,20},{1,9},{5... | collective-permute-start | bytes 786440 | tf_op jit(solution)/shard_map/ppermute | solution.py:437
  406.2 31.0 %collective-permute-start.65 = (bf16[1,64,2560]{2,1,0:T(8,128)(2,1)S(1)}, bf16[1,64,2560]{2,1,0:T(8,128)(2,1)}, u32[]{:S(2)}, u32[]{:S(2)}) collective-permute-start(bf16[1,64,2560]{2,1,0:T(8,128)(2,1)S(1)} %fusion.14.refs_10_), channel_id=1, source_target_pairs={{0,16},{4,20},{8,24},{12,28},{16,0},{20,4},{24,8},{28,12},{1,17},{... | collective-permute-start | bytes 983048 | tf_op jit(solution)/shard_map/ppermute | solution.py:437
  421.4 33.5 %collective-permute-start.66 = (bf16[1,128,512]{2,1,0:T(8,128)(2,1)S(1)}, bf16[1,128,512]{2,1,0:T(8,128)(2,1)}, u32[]{:S(2)}, u32[]{:S(2)}) collective-permute-start(bf16[1,128,512]{2,1,0:T(8,128)(2,1)S(1)} %fusion.38.refs_10_), channel_id=1, source_target_pairs={{0,16},{4,20},{8,24},{12,28},{16,0},{20,4},{24,8},{28,12},{1,17},{... | collective-permute-start | bytes 393224 | tf_op jit(solution)/shard_map/ppermute | solution.py:437
  424.5 50.6 %collective-permute-start.67 = (bf16[4,64,1024]{2,1,0:T(8,128)(2,1)S(1)}, bf16[4,64,1024]{2,1,0:T(8,128)(2,1)}, u32[]{:S(2)}, u32[]{:S(2)}) collective-permute-start(bf16[4,64,1024]{2,1,0:T(8,128)(2,1)S(1)} %get-tuple-element.174.refs_9_), channel_id=1, source_target_pairs={{0,4},{4,0},{8,12},{12,8},{16,20},{20,16},{24,28},{28,24},{1,5},{5... | collective-permute-start | bytes 1572872 | tf_op jit(solution)/shard_map/ppermute | solution.py:437
  439.1 31.8 %collective-permute-start.76 = (bf16[32,2560]{1,0:T(8,128)(2,1)S(1)}, bf16[32,2560]{1,0:T(8,128)(2,1)}, u32[]{:S(2)}, u32[]{:S(2)}) collective-permute-start(bf16[32,2560]{1,0:T(8,128)(2,1)S(1)} %fusion.32), channel_id=1, source_target_pairs={{0,1},{1,0},{2,3},{3,2},{4,5},{5,4},{6,7},{7,6},{8,9},{9,8},{10,11... | collective-permute-start | bytes 491528 | tf_op jit(solution)/shard_map/ppermute | solution.py:437
  442.2 34.5 %collective-permute-start.68 = (bf16[4,64,1152]{2,1,0:T(8,128)(2,1)S(1)}, bf16[4,64,1152]{2,1,0:T(8,128)(2,1)}, u32[]{:S(2)}, u32[]{:S(2)}) collective-permute-start(bf16[4,64,1152]{2,1,0:T(8,128)(2,1)S(1)} %get-tuple-element.172.refs_9_), channel_id=1, source_target_pairs={{0,2},{2,0},{1,3},{3,1},{4,6},{6,4},{5,7},{7,5},{8,10},{10,8},{9,1... | collective-permute-start | bytes 1769480 | tf_op jit(solution)/shard_map/ppermute | solution.py:437
  470.4 32.4 %collective-permute-start.75 = (bf16[64,512]{1,0:T(8,128)(2,1)S(1)}, bf16[64,512]{1,0:T(8,128)(2,1)S(1)}, u32[]{:S(2)}, u32[]{:S(2)}) collective-permute-start(bf16[64,512]{1,0:T(8,128)(2,1)S(1)} %fusion.41), channel_id=1, source_target_pairs={{0,1},{1,0},{2,3},{3,2},{4,5},{5,4},{6,7},{7,6},{8,9},{9,8},{10,11... | collective-permute-start | bytes 196616 | tf_op jit(solution)/shard_map/ppermute | solution.py:437
  478.5 14.9 %collective-permute-start.69 = (bf16[2,64,2176]{2,1,0:T(8,128)(2,1)S(1)}, bf16[2,64,2176]{2,1,0:T(8,128)(2,1)S(1)}, u32[]{:S(2)}, u32[]{:S(2)}) collective-permute-start(bf16[2,64,2176]{2,1,0:T(8,128)(2,1)S(1)} %pad_maximum_fusion.11.refs_12_), channel_id=1, source_target_pairs={{0,8},{4,12},{8,0},{12,4},{16,24},{20,28},{24,16},{28,20},{1,9},{5... | collective-permute-start | bytes 1671176 | tf_op jit(solution)/shard_map/ppermute | solution.py:437
  505.6 11.3 %collective-permute-start.72 = (f32[84,128]{1,0:T(8,128)S(1)}, f32[84,128]{1,0:T(8,128)S(1)}, u32[]{:S(2)}, u32[]{:S(2)}) collective-permute-start(f32[84,128]{1,0:T(8,128)S(1)} %pad_maximum_fusion.38), channel_id=1, source_target_pairs={{0,16},{4,20},{8,24},{12,28},{16,0},{20,4},{24,8},{28,12},{1,17},{... | collective-permute-start | bytes 129032 | tf_op jit(solution)/shard_map/ppermute | solution.py:437
  508.7 13.0 %collective-permute-start.73 = (bf16[1,64,2176]{2,1,0:T(8,128)(2,1)S(1)}, bf16[1,64,2176]{2,1,0:T(8,128)(2,1)S(1)}, u32[]{:S(2)}, u32[]{:S(2)}) collective-permute-start(bf16[1,64,2176]{2,1,0:T(8,128)(2,1)S(1)} %copy-done.59), channel_id=1, source_target_pairs={{0,16},{4,20},{8,24},{12,28},{16,0},{20,4},{24,8},{28,12},{1,17},{... | collective-permute-start | bytes 835592 | tf_op jit(solution)/shard_map/ppermute | solution.py:437
  524.5 8.4 %collective-permute-start.74 = (bf16[32,2176]{1,0:T(8,128)(2,1)S(1)}, bf16[32,2176]{1,0:T(8,128)(2,1)S(1)}, u32[]{:S(2)}, u32[]{:S(2)}) collective-permute-start(bf16[32,2176]{1,0:T(8,128)(2,1)S(1)} %fusion.36), channel_id=1, source_target_pairs={{0,1},{1,0},{2,3},{3,2},{4,5},{5,4},{6,7},{7,6},{8,9},{9,8},{10,11... | collective-permute-start | bytes 417800 | tf_op jit(solution)/shard_map/ppermute | solution.py:437
  (105 other events, 704.2 us)

commit v4 on v3

--- a/solution.py
+++ b/solution.py
@@ -200,7 +200,7 @@
             return tuple(fresh)
 
         zero = jnp.zeros((SUB, LANES), f32)
-        state = lax.fori_loop(0, rows, step, (zero,) * (2 * half), unroll=8)
+        state = lax.fori_loop(0, rows, step, (zero,) * (2 * half), unroll=32)
         for n in range(half):
             end_ref[pl.ds((start + n) * SUB, SUB), :] = state[2 * n]
             end_ref[pl.ds((ndim + start + n) * SUB, SUB), :] = state[2 * n + 1]
@@ -264,7 +264,7 @@
             state = []
             for n in range(half):
                 state += [state_ref[re_at[n], :], state_ref[im_at[n], :]]
-            state = lax.fori_loop(0, SPAN, step, tuple(state), unroll=8)
+            state = lax.fori_loop(0, SPAN, step, tuple(state), unroll=SPAN)
             for n in range(half):
                 state_ref[re_at[n], :] = state[2 * n]
                 state_ref[im_at[n], :] = state[2 * n + 1]
@@ -332,7 +332,7 @@
             state = []
             for n in range(part):
                 state += [keep_ref[i, re_at[n], :], keep_ref[i, im_at[n], :]]
-            lax.fori_loop(0, SPAN, forward, tuple(state), unroll=8)
+            lax.fori_loop(0, SPAN, forward, tuple(state), unroll=SPAN)
 
             def backward(k, held, start=start, a=a, b=b, g=g):
                 t = SPAN - 1 - k
@@ -364,7 +364,7 @@
             for n in range(part):
                 held += [state_ref[re_at[n], :], state_ref[im_at[n], :]]
                 held += [sums_ref[re_at[n], :], sums_ref[im_at[n], :], sums_ref[last_at[n], :]]
-            held = lax.fori_loop(0, SPAN, backward, tuple(held), unroll=8)
+            held = lax.fori_loop(0, SPAN, backward, tuple(held), unroll=SPAN)
             for n in range(part):
                 state_ref[re_at[n], :] = held[5 * n]
                 state_ref[im_at[n], :] = held[5 * n + 1]
@@ -674,46 +674,57 @@
     return (key <= query) & same & (usable | (key == query))
 
 
-def attention_kernel(weight1, tile, *refs):
+def attention_kernel(weight1, tile, me_ref, norm_ref, mix_ref, segc_ref, segr_ref, validr_ref, qg_ref, qb_ref, kg_ref,
+                     *refs):
     n1 = len(weight1.arrays)
-    me_ref, norm_ref, mix_ref, segc_ref, segr_ref, validr_ref, qg_ref, qb_ref, kg_ref = refs[:9]
-    w1_refs = refs[9 : 9 + n1]
-    shared_ref, q_ref, k_ref, lse_ref, vpre_ref, values_ref, gpre_ref, att_ref, gated_ref, w1, probs_ref, sem1 = refs[9 + n1 :]
-    me = me_ref[0]
-    values_width = values_ref.shape[1]
-    copies1 = weight1.copies(w1_refs, w1, me, sem1)
-    for copy in copies1:
-        copy.start()
-    for copy in copies1:
-        copy.wait()
-    shared = dot(mix_ref[...], w1[:, 2 * values_width :])
-    shared_ref[...] = shared
-    queries = (shared * qg_ref[...] + qb_ref[...]).astype(bf16)
-    keys = (shared * kg_ref[...]).astype(bf16)
-    q_ref[...] = queries
-    k_ref[...] = keys
-    scores = mul_t(queries, keys) * (queries.shape[1] ** -0.5)
-    masked = jnp.where(allowed_pairs(segc_ref, segr_ref, validr_ref), scores, -1e30)
-    top = jnp.max(masked, axis=1, keepdims=True)
-    weights = jnp.exp(masked - top)
-    total = jnp.sum(weights, axis=1, keepdims=True)
-    probs_ref[...] = (weights / total).astype(bf16)
-    lse_ref[...] = top + jnp.log(total)
-
-    def columns(i, _):
-        at = pl.ds(pl.multiple_of(i * tile, tile), tile)
-        value_pre = dot(norm_ref[...], w1[:, at])
-        vpre_ref[:, at] = value_pre.astype(bf16)
-        values = (value_pre * sigmoid(value_pre)).astype(bf16)
-        values_ref[:, at] = values
-        gate_pre = dot(mix_ref[...], w1[:, pl.ds(pl.multiple_of(values_width + i * tile, tile), tile)])
-        gpre_ref[:, at] = gate_pre.astype(bf16)
-        attended = dot(probs_ref[...], values)
-        att_ref[:, at] = attended.astype(bf16)
-        gated_ref[:, at] = (attended * (gate_pre * sigmoid(gate_pre))).astype(bf16)
-        return 0
-
-    lax.fori_loop(0, values_width // tile, columns, 0)
+    shared_ref, q_ref, k_ref, lse_ref, vpre_ref, values_ref, gpre_ref, att_ref, gated_ref, w1, probs_ref, sems = refs[n1:]
+    step, steps = pl.program_id(0), pl.num_programs(0)
+    values_width = tile * weight1.tiles
+    half = values_width // 2
+
+    def copies(n):
+        made = []
+        if n == 0:
+            made += weight1.copies(refs[:n1], w1, me_ref[0], sems.at[0], 1, (values_width, w1.shape[1] - 2 * values_width))
+        for part in range(2):
+            made += weight1.copies(refs[:n1], w1, me_ref[0], sems.at[n], part, (n * half, half))
+        return made
+
+    @pl.when(step == 0)
+    def _():
+        for n in range(2):
+            for copy in copies(n):
+                copy.start()
+        for copy in copies(0):
+            copy.wait()
+        shared = dot(mix_ref[...], w1[:, 2 * values_width :])
+        shared_ref[...] = shared
+        queries = (shared * qg_ref[...] + qb_ref[...]).astype(bf16)
+        keys = (shared * kg_ref[...]).astype(bf16)
+        q_ref[...] = queries
+        k_ref[...] = keys
+        scores = mul_t(queries, keys) * (queries.shape[1] ** -0.5)
+        masked = jnp.where(allowed_pairs(segc_ref, segr_ref, validr_ref), scores, -1e30)
+        top = jnp.max(masked, axis=1, keepdims=True)
+        weights = jnp.exp(masked - top)
+        total = jnp.sum(weights, axis=1, keepdims=True)
+        probs_ref[...] = (weights / total).astype(bf16)
+        lse_ref[...] = top + jnp.log(total)
+
+    @pl.when(step == lax.div(steps, 2))
+    def _():
+        for copy in copies(1):
+            copy.wait()
+
+    value_pre = dot(norm_ref[...], w1[:, pl.ds(pl.multiple_of(step * tile, tile), tile)])
+    vpre_ref[...] = value_pre.astype(bf16)
+    values = (value_pre * sigmoid(value_pre)).astype(bf16)
+    values_ref[...] = values
+    gate_pre = dot(mix_ref[...], w1[:, pl.ds(pl.multiple_of(values_width + step * tile, tile), tile)])
+    gpre_ref[...] = gate_pre.astype(bf16)
+    attended = dot(probs_ref[...], values)
+    att_ref[...] = attended.astype(bf16)
+    gated_ref[...] = (attended * (gate_pre * sigmoid(gate_pre))).astype(bf16)
 
 
 def project_kernel(weight2, *refs):
@@ -845,74 +856,106 @@
     low_oth[...] = low_ref[:, pl.ds(pl.multiple_of((1 - core) * part, part), part)]
 
 
-def attention_back_kernel(weight2, tile, *refs):
+def attention_back_kernel(weight2, tile, me_ref, low_ref, q_ref, k_ref, lse_ref, shared_ref, segc_ref, segr_ref,
+                          validr_ref, qg_ref, kg_ref, vpre_ref, values_ref, gpre_ref, att_ref, *refs):
     n2 = len(weight2.arrays)
-    (me_ref, low_ref, q_ref, k_ref, lse_ref, shared_ref, vpre_ref, values_ref, gpre_ref, att_ref, segc_ref, segr_ref,
-     validr_ref, qg_ref, kg_ref) = refs[:15]
-    (gv_ref, gr_ref, gv_own, gv_oth, gr_own, gr_oth, dgain_ref, w2, low_probs_ref, gprobs_ref, gsh_ref, sem2) = refs[15 + n2 :]
+    (gv_ref, gr_ref, gv_own, gv_oth, gr_own, gr_oth, gsh_ref, dgain_ref, w2, probs_ref, low_probs_ref, gprobs_ref,
+     sems) = refs[n2:]
     core = me_ref[1]
     rows = low_ref.shape[0]
-    values_width = values_ref.shape[1]
-    copies2 = weight2.copies(refs[15 : 15 + n2], w2, me_ref[0], sem2)
-    for copy in copies2:
-        copy.start()
-    queries, keys = q_ref[...], k_ref[...]
-    factor = queries.shape[1] ** -0.5
-    scores = mul_t(queries, keys) * factor
-    masked = jnp.where(allowed_pairs(segc_ref, segr_ref, validr_ref), scores, -1e30)
-    probs = jnp.exp(masked - lse_ref[...])
-    low_probs_ref[...] = probs.astype(bf16)
-    gprobs_ref[...] = jnp.zeros((rows, rows), f32)
-    for copy in copies2:
-        copy.wait()
-
-    def columns(i, _):
-        at = pl.ds(pl.multiple_of(i * tile, tile), tile)
-        grad = mul_t(low_ref[...], w2[at, :]).astype(bf16).astype(f32)
-        gate_pre = gpre_ref[:, at].astype(f32)
-        sigma = sigmoid(gate_pre)
-        act = gate_pre * sigma
-        grad_att = (grad * act).astype(bf16)
-        gr_ref[:, at] = (grad * att_ref[:, at].astype(f32) * (sigma + act * (1.0 - sigma))).astype(bf16)
-        gprobs_ref[...] += mul_t(grad_att, values_ref[:, at])
-        grad_values = t_mul(low_probs_ref[...], grad_att)
-        gv_ref[:, at] = (grad_values * silu_grad(vpre_ref[:, at].astype(f32))).astype(bf16)
-        return 0
-
-    lax.fori_loop(0, values_width // tile, columns, 0)
-    grad_probs = gprobs_ref[...]
-    grad_scores = (probs * (grad_probs - jnp.sum(probs * grad_probs, axis=1, keepdims=True))).astype(bf16)
-    grad_queries = dot(grad_scores, keys) * factor
-    grad_keys = t_mul(grad_scores, queries) * factor
-    shared = shared_ref[...]
-    dgain_ref[0:1, :] = jnp.sum(grad_queries * shared, axis=0, keepdims=True)
-    dgain_ref[1:2, :] = jnp.sum(grad_queries, axis=0, keepdims=True)
-    dgain_ref[2:3, :] = jnp.sum(grad_keys * shared, axis=0, keepdims=True)
-    gsh_ref[...] = (grad_queries * qg_ref[...] + grad_keys * kg_ref[...]).astype(bf16)
-    gr_ref[:, values_width:] = gsh_ref[...]
-    for source, own, other, start in (
-        (gv_ref, gv_own, gv_oth, 0), (gr_ref, gr_own, gr_oth, 0), (gsh_ref, gr_own, gr_oth, values_width // 2)
-    ):
-        part = (values_width if start == 0 else source.shape[1]) // 2
-        own[:, start : start + part] = source[:, pl.ds(pl.multiple_of(core * part, part), part)]
-        other[:, start : start + part] = source[:, pl.ds(pl.multiple_of((1 - core) * part, part), part)]
+    step, steps = pl.program_id(0), pl.num_programs(0)
+    strips = steps // 2
+    values_width = gv_own.shape[1] * 2
+    factor = q_ref.shape[1] ** -0.5
+
+    def copies(n):
+        return weight2.copies(refs[:n2], w2, me_ref[0], sems.at[n], near=weight2.nears[n])
+
+    @pl.when(step == 0)
+    def _():
+        for n in range(len(weight2.nears)):
+            for copy in copies(n):
+                copy.start()
+        scores = mul_t(q_ref[...], k_ref[...]) * factor
+        masked = jnp.where(allowed_pairs(segc_ref, segr_ref, validr_ref), scores, -1e30)
+        probs = jnp.exp(masked - lse_ref[...])
+        probs_ref[...] = probs
+        low_probs_ref[...] = probs.astype(bf16)
+        gprobs_ref[...] = jnp.zeros((rows, rows), f32)
+        for copy in copies(0):
+            copy.wait()
+
+    if len(weight2.nears) > 1:
+
+        @pl.when(step == strips)
+        def _():
+            for copy in copies(1):
+                copy.wait()
+
+    tile_at = tile_order(weight2, step, strips, me_ref)
+    grad = mul_t(low_ref[...], w2[pl.ds(pl.multiple_of(tile_at * tile, tile), tile), :]).astype(bf16).astype(f32)
+    gate_pre = gpre_ref[...].astype(f32)
+    sigma = sigmoid(gate_pre)
+    act = gate_pre * sigma
+    grad_att = (grad * act).astype(bf16)
+    grad_gate = (grad * att_ref[...].astype(f32) * (sigma + act * (1.0 - sigma))).astype(bf16)
+    gr_ref[...] = grad_gate
+    gprobs_ref[...] += mul_t(grad_att, values_ref[...])
+    grad_values = (t_mul(low_probs_ref[...], grad_att) * silu_grad(vpre_ref[...].astype(f32))).astype(bf16)
+    gv_ref[...] = grad_values
+    inside = pl.ds(pl.multiple_of(lax.rem(tile_at, strips) * tile, tile), tile)
+    mine = lax.div(tile_at, strips) == core
+
+    @pl.when(mine)
+    def _():
+        gv_own[:, inside] = grad_values
+        gr_own[:, inside] = grad_gate
+
+    @pl.when(jnp.logical_not(mine))
+    def _():
+        gv_oth[:, inside] = grad_values
+        gr_oth[:, inside] = grad_gate
+
+    @pl.when(step == steps - 1)
+    def _():
+        probs, grad_probs = probs_ref[...], gprobs_ref[...]
+        grad_scores = (probs * (grad_probs - jnp.sum(probs * grad_probs, axis=1, keepdims=True))).astype(bf16)
+        grad_queries = dot(grad_scores, k_ref[...]) * factor
+        grad_keys = t_mul(grad_scores, q_ref[...]) * factor
+        shared = shared_ref[...]
+        dgain_ref[0:1, :] = jnp.sum(grad_queries * shared, axis=0, keepdims=True)
+        dgain_ref[1:2, :] = jnp.sum(grad_queries, axis=0, keepdims=True)
+        dgain_ref[2:3, :] = jnp.sum(grad_keys * shared, axis=0, keepdims=True)
+        gsh_ref[...] = (grad_queries * qg_ref[...] + grad_keys * kg_ref[...]).astype(bf16)
+        part = gsh_ref.shape[1] // 2
+        start = values_width // 2
+        gr_own[:, start:] = gsh_ref[:, pl.ds(pl.multiple_of(core * part, part), part)]
+        gr_oth[:, start:] = gsh_ref[:, pl.ds(pl.multiple_of((1 - core) * part, part), part)]
+
+
+def tile_order(weight, step, strips, me):
+    if len(weight.nears) == 1:
+        return step
+    return (lax.shift_right_logical(me[0], weight.top) ^ lax.div(step, strips)) * strips + lax.rem(step, strips)
 
 
 def sent_back_kernel(weight1, *refs):
     n1 = len(weight1.arrays)
-    me_ref, gv_ref, gr_ref = refs[:3]
-    gmix_ref, gnorm_ref, w1, sems = refs[3 + n1 :]
+    me_ref, gv_ref, gr_ref, gsh_ref = refs[:4]
+    gmix_ref, gnorm_ref, w1, sems = refs[4 + n1 :]
     me, width, values_width = me_ref[0], gmix_ref.shape[1], gv_ref.shape[1]
     parts, edge = (2, width // 2) if weight1.split else (1, width)
     for part in range(parts):
-        for copy in weight1.copies(refs[3 : 3 + n1], w1, me, sems.at[part], near=weight1.nears[part]):
+        for copy in weight1.copies(refs[4 : 4 + n1], w1, me, sems.at[part], near=weight1.nears[part]):
             copy.start()
     for part in range(parts):
-        for copy in weight1.copies(refs[3 : 3 + n1], w1, me, sems.at[part], near=weight1.nears[part]):
+        for copy in weight1.copies(refs[4 : 4 + n1], w1, me, sems.at[part], near=weight1.nears[part]):
             copy.wait()
         base = pl.multiple_of((lax.shift_right_logical(me, weight1.top) ^ part) * edge, edge) if parts == 2 else 0
         at = pl.ds(base, edge)
-        gmix_ref[:, at] = mul_t(gr_ref[...], w1[at, values_width:]).astype(bf16)
+        gmix_ref[:, at] = (
+            mul_t(gr_ref[...], w1[at, values_width : 2 * values_width]) + mul_t(gsh_ref[...], w1[at, 2 * values_width :])
+        ).astype(bf16)
         gnorm_ref[:, at] = mul_t(gv_ref[...], w1[at, :values_width]).astype(bf16)
 
 
@@ -1162,14 +1205,25 @@
     def any_of(*groups):
         return [ANY] * sum(len(group.arrays) for group in groups)
 
-    shared, queries, keys, log_total, value_pre, values, gate_pre, attended, gated = kernel_call(
+    tile = 512
+    weight1.tiles = values_width // tile
+    strip = ((rows, values_width), bf16, (rows, tile), lambda g, me: (0, g))
+
+    def still(shape, dtype):
+        return (shape, dtype, shape, lambda g, me: (0, 0))
+
+    def loose(*groups):
+        return [(array, None, None) for group in groups for array in group.arrays]
+
+    shared, queries, keys, log_total, value_pre, values, gate_pre, attended, gated = grid_call(
         functools.partial(attention_kernel, weight1, tile),
-        [((rows, z_width), f32), ((rows, z_width), bf16), ((rows, z_width), bf16), ((rows, 1), f32), wide, wide, wide,
-         wide, wide],
-        [me, sent_norm, sent_mix, seg_col, seg_row, valid_row, full_qg, full_qb, full_kg, *weight1.arrays],
-        [SM] + [VM] * 8 + any_of(weight1),
-        scratch=[pltpu.VMEM(w1_shape, bf16), pltpu.VMEM((rows, rows), bf16), dma],
-        name="attention", micros=18, after=third_gate + third_up + (norm_other,),
+        [still((rows, z_width), f32), still((rows, z_width), bf16), still((rows, z_width), bf16), still((rows, 1), f32)]
+        + [strip] * 5,
+        [whole(array) for array in (sent_norm, sent_mix, seg_col, seg_row, valid_row, full_qg, full_qb, full_kg)]
+        + loose(weight1),
+        weight1.tiles, me,
+        scratch=[pltpu.VMEM(w1_shape, bf16), pltpu.VMEM((rows, rows), bf16), pltpu.SemaphoreType.DMA((2,))],
+        name="attention", micros=15, after=third_gate + third_up + (norm_other,),
     )
     middle, ffn_in, inverse = kernel_call(
         functools.partial(project_kernel, weight2),
@@ -1229,24 +1283,31 @@
     heads = weight_grad(
         (gated, gated_other), (low_own, other_core(low_oth)), reduce_b, me, chips, "grad_h", after=down.step(low_own)
     )
-    half_values = ((rows, values_width // 2), bf16)
-    half_mixed = ((rows, (values_width + z_width) // 2), bf16)
-    grad_v, grad_r, gv_own, gv_oth, gr_own, gr_oth, dgains = kernel_call(
+    half_values = still((rows, values_width // 2), bf16)
+    half_mixed = still((rows, (values_width + z_width) // 2), bf16)
+    strips = values_width // tile // 2
+
+    def turn(g, me):
+        return (0, tile_order(weight2, g, strips, me))
+
+    strip = ((rows, values_width), bf16, (rows, tile), turn)
+    grad_v, grad_r, gv_own, gv_oth, gr_own, gr_oth, grad_z, dgains = grid_call(
         functools.partial(attention_back_kernel, weight2, tile),
-        [((rows, values_width), bf16), ((rows, values_width + z_width), bf16)] + [half_values] * 2 + [half_mixed] * 2
-        + [((3, z_width), f32)],
-        [me, middle_low, queries, keys, log_total, shared, value_pre, values, gate_pre, attended, seg_col, seg_row,
-         valid_row, full_qg, full_kg, *weight2.arrays],
-        [SM] + [VM] * 14 + any_of(weight2),
-        scratch=[pltpu.VMEM(w2_shape, bf16), pltpu.VMEM((rows, rows), bf16), pltpu.VMEM((rows, rows), f32),
-                 pltpu.VMEM((rows, z_width), bf16), dma],
+        [strip, strip] + [half_values] * 2 + [half_mixed] * 2
+        + [still((rows, z_width), bf16), still((3, z_width), f32)],
+        [whole(array) for array in (middle_low, queries, keys, log_total, shared, seg_col, seg_row, valid_row, full_qg,
+                                    full_kg)]
+        + [columns_of(array, tile, turn) for array in (value_pre, values, gate_pre, attended)] + loose(weight2),
+        2 * strips, me,
+        scratch=[pltpu.VMEM(w2_shape, bf16), pltpu.VMEM((rows, rows), f32), pltpu.VMEM((rows, rows), bf16),
+                 pltpu.VMEM((rows, rows), f32), pltpu.SemaphoreType.DMA((2,))],
         name="attention_back", micros=19, after=(heads.sent,) + gate.step(heads.sent),
     )
     grad_mix_rows, grad_norm_rows = kernel_call(
         functools.partial(sent_back_kernel, weight1),
         [((rows, width), bf16)] * 2,
-        [me, grad_v, grad_r, *weight1.arrays],
-        [SM, VM, VM] + any_of(weight1),
+        [me, grad_v, grad_r, grad_z, *weight1.arrays],
+        [SM, VM, VM, VM] + any_of(weight1),
         scratch=[pltpu.VMEM(w1_shape, bf16), pltpu.SemaphoreType.DMA((2,))],
         name="sent_back", micros=11, after=up.step(gv_oth) + down.step(gv_oth),
     )

time: 542 us -> 532 us (0.982)
  Pallas kernels: 247 us -> 234 us
  waiting for transfers between devices: 90.8 us -> 99.8 us
    pallas_call x16 -> x14, Pallas kernels: 180 us -> 137 us  [kernel_call(): pl.pallas_call(run, out_shape=tuple((jax.ShapeDtypeStruct(shape, dtype) f...]
    pallas_call x7 -> x9, Pallas kernels: 60.7 us -> 90.5 us  [grid_call(): pl.pallas_call(run, out_shape=tuple((jax.ShapeDtypeStruct(shape, dtype) f...]
    ppermute x80, waiting for transfers between devices: 90.8 us -> 99.8 us  [swap(): return lax.ppermute(value, axis, [(i, i ^ bit) for i in range(count)])]
  transfers between devices with their start and end apart: 80 -> 80, of which waited for: 26 -> 29; matrix products, arithmetic and copies ran while one was open for 18% -> 18% of each run, Pallas kernels for 43% -> 41%
where the time goes in v4:
time: 532 us; the launch traced here: 526 us
  Pallas kernels  234 us (44%)
  waiting for transfers between devices  99.8 us (19%)
  other arithmetic  85.7 us (16%)
  starting transfers between devices  69.4 us (13%)
  local copies, waits for them, and re-layouts  28 us (5%)
  between operations  9.13 us (2%)
    pallas_call x14, Pallas kernels, kernel_call(): pl.pallas_call(run, out_shape=tuple((jax.ShapeDtypeStruct(shape, dtype) f...  137 us
    ppermute x80, waiting for transfers between devices, swap(): return lax.ppermute(value, axis, [(i, i ^ bit) for i in range(count)])  99.8 us
    pallas_call x9, Pallas kernels, grid_call(): pl.pallas_call(run, out_shape=tuple((jax.ShapeDtypeStruct(shape, dtype) f...  90.5 us
    ppermute x80, starting transfers between devices, swap(): return lax.ppermute(value, axis, [(i, i ^ bit) for i in range(count)])  69.4 us
    add x16, other arithmetic, add_low(): return left + right + zero  32.3 us
    concatenate x15, other arithmetic, step(): self.arrays = [jnp.concatenate([mine[0], others[0]], axis=0)]  17.3 us
    unnamed x185, local copies, waits for them, and re-layouts  13.7 us
  transfers between devices with their start and end apart: 80, of which 29 were waited for; matrix products, arithmetic and copies ran while one was open for 18% of the time, Pallas kernels for 41%

profile of v4, /device:TPU:0, one launch (start us, length us, event | category | flops | bytes accessed | tf_op | source)
XLA Modules:
  0.0 525.7 jit_solution(12877000586982185892)
XLA Ops:
  5.2 3.7 collective-permute-start.3
  13.4 4.4 stats.1
  25.0 2.8 collective-permute-done.4
  30.0 3.2 collective-permute-done.5
  33.2 2.4 collective-permute-start.6
  44.7 12.1 %norm.1 = (bf16[512,1024]{1,0:T(8,128)(2,1)}, f32[4096,128]{1,0:T(8,128)}, f32[256,128]{1,0:T(8,128)}) custom-call(bf16[512,1024]{1,0:T(8,128)(2,1)} %bitcast.198, f32[512,1]{1,0:T(8,128)} %copy.86.refs_1_.refs_3_.refs_6_.refs_4_, s32[512,1]{1,0:T(8,128)} %copy.87.refs_2_.refs_3_.refs_6_.refs_7_.refs_5_, ...), custom_call_target="tpu_custom_call" | custom-call | flops 650000000 | bytes 1950000 | tf_op jit(solution)/shard_map/norm/pallas_call | solution.py:75
  61.2 4.9 collective-permute-done.10
  72.2 2.6 collective-permute-start.17
  78.3 4.8 collective-permute-done.16
  85.5 2.5 collective-permute-done.17
  88.8 2.6 collective-permute-done.13
  96.3 2.1 collective-permute-start.20
  98.4 2.0 collective-permute-start.18
  100.5 6.4 %collective-permute-done.19 = bf16[2,32,2560]{2,1,0:T(8,128)(2,1)S(1)} collective-permute-done((bf16[2,32,2560]{2,1,0:T(8,128)(2,1)}, bf16[2,32,2560]{2,1,0:T(8,128)(2,1)S(1)}, u32[]{:S(2)}, u32[]{:S(2)}) %collective-permute-start.19) | collective-permute-done | bytes 327712 | tf_op jit(solution)/shard_map/ppermute | solution.py:437
  108.7 3.2 collective-permute-done.18
  113.4 14.7 %mix.1 = (f32[4096,128]{1,0:T(8,128)}, bf16[512,1024]{1,0:T(8,128)(2,1)}, f32[16,256,128]{2,1,0:T(8,128)}) custom-call(f32[4096,128]{1,0:T(8,128)} %get-tuple-element.89.refs_0_, f32[256,128]{1,0:T(8,128)} %bitcast.218, f32[128,128]{1,0:T(8,128)} %bitcast.212, f32[128,128]{1,0:T(8,128)} %bitcast.205, f32[128,128]{1,0:T(8,128)} %bitcast.225, ...), custom_call_target="tpu_custom_call" | custom-call | flops 800000000 | bytes 2400000 | tf_op jit(solution)/shard_map/mix/pallas_call | solution.py:75
  137.4 2.5 pad_maximum_fusion.4.refs_0_
  139.9 3.7 collective-permute-done.27
  143.6 2.3 pad_maximum_fusion.3.refs_18_.refs_0_.refs_2_
  146.0 6.2 %collective-permute-done.26 = bf16[4,32,2560]{2,1,0:T(8,128)(2,1)S(1)} collective-permute-done((bf16[4,32,2560]{2,1,0:T(8,128)(2,1)}, bf16[4,32,2560]{2,1,0:T(8,128)(2,1)S(1)}, u32[]{:S(2)}, u32[]{:S(2)}) %collective-permute-start.26) | collective-permute-done | bytes 655392 | tf_op jit(solution)/shard_map/ppermute | solution.py:437
  160.1 13.3 %attention.1 = (f32[512,256]{1,0:T(8,128)}, bf16[512,256]{1,0:T(8,128)(2,1)}, bf16[512,256]{1,0:T(8,128)(2,1)}, f32[512,1]{1,0:T(8,128)}, bf16[512,2048]{1,0:T(8...) custom-call(s32[2]{0:T(128)} %pad_add_fusion.refs_0_, ...), custom_call_target="tpu_custom_call" | custom-call | flops 750000000 | bytes 2250000 | tf_op jit(solution)/shard_map/attention/pallas_call | solution.py:102
  173.4 7.9 %project.1 = (f32[512,1024]{1,0:T(8,128)}, bf16[512,1024]{1,0:T(8,128)(2,1)}, f32[512,1]{1,0:T(8,128)}) custom-call(s32[2]{0:T(128)} %pad_add_fusion.refs_0_, bf16[512,2048]{1,0:T(8,128)(2,1)} %get-tuple-element.93.refs_1_, bf16[512,1024]{1,0:T(8,128)(2,1)} %bitcast.199, f32[512,1]{1,0:T(8,128)} %copy.86.refs_1_.refs_3_.refs_6_.refs_4_, ...), custom_call_target="tpu_custom_call" | custom-call | flops 300000000 | bytes 900000 | tf_op jit(solution)/shard_map/project/pallas_call | solution.py:75
  181.3 3.5 collective-permute-done.36.refs_0_
  185.9 2.2 dynamic-slice_bitcast_fusion
  189.2 3.4 collective-permute-done.39.refs_15_.refs_4_
  193.6 5.3 %collective-permute-done.34.refs_10_.refs_14_ = bf16[8,32,2560]{2,1,0:T(8,128)(2,1)S(1)} collective-permute-done((bf16[8,32,2560]{2,1,0:T(8,128)(2,1)}, bf16[8,32,2560]{2,1,0:T(8,128)(2,1)S(1)}, u32[]{:S(2)}, u32[]{:S(2)}) %collective-permute-start.34) | collective-permute-done | bytes 1310752 | tf_op jit(solution)/shard_map/ppermute | solution.py:437
  199.0 3.7 collective-permute-done.31.refs_6_.refs_10_
  204.2 19.0 %hidden.1 = (bf16[512,2560]{1,0:T(8,128)(2,1)}, bf16[512,2560]{1,0:T(8,128)(2,1)}, bf16[512,2560]{1,0:T(8,128)(2,1)}) custom-call(s32[2]{0:T(128)} %pad_add_fusion.refs_0_, bf16[512,1024]{1,0:T(8,128)(2,1)} %get-tuple-element.94.refs_1_, bf16[512,1024]{1,0:T(8,128)(2,1)} %bitcast.202, bf16[8,32,2560]{2,1,0:T(8,128)(2,1)} %tie.55.refs_3_.refs_7_, ...), custom_call_target="tpu_custom_call" | custom-call | flops 750000000 | bytes 2250000 | tf_op jit(solution)/shard_map/hidden/pallas_call | solution.py:102
  223.9 8.2 %out.1.refs_5_ = bf16[512,1024]{1,0:T(8,128)(2,1)} custom-call(s32[2]{0:T(128)} %pad_add_fusion.refs_0_, bf16[512,2560]{1,0:T(8,128)(2,1)} %get-tuple-element.95.refs_1_, f32[512,1024]{1,0:T(8,128)} %get-tuple-element.96.refs_2_.refs_3_, bf16[8,80,1024]{2,1,0:T(8,128)(2,1)} %tie.61.refs_11_.refs_3_, bf16[8,80,1024]{2,1,0:T(8,128)(2,1)} %tie.62.refs_12_.refs_4_, ...), custom_call_target="tpu_custom_call" | custom-call | flops 350000000 | bytes 1050000 | tf_op jit(solution)/shard_map/out/pallas_call | solution.py:75
  232.1 7.5 %grad_down.1 = (bf16[8,160,512]{2,1,0:T(8,128)(2,1)}, bf16[8,160,512]{2,1,0:T(8,128)(2,1)}) custom-call(s32[2]{0:T(128)} %pad_add_fusion.refs_0_, bf16[512,2560]{1,0:T(8,128)(2,1)} %get-tuple-element.95.refs_1_, bf16[512,2560]{1,0:T(8,128)(2,1)} %collective-permute-done.44.refs_2_, bf16[512,512]{1,0:T(8,128)(2,1)} %get-tuple-element.191.refs_3_, ...), custom_call_target="tpu_custom_call" | custom-call | flops 300000000 | bytes 900000 | tf_op jit(solution)/shard_map/grad_down/pallas_call | solution.py:102
  242.5 7.0 %grad_gate.1 = (bf16[8,64,1280]{2,1,0:T(8,128)(2,1)}, bf16[8,64,1280]{2,1,0:T(8,128)(2,1)}) custom-call(s32[2]{0:T(128)} %pad_add_fusion.refs_0_, bf16[512,1024]{1,0:T(8,128)(2,1)} %get-tuple-element.94.refs_1_, bf16[512,1024]{1,0:T(8,128)(2,1)} %collective-permute-done.42.refs_2_, bf16[512,2560]{1,0:T(8,128)(2,1)} %get-tuple-element.97.refs_3_.refs_1_, ...), custom_call_target="tpu_custom_call" | custom-call | flops 300000000 | bytes 900000 | tf_op jit(solution)/shard_map/grad_gate/pallas_call | solution.py:102
  250.6 7.2 %grad_up.1 = (bf16[8,64,1280]{2,1,0:T(8,128)(2,1)}, bf16[8,64,1280]{2,1,0:T(8,128)(2,1)}) custom-call(s32[2]{0:T(128)} %pad_add_fusion.refs_0_, bf16[512,1024]{1,0:T(8,128)(2,1)} %get-tuple-element.94.refs_1_, bf16[512,1024]{1,0:T(8,128)(2,1)} %collective-permute-done.42.refs_2_, bf16[512,2560]{1,0:T(8,128)(2,1)} %get-tuple-element.97.refs_3_.refs_1_, ...), custom_call_target="tpu_custom_call" | custom-call | flops 300000000 | bytes 900000 | tf_op jit(solution)/shard_map/grad_up/pallas_call | solution.py:102
  257.8 14.9 %ffn_back.1 = (f32[512,1024]{1,0:T(8,128)}, bf16[512,512]{1,0:T(8,128)(2,1)}, bf16[512,512]{1,0:T(8,128)(2,1)}, bf16[512,1024]{1,0:T(8,128)(2,1)}, f32[1,1024]{1,0:T(1,128)}) custom-call(s32[2]{0:T(128)} %pad_add_fusion.refs_0_, bf16[512,2560]{1,0:T(8,128)(2,1)} %get-tuple-element.97.refs_3_.refs_1_, bf16[512,2560]{1,0:T(8,128)(2,1)} %get-tuple-element.98.refs_2_, ...), custom_call_target="tpu_custom_call" | custom-call | flops 850000000 | bytes 2550000 | tf_op jit(solution)/shard_map/ffn_back/pallas_call | solution.py:75
  278.0 2.9 fusion.2
  281.9 6.9 %grad_h.1 = (bf16[8,128,512]{2,1,0:T(8,128)(2,1)}, bf16[8,128,512]{2,1,0:T(8,128)(2,1)}) custom-call(s32[2]{0:T(128)} %pad_add_fusion.refs_0_, bf16[512,2048]{1,0:T(8,128)(2,1)} %get-tuple-element.93.refs_1_, bf16[512,2048]{1,0:T(8,128)(2,1)} %collective-permute-done.40.refs_16_.refs_2_, bf16[512,512]{1,0:T(8,128)(2,1)} %get-tuple-element.112.refs_1_.refs_3_, ...), custom_call_target="tpu_custom_call" | custom-call | flops 300000000 | bytes 900000 | tf_op jit(solution)/shard_map/grad_h/pallas_call | solution.py:102
  291.3 16.6 %attention_back.1 = (bf16[512,2048]{1,0:T(8,128)(2,1)}, bf16[512,2048]{1,0:T(8,128)(2,1)}, bf16[512,1024]{1,0:T(8,128)(2,1)}, bf16[512,1024]{1,0:T(8,128)(2,1)},...) custom-call(s32[2]{0:T(128)} %pad_add_fusion.refs_0_, ...), custom_call_target="tpu_custom_call" | custom-call | flops 950000000 | bytes 2850000 | tf_op jit(solution)/shard_map/attention_back/pallas_call | solution.py:102
  313.3 3.1 fusion
  318.0 10.6 %sent_back.1 = (bf16[512,1024]{1,0:T(8,128)(2,1)}, bf16[512,1024]{1,0:T(8,128)(2,1)}) custom-call(s32[2]{0:T(128)} %pad_add_fusion.refs_0_, bf16[512,2048]{1,0:T(8,128)(2,1)} %get-tuple-element.117.refs_1_, bf16[512,2048]{1,0:T(8,128)(2,1)} %get-tuple-element.118.refs_2_, bf16[512,256]{1,0:T(8,128)(2,1)} %get-tuple-element.119.refs_3_, ...), custom_call_target="tpu_custom_call" | custom-call | flops 550000000 | bytes 1650000 | tf_op jit(solution)/shard_map/sent_back/pallas_call | solution.py:75
  329.9 2.2 fusion.34.refs_5_
  332.0 4.0 collective-permute-done.50
  337.0 2.8 fusion.10
  339.9 11.9 %back_ends.1 = (f32[4096,128]{1,0:T(8,128)}, f32[256,128]{1,0:T(8,128)}) custom-call(bf16[512,1024]{1,0:T(8,128)(2,1)} %get-tuple-element.122.refs_1_.refs_0_, f32[4096,128]{1,0:T(8,128)} %get-tuple-element.92.refs_1_, f32[128,128]{1,0:T(8,128)} %bitcast.213, f32[128,128]{1,0:T(8,128)} %bitcast.206, bf16[4,128,512]{2,1,0:T(8,128)(2,1)} %get-tuple-element.178.refs_4_, ...), custom_call_target="tpu_custom_call" | custom-call | flops 600000000 | bytes 1800000 | tf_op jit(solution)/shard_map/back_ends/pallas_call | solution.py:75
  355.0 2.0 fusion.16
  361.0 6.3 %grad_v.1 = (bf16[8,64,1024]{2,1,0:T(8,128)(2,1)}, bf16[8,64,1024]{2,1,0:T(8,128)(2,1)}) custom-call(s32[2]{0:T(128)} %pad_add_fusion.refs_0_, bf16[512,1024]{1,0:T(8,128)(2,1)} %get-tuple-element.88.refs_1_, bf16[512,1024]{1,0:T(8,128)(2,1)} %collective-permute-done.28.refs_19_.refs_2_, bf16[512,1024]{1,0:T(8,128)(2,1)} %get-tuple-element.127.refs_3_, ...), custom_call_target="tpu_custom_call" | custom-call | flops 300000000 | bytes 900000 | tf_op jit(solution)/shard_map/grad_v/pallas_call | solution.py:102
  368.4 2.4 add_add_fusion.2.refs_7_
  370.8 6.9 %grad_r.1 = (bf16[8,64,1152]{2,1,0:T(8,128)(2,1)}, bf16[8,64,1152]{2,1,0:T(8,128)(2,1)}) custom-call(s32[2]{0:T(128)} %pad_add_fusion.refs_0_, bf16[512,1024]{1,0:T(8,128)(2,1)} %get-tuple-element.91.refs_2_.refs_1_, bf16[512,1024]{1,0:T(8,128)(2,1)} %collective-permute-done.41.refs_17_.refs_2_, bf16[512,1152]{1,0:T(8,128)(2,1)} %get-tuple-element.130.refs_3_, ...), custom_call_target="tpu_custom_call" | custom-call | flops 300000000 | bytes 900000 | tf_op jit(solution)/shard_map/grad_r/pallas_call | solution.py:102
  382.3 2.8 collective-permute-done.55
  387.7 7.8 %collective-permute-done.59 = f32[32,8,128]{2,1,0:T(8,128)S(1)} collective-permute-done((f32[32,8,128]{2,1,0:T(8,128)}, f32[32,8,128]{2,1,0:T(8,128)S(1)}, u32[]{:S(2)}, u32[]{:S(2)}) %collective-permute-start.59) | collective-permute-done | bytes 131104 | tf_op jit(solution)/shard_map/ppermute | solution.py:437
  399.7 2.3 collective-permute-start.65
  402.7 9.8 %back.4 = (f32[1024,128]{1,0:T(8,128)}, f32[256,128]{1,0:T(8,128)}, f32[392,128]{1,0:T(8,128)}) custom-call(f32[4096,128]{1,0:T(8,128)} %get-tuple-element.89.refs_0_, f32[4096,128]{1,0:T(8,128)} %get-tuple-element.124.refs_1_, f32[16,256,128]{2,1,0:T(8,128)} %get-tuple-element.125.refs_2_, f32[256,128]{1,0:T(8,128)} %maximum_bitcast_fusion.2.refs_3_, ...), custom_call_target="tpu_custom_call" | custom-call | flops 500000000 | bytes 1500000 | tf_op jit(solution)/shard_map/back/pallas_call | solution.py:75
  414.5 2.7 fusion.8
  418.1 9.9 %back.5 = (f32[1024,128]{1,0:T(8,128)}, f32[256,128]{1,0:T(8,128)}, f32[392,128]{1,0:T(8,128)}) custom-call(f32[4096,128]{1,0:T(8,128)} %get-tuple-element.89.refs_0_, f32[4096,128]{1,0:T(8,128)} %get-tuple-element.124.refs_1_, f32[16,256,128]{2,1,0:T(8,128)} %get-tuple-element.125.refs_2_, f32[256,128]{1,0:T(8,128)} %get-tuple-element.132.refs_3_, ...), custom_call_target="tpu_custom_call" | custom-call | flops 500000000 | bytes 1500000 | tf_op jit(solution)/shard_map/back/pallas_call | solution.py:75
  432.1 2.1 fusion.6
  435.5 9.7 %back.6 = (f32[1024,128]{1,0:T(8,128)}, f32[256,128]{1,0:T(8,128)}, f32[392,128]{1,0:T(8,128)}) custom-call(f32[4096,128]{1,0:T(8,128)} %get-tuple-element.89.refs_0_, f32[4096,128]{1,0:T(8,128)} %get-tuple-element.124.refs_1_, f32[16,256,128]{2,1,0:T(8,128)} %get-tuple-element.125.refs_2_, f32[256,128]{1,0:T(8,128)} %get-tuple-element.136.refs_3_, ...), custom_call_target="tpu_custom_call" | custom-call | flops 500000000 | bytes 1500000 | tf_op jit(solution)/shard_map/back/pallas_call | solution.py:75
  448.8 9.8 %back.7 = (f32[1024,128]{1,0:T(8,128)}, f32[256,128]{1,0:T(8,128)}, f32[392,128]{1,0:T(8,128)}) custom-call(f32[4096,128]{1,0:T(8,128)} %get-tuple-element.89.refs_0_, f32[4096,128]{1,0:T(8,128)} %get-tuple-element.124.refs_1_, f32[16,256,128]{2,1,0:T(8,128)} %get-tuple-element.125.refs_2_, f32[256,128]{1,0:T(8,128)} %get-tuple-element.140.refs_3_, ...), custom_call_target="tpu_custom_call" | custom-call | flops 500000000 | bytes 1500000 | tf_op jit(solution)/shard_map/back/pallas_call | solution.py:75
  469.1 2.1 collective-permute-start.69
  471.1 6.9 %back_norm.1 = (f32[512,1024]{1,0:T(8,128)}, f32[1,1024]{1,0:T(1,128)}, f32[512,128]{1,0:T(8,128)}, f32[16,128]{1,0:T(8,128)}) custom-call(f32[1024,128]{1,0:T(8,128)} %get-tuple-element.143.refs_1_.refs_0_, f32[1024,128]{1,0:T(8,128)} %get-tuple-element.142.refs_1_, f32[1024,128]{1,0:T(8,128)} %get-tuple-element.139.refs_1_.refs_2_, ...), custom_call_target="tpu_custom_call" | custom-call | flops 300000000 | bytes 900000 | tf_op jit(solution)/shard_map/back_norm/pallas_call | solution.py:75
  480.1 4.2 collective-permute-done.69
  488.4 3.7 collective-permute-done.70
  493.8 2.9 collective-permute-done.71
  496.8 2.1 collective-permute-start.72
  500.5 7.6 %collective-permute-done.72 = f32[84,128]{1,0:T(8,128)S(1)} collective-permute-done((f32[84,128]{1,0:T(8,128)S(1)}, f32[84,128]{1,0:T(8,128)S(1)}, u32[]{:S(2)}, u32[]{:S(2)}) %collective-permute-start.72) | collective-permute-done | bytes 43040 | tf_op jit(solution)/shard_map/ppermute | solution.py:437
  509.8 3.4 collective-permute-done.73
  514.8 5.9 %input.1 = f32[512,1024]{1,0:T(8,128)} custom-call(f32[512,1024]{1,0:T(8,128)} %get-tuple-element.145.refs_0_, f32[512,128]{1,0:T(8,128)} %get-tuple-element.146.refs_1_, f32[1,128]{1,0:T(1,128)} %fusion.53.refs_1_.refs_2_, bf16[512,1024]{1,0:T(8,128)(2,1)} %bitcast.201, f32[512,1]{1,0:T(8,128)} %copy.86.refs_1_.refs_3_.refs_6_.refs_4_, ...), custom_call_target="tpu_custom_call" | custom-call | flops 300000000 | bytes 900000 | tf_op jit(solution)/shard_map/input/pallas_call | solution.py:75
  (510 shorter events, 150.3 us)
Async XLA Ops:
  2.8 8.8 %collective-permute-start = (f32[1,1,56]{2,1,0:T(1,128)S(1)}, f32[1,1,56]{2,1,0:T(1,128)S(1)}, u32[]{:S(2)}, u32[]{:S(2)}) collective-permute-start(f32[1,1,56]{2,1,0:T(1,128)S(1)} %maximum_convert_fusion), channel_id=1, source_target_pairs={{0,1},{1,0},{2,3},{3,2},{4,5},{5,4},{6,7},{7,6},{8,9},{9,8},{10,11... | collective-permute-start | bytes 680 | tf_op jit(solution)/shard_map/ppermute | solution.py:437
  5.2 19.0 %collective-permute-start.3 = (bf16[1,32,3072]{2,1,0:T(8,128)(2,1)S(1)}, bf16[1,32,3072]{2,1,0:T(8,128)(2,1)S(1)}, u32[]{:S(2)}, u32[]{:S(2)}) collective-permute-start(bf16[1,32,3072]{2,1,0:T(8,128)(2,1)S(1)} %maximum_bitcast_fusion.1), channel_id=1, source_target_pairs={{0,16},{4,20},{8,24},{12,28},{16,0},{20,4},{24,8},{28,12},{1,17},{... | collective-permute-start | bytes 589832 | tf_op jit(solution)/shard_map/ppermute | solution.py:437
  9.0 18.8 %collective-permute-start.4 = (bf16[1,32,3328]{2,1,0:T(8,128)(2,1)S(1)}, bf16[1,32,3328]{2,1,0:T(8,128)(2,1)S(1)}, u32[]{:S(2)}, u32[]{:S(2)}) collective-permute-start(bf16[1,32,3328]{2,1,0:T(8,128)(2,1)S(1)} %maximum_bitcast_fusion), channel_id=1, source_target_pairs={{0,16},{4,20},{8,24},{12,28},{16,0},{20,4},{24,8},{28,12},{1,17},{... | collective-permute-start | bytes 638984 | tf_op jit(solution)/shard_map/ppermute | solution.py:437
  20.3 19.2 %collective-permute-start.7 = (bf16[1,80,1024]{2,1,0:T(8,128)(2,1)S(1)}, bf16[1,80,1024]{2,1,0:T(8,128)(2,1)S(1)}, u32[]{:S(2)}, u32[]{:S(2)}) collective-permute-start(bf16[1,80,1024]{2,1,0:T(8,128)(2,1)S(1)} %convert_bitcast_fusion.2), channel_id=1, source_target_pairs={{0,2},{2,0},{1,3},{3,1},{4,6},{6,4},{5,7},{7,5},{8,10},{10,8},{9,1... | collective-permute-start | bytes 491528 | tf_op jit(solution)/shard_map/ppermute | solution.py:437
  33.2 9.1 %collective-permute-start.6 = (f32[288,128]{1,0:T(8,128)S(1)}, f32[288,128]{1,0:T(8,128)S(1)}, u32[]{:S(2)}, u32[]{:S(2)}) collective-permute-start(f32[288,128]{1,0:T(8,128)S(1)} %pad_maximum_fusion.27), channel_id=1, source_target_pairs={{0,16},{4,20},{8,24},{12,28},{16,0},{20,4},{24,8},{28,12},{1,17},{... | collective-permute-start | bytes 442376 | tf_op jit(solution)/shard_map/ppermute | solution.py:437
  40.3 18.0 %collective-permute-start.8 = (bf16[2,32,3072]{2,1,0:T(8,128)(2,1)S(1)}, bf16[2,32,3072]{2,1,0:T(8,128)(2,1)S(1)}, u32[]{:S(2)}, u32[]{:S(2)}) collective-permute-start(bf16[2,32,3072]{2,1,0:T(8,128)(2,1)S(1)} %copy-done.24), channel_id=1, source_target_pairs={{0,8},{4,12},{8,0},{12,4},{16,24},{20,28},{24,16},{28,20},{1,9},{5... | collective-permute-start | bytes 1179656 | tf_op jit(solution)/shard_map/ppermute | solution.py:437
  42.1 17.8 %collective-permute-start.9 = (bf16[2,32,3328]{2,1,0:T(8,128)(2,1)S(1)}, bf16[2,32,3328]{2,1,0:T(8,128)(2,1)S(1)}, u32[]{:S(2)}, u32[]{:S(2)}) collective-permute-start(bf16[2,32,3328]{2,1,0:T(8,128)(2,1)S(1)} %copy-done.39), channel_id=1, source_target_pairs={{0,8},{4,12},{8,0},{12,4},{16,24},{20,28},{24,16},{28,20},{1,9},{5... | collective-permute-start | bytes 1277960 | tf_op jit(solution)/shard_map/ppermute | solution.py:437
  56.7 9.3 %collective-permute-start.10 = (bf16[2,80,1024]{2,1,0:T(8,128)(2,1)}, bf16[2,80,1024]{2,1,0:T(8,128)(2,1)}, u32[]{:S(2)}, u32[]{:S(2)}) collective-permute-start(bf16[2,80,1024]{2,1,0:T(8,128)(2,1)} %tie.41), channel_id=1, source_target_pairs={{0,4},{4,0},{8,12},{12,8},{16,20},{20,16},{24,28},{28,24},{1,5},{5... | collective-permute-start | bytes 983048 | tf_op jit(solution)/shard_map/ppermute | solution.py:437
  69.6 13.6 %collective-permute-start.16 = (bf16[1,32,2560]{2,1,0:T(8,128)(2,1)S(1)}, bf16[1,32,2560]{2,1,0:T(8,128)(2,1)S(1)}, u32[]{:S(2)}, u32[]{:S(2)}) collective-permute-start(bf16[1,32,2560]{2,1,0:T(8,128)(2,1)S(1)} %copy-done.52), channel_id=1, source_target_pairs={{0,16},{4,20},{8,24},{12,28},{16,0},{20,4},{24,8},{28,12},{1,17},{... | collective-permute-start | bytes 491528 | tf_op jit(solution)/shard_map/ppermute | solution.py:437
  69.6 22.5 %collective-permute-start.14 = (bf16[4,32,3072]{2,1,0:T(8,128)(2,1)S(1)}, bf16[4,32,3072]{2,1,0:T(8,128)(2,1)S(1)}, u32[]{:S(2)}, u32[]{:S(2)}) collective-permute-start(bf16[4,32,3072]{2,1,0:T(8,128)(2,1)S(1)} %copy-done.18), channel_id=1, source_target_pairs={{0,4},{4,0},{8,12},{12,8},{16,20},{20,16},{24,28},{28,24},{1,5},{5... | collective-permute-start | bytes 2359304 | tf_op jit(solution)/shard_map/ppermute | solution.py:437
  70.7 22.7 %collective-permute-start.15 = (bf16[4,32,3328]{2,1,0:T(8,128)(2,1)S(1)}, bf16[4,32,3328]{2,1,0:T(8,128)(2,1)S(1)}, u32[]{:S(2)}, u32[]{:S(2)}) collective-permute-start(bf16[4,32,3328]{2,1,0:T(8,128)(2,1)S(1)} %copy-done.17), channel_id=1, source_target_pairs={{0,2},{2,0},{1,3},{3,1},{4,6},{6,4},{5,7},{7,5},{8,10},{10,8},{9,1... | collective-permute-start | bytes 2555912 | tf_op jit(solution)/shard_map/ppermute | solution.py:437
  72.2 15.9 %collective-permute-start.17 = (bf16[1,32,2560]{2,1,0:T(8,128)(2,1)S(1)}, bf16[1,32,2560]{2,1,0:T(8,128)(2,1)S(1)}, u32[]{:S(2)}, u32[]{:S(2)}) collective-permute-start(bf16[1,32,2560]{2,1,0:T(8,128)(2,1)S(1)} %copy-done.53), channel_id=1, source_target_pairs={{0,16},{4,20},{8,24},{12,28},{16,0},{20,4},{24,8},{28,12},{1,17},{... | collective-permute-start | bytes 491528 | tf_op jit(solution)/shard_map/ppermute | solution.py:437
  94.7 36.2 %collective-permute-start.23 = (bf16[8,32,3328]{2,1,0:T(8,128)(2,1)}, bf16[8,32,3328]{2,1,0:T(8,128)(2,1)}, u32[]{:S(2)}, u32[]{:S(2)}) collective-permute-start(bf16[8,32,3328]{2,1,0:T(8,128)(2,1)} %tie.51.refs_13_.refs_9_.refs_19_.refs_8_), channel_id=1, source_target_pairs={{0,4},{4,0},{8,12},{12,8},{16,20},{20,16},{24,28},{28,24},{1,5},{5... | collective-permute-start | bytes 5111816 | tf_op jit(solution)/shard_map/ppermute | solution.py:437
  96.3 32.6 %collective-permute-start.20 = (bf16[8,32,3072]{2,1,0:T(8,128)(2,1)}, bf16[8,32,3072]{2,1,0:T(8,128)(2,1)}, u32[]{:S(2)}, u32[]{:S(2)}) collective-permute-start(bf16[8,32,3072]{2,1,0:T(8,128)(2,1)} %tie.50.refs_9_.refs_5_.refs_15_.refs_4_), channel_id=1, source_target_pairs={{0,2},{2,0},{1,3},{3,1},{4,6},{6,4},{5,7},{7,5},{8,10},{10,8},{9,1... | collective-permute-start | bytes 4718600 | tf_op jit(solution)/shard_map/ppermute | solution.py:437
  98.4 8.4 %collective-permute-start.19 = (bf16[2,32,2560]{2,1,0:T(8,128)(2,1)}, bf16[2,32,2560]{2,1,0:T(8,128)(2,1)S(1)}, u32[]{:S(2)}, u32[]{:S(2)}) collective-permute-start(bf16[2,32,2560]{2,1,0:T(8,128)(2,1)} %tie.49), channel_id=1, source_target_pairs={{0,8},{4,12},{8,0},{12,4},{16,24},{20,28},{24,16},{28,20},{1,9},{5... | collective-permute-start | bytes 983048 | tf_op jit(solution)/shard_map/ppermute | solution.py:437
  98.4 13.5 %collective-permute-start.18 = (bf16[2,32,2560]{2,1,0:T(8,128)(2,1)}, bf16[2,32,2560]{2,1,0:T(8,128)(2,1)S(1)}, u32[]{:S(2)}, u32[]{:S(2)}) collective-permute-start(bf16[2,32,2560]{2,1,0:T(8,128)(2,1)} %tie.48), channel_id=1, source_target_pairs={{0,8},{4,12},{8,0},{12,4},{16,24},{20,28},{24,16},{28,20},{1,9},{5... | collective-permute-start | bytes 983048 | tf_op jit(solution)/shard_map/ppermute | solution.py:437
  112.8 24.6 %collective-permute-start.35 = (bf16[4,80,1024]{2,1,0:T(8,128)(2,1)}, bf16[4,80,1024]{2,1,0:T(8,128)(2,1)}, u32[]{:S(2)}, u32[]{:S(2)}) collective-permute-start(bf16[4,80,1024]{2,1,0:T(8,128)(2,1)} %tie.59), channel_id=1, source_target_pairs={{0,16},{4,20},{8,24},{12,28},{16,0},{20,4},{24,8},{28,12},{1,17},{... | collective-permute-start | bytes 1966088 | tf_op jit(solution)/shard_map/ppermute | solution.py:437
  130.9 12.8 %collective-permute-start.27 = (bf16[4,32,2560]{2,1,0:T(8,128)(2,1)}, bf16[4,32,2560]{2,1,0:T(8,128)(2,1)}, u32[]{:S(2)}, u32[]{:S(2)}) collective-permute-start(bf16[4,32,2560]{2,1,0:T(8,128)(2,1)} %tie.53), channel_id=1, source_target_pairs={{0,2},{2,0},{1,3},{3,1},{4,6},{6,4},{5,7},{7,5},{8,10},{10,8},{9,1... | collective-permute-start | bytes 1966088 | tf_op jit(solution)/shard_map/ppermute | solution.py:437
  133.4 20.0 %collective-permute-start.28 = (bf16[512,1024]{1,0:T(8,128)(2,1)}, bf16[512,1024]{1,0:T(8,128)(2,1)}, u32[]{:S(2)}, u32[]{:S(2)}) collective-permute-start(bf16[512,1024]{1,0:T(8,128)(2,1)} %tie.54), channel_id=1, source_target_pairs={{0,1},{1,0},{2,3},{3,2},{4,5},{5,4},{6,7},{7,6},{8,9},{9,8},{10,11... | collective-permute-start | bytes 3145736 | tf_op jit(solution)/shard_map/ppermute | solution.py:437
  134.8 19.2 %collective-permute-start.21 = (bf16[8,32,3072]{2,1,0:T(8,128)(2,1)S(1)}, bf16[8,32,3072]{2,1,0:T(8,128)(2,1)}, u32[]{:S(2)}, u32[]{:S(2)}) collective-permute-start(bf16[8,32,3072]{2,1,0:T(8,128)(2,1)S(1)} %copy-done.2), channel_id=1, source_target_pairs={{0,1},{1,0},{2,3},{3,2},{4,5},{5,4},{6,7},{7,6},{8,9},{9,8},{10,11... | collective-permute-start | bytes 4718600 | tf_op jit(solution)/shard_map/ppermute | solution.py:437
  134.8 17.4 %collective-permute-start.26 = (bf16[4,32,2560]{2,1,0:T(8,128)(2,1)}, bf16[4,32,2560]{2,1,0:T(8,128)(2,1)S(1)}, u32[]{:S(2)}, u32[]{:S(2)}) collective-permute-start(bf16[4,32,2560]{2,1,0:T(8,128)(2,1)} %tie.52), channel_id=1, source_target_pairs={{0,4},{4,0},{8,12},{12,8},{16,20},{20,16},{24,28},{28,24},{1,5},{5... | collective-permute-start | bytes 1966088 | tf_op jit(solution)/shard_map/ppermute | solution.py:437
  137.4 17.8 %collective-permute-start.24 = (bf16[8,32,3328]{2,1,0:T(8,128)(2,1)S(1)}, bf16[8,32,3328]{2,1,0:T(8,128)(2,1)}, u32[]{:S(2)}, u32[]{:S(2)}) collective-permute-start(bf16[8,32,3328]{2,1,0:T(8,128)(2,1)S(1)} %copy-done.1), channel_id=1, source_target_pairs={{0,1},{1,0},{2,3},{3,2},{4,5},{5,4},{6,7},{7,6},{8,9},{9,8},{10,11... | collective-permute-start | bytes 5111816 | tf_op jit(solution)/shard_map/ppermute | solution.py:437
  143.6 16.4 %collective-permute-start.25 = (bf16[8,32,3328]{2,1,0:T(8,128)(2,1)}, bf16[8,32,3328]{2,1,0:T(8,128)(2,1)}, u32[]{:S(2)}, u32[]{:S(2)}) collective-permute-start(bf16[8,32,3328]{2,1,0:T(8,128)(2,1)} %collective-permute-done.23.refs_3_.refs_14_.refs_10_.refs_20_.refs_9_), channel_id=1, source_target_pairs={{0,1},{1,0},{2,3},{3,2},{4,5},{5,4},{6,7},{7,6},{8,9},{9,8},{10,11... | collective-permute-start | bytes 5111816 | tf_op jit(solution)/shard_map/ppermute | solution.py:437
  152.1 7.9 %collective-permute-start.22 = (bf16[8,32,3072]{2,1,0:T(8,128)(2,1)}, bf16[8,32,3072]{2,1,0:T(8,128)(2,1)}, u32[]{:S(2)}, u32[]{:S(2)}) collective-permute-start(bf16[8,32,3072]{2,1,0:T(8,128)(2,1)} %collective-permute-done.20.refs_2_.refs_10_.refs_6_.refs_16_.refs_5_), channel_id=1, source_target_pairs={{0,1},{1,0},{2,3},{3,2},{4,5},{5,4},{6,7},{7,6},{8,9},{9,8},{10,11... | collective-permute-start | bytes 4718600 | tf_op jit(solution)/shard_map/ppermute | solution.py:437
  153.3 31.5 %collective-permute-start.36 = (bf16[8,80,1024]{2,1,0:T(8,128)(2,1)}, bf16[8,80,1024]{2,1,0:T(8,128)(2,1)}, u32[]{:S(2)}, u32[]{:S(2)}) collective-permute-start(bf16[8,80,1024]{2,1,0:T(8,128)(2,1)} %tie.60.refs_0_), channel_id=1, source_target_pairs={{0,8},{4,12},{8,0},{12,4},{16,24},{20,28},{24,16},{28,20},{1,9},{5... | collective-permute-start | bytes 3932168 | tf_op jit(solution)/shard_map/ppermute | solution.py:437
  153.9 31.4 %collective-permute-start.32 = (bf16[8,32,2560]{2,1,0:T(8,128)(2,1)}, bf16[8,32,2560]{2,1,0:T(8,128)(2,1)S(1)}, u32[]{:S(2)}, u32[]{:S(2)}) collective-permute-start(bf16[8,32,2560]{2,1,0:T(8,128)(2,1)} %pad_maximum_fusion.3.refs_18_.refs_0_.refs_2_), channel_id=1, source_target_pairs={{0,4},{4,0},{8,12},{12,8},{16,20},{20,16},{24,28},{28,24},{1,5},{5... | collective-permute-start | bytes 3932168 | tf_op jit(solution)/shard_map/ppermute | solution.py:437
  155.2 32.9 %collective-permute-start.29 = (bf16[8,32,2560]{2,1,0:T(8,128)(2,1)}, bf16[8,32,2560]{2,1,0:T(8,128)(2,1)S(1)}, u32[]{:S(2)}, u32[]{:S(2)}) collective-permute-start(bf16[8,32,2560]{2,1,0:T(8,128)(2,1)} %pad_maximum_fusion.2.refs_17_.refs_0_.refs_1_), channel_id=1, source_target_pairs={{0,2},{2,0},{1,3},{3,1},{4,6},{6,4},{5,7},{7,5},{8,10},{10,8},{9,1... | collective-permute-start | bytes 3932168 | tf_op jit(solution)/shard_map/ppermute | solution.py:437
  184.8 8.3 %collective-permute-start.38 = (bf16[8,80,1024]{2,1,0:T(8,128)(2,1)}, bf16[8,80,1024]{2,1,0:T(8,128)(2,1)}, u32[]{:S(2)}, u32[]{:S(2)}) collective-permute-start(bf16[8,80,1024]{2,1,0:T(8,128)(2,1)} %tie.62.refs_12_.refs_4_), channel_id=1, source_target_pairs={{0,1},{1,0},{2,3},{3,2},{4,5},{5,4},{6,7},{7,6},{8,9},{9,8},{10,11... | collective-permute-start | bytes 3932168 | tf_op jit(solution)/shard_map/ppermute | solution.py:437
  184.8 8.6 %collective-permute-start.37 = (bf16[8,80,1024]{2,1,0:T(8,128)(2,1)}, bf16[8,80,1024]{2,1,0:T(8,128)(2,1)}, u32[]{:S(2)}, u32[]{:S(2)}) collective-permute-start(bf16[8,80,1024]{2,1,0:T(8,128)(2,1)} %tie.61.refs_11_.refs_3_), channel_id=1, source_target_pairs={{0,1},{1,0},{2,3},{3,2},{4,5},{5,4},{6,7},{7,6},{8,9},{9,8},{10,11... | collective-permute-start | bytes 3932168 | tf_op jit(solution)/shard_map/ppermute | solution.py:437
  185.4 17.4 %collective-permute-start.40 = (bf16[512,2048]{1,0:T(8,128)(2,1)}, bf16[512,2048]{1,0:T(8,128)(2,1)}, u32[]{:S(2)}, u32[]{:S(2)}) collective-permute-start(bf16[512,2048]{1,0:T(8,128)(2,1)} %get-tuple-element.93.refs_1_), channel_id=1, source_target_pairs={{0,1},{1,0},{2,3},{3,2},{4,5},{5,4},{6,7},{7,6},{8,9},{9,8},{10,11... | collective-permute-start | bytes 6291464 | tf_op jit(solution)/shard_map/ppermute | solution.py:437
  193.1 9.6 %collective-permute-start.31 = (bf16[8,32,2560]{2,1,0:T(8,128)(2,1)}, bf16[8,32,2560]{2,1,0:T(8,128)(2,1)S(1)}, u32[]{:S(2)}, u32[]{:S(2)}) collective-permute-start(bf16[8,32,2560]{2,1,0:T(8,128)(2,1)} %tie.56.refs_4_.refs_8_), channel_id=1, source_target_pairs={{0,1},{1,0},{2,3},{3,2},{4,5},{5,4},{6,7},{7,6},{8,9},{9,8},{10,11... | collective-permute-start | bytes 3932168 | tf_op jit(solution)/shard_map/ppermute | solution.py:437
  193.5 9.2 %collective-permute-start.30 = (bf16[8,32,2560]{2,1,0:T(8,128)(2,1)S(1)}, bf16[8,32,2560]{2,1,0:T(8,128)(2,1)S(1)}, u32[]{:S(2)}, u32[]{:S(2)}) collective-permute-start(bf16[8,32,2560]{2,1,0:T(8,128)(2,1)S(1)} %copy-done.4), channel_id=1, source_target_pairs={{0,1},{1,0},{2,3},{3,2},{4,5},{5,4},{6,7},{7,6},{8,9},{9,8},{10,11... | collective-permute-start | bytes 3932168 | tf_op jit(solution)/shard_map/ppermute | solution.py:437
  223.2 8.9 %collective-permute-start.44 = (bf16[512,2560]{1,0:T(8,128)(2,1)}, bf16[512,2560]{1,0:T(8,128)(2,1)}, u32[]{:S(2)}, u32[]{:S(2)}) collective-permute-start(bf16[512,2560]{1,0:T(8,128)(2,1)} %get-tuple-element.95.refs_1_), channel_id=1, source_target_pairs={{0,1},{1,0},{2,3},{3,2},{4,5},{5,4},{6,7},{7,6},{8,9},{9,8},{10,11... | collective-permute-start | bytes 7864328 | tf_op jit(solution)/shard_map/ppermute | solution.py:437
  223.4 17.5 %collective-permute-start.43 = (bf16[512,2560]{1,0:T(8,128)(2,1)}, bf16[512,2560]{1,0:T(8,128)(2,1)S(1)}, u32[]{:S(2)}, u32[]{:S(2)}) collective-permute-start(bf16[512,2560]{1,0:T(8,128)(2,1)} %get-tuple-element.98.refs_2_), channel_id=1, source_target_pairs={{0,1},{1,0},{2,3},{3,2},{4,5},{5,4},{6,7},{7,6},{8,9},{9,8},{10,11... | collective-permute-start | bytes 7864328 | tf_op jit(solution)/shard_map/ppermute | solution.py:437
  223.8 17.1 %collective-permute-start.42 = (bf16[512,1024]{1,0:T(8,128)(2,1)S(1)}, bf16[512,1024]{1,0:T(8,128)(2,1)}, u32[]{:S(2)}, u32[]{:S(2)}) collective-permute-start(bf16[512,1024]{1,0:T(8,128)(2,1)S(1)} %copy-done), channel_id=1, source_target_pairs={{0,1},{1,0},{2,3},{3,2},{4,5},{5,4},{6,7},{7,6},{8,9},{9,8},{10,11... | collective-permute-start | bytes 3145736 | tf_op jit(solution)/shard_map/ppermute | solution.py:437
  239.6 38.4 %collective-permute-start.46 = (bf16[8,160,512]{2,1,0:T(8,128)(2,1)}, bf16[8,160,512]{2,1,0:T(8,128)(2,1)}, u32[]{:S(2)}, u32[]{:S(2)}) collective-permute-start(bf16[8,160,512]{2,1,0:T(8,128)(2,1)} %get-tuple-element.114), channel_id=1, source_target_pairs={{0,2},{2,0},{1,3},{3,1},{4,6},{6,4},{5,7},{7,5},{8,10},{10,8},{9,1... | collective-permute-start | bytes 3932168 | tf_op jit(solution)/shard_map/ppermute | solution.py:437
  249.5 39.9 %collective-permute-start.47 = (bf16[8,64,1280]{2,1,0:T(8,128)(2,1)}, bf16[8,64,1280]{2,1,0:T(8,128)(2,1)S(1)}, u32[]{:S(2)}, u32[]{:S(2)}) collective-permute-start(bf16[8,64,1280]{2,1,0:T(8,128)(2,1)} %get-tuple-element.116), channel_id=1, source_target_pairs={{0,4},{4,0},{8,12},{12,8},{16,20},{20,16},{24,28},{28,24},{1,5},{5... | collective-permute-start | bytes 3932168 | tf_op jit(solution)/shard_map/ppermute | solution.py:437
  272.7 9.2 %collective-permute-start.45 = (bf16[512,512]{1,0:T(8,128)(2,1)}, bf16[512,512]{1,0:T(8,128)(2,1)}, u32[]{:S(2)}, u32[]{:S(2)}) collective-permute-start(bf16[512,512]{1,0:T(8,128)(2,1)} %get-tuple-element.113), channel_id=1, source_target_pairs={{0,1},{1,0},{2,3},{3,2},{4,5},{5,4},{6,7},{7,6},{8,9},{9,8},{10,11... | collective-permute-start | bytes 1572872 | tf_op jit(solution)/shard_map/ppermute | solution.py:437
  272.8 40.6 %collective-permute-start.48 = (bf16[8,64,1280]{2,1,0:T(8,128)(2,1)}, bf16[8,64,1280]{2,1,0:T(8,128)(2,1)}, u32[]{:S(2)}, u32[]{:S(2)}) collective-permute-start(bf16[8,64,1280]{2,1,0:T(8,128)(2,1)} %get-tuple-element.120), channel_id=1, source_target_pairs={{0,2},{2,0},{1,3},{3,1},{4,6},{6,4},{5,7},{7,5},{8,10},{10,8},{9,1... | collective-permute-start | bytes 3932168 | tf_op jit(solution)/shard_map/ppermute | solution.py:437
  280.9 29.9 %collective-permute-start.49 = (bf16[4,160,512]{2,1,0:T(8,128)(2,1)S(1)}, bf16[4,160,512]{2,1,0:T(8,128)(2,1)}, u32[]{:S(2)}, u32[]{:S(2)}) collective-permute-start(bf16[4,160,512]{2,1,0:T(8,128)(2,1)S(1)} %get-tuple-element.172.refs_5_), channel_id=1, source_target_pairs={{0,4},{4,0},{8,12},{12,8},{16,20},{20,16},{24,28},{28,24},{1,5},{5... | collective-permute-start | bytes 1966088 | tf_op jit(solution)/shard_map/ppermute | solution.py:437
  308.4 50.5 %collective-permute-start.53 = (bf16[512,1024]{1,0:T(8,128)(2,1)}, bf16[512,1024]{1,0:T(8,128)(2,1)}, u32[]{:S(2)}, u32[]{:S(2)}) collective-permute-start(bf16[512,1024]{1,0:T(8,128)(2,1)} %get-tuple-element.121.refs_1_), channel_id=1, source_target_pairs={{0,1},{1,0},{2,3},{3,2},{4,5},{5,4},{6,7},{7,6},{8,9},{9,8},{10,11... | collective-permute-start | bytes 3145736 | tf_op jit(solution)/shard_map/ppermute | solution.py:437
  308.5 43.9 %collective-permute-start.56 = (bf16[4,64,1280]{2,1,0:T(8,128)(2,1)S(1)}, bf16[4,64,1280]{2,1,0:T(8,128)(2,1)}, u32[]{:S(2)}, u32[]{:S(2)}) collective-permute-start(bf16[4,64,1280]{2,1,0:T(8,128)(2,1)S(1)} %copy-done.42), channel_id=1, source_target_pairs={{0,2},{2,0},{1,3},{3,1},{4,6},{6,4},{5,7},{7,5},{8,10},{10,8},{9,1... | collective-permute-start | bytes 1966088 | tf_op jit(solution)/shard_map/ppermute | solution.py:437
  309.8 26.3 %collective-permute-start.50 = (bf16[8,128,512]{2,1,0:T(8,128)(2,1)}, bf16[8,128,512]{2,1,0:T(8,128)(2,1)}, u32[]{:S(2)}, u32[]{:S(2)}) collective-permute-start(bf16[8,128,512]{2,1,0:T(8,128)(2,1)} %get-tuple-element.123), channel_id=1, source_target_pairs={{0,4},{4,0},{8,12},{12,8},{16,20},{20,16},{24,28},{28,24},{1,5},{5... | collective-permute-start | bytes 3145736 | tf_op jit(solution)/shard_map/ppermute | solution.py:437
  312.8 16.3 %collective-permute-start.51 = (bf16[2,160,512]{2,1,0:T(8,128)(2,1)S(1)}, bf16[2,160,512]{2,1,0:T(8,128)(2,1)S(1)}, u32[]{:S(2)}, u32[]{:S(2)}) collective-permute-start(bf16[2,160,512]{2,1,0:T(8,128)(2,1)S(1)} %get-tuple-element.184.refs_13_), channel_id=1, source_target_pairs={{0,8},{4,12},{8,0},{12,4},{16,24},{20,28},{24,16},{28,20},{1,9},{5... | collective-permute-start | bytes 983048 | tf_op jit(solution)/shard_map/ppermute | solution.py:437
  316.5 38.6 %collective-permute-start.57 = (bf16[4,64,1280]{2,1,0:T(8,128)(2,1)}, bf16[4,64,1280]{2,1,0:T(8,128)(2,1)}, u32[]{:S(2)}, u32[]{:S(2)}) collective-permute-start(bf16[4,64,1280]{2,1,0:T(8,128)(2,1)} %get-tuple-element.170.refs_12_), channel_id=1, source_target_pairs={{0,4},{4,0},{8,12},{12,8},{16,20},{20,16},{24,28},{28,24},{1,5},{5... | collective-permute-start | bytes 1966088 | tf_op jit(solution)/shard_map/ppermute | solution.py:437
  329.9 30.1 %collective-permute-start.54 = (bf16[512,1152]{1,0:T(8,128)(2,1)}, bf16[512,1152]{1,0:T(8,128)(2,1)S(1)}, u32[]{:S(2)}, u32[]{:S(2)}) collective-permute-start(bf16[512,1152]{1,0:T(8,128)(2,1)} %get-tuple-element.128), channel_id=1, source_target_pairs={{0,1},{1,0},{2,3},{3,2},{4,5},{5,4},{6,7},{7,6},{8,9},{9,8},{10,11... | collective-permute-start | bytes 3538952 | tf_op jit(solution)/shard_map/ppermute | solution.py:437
  336.1 32.3 %collective-permute-start.58 = (bf16[1,160,512]{2,1,0:T(8,128)(2,1)}, bf16[1,160,512]{2,1,0:T(8,128)(2,1)}, u32[]{:S(2)}, u32[]{:S(2)}) collective-permute-start(bf16[1,160,512]{2,1,0:T(8,128)(2,1)} %fusion.34.refs_5_), channel_id=1, source_target_pairs={{0,16},{4,20},{8,24},{12,28},{16,0},{20,4},{24,8},{28,12},{1,17},{... | collective-permute-start | bytes 491528 | tf_op jit(solution)/shard_map/ppermute | solution.py:437
  352.3 43.9 %collective-permute-start.60 = (bf16[4,128,512]{2,1,0:T(8,128)(2,1)}, bf16[4,128,512]{2,1,0:T(8,128)(2,1)}, u32[]{:S(2)}, u32[]{:S(2)}) collective-permute-start(bf16[4,128,512]{2,1,0:T(8,128)(2,1)} %get-tuple-element.178.refs_4_), channel_id=1, source_target_pairs={{0,2},{2,0},{1,3},{3,1},{4,6},{6,4},{5,7},{7,5},{8,10},{10,8},{9,1... | collective-permute-start | bytes 1572872 | tf_op jit(solution)/shard_map/ppermute | solution.py:437
  357.1 40.9 %collective-permute-start.61 = (bf16[2,64,2560]{2,1,0:T(8,128)(2,1)S(1)}, bf16[2,64,2560]{2,1,0:T(8,128)(2,1)}, u32[]{:S(2)}, u32[]{:S(2)}) collective-permute-start(bf16[2,64,2560]{2,1,0:T(8,128)(2,1)S(1)} %pad_maximum_fusion.10.refs_6_), channel_id=1, source_target_pairs={{0,8},{4,12},{8,0},{12,4},{16,24},{20,28},{24,16},{28,20},{1,9},{5... | collective-permute-start | bytes 1966088 | tf_op jit(solution)/shard_map/ppermute | solution.py:437
  358.9 19.3 %collective-permute-start.52 = (f32[32,8,128]{2,1,0:T(8,128)}, f32[32,8,128]{2,1,0:T(8,128)S(1)}, u32[]{:S(2)}, u32[]{:S(2)}) collective-permute-start(f32[32,8,128]{2,1,0:T(8,128)} %bitcast.41), channel_id=1, source_target_pairs={{0,4},{4,0},{8,12},{12,8},{16,20},{20,16},{24,28},{28,24},{1,5},{5... | collective-permute-start | bytes 393224 | tf_op jit(solution)/shard_map/ppermute | solution.py:437
  380.1 34.3 %collective-permute-start.62 = (bf16[8,64,1024]{2,1,0:T(8,128)(2,1)}, bf16[8,64,1024]{2,1,0:T(8,128)(2,1)}, u32[]{:S(2)}, u32[]{:S(2)}) collective-permute-start(bf16[8,64,1024]{2,1,0:T(8,128)(2,1)} %get-tuple-element.134), channel_id=1, source_target_pairs={{0,2},{2,0},{1,3},{3,1},{4,6},{6,4},{5,7},{7,5},{8,10},{10,8},{9,1... | collective-permute-start | bytes 3145736 | tf_op jit(solution)/shard_map/ppermute | solution.py:437
  381.3 50.8 %collective-permute-start.64 = (bf16[8,64,1152]{2,1,0:T(8,128)(2,1)}, bf16[8,64,1152]{2,1,0:T(8,128)(2,1)}, u32[]{:S(2)}, u32[]{:S(2)}) collective-permute-start(bf16[8,64,1152]{2,1,0:T(8,128)(2,1)} %get-tuple-element.138), channel_id=1, source_target_pairs={{0,4},{4,0},{8,12},{12,8},{16,20},{20,16},{24,28},{28,24},{1,5},{5... | collective-permute-start | bytes 3538952 | tf_op jit(solution)/shard_map/ppermute | solution.py:437
  386.3 9.2 %collective-permute-start.59 = (f32[32,8,128]{2,1,0:T(8,128)}, f32[32,8,128]{2,1,0:T(8,128)S(1)}, u32[]{:S(2)}, u32[]{:S(2)}) collective-permute-start(f32[32,8,128]{2,1,0:T(8,128)} %tie.71), channel_id=1, source_target_pairs={{0,16},{4,20},{8,24},{12,28},{16,0},{20,4},{24,8},{28,12},{1,17},{... | collective-permute-start | bytes 393224 | tf_op jit(solution)/shard_map/ppermute | solution.py:437
  397.9 15.1 %collective-permute-start.63 = (bf16[2,128,512]{2,1,0:T(8,128)(2,1)S(1)}, bf16[2,128,512]{2,1,0:T(8,128)(2,1)S(1)}, u32[]{:S(2)}, u32[]{:S(2)}) collective-permute-start(bf16[2,128,512]{2,1,0:T(8,128)(2,1)S(1)} %get-tuple-element.190.refs_9_), channel_id=1, source_target_pairs={{0,8},{4,12},{8,0},{12,4},{16,24},{20,28},{24,16},{28,20},{1,9},{5... | collective-permute-start | bytes 786440 | tf_op jit(solution)/shard_map/ppermute | solution.py:437
  399.7 29.6 %collective-permute-start.65 = (bf16[1,64,2560]{2,1,0:T(8,128)(2,1)S(1)}, bf16[1,64,2560]{2,1,0:T(8,128)(2,1)}, u32[]{:S(2)}, u32[]{:S(2)}) collective-permute-start(bf16[1,64,2560]{2,1,0:T(8,128)(2,1)S(1)} %fusion.14.refs_10_), channel_id=1, source_target_pairs={{0,16},{4,20},{8,24},{12,28},{16,0},{20,4},{24,8},{28,12},{1,17},{... | collective-permute-start | bytes 983048 | tf_op jit(solution)/shard_map/ppermute | solution.py:437
  413.7 32.7 %collective-permute-start.66 = (bf16[1,128,512]{2,1,0:T(8,128)(2,1)S(1)}, bf16[1,128,512]{2,1,0:T(8,128)(2,1)}, u32[]{:S(2)}, u32[]{:S(2)}) collective-permute-start(bf16[1,128,512]{2,1,0:T(8,128)(2,1)S(1)} %fusion.38.refs_10_), channel_id=1, source_target_pairs={{0,16},{4,20},{8,24},{12,28},{16,0},{20,4},{24,8},{28,12},{1,17},{... | collective-permute-start | bytes 393224 | tf_op jit(solution)/shard_map/ppermute | solution.py:437
  417.2 48.4 %collective-permute-start.67 = (bf16[4,64,1024]{2,1,0:T(8,128)(2,1)S(1)}, bf16[4,64,1024]{2,1,0:T(8,128)(2,1)}, u32[]{:S(2)}, u32[]{:S(2)}) collective-permute-start(bf16[4,64,1024]{2,1,0:T(8,128)(2,1)S(1)} %get-tuple-element.176.refs_9_), channel_id=1, source_target_pairs={{0,4},{4,0},{8,12},{12,8},{16,20},{20,16},{24,28},{28,24},{1,5},{5... | collective-permute-start | bytes 1572872 | tf_op jit(solution)/shard_map/ppermute | solution.py:437
  431.2 30.3 %collective-permute-start.76 = (bf16[32,2560]{1,0:T(8,128)(2,1)S(1)}, bf16[32,2560]{1,0:T(8,128)(2,1)}, u32[]{:S(2)}, u32[]{:S(2)}) collective-permute-start(bf16[32,2560]{1,0:T(8,128)(2,1)S(1)} %fusion.32), channel_id=1, source_target_pairs={{0,1},{1,0},{2,3},{3,2},{4,5},{5,4},{6,7},{7,6},{8,9},{9,8},{10,11... | collective-permute-start | bytes 491528 | tf_op jit(solution)/shard_map/ppermute | solution.py:437
  434.3 33.0 %collective-permute-start.68 = (bf16[4,64,1152]{2,1,0:T(8,128)(2,1)S(1)}, bf16[4,64,1152]{2,1,0:T(8,128)(2,1)}, u32[]{:S(2)}, u32[]{:S(2)}) collective-permute-start(bf16[4,64,1152]{2,1,0:T(8,128)(2,1)S(1)} %get-tuple-element.174.refs_9_), channel_id=1, source_target_pairs={{0,2},{2,0},{1,3},{3,1},{4,6},{6,4},{5,7},{7,5},{8,10},{10,8},{9,1... | collective-permute-start | bytes 1769480 | tf_op jit(solution)/shard_map/ppermute | solution.py:437
  461.3 32.5 %collective-permute-start.75 = (bf16[64,512]{1,0:T(8,128)(2,1)S(1)}, bf16[64,512]{1,0:T(8,128)(2,1)S(1)}, u32[]{:S(2)}, u32[]{:S(2)}) collective-permute-start(bf16[64,512]{1,0:T(8,128)(2,1)S(1)} %fusion.41), channel_id=1, source_target_pairs={{0,1},{1,0},{2,3},{3,2},{4,5},{5,4},{6,7},{7,6},{8,9},{9,8},{10,11... | collective-permute-start | bytes 196616 | tf_op jit(solution)/shard_map/ppermute | solution.py:437
  469.1 15.2 %collective-permute-start.69 = (bf16[2,64,2176]{2,1,0:T(8,128)(2,1)S(1)}, bf16[2,64,2176]{2,1,0:T(8,128)(2,1)S(1)}, u32[]{:S(2)}, u32[]{:S(2)}) collective-permute-start(bf16[2,64,2176]{2,1,0:T(8,128)(2,1)S(1)} %pad_maximum_fusion.11.refs_12_), channel_id=1, source_target_pairs={{0,8},{4,12},{8,0},{12,4},{16,24},{20,28},{24,16},{28,20},{1,9},{5... | collective-permute-start | bytes 1671176 | tf_op jit(solution)/shard_map/ppermute | solution.py:437
  496.8 11.3 %collective-permute-start.72 = (f32[84,128]{1,0:T(8,128)S(1)}, f32[84,128]{1,0:T(8,128)S(1)}, u32[]{:S(2)}, u32[]{:S(2)}) collective-permute-start(f32[84,128]{1,0:T(8,128)S(1)} %pad_maximum_fusion.38), channel_id=1, source_target_pairs={{0,16},{4,20},{8,24},{12,28},{16,0},{20,4},{24,8},{28,12},{1,17},{... | collective-permute-start | bytes 129032 | tf_op jit(solution)/shard_map/ppermute | solution.py:437
  499.6 13.6 %collective-permute-start.73 = (bf16[1,64,2176]{2,1,0:T(8,128)(2,1)S(1)}, bf16[1,64,2176]{2,1,0:T(8,128)(2,1)S(1)}, u32[]{:S(2)}, u32[]{:S(2)}) collective-permute-start(bf16[1,64,2176]{2,1,0:T(8,128)(2,1)S(1)} %copy-done.59), channel_id=1, source_target_pairs={{0,16},{4,20},{8,24},{12,28},{16,0},{20,4},{24,8},{28,12},{1,17},{... | collective-permute-start | bytes 835592 | tf_op jit(solution)/shard_map/ppermute | solution.py:437
  514.3 8.8 %collective-permute-start.74 = (bf16[32,2176]{1,0:T(8,128)(2,1)S(1)}, bf16[32,2176]{1,0:T(8,128)(2,1)S(1)}, u32[]{:S(2)}, u32[]{:S(2)}) collective-permute-start(bf16[32,2176]{1,0:T(8,128)(2,1)S(1)} %fusion.36), channel_id=1, source_target_pairs={{0,1},{1,0},{2,3},{3,2},{4,5},{5,4},{6,7},{7,6},{8,9},{9,8},{10,11... | collective-permute-start | bytes 417800 | tf_op jit(solution)/shard_map/ppermute | solution.py:437
  (105 other events, 685.6 us)

commit v5 on v4

--- a/solution.py
+++ b/solution.py
@@ -18,7 +18,7 @@
 bf16 = jnp.bfloat16
 f32 = jnp.float32
 VMEM_LIMIT = 60 * 1024 * 1024
-PACE = 0.05
+PACE = 0.1
 
 
 def split3(value):

time: 532 us -> 528 us (level)
  waiting for transfers between devices: 99.8 us -> 89.6 us
    ppermute x80, waiting for transfers between devices: 99.8 us -> 89.6 us  [swap(): return lax.ppermute(value, axis, [(i, i ^ bit) for i in range(count)])]
    unnamed x185 -> x187, local copies, waits for them, and re-layouts: 13.7 us -> 13.2 us
  transfers between devices with their start and end apart: 80 -> 80, of which waited for: 29 -> 29; matrix products, arithmetic and copies ran while one was open for 18% -> 19% of each run, Pallas kernels for 41% -> 41%
where the time goes in v5:
time: 528 us; the launch traced here: 522 us
  Pallas kernels  234 us (44%)
  other arithmetic  90.2 us (17%)
  waiting for transfers between devices  89.6 us (17%)
  starting transfers between devices  71.2 us (13%)
  local copies, waits for them, and re-layouts  27.7 us (5%)
  between operations  9.07 us (2%)
    pallas_call x14, Pallas kernels, kernel_call(): pl.pallas_call(run, out_shape=tuple((jax.ShapeDtypeStruct(shape, dtype) f...  137 us
    pallas_call x9, Pallas kernels, grid_call(): pl.pallas_call(run, out_shape=tuple((jax.ShapeDtypeStruct(shape, dtype) f...  90.7 us
    ppermute x80, waiting for transfers between devices, swap(): return lax.ppermute(value, axis, [(i, i ^ bit) for i in range(count)])  89.6 us
    ppermute x80, starting transfers between devices, swap(): return lax.ppermute(value, axis, [(i, i ^ bit) for i in range(count)])  71.2 us
    add x16, other arithmetic, add_low(): return left + right + zero  33.1 us
    concatenate x15, other arithmetic, step(): self.arrays = [jnp.concatenate([mine[0], others[0]], axis=0)]  20.4 us
    unnamed x187, local copies, waits for them, and re-layouts  13.2 us
  transfers between devices with their start and end apart: 80, of which 29 were waited for; matrix products, arithmetic and copies ran while one was open for 19% of the time, Pallas kernels for 41%

profile of v5, /device:TPU:0, one launch (start us, length us, event | category | flops | bytes accessed | tf_op | source)
XLA Modules:
  0.0 521.7 jit_solution(18119916115629455396)
XLA Ops:
  5.2 3.7 collective-permute-start.3
  13.4 4.4 stats.1
  25.0 2.8 collective-permute-done.4
  30.0 3.2 collective-permute-done.5
  33.2 2.4 collective-permute-start.6
  44.6 12.1 %norm.1 = (bf16[512,1024]{1,0:T(8,128)(2,1)}, f32[4096,128]{1,0:T(8,128)}, f32[256,128]{1,0:T(8,128)}) custom-call(bf16[512,1024]{1,0:T(8,128)(2,1)} %bitcast.200, f32[512,1]{1,0:T(8,128)} %copy.86.refs_1_.refs_3_.refs_6_.refs_4_, s32[512,1]{1,0:T(8,128)} %copy.87.refs_2_.refs_3_.refs_6_.refs_7_.refs_5_, ...), custom_call_target="tpu_custom_call" | custom-call | flops 1300000000 | bytes 3900000 | tf_op jit(solution)/shard_map/norm/pallas_call | solution.py:75
  62.8 3.2 collective-permute-done.10
  72.1 2.6 collective-permute-start.17
  78.4 4.7 collective-permute-done.16
  85.6 2.4 collective-permute-done.17
  88.7 2.6 collective-permute-done.13
  95.9 2.6 collective-permute-start.20
  100.5 6.3 %collective-permute-done.19 = bf16[2,32,2560]{2,1,0:T(8,128)(2,1)S(1)} collective-permute-done((bf16[2,32,2560]{2,1,0:T(8,128)(2,1)}, bf16[2,32,2560]{2,1,0:T(8,128)(2,1)S(1)}, u32[]{:S(2)}, u32[]{:S(2)}) %collective-permute-start.19) | collective-permute-done | bytes 327712 | tf_op jit(solution)/shard_map/ppermute | solution.py:437
  108.7 3.3 collective-permute-done.18
  113.4 14.7 %mix.1 = (f32[4096,128]{1,0:T(8,128)}, bf16[512,1024]{1,0:T(8,128)(2,1)}, f32[16,256,128]{2,1,0:T(8,128)}) custom-call(f32[4096,128]{1,0:T(8,128)} %get-tuple-element.89.refs_0_, f32[256,128]{1,0:T(8,128)} %bitcast.205, f32[128,128]{1,0:T(8,128)} %bitcast.220, f32[128,128]{1,0:T(8,128)} %bitcast.213, f32[128,128]{1,0:T(8,128)} %bitcast.226, ...), custom_call_target="tpu_custom_call" | custom-call | flops 1600000000 | bytes 4800000 | tf_op jit(solution)/shard_map/mix/pallas_call | solution.py:75
  128.9 2.3 collective-permute-done.23.refs_3_.refs_14_.refs_10_.refs_20_.refs_9_
  131.2 2.2 collective-permute-start.27
  137.4 2.5 pad_maximum_fusion.4.refs_0_
  139.9 3.7 collective-permute-done.27
  144.9 2.3 pad_maximum_fusion.3.refs_18_.refs_0_.refs_2_
  147.2 2.3 pad_maximum_fusion.2.refs_17_.refs_0_.refs_1_
  156.6 13.3 %attention.1 = (f32[512,256]{1,0:T(8,128)}, bf16[512,256]{1,0:T(8,128)(2,1)}, bf16[512,256]{1,0:T(8,128)(2,1)}, f32[512,1]{1,0:T(8,128)}, bf16[512,2048]{1,0:T(8...) custom-call(s32[2]{0:T(128)} %pad_add_fusion.refs_0_, ...), custom_call_target="tpu_custom_call" | custom-call | flops 1500000000 | bytes 4500000 | tf_op jit(solution)/shard_map/attention/pallas_call | solution.py:102
  170.0 7.9 %project.1 = (f32[512,1024]{1,0:T(8,128)}, bf16[512,1024]{1,0:T(8,128)(2,1)}, f32[512,1]{1,0:T(8,128)}) custom-call(s32[2]{0:T(128)} %pad_add_fusion.refs_0_, bf16[512,2048]{1,0:T(8,128)(2,1)} %get-tuple-element.93.refs_1_, bf16[512,1024]{1,0:T(8,128)(2,1)} %bitcast.201, f32[512,1]{1,0:T(8,128)} %copy.86.refs_1_.refs_3_.refs_6_.refs_4_, ...), custom_call_target="tpu_custom_call" | custom-call | flops 600000000 | bytes 1800000 | tf_op jit(solution)/shard_map/project/pallas_call | solution.py:75
  177.8 3.2 collective-permute-done.36.refs_0_
  182.1 2.4 dynamic-slice_bitcast_fusion
  185.5 3.3 collective-permute-done.39.refs_15_.refs_4_
  189.8 5.3 %collective-permute-done.34.refs_10_.refs_14_ = bf16[8,32,2560]{2,1,0:T(8,128)(2,1)S(1)} collective-permute-done((bf16[8,32,2560]{2,1,0:T(8,128)(2,1)}, bf16[8,32,2560]{2,1,0:T(8,128)(2,1)S(1)}, u32[]{:S(2)}, u32[]{:S(2)}) %collective-permute-start.34) | collective-permute-done | bytes 1310752 | tf_op jit(solution)/shard_map/ppermute | solution.py:437
  195.2 3.7 collective-permute-done.31.refs_6_.refs_10_
  200.4 19.0 %hidden.1 = (bf16[512,2560]{1,0:T(8,128)(2,1)}, bf16[512,2560]{1,0:T(8,128)(2,1)}, bf16[512,2560]{1,0:T(8,128)(2,1)}) custom-call(s32[2]{0:T(128)} %pad_add_fusion.refs_0_, bf16[512,1024]{1,0:T(8,128)(2,1)} %get-tuple-element.94.refs_1_, bf16[512,1024]{1,0:T(8,128)(2,1)} %bitcast.197, bf16[8,32,2560]{2,1,0:T(8,128)(2,1)} %tie.55.refs_3_.refs_7_, ...), custom_call_target="tpu_custom_call" | custom-call | flops 1500000000 | bytes 4500000 | tf_op jit(solution)/shard_map/hidden/pallas_call | solution.py:102
  220.2 8.2 %out.1.refs_5_ = bf16[512,1024]{1,0:T(8,128)(2,1)} custom-call(s32[2]{0:T(128)} %pad_add_fusion.refs_0_, bf16[512,2560]{1,0:T(8,128)(2,1)} %get-tuple-element.95.refs_1_, f32[512,1024]{1,0:T(8,128)} %get-tuple-element.96.refs_2_.refs_3_, bf16[8,80,1024]{2,1,0:T(8,128)(2,1)} %tie.61.refs_11_.refs_3_, bf16[8,80,1024]{2,1,0:T(8,128)(2,1)} %tie.62.refs_12_.refs_4_, ...), custom_call_target="tpu_custom_call" | custom-call | flops 700000000 | bytes 2100000 | tf_op jit(solution)/shard_map/out/pallas_call | solution.py:75
  228.4 7.5 %grad_down.1 = (bf16[8,160,512]{2,1,0:T(8,128)(2,1)}, bf16[8,160,512]{2,1,0:T(8,128)(2,1)}) custom-call(s32[2]{0:T(128)} %pad_add_fusion.refs_0_, bf16[512,2560]{1,0:T(8,128)(2,1)} %get-tuple-element.95.refs_1_, bf16[512,2560]{1,0:T(8,128)(2,1)} %collective-permute-done.44.refs_2_, bf16[512,512]{1,0:T(8,128)(2,1)} %get-tuple-element.191.refs_3_, ...), custom_call_target="tpu_custom_call" | custom-call | flops 600000000 | bytes 1800000 | tf_op jit(solution)/shard_map/grad_down/pallas_call | solution.py:102
  239.1 7.0 %grad_gate.1 = (bf16[8,64,1280]{2,1,0:T(8,128)(2,1)}, bf16[8,64,1280]{2,1,0:T(8,128)(2,1)}) custom-call(s32[2]{0:T(128)} %pad_add_fusion.refs_0_, bf16[512,1024]{1,0:T(8,128)(2,1)} %get-tuple-element.94.refs_1_, bf16[512,1024]{1,0:T(8,128)(2,1)} %collective-permute-done.42.refs_2_, bf16[512,2560]{1,0:T(8,128)(2,1)} %get-tuple-element.97.refs_3_.refs_1_, ...), custom_call_target="tpu_custom_call" | custom-call | flops 600000000 | bytes 1800000 | tf_op jit(solution)/shard_map/grad_gate/pallas_call | solution.py:102
  247.2 7.2 %grad_up.1 = (bf16[8,64,1280]{2,1,0:T(8,128)(2,1)}, bf16[8,64,1280]{2,1,0:T(8,128)(2,1)}) custom-call(s32[2]{0:T(128)} %pad_add_fusion.refs_0_, bf16[512,1024]{1,0:T(8,128)(2,1)} %get-tuple-element.94.refs_1_, bf16[512,1024]{1,0:T(8,128)(2,1)} %collective-permute-done.42.refs_2_, bf16[512,2560]{1,0:T(8,128)(2,1)} %get-tuple-element.97.refs_3_.refs_1_, ...), custom_call_target="tpu_custom_call" | custom-call | flops 600000000 | bytes 1800000 | tf_op jit(solution)/shard_map/grad_up/pallas_call | solution.py:102
  254.4 14.9 %ffn_back.1 = (f32[512,1024]{1,0:T(8,128)}, bf16[512,512]{1,0:T(8,128)(2,1)}, bf16[512,512]{1,0:T(8,128)(2,1)}, bf16[512,1024]{1,0:T(8,128)(2,1)}, f32[1,1024]{1,0:T(1,128)}) custom-call(s32[2]{0:T(128)} %pad_add_fusion.refs_0_, bf16[512,2560]{1,0:T(8,128)(2,1)} %get-tuple-element.97.refs_3_.refs_1_, bf16[512,2560]{1,0:T(8,128)(2,1)} %get-tuple-element.98.refs_2_, ...), custom_call_target="tpu_custom_call" | custom-call | flops 1700000000 | bytes 5100000 | tf_op jit(solution)/shard_map/ffn_back/pallas_call | solution.py:75
  275.0 2.9 fusion.2
  278.8 6.9 %grad_h.1 = (bf16[8,128,512]{2,1,0:T(8,128)(2,1)}, bf16[8,128,512]{2,1,0:T(8,128)(2,1)}) custom-call(s32[2]{0:T(128)} %pad_add_fusion.refs_0_, bf16[512,2048]{1,0:T(8,128)(2,1)} %get-tuple-element.93.refs_1_, bf16[512,2048]{1,0:T(8,128)(2,1)} %collective-permute-done.40.refs_16_.refs_2_, bf16[512,512]{1,0:T(8,128)(2,1)} %get-tuple-element.112.refs_1_.refs_3_, ...), custom_call_target="tpu_custom_call" | custom-call | flops 600000000 | bytes 1800000 | tf_op jit(solution)/shard_map/grad_h/pallas_call | solution.py:102
  288.2 16.6 %attention_back.1 = (bf16[512,2048]{1,0:T(8,128)(2,1)}, bf16[512,2048]{1,0:T(8,128)(2,1)}, bf16[512,1024]{1,0:T(8,128)(2,1)}, bf16[512,1024]{1,0:T(8,128)(2,1)},...) custom-call(s32[2]{0:T(128)} %pad_add_fusion.refs_0_, ...), custom_call_target="tpu_custom_call" | custom-call | flops 1900000000 | bytes 5700000 | tf_op jit(solution)/shard_map/attention_back/pallas_call | solution.py:102
  308.1 3.3 fusion
  315.3 10.6 %sent_back.1 = (bf16[512,1024]{1,0:T(8,128)(2,1)}, bf16[512,1024]{1,0:T(8,128)(2,1)}) custom-call(s32[2]{0:T(128)} %pad_add_fusion.refs_0_, bf16[512,2048]{1,0:T(8,128)(2,1)} %get-tuple-element.117.refs_1_, bf16[512,2048]{1,0:T(8,128)(2,1)} %get-tuple-element.118.refs_2_, bf16[512,256]{1,0:T(8,128)(2,1)} %get-tuple-element.119.refs_3_, ...), custom_call_target="tpu_custom_call" | custom-call | flops 1100000000 | bytes 3300000 | tf_op jit(solution)/shard_map/sent_back/pallas_call | solution.py:75
  327.1 2.2 fusion.34.refs_5_
  329.3 4.0 collective-permute-done.50
  334.2 2.9 fusion.10
  337.1 11.9 %back_ends.1 = (f32[4096,128]{1,0:T(8,128)}, f32[256,128]{1,0:T(8,128)}) custom-call(bf16[512,1024]{1,0:T(8,128)(2,1)} %get-tuple-element.122.refs_1_.refs_0_, f32[4096,128]{1,0:T(8,128)} %get-tuple-element.92.refs_1_, f32[128,128]{1,0:T(8,128)} %bitcast.221, f32[128,128]{1,0:T(8,128)} %bitcast.214, bf16[4,128,512]{2,1,0:T(8,128)(2,1)} %get-tuple-element.178.refs_4_, ...), custom_call_target="tpu_custom_call" | custom-call | flops 1200000000 | bytes 3600000 | tf_op jit(solution)/shard_map/back_ends/pallas_call | solution.py:75
  358.6 6.3 %grad_v.1 = (bf16[8,64,1024]{2,1,0:T(8,128)(2,1)}, bf16[8,64,1024]{2,1,0:T(8,128)(2,1)}) custom-call(s32[2]{0:T(128)} %pad_add_fusion.refs_0_, bf16[512,1024]{1,0:T(8,128)(2,1)} %get-tuple-element.88.refs_1_, bf16[512,1024]{1,0:T(8,128)(2,1)} %collective-permute-done.28.refs_19_.refs_2_, bf16[512,1024]{1,0:T(8,128)(2,1)} %get-tuple-element.127.refs_3_, ...), custom_call_target="tpu_custom_call" | custom-call | flops 600000000 | bytes 1800000 | tf_op jit(solution)/shard_map/grad_v/pallas_call | solution.py:102
  366.0 2.3 add_add_fusion.2.refs_7_
  368.4 7.0 %grad_r.1 = (bf16[8,64,1152]{2,1,0:T(8,128)(2,1)}, bf16[8,64,1152]{2,1,0:T(8,128)(2,1)}) custom-call(s32[2]{0:T(128)} %pad_add_fusion.refs_0_, bf16[512,1024]{1,0:T(8,128)(2,1)} %get-tuple-element.91.refs_2_.refs_1_, bf16[512,1024]{1,0:T(8,128)(2,1)} %collective-permute-done.41.refs_17_.refs_2_, bf16[512,1152]{1,0:T(8,128)(2,1)} %get-tuple-element.130.refs_3_, ...), custom_call_target="tpu_custom_call" | custom-call | flops 600000000 | bytes 1800000 | tf_op jit(solution)/shard_map/grad_r/pallas_call | solution.py:102
  379.4 2.5 collective-permute-done.55
  386.0 6.5 %collective-permute-done.59 = f32[32,8,128]{2,1,0:T(8,128)S(1)} collective-permute-done((f32[32,8,128]{2,1,0:T(8,128)}, f32[32,8,128]{2,1,0:T(8,128)S(1)}, u32[]{:S(2)}, u32[]{:S(2)}) %collective-permute-start.59) | collective-permute-done | bytes 131104 | tf_op jit(solution)/shard_map/ppermute | solution.py:437
  393.2 2.5 fusion.30
  397.4 2.7 collective-permute-start.65
  400.8 9.8 %back.4 = (f32[1024,128]{1,0:T(8,128)}, f32[256,128]{1,0:T(8,128)}, f32[392,128]{1,0:T(8,128)}) custom-call(f32[4096,128]{1,0:T(8,128)} %get-tuple-element.89.refs_0_, f32[4096,128]{1,0:T(8,128)} %get-tuple-element.124.refs_1_, f32[16,256,128]{2,1,0:T(8,128)} %get-tuple-element.125.refs_2_, f32[256,128]{1,0:T(8,128)} %maximum_bitcast_fusion.2.refs_3_, ...), custom_call_target="tpu_custom_call" | custom-call | flops 1000000000 | bytes 3000000 | tf_op jit(solution)/shard_map/back/pallas_call | solution.py:75
  415.6 9.9 %back.5 = (f32[1024,128]{1,0:T(8,128)}, f32[256,128]{1,0:T(8,128)}, f32[392,128]{1,0:T(8,128)}) custom-call(f32[4096,128]{1,0:T(8,128)} %get-tuple-element.89.refs_0_, f32[4096,128]{1,0:T(8,128)} %get-tuple-element.124.refs_1_, f32[16,256,128]{2,1,0:T(8,128)} %get-tuple-element.125.refs_2_, f32[256,128]{1,0:T(8,128)} %get-tuple-element.132.refs_3_, ...), custom_call_target="tpu_custom_call" | custom-call | flops 1000000000 | bytes 3000000 | tf_op jit(solution)/shard_map/back/pallas_call | solution.py:75
  429.5 2.1 fusion.6
  433.2 9.7 %back.6 = (f32[1024,128]{1,0:T(8,128)}, f32[256,128]{1,0:T(8,128)}, f32[392,128]{1,0:T(8,128)}) custom-call(f32[4096,128]{1,0:T(8,128)} %get-tuple-element.89.refs_0_, f32[4096,128]{1,0:T(8,128)} %get-tuple-element.124.refs_1_, f32[16,256,128]{2,1,0:T(8,128)} %get-tuple-element.125.refs_2_, f32[256,128]{1,0:T(8,128)} %get-tuple-element.136.refs_3_, ...), custom_call_target="tpu_custom_call" | custom-call | flops 1000000000 | bytes 3000000 | tf_op jit(solution)/shard_map/back/pallas_call | solution.py:75
  446.4 9.8 %back.7 = (f32[1024,128]{1,0:T(8,128)}, f32[256,128]{1,0:T(8,128)}, f32[392,128]{1,0:T(8,128)}) custom-call(f32[4096,128]{1,0:T(8,128)} %get-tuple-element.89.refs_0_, f32[4096,128]{1,0:T(8,128)} %get-tuple-element.124.refs_1_, f32[16,256,128]{2,1,0:T(8,128)} %get-tuple-element.125.refs_2_, f32[256,128]{1,0:T(8,128)} %get-tuple-element.140.refs_3_, ...), custom_call_target="tpu_custom_call" | custom-call | flops 1000000000 | bytes 3000000 | tf_op jit(solution)/shard_map/back/pallas_call | solution.py:75
  465.3 2.1 collective-permute-start.69
  467.4 6.9 %back_norm.1 = (f32[512,1024]{1,0:T(8,128)}, f32[1,1024]{1,0:T(1,128)}, f32[512,128]{1,0:T(8,128)}, f32[16,128]{1,0:T(8,128)}) custom-call(f32[1024,128]{1,0:T(8,128)} %get-tuple-element.143.refs_1_.refs_0_, f32[1024,128]{1,0:T(8,128)} %get-tuple-element.142.refs_1_, f32[1024,128]{1,0:T(8,128)} %get-tuple-element.139.refs_1_.refs_2_, ...), custom_call_target="tpu_custom_call" | custom-call | flops 600000000 | bytes 1800000 | tf_op jit(solution)/shard_map/back_norm/pallas_call | solution.py:75
  475.7 4.8 collective-permute-done.69
  484.6 3.7 collective-permute-done.70
  490.8 2.1 collective-permute-done.71
  492.9 2.1 collective-permute-start.72
  496.7 7.6 %collective-permute-done.72 = f32[84,128]{1,0:T(8,128)S(1)} collective-permute-done((f32[84,128]{1,0:T(8,128)S(1)}, f32[84,128]{1,0:T(8,128)S(1)}, u32[]{:S(2)}, u32[]{:S(2)}) %collective-permute-start.72) | collective-permute-done | bytes 43040 | tf_op jit(solution)/shard_map/ppermute | solution.py:437
  506.1 3.2 collective-permute-done.73
  510.7 5.9 %input.1 = f32[512,1024]{1,0:T(8,128)} custom-call(f32[512,1024]{1,0:T(8,128)} %get-tuple-element.145.refs_0_, f32[512,128]{1,0:T(8,128)} %get-tuple-element.146.refs_1_, f32[1,128]{1,0:T(1,128)} %fusion.53.refs_1_.refs_2_, bf16[512,1024]{1,0:T(8,128)(2,1)} %bitcast.203, f32[512,1]{1,0:T(8,128)} %copy.86.refs_1_.refs_3_.refs_6_.refs_4_, ...), custom_call_target="tpu_custom_call" | custom-call | flops 600000000 | bytes 1800000 | tf_op jit(solution)/shard_map/input/pallas_call | solution.py:75
  (512 shorter events, 153.2 us)
Async XLA Ops:
  2.8 8.8 %collective-permute-start = (f32[1,1,56]{2,1,0:T(1,128)S(1)}, f32[1,1,56]{2,1,0:T(1,128)S(1)}, u32[]{:S(2)}, u32[]{:S(2)}) collective-permute-start(f32[1,1,56]{2,1,0:T(1,128)S(1)} %maximum_convert_fusion), channel_id=1, source_target_pairs={{0,1},{1,0},{2,3},{3,2},{4,5},{5,4},{6,7},{7,6},{8,9},{9,8},{10,11... | collective-permute-start | bytes 680 | tf_op jit(solution)/shard_map/ppermute | solution.py:437
  5.2 19.0 %collective-permute-start.3 = (bf16[1,32,3072]{2,1,0:T(8,128)(2,1)S(1)}, bf16[1,32,3072]{2,1,0:T(8,128)(2,1)S(1)}, u32[]{:S(2)}, u32[]{:S(2)}) collective-permute-start(bf16[1,32,3072]{2,1,0:T(8,128)(2,1)S(1)} %maximum_bitcast_fusion.1), channel_id=1, source_target_pairs={{0,16},{4,20},{8,24},{12,28},{16,0},{20,4},{24,8},{28,12},{1,17},{... | collective-permute-start | bytes 589832 | tf_op jit(solution)/shard_map/ppermute | solution.py:437
  9.0 18.8 %collective-permute-start.4 = (bf16[1,32,3328]{2,1,0:T(8,128)(2,1)S(1)}, bf16[1,32,3328]{2,1,0:T(8,128)(2,1)S(1)}, u32[]{:S(2)}, u32[]{:S(2)}) collective-permute-start(bf16[1,32,3328]{2,1,0:T(8,128)(2,1)S(1)} %maximum_bitcast_fusion), channel_id=1, source_target_pairs={{0,16},{4,20},{8,24},{12,28},{16,0},{20,4},{24,8},{28,12},{1,17},{... | collective-permute-start | bytes 638984 | tf_op jit(solution)/shard_map/ppermute | solution.py:437
  20.3 19.2 %collective-permute-start.7 = (bf16[1,80,1024]{2,1,0:T(8,128)(2,1)S(1)}, bf16[1,80,1024]{2,1,0:T(8,128)(2,1)S(1)}, u32[]{:S(2)}, u32[]{:S(2)}) collective-permute-start(bf16[1,80,1024]{2,1,0:T(8,128)(2,1)S(1)} %convert_bitcast_fusion.2), channel_id=1, source_target_pairs={{0,2},{2,0},{1,3},{3,1},{4,6},{6,4},{5,7},{7,5},{8,10},{10,8},{9,1... | collective-permute-start | bytes 491528 | tf_op jit(solution)/shard_map/ppermute | solution.py:437
  33.2 9.1 %collective-permute-start.6 = (f32[288,128]{1,0:T(8,128)S(1)}, f32[288,128]{1,0:T(8,128)S(1)}, u32[]{:S(2)}, u32[]{:S(2)}) collective-permute-start(f32[288,128]{1,0:T(8,128)S(1)} %pad_maximum_fusion.27), channel_id=1, source_target_pairs={{0,16},{4,20},{8,24},{12,28},{16,0},{20,4},{24,8},{28,12},{1,17},{... | collective-permute-start | bytes 442376 | tf_op jit(solution)/shard_map/ppermute | solution.py:437
  40.3 18.0 %collective-permute-start.8 = (bf16[2,32,3072]{2,1,0:T(8,128)(2,1)S(1)}, bf16[2,32,3072]{2,1,0:T(8,128)(2,1)}, u32[]{:S(2)}, u32[]{:S(2)}) collective-permute-start(bf16[2,32,3072]{2,1,0:T(8,128)(2,1)S(1)} %copy-done.30), channel_id=1, source_target_pairs={{0,8},{4,12},{8,0},{12,4},{16,24},{20,28},{24,16},{28,20},{1,9},{5... | collective-permute-start | bytes 1179656 | tf_op jit(solution)/shard_map/ppermute | solution.py:437
  42.1 18.5 %collective-permute-start.9 = (bf16[2,32,3328]{2,1,0:T(8,128)(2,1)S(1)}, bf16[2,32,3328]{2,1,0:T(8,128)(2,1)}, u32[]{:S(2)}, u32[]{:S(2)}) collective-permute-start(bf16[2,32,3328]{2,1,0:T(8,128)(2,1)S(1)} %copy-done.54), channel_id=1, source_target_pairs={{0,8},{4,12},{8,0},{12,4},{16,24},{20,28},{24,16},{28,20},{1,9},{5... | collective-permute-start | bytes 1277960 | tf_op jit(solution)/shard_map/ppermute | solution.py:437
  56.7 9.3 %collective-permute-start.10 = (bf16[2,80,1024]{2,1,0:T(8,128)(2,1)}, bf16[2,80,1024]{2,1,0:T(8,128)(2,1)}, u32[]{:S(2)}, u32[]{:S(2)}) collective-permute-start(bf16[2,80,1024]{2,1,0:T(8,128)(2,1)} %tie.41), channel_id=1, source_target_pairs={{0,4},{4,0},{8,12},{12,8},{16,20},{20,16},{24,28},{28,24},{1,5},{5... | collective-permute-start | bytes 983048 | tf_op jit(solution)/shard_map/ppermute | solution.py:437
  69.5 13.6 %collective-permute-start.16 = (bf16[1,32,2560]{2,1,0:T(8,128)(2,1)S(1)}, bf16[1,32,2560]{2,1,0:T(8,128)(2,1)S(1)}, u32[]{:S(2)}, u32[]{:S(2)}) collective-permute-start(bf16[1,32,2560]{2,1,0:T(8,128)(2,1)S(1)} %copy-done.55), channel_id=1, source_target_pairs={{0,16},{4,20},{8,24},{12,28},{16,0},{20,4},{24,8},{28,12},{1,17},{... | collective-permute-start | bytes 491528 | tf_op jit(solution)/shard_map/ppermute | solution.py:437
  69.5 22.5 %collective-permute-start.14 = (bf16[4,32,3072]{2,1,0:T(8,128)(2,1)S(1)}, bf16[4,32,3072]{2,1,0:T(8,128)(2,1)S(1)}, u32[]{:S(2)}, u32[]{:S(2)}) collective-permute-start(bf16[4,32,3072]{2,1,0:T(8,128)(2,1)S(1)} %copy-done.18), channel_id=1, source_target_pairs={{0,4},{4,0},{8,12},{12,8},{16,20},{20,16},{24,28},{28,24},{1,5},{5... | collective-permute-start | bytes 2359304 | tf_op jit(solution)/shard_map/ppermute | solution.py:437
  70.7 22.7 %collective-permute-start.15 = (bf16[4,32,3328]{2,1,0:T(8,128)(2,1)S(1)}, bf16[4,32,3328]{2,1,0:T(8,128)(2,1)S(1)}, u32[]{:S(2)}, u32[]{:S(2)}) collective-permute-start(bf16[4,32,3328]{2,1,0:T(8,128)(2,1)S(1)} %copy-done.17), channel_id=1, source_target_pairs={{0,2},{2,0},{1,3},{3,1},{4,6},{6,4},{5,7},{7,5},{8,10},{10,8},{9,1... | collective-permute-start | bytes 2555912 | tf_op jit(solution)/shard_map/ppermute | solution.py:437
  72.1 15.8 %collective-permute-start.17 = (bf16[1,32,2560]{2,1,0:T(8,128)(2,1)S(1)}, bf16[1,32,2560]{2,1,0:T(8,128)(2,1)S(1)}, u32[]{:S(2)}, u32[]{:S(2)}) collective-permute-start(bf16[1,32,2560]{2,1,0:T(8,128)(2,1)S(1)} %copy-done.56), channel_id=1, source_target_pairs={{0,16},{4,20},{8,24},{12,28},{16,0},{20,4},{24,8},{28,12},{1,17},{... | collective-permute-start | bytes 491528 | tf_op jit(solution)/shard_map/ppermute | solution.py:437
  94.7 36.5 %collective-permute-start.23 = (bf16[8,32,3328]{2,1,0:T(8,128)(2,1)}, bf16[8,32,3328]{2,1,0:T(8,128)(2,1)}, u32[]{:S(2)}, u32[]{:S(2)}) collective-permute-start(bf16[8,32,3328]{2,1,0:T(8,128)(2,1)} %tie.51.refs_13_.refs_9_.refs_19_.refs_8_), channel_id=1, source_target_pairs={{0,4},{4,0},{8,12},{12,8},{16,20},{20,16},{24,28},{28,24},{1,5},{5... | collective-permute-start | bytes 5111816 | tf_op jit(solution)/shard_map/ppermute | solution.py:437
  95.9 33.0 %collective-permute-start.20 = (bf16[8,32,3072]{2,1,0:T(8,128)(2,1)}, bf16[8,32,3072]{2,1,0:T(8,128)(2,1)}, u32[]{:S(2)}, u32[]{:S(2)}) collective-permute-start(bf16[8,32,3072]{2,1,0:T(8,128)(2,1)} %tie.50.refs_9_.refs_5_.refs_15_.refs_4_), channel_id=1, source_target_pairs={{0,2},{2,0},{1,3},{3,1},{4,6},{6,4},{5,7},{7,5},{8,10},{10,8},{9,1... | collective-permute-start | bytes 4718600 | tf_op jit(solution)/shard_map/ppermute | solution.py:437
  98.5 8.3 %collective-permute-start.19 = (bf16[2,32,2560]{2,1,0:T(8,128)(2,1)}, bf16[2,32,2560]{2,1,0:T(8,128)(2,1)S(1)}, u32[]{:S(2)}, u32[]{:S(2)}) collective-permute-start(bf16[2,32,2560]{2,1,0:T(8,128)(2,1)} %tie.49), channel_id=1, source_target_pairs={{0,8},{4,12},{8,0},{12,4},{16,24},{20,28},{24,16},{28,20},{1,9},{5... | collective-permute-start | bytes 983048 | tf_op jit(solution)/shard_map/ppermute | solution.py:437
  98.5 13.4 %collective-permute-start.18 = (bf16[2,32,2560]{2,1,0:T(8,128)(2,1)}, bf16[2,32,2560]{2,1,0:T(8,128)(2,1)S(1)}, u32[]{:S(2)}, u32[]{:S(2)}) collective-permute-start(bf16[2,32,2560]{2,1,0:T(8,128)(2,1)} %tie.48), channel_id=1, source_target_pairs={{0,8},{4,12},{8,0},{12,4},{16,24},{20,28},{24,16},{28,20},{1,9},{5... | collective-permute-start | bytes 983048 | tf_op jit(solution)/shard_map/ppermute | solution.py:437
  112.9 24.4 %collective-permute-start.35 = (bf16[4,80,1024]{2,1,0:T(8,128)(2,1)}, bf16[4,80,1024]{2,1,0:T(8,128)(2,1)}, u32[]{:S(2)}, u32[]{:S(2)}) collective-permute-start(bf16[4,80,1024]{2,1,0:T(8,128)(2,1)} %tie.59), channel_id=1, source_target_pairs={{0,16},{4,20},{8,24},{12,28},{16,0},{20,4},{24,8},{28,12},{1,17},{... | collective-permute-start | bytes 1966088 | tf_op jit(solution)/shard_map/ppermute | solution.py:437
  131.2 12.4 %collective-permute-start.27 = (bf16[4,32,2560]{2,1,0:T(8,128)(2,1)}, bf16[4,32,2560]{2,1,0:T(8,128)(2,1)}, u32[]{:S(2)}, u32[]{:S(2)}) collective-permute-start(bf16[4,32,2560]{2,1,0:T(8,128)(2,1)} %tie.53), channel_id=1, source_target_pairs={{0,2},{2,0},{1,3},{3,1},{4,6},{6,4},{5,7},{7,5},{8,10},{10,8},{9,1... | collective-permute-start | bytes 1966088 | tf_op jit(solution)/shard_map/ppermute | solution.py:437
  133.4 11.5 %collective-permute-start.26 = (bf16[4,32,2560]{2,1,0:T(8,128)(2,1)}, bf16[4,32,2560]{2,1,0:T(8,128)(2,1)}, u32[]{:S(2)}, u32[]{:S(2)}) collective-permute-start(bf16[4,32,2560]{2,1,0:T(8,128)(2,1)} %tie.52), channel_id=1, source_target_pairs={{0,4},{4,0},{8,12},{12,8},{16,20},{20,16},{24,28},{28,24},{1,5},{5... | collective-permute-start | bytes 1966088 | tf_op jit(solution)/shard_map/ppermute | solution.py:437
  135.5 14.0 %collective-permute-start.28 = (bf16[512,1024]{1,0:T(8,128)(2,1)}, bf16[512,1024]{1,0:T(8,128)(2,1)}, u32[]{:S(2)}, u32[]{:S(2)}) collective-permute-start(bf16[512,1024]{1,0:T(8,128)(2,1)} %tie.54), channel_id=1, source_target_pairs={{0,1},{1,0},{2,3},{3,2},{4,5},{5,4},{6,7},{7,6},{8,9},{9,8},{10,11... | collective-permute-start | bytes 3145736 | tf_op jit(solution)/shard_map/ppermute | solution.py:437
  136.9 13.7 %collective-permute-start.21 = (bf16[8,32,3072]{2,1,0:T(8,128)(2,1)S(1)}, bf16[8,32,3072]{2,1,0:T(8,128)(2,1)}, u32[]{:S(2)}, u32[]{:S(2)}) collective-permute-start(bf16[8,32,3072]{2,1,0:T(8,128)(2,1)S(1)} %copy-done.2), channel_id=1, source_target_pairs={{0,1},{1,0},{2,3},{3,2},{4,5},{5,4},{6,7},{7,6},{8,9},{9,8},{10,11... | collective-permute-start | bytes 4718600 | tf_op jit(solution)/shard_map/ppermute | solution.py:437
  137.4 14.1 %collective-permute-start.24 = (bf16[8,32,3328]{2,1,0:T(8,128)(2,1)S(1)}, bf16[8,32,3328]{2,1,0:T(8,128)(2,1)}, u32[]{:S(2)}, u32[]{:S(2)}) collective-permute-start(bf16[8,32,3328]{2,1,0:T(8,128)(2,1)S(1)} %copy-done.1), channel_id=1, source_target_pairs={{0,1},{1,0},{2,3},{3,2},{4,5},{5,4},{6,7},{7,6},{8,9},{9,8},{10,11... | collective-permute-start | bytes 5111816 | tf_op jit(solution)/shard_map/ppermute | solution.py:437
  143.6 13.0 %collective-permute-start.22 = (bf16[8,32,3072]{2,1,0:T(8,128)(2,1)}, bf16[8,32,3072]{2,1,0:T(8,128)(2,1)}, u32[]{:S(2)}, u32[]{:S(2)}) collective-permute-start(bf16[8,32,3072]{2,1,0:T(8,128)(2,1)} %collective-permute-done.20.refs_2_.refs_10_.refs_6_.refs_16_.refs_5_), channel_id=1, source_target_pairs={{0,1},{1,0},{2,3},{3,2},{4,5},{5,4},{6,7},{7,6},{8,9},{9,8},{10,11... | collective-permute-start | bytes 4718600 | tf_op jit(solution)/shard_map/ppermute | solution.py:437
  144.9 11.7 %collective-permute-start.25 = (bf16[8,32,3328]{2,1,0:T(8,128)(2,1)}, bf16[8,32,3328]{2,1,0:T(8,128)(2,1)}, u32[]{:S(2)}, u32[]{:S(2)}) collective-permute-start(bf16[8,32,3328]{2,1,0:T(8,128)(2,1)} %collective-permute-done.23.refs_3_.refs_14_.refs_10_.refs_20_.refs_9_), channel_id=1, source_target_pairs={{0,1},{1,0},{2,3},{3,2},{4,5},{5,4},{6,7},{7,6},{8,9},{9,8},{10,11... | collective-permute-start | bytes 5111816 | tf_op jit(solution)/shard_map/ppermute | solution.py:437
  149.5 31.5 %collective-permute-start.36 = (bf16[8,80,1024]{2,1,0:T(8,128)(2,1)}, bf16[8,80,1024]{2,1,0:T(8,128)(2,1)}, u32[]{:S(2)}, u32[]{:S(2)}) collective-permute-start(bf16[8,80,1024]{2,1,0:T(8,128)(2,1)} %tie.60.refs_0_), channel_id=1, source_target_pairs={{0,8},{4,12},{8,0},{12,4},{16,24},{20,28},{24,16},{28,20},{1,9},{5... | collective-permute-start | bytes 3932168 | tf_op jit(solution)/shard_map/ppermute | solution.py:437
  150.6 31.1 %collective-permute-start.32 = (bf16[8,32,2560]{2,1,0:T(8,128)(2,1)}, bf16[8,32,2560]{2,1,0:T(8,128)(2,1)S(1)}, u32[]{:S(2)}, u32[]{:S(2)}) collective-permute-start(bf16[8,32,2560]{2,1,0:T(8,128)(2,1)} %pad_maximum_fusion.3.refs_18_.refs_0_.refs_2_), channel_id=1, source_target_pairs={{0,4},{4,0},{8,12},{12,8},{16,20},{20,16},{24,28},{28,24},{1,5},{5... | collective-permute-start | bytes 3932168 | tf_op jit(solution)/shard_map/ppermute | solution.py:437
  151.5 33.0 %collective-permute-start.29 = (bf16[8,32,2560]{2,1,0:T(8,128)(2,1)}, bf16[8,32,2560]{2,1,0:T(8,128)(2,1)S(1)}, u32[]{:S(2)}, u32[]{:S(2)}) collective-permute-start(bf16[8,32,2560]{2,1,0:T(8,128)(2,1)} %pad_maximum_fusion.2.refs_17_.refs_0_.refs_1_), channel_id=1, source_target_pairs={{0,2},{2,0},{1,3},{3,1},{4,6},{6,4},{5,7},{7,5},{8,10},{10,8},{9,1... | collective-permute-start | bytes 3932168 | tf_op jit(solution)/shard_map/ppermute | solution.py:437
  181.0 8.3 %collective-permute-start.38 = (bf16[8,80,1024]{2,1,0:T(8,128)(2,1)}, bf16[8,80,1024]{2,1,0:T(8,128)(2,1)}, u32[]{:S(2)}, u32[]{:S(2)}) collective-permute-start(bf16[8,80,1024]{2,1,0:T(8,128)(2,1)} %tie.62.refs_12_.refs_4_), channel_id=1, source_target_pairs={{0,1},{1,0},{2,3},{3,2},{4,5},{5,4},{6,7},{7,6},{8,9},{9,8},{10,11... | collective-permute-start | bytes 3932168 | tf_op jit(solution)/shard_map/ppermute | solution.py:437
  181.0 8.6 %collective-permute-start.37 = (bf16[8,80,1024]{2,1,0:T(8,128)(2,1)}, bf16[8,80,1024]{2,1,0:T(8,128)(2,1)}, u32[]{:S(2)}, u32[]{:S(2)}) collective-permute-start(bf16[8,80,1024]{2,1,0:T(8,128)(2,1)} %tie.61.refs_11_.refs_3_), channel_id=1, source_target_pairs={{0,1},{1,0},{2,3},{3,2},{4,5},{5,4},{6,7},{7,6},{8,9},{9,8},{10,11... | collective-permute-start | bytes 3932168 | tf_op jit(solution)/shard_map/ppermute | solution.py:437
  181.7 17.2 %collective-permute-start.40 = (bf16[512,2048]{1,0:T(8,128)(2,1)}, bf16[512,2048]{1,0:T(8,128)(2,1)}, u32[]{:S(2)}, u32[]{:S(2)}) collective-permute-start(bf16[512,2048]{1,0:T(8,128)(2,1)} %get-tuple-element.93.refs_1_), channel_id=1, source_target_pairs={{0,1},{1,0},{2,3},{3,2},{4,5},{5,4},{6,7},{7,6},{8,9},{9,8},{10,11... | collective-permute-start | bytes 6291464 | tf_op jit(solution)/shard_map/ppermute | solution.py:437
  189.3 9.6 %collective-permute-start.31 = (bf16[8,32,2560]{2,1,0:T(8,128)(2,1)}, bf16[8,32,2560]{2,1,0:T(8,128)(2,1)S(1)}, u32[]{:S(2)}, u32[]{:S(2)}) collective-permute-start(bf16[8,32,2560]{2,1,0:T(8,128)(2,1)} %tie.56.refs_4_.refs_8_), channel_id=1, source_target_pairs={{0,1},{1,0},{2,3},{3,2},{4,5},{5,4},{6,7},{7,6},{8,9},{9,8},{10,11... | collective-permute-start | bytes 3932168 | tf_op jit(solution)/shard_map/ppermute | solution.py:437
  189.7 9.2 %collective-permute-start.30 = (bf16[8,32,2560]{2,1,0:T(8,128)(2,1)S(1)}, bf16[8,32,2560]{2,1,0:T(8,128)(2,1)S(1)}, u32[]{:S(2)}, u32[]{:S(2)}) collective-permute-start(bf16[8,32,2560]{2,1,0:T(8,128)(2,1)S(1)} %copy-done.4), channel_id=1, source_target_pairs={{0,1},{1,0},{2,3},{3,2},{4,5},{5,4},{6,7},{7,6},{8,9},{9,8},{10,11... | collective-permute-start | bytes 3932168 | tf_op jit(solution)/shard_map/ppermute | solution.py:437
  219.4 8.9 %collective-permute-start.44 = (bf16[512,2560]{1,0:T(8,128)(2,1)}, bf16[512,2560]{1,0:T(8,128)(2,1)}, u32[]{:S(2)}, u32[]{:S(2)}) collective-permute-start(bf16[512,2560]{1,0:T(8,128)(2,1)} %get-tuple-element.95.refs_1_), channel_id=1, source_target_pairs={{0,1},{1,0},{2,3},{3,2},{4,5},{5,4},{6,7},{7,6},{8,9},{9,8},{10,11... | collective-permute-start | bytes 7864328 | tf_op jit(solution)/shard_map/ppermute | solution.py:437
  219.6 17.8 %collective-permute-start.43 = (bf16[512,2560]{1,0:T(8,128)(2,1)}, bf16[512,2560]{1,0:T(8,128)(2,1)S(1)}, u32[]{:S(2)}, u32[]{:S(2)}) collective-permute-start(bf16[512,2560]{1,0:T(8,128)(2,1)} %get-tuple-element.98.refs_2_), channel_id=1, source_target_pairs={{0,1},{1,0},{2,3},{3,2},{4,5},{5,4},{6,7},{7,6},{8,9},{9,8},{10,11... | collective-permute-start | bytes 7864328 | tf_op jit(solution)/shard_map/ppermute | solution.py:437
  220.0 17.5 %collective-permute-start.42 = (bf16[512,1024]{1,0:T(8,128)(2,1)S(1)}, bf16[512,1024]{1,0:T(8,128)(2,1)}, u32[]{:S(2)}, u32[]{:S(2)}) collective-permute-start(bf16[512,1024]{1,0:T(8,128)(2,1)S(1)} %copy-done), channel_id=1, source_target_pairs={{0,1},{1,0},{2,3},{3,2},{4,5},{5,4},{6,7},{7,6},{8,9},{9,8},{10,11... | collective-permute-start | bytes 3145736 | tf_op jit(solution)/shard_map/ppermute | solution.py:437
  235.9 39.1 %collective-permute-start.46 = (bf16[8,160,512]{2,1,0:T(8,128)(2,1)}, bf16[8,160,512]{2,1,0:T(8,128)(2,1)}, u32[]{:S(2)}, u32[]{:S(2)}) collective-permute-start(bf16[8,160,512]{2,1,0:T(8,128)(2,1)} %get-tuple-element.114), channel_id=1, source_target_pairs={{0,2},{2,0},{1,3},{3,1},{4,6},{6,4},{5,7},{7,5},{8,10},{10,8},{9,1... | collective-permute-start | bytes 3932168 | tf_op jit(solution)/shard_map/ppermute | solution.py:437
  246.1 40.1 %collective-permute-start.47 = (bf16[8,64,1280]{2,1,0:T(8,128)(2,1)}, bf16[8,64,1280]{2,1,0:T(8,128)(2,1)S(1)}, u32[]{:S(2)}, u32[]{:S(2)}) collective-permute-start(bf16[8,64,1280]{2,1,0:T(8,128)(2,1)} %get-tuple-element.116), channel_id=1, source_target_pairs={{0,4},{4,0},{8,12},{12,8},{16,20},{20,16},{24,28},{28,24},{1,5},{5... | collective-permute-start | bytes 3932168 | tf_op jit(solution)/shard_map/ppermute | solution.py:437
  269.3 9.5 %collective-permute-start.45 = (bf16[512,512]{1,0:T(8,128)(2,1)}, bf16[512,512]{1,0:T(8,128)(2,1)}, u32[]{:S(2)}, u32[]{:S(2)}) collective-permute-start(bf16[512,512]{1,0:T(8,128)(2,1)} %get-tuple-element.113), channel_id=1, source_target_pairs={{0,1},{1,0},{2,3},{3,2},{4,5},{5,4},{6,7},{7,6},{8,9},{9,8},{10,11... | collective-permute-start | bytes 1572872 | tf_op jit(solution)/shard_map/ppermute | solution.py:437
  269.4 38.7 %collective-permute-start.48 = (bf16[8,64,1280]{2,1,0:T(8,128)(2,1)}, bf16[8,64,1280]{2,1,0:T(8,128)(2,1)}, u32[]{:S(2)}, u32[]{:S(2)}) collective-permute-start(bf16[8,64,1280]{2,1,0:T(8,128)(2,1)} %get-tuple-element.120), channel_id=1, source_target_pairs={{0,2},{2,0},{1,3},{3,1},{4,6},{6,4},{5,7},{7,5},{8,10},{10,8},{9,1... | collective-permute-start | bytes 3932168 | tf_op jit(solution)/shard_map/ppermute | solution.py:437
  277.9 34.4 %collective-permute-start.49 = (bf16[4,160,512]{2,1,0:T(8,128)(2,1)S(1)}, bf16[4,160,512]{2,1,0:T(8,128)(2,1)}, u32[]{:S(2)}, u32[]{:S(2)}) collective-permute-start(bf16[4,160,512]{2,1,0:T(8,128)(2,1)S(1)} %get-tuple-element.172.refs_5_), channel_id=1, source_target_pairs={{0,4},{4,0},{8,12},{12,8},{16,20},{20,16},{24,28},{28,24},{1,5},{5... | collective-permute-start | bytes 1966088 | tf_op jit(solution)/shard_map/ppermute | solution.py:437
  305.3 51.2 %collective-permute-start.53 = (bf16[512,1024]{1,0:T(8,128)(2,1)}, bf16[512,1024]{1,0:T(8,128)(2,1)}, u32[]{:S(2)}, u32[]{:S(2)}) collective-permute-start(bf16[512,1024]{1,0:T(8,128)(2,1)} %get-tuple-element.121.refs_1_), channel_id=1, source_target_pairs={{0,1},{1,0},{2,3},{3,2},{4,5},{5,4},{6,7},{7,6},{8,9},{9,8},{10,11... | collective-permute-start | bytes 3145736 | tf_op jit(solution)/shard_map/ppermute | solution.py:437
  305.4 44.2 %collective-permute-start.56 = (bf16[4,64,1280]{2,1,0:T(8,128)(2,1)S(1)}, bf16[4,64,1280]{2,1,0:T(8,128)(2,1)}, u32[]{:S(2)}, u32[]{:S(2)}) collective-permute-start(bf16[4,64,1280]{2,1,0:T(8,128)(2,1)S(1)} %copy-done.43), channel_id=1, source_target_pairs={{0,2},{2,0},{1,3},{3,1},{4,6},{6,4},{5,7},{7,5},{8,10},{10,8},{9,1... | collective-permute-start | bytes 1966088 | tf_op jit(solution)/shard_map/ppermute | solution.py:437
  307.0 26.3 %collective-permute-start.50 = (bf16[8,128,512]{2,1,0:T(8,128)(2,1)}, bf16[8,128,512]{2,1,0:T(8,128)(2,1)}, u32[]{:S(2)}, u32[]{:S(2)}) collective-permute-start(bf16[8,128,512]{2,1,0:T(8,128)(2,1)} %get-tuple-element.123), channel_id=1, source_target_pairs={{0,4},{4,0},{8,12},{12,8},{16,20},{20,16},{24,28},{28,24},{1,5},{5... | collective-permute-start | bytes 3145736 | tf_op jit(solution)/shard_map/ppermute | solution.py:437
  311.3 40.5 %collective-permute-start.57 = (bf16[4,64,1280]{2,1,0:T(8,128)(2,1)}, bf16[4,64,1280]{2,1,0:T(8,128)(2,1)}, u32[]{:S(2)}, u32[]{:S(2)}) collective-permute-start(bf16[4,64,1280]{2,1,0:T(8,128)(2,1)} %get-tuple-element.170.refs_12_), channel_id=1, source_target_pairs={{0,4},{4,0},{8,12},{12,8},{16,20},{20,16},{24,28},{28,24},{1,5},{5... | collective-permute-start | bytes 1966088 | tf_op jit(solution)/shard_map/ppermute | solution.py:437
  314.2 12.2 %collective-permute-start.51 = (bf16[2,160,512]{2,1,0:T(8,128)(2,1)S(1)}, bf16[2,160,512]{2,1,0:T(8,128)(2,1)S(1)}, u32[]{:S(2)}, u32[]{:S(2)}) collective-permute-start(bf16[2,160,512]{2,1,0:T(8,128)(2,1)S(1)} %get-tuple-element.184.refs_13_), channel_id=1, source_target_pairs={{0,8},{4,12},{8,0},{12,4},{16,24},{20,28},{24,16},{28,20},{1,9},{5... | collective-permute-start | bytes 983048 | tf_op jit(solution)/shard_map/ppermute | solution.py:437
  327.1 30.5 %collective-permute-start.54 = (bf16[512,1152]{1,0:T(8,128)(2,1)}, bf16[512,1152]{1,0:T(8,128)(2,1)S(1)}, u32[]{:S(2)}, u32[]{:S(2)}) collective-permute-start(bf16[512,1152]{1,0:T(8,128)(2,1)} %get-tuple-element.128), channel_id=1, source_target_pairs={{0,1},{1,0},{2,3},{3,2},{4,5},{5,4},{6,7},{7,6},{8,9},{9,8},{10,11... | collective-permute-start | bytes 3538952 | tf_op jit(solution)/shard_map/ppermute | solution.py:437
  333.3 32.7 %collective-permute-start.58 = (bf16[1,160,512]{2,1,0:T(8,128)(2,1)}, bf16[1,160,512]{2,1,0:T(8,128)(2,1)}, u32[]{:S(2)}, u32[]{:S(2)}) collective-permute-start(bf16[1,160,512]{2,1,0:T(8,128)(2,1)} %fusion.34.refs_5_), channel_id=1, source_target_pairs={{0,16},{4,20},{8,24},{12,28},{16,0},{20,4},{24,8},{28,12},{1,17},{... | collective-permute-start | bytes 491528 | tf_op jit(solution)/shard_map/ppermute | solution.py:437
  349.6 43.7 %collective-permute-start.60 = (bf16[4,128,512]{2,1,0:T(8,128)(2,1)}, bf16[4,128,512]{2,1,0:T(8,128)(2,1)}, u32[]{:S(2)}, u32[]{:S(2)}) collective-permute-start(bf16[4,128,512]{2,1,0:T(8,128)(2,1)} %get-tuple-element.178.refs_4_), channel_id=1, source_target_pairs={{0,2},{2,0},{1,3},{3,1},{4,6},{6,4},{5,7},{7,5},{8,10},{10,8},{9,1... | collective-permute-start | bytes 1572872 | tf_op jit(solution)/shard_map/ppermute | solution.py:437
  354.7 41.0 %collective-permute-start.61 = (bf16[2,64,2560]{2,1,0:T(8,128)(2,1)}, bf16[2,64,2560]{2,1,0:T(8,128)(2,1)}, u32[]{:S(2)}, u32[]{:S(2)}) collective-permute-start(bf16[2,64,2560]{2,1,0:T(8,128)(2,1)} %pad_maximum_fusion.10.refs_6_), channel_id=1, source_target_pairs={{0,8},{4,12},{8,0},{12,4},{16,24},{20,28},{24,16},{28,20},{1,9},{5... | collective-permute-start | bytes 1966088 | tf_op jit(solution)/shard_map/ppermute | solution.py:437
  356.5 19.4 %collective-permute-start.52 = (f32[32,8,128]{2,1,0:T(8,128)S(1)}, f32[32,8,128]{2,1,0:T(8,128)S(1)}, u32[]{:S(2)}, u32[]{:S(2)}) collective-permute-start(f32[32,8,128]{2,1,0:T(8,128)S(1)} %bitcast.233), channel_id=1, source_target_pairs={{0,4},{4,0},{8,12},{12,8},{16,20},{20,16},{24,28},{28,24},{1,5},{5... | collective-permute-start | bytes 393224 | tf_op jit(solution)/shard_map/ppermute | solution.py:437
  377.0 36.1 %collective-permute-start.62 = (bf16[8,64,1024]{2,1,0:T(8,128)(2,1)}, bf16[8,64,1024]{2,1,0:T(8,128)(2,1)S(1)}, u32[]{:S(2)}, u32[]{:S(2)}) collective-permute-start(bf16[8,64,1024]{2,1,0:T(8,128)(2,1)} %get-tuple-element.134), channel_id=1, source_target_pairs={{0,2},{2,0},{1,3},{3,1},{4,6},{6,4},{5,7},{7,5},{8,10},{10,8},{9,1... | collective-permute-start | bytes 3145736 | tf_op jit(solution)/shard_map/ppermute | solution.py:437
  378.5 51.0 %collective-permute-start.64 = (bf16[8,64,1152]{2,1,0:T(8,128)(2,1)}, bf16[8,64,1152]{2,1,0:T(8,128)(2,1)}, u32[]{:S(2)}, u32[]{:S(2)}) collective-permute-start(bf16[8,64,1152]{2,1,0:T(8,128)(2,1)} %get-tuple-element.138), channel_id=1, source_target_pairs={{0,4},{4,0},{8,12},{12,8},{16,20},{20,16},{24,28},{28,24},{1,5},{5... | collective-permute-start | bytes 3538952 | tf_op jit(solution)/shard_map/ppermute | solution.py:437
  383.3 9.2 %collective-permute-start.59 = (f32[32,8,128]{2,1,0:T(8,128)}, f32[32,8,128]{2,1,0:T(8,128)S(1)}, u32[]{:S(2)}, u32[]{:S(2)}) collective-permute-start(f32[32,8,128]{2,1,0:T(8,128)} %tie.71), channel_id=1, source_target_pairs={{0,16},{4,20},{8,24},{12,28},{16,0},{20,4},{24,8},{28,12},{1,17},{... | collective-permute-start | bytes 393224 | tf_op jit(solution)/shard_map/ppermute | solution.py:437
  395.7 15.4 %collective-permute-start.63 = (bf16[2,128,512]{2,1,0:T(8,128)(2,1)}, bf16[2,128,512]{2,1,0:T(8,128)(2,1)}, u32[]{:S(2)}, u32[]{:S(2)}) collective-permute-start(bf16[2,128,512]{2,1,0:T(8,128)(2,1)} %get-tuple-element.190.refs_9_), channel_id=1, source_target_pairs={{0,8},{4,12},{8,0},{12,4},{16,24},{20,28},{24,16},{28,20},{1,9},{5... | collective-permute-start | bytes 786440 | tf_op jit(solution)/shard_map/ppermute | solution.py:437
  397.4 29.3 %collective-permute-start.65 = (bf16[1,64,2560]{2,1,0:T(8,128)(2,1)S(1)}, bf16[1,64,2560]{2,1,0:T(8,128)(2,1)}, u32[]{:S(2)}, u32[]{:S(2)}) collective-permute-start(bf16[1,64,2560]{2,1,0:T(8,128)(2,1)S(1)} %fusion.14.refs_10_), channel_id=1, source_target_pairs={{0,16},{4,20},{8,24},{12,28},{16,0},{20,4},{24,8},{28,12},{1,17},{... | collective-permute-start | bytes 983048 | tf_op jit(solution)/shard_map/ppermute | solution.py:437
  412.7 31.4 %collective-permute-start.66 = (bf16[1,128,512]{2,1,0:T(8,128)(2,1)S(1)}, bf16[1,128,512]{2,1,0:T(8,128)(2,1)}, u32[]{:S(2)}, u32[]{:S(2)}) collective-permute-start(bf16[1,128,512]{2,1,0:T(8,128)(2,1)S(1)} %fusion.38.refs_10_), channel_id=1, source_target_pairs={{0,16},{4,20},{8,24},{12,28},{16,0},{20,4},{24,8},{28,12},{1,17},{... | collective-permute-start | bytes 393224 | tf_op jit(solution)/shard_map/ppermute | solution.py:437
  414.8 46.9 %collective-permute-start.67 = (bf16[4,64,1024]{2,1,0:T(8,128)(2,1)}, bf16[4,64,1024]{2,1,0:T(8,128)(2,1)}, u32[]{:S(2)}, u32[]{:S(2)}) collective-permute-start(bf16[4,64,1024]{2,1,0:T(8,128)(2,1)} %get-tuple-element.176.refs_9_), channel_id=1, source_target_pairs={{0,4},{4,0},{8,12},{12,8},{16,20},{20,16},{24,28},{28,24},{1,5},{5... | collective-permute-start | bytes 1572872 | tf_op jit(solution)/shard_map/ppermute | solution.py:437
  429.4 29.8 %collective-permute-start.76 = (bf16[32,2560]{1,0:T(8,128)(2,1)}, bf16[32,2560]{1,0:T(8,128)(2,1)}, u32[]{:S(2)}, u32[]{:S(2)}) collective-permute-start(bf16[32,2560]{1,0:T(8,128)(2,1)} %fusion.32), channel_id=1, source_target_pairs={{0,1},{1,0},{2,3},{3,2},{4,5},{5,4},{6,7},{7,6},{8,9},{9,8},{10,11... | collective-permute-start | bytes 491528 | tf_op jit(solution)/shard_map/ppermute | solution.py:437
  431.6 31.9 %collective-permute-start.68 = (bf16[4,64,1152]{2,1,0:T(8,128)(2,1)S(1)}, bf16[4,64,1152]{2,1,0:T(8,128)(2,1)}, u32[]{:S(2)}, u32[]{:S(2)}) collective-permute-start(bf16[4,64,1152]{2,1,0:T(8,128)(2,1)S(1)} %get-tuple-element.174.refs_9_), channel_id=1, source_target_pairs={{0,2},{2,0},{1,3},{3,1},{4,6},{6,4},{5,7},{7,5},{8,10},{10,8},{9,1... | collective-permute-start | bytes 1769480 | tf_op jit(solution)/shard_map/ppermute | solution.py:437
  458.9 31.0 %collective-permute-start.75 = (bf16[64,512]{1,0:T(8,128)(2,1)}, bf16[64,512]{1,0:T(8,128)(2,1)}, u32[]{:S(2)}, u32[]{:S(2)}) collective-permute-start(bf16[64,512]{1,0:T(8,128)(2,1)} %fusion.41), channel_id=1, source_target_pairs={{0,1},{1,0},{2,3},{3,2},{4,5},{5,4},{6,7},{7,6},{8,9},{9,8},{10,11... | collective-permute-start | bytes 196616 | tf_op jit(solution)/shard_map/ppermute | solution.py:437
  465.3 15.2 %collective-permute-start.69 = (bf16[2,64,2176]{2,1,0:T(8,128)(2,1)S(1)}, bf16[2,64,2176]{2,1,0:T(8,128)(2,1)S(1)}, u32[]{:S(2)}, u32[]{:S(2)}) collective-permute-start(bf16[2,64,2176]{2,1,0:T(8,128)(2,1)S(1)} %pad_maximum_fusion.11.refs_12_), channel_id=1, source_target_pairs={{0,8},{4,12},{8,0},{12,4},{16,24},{20,28},{24,16},{28,20},{1,9},{5... | collective-permute-start | bytes 1671176 | tf_op jit(solution)/shard_map/ppermute | solution.py:437
  492.9 11.3 %collective-permute-start.72 = (f32[84,128]{1,0:T(8,128)S(1)}, f32[84,128]{1,0:T(8,128)S(1)}, u32[]{:S(2)}, u32[]{:S(2)}) collective-permute-start(f32[84,128]{1,0:T(8,128)S(1)} %pad_maximum_fusion.38), channel_id=1, source_target_pairs={{0,16},{4,20},{8,24},{12,28},{16,0},{20,4},{24,8},{28,12},{1,17},{... | collective-permute-start | bytes 129032 | tf_op jit(solution)/shard_map/ppermute | solution.py:437
  495.7 13.5 %collective-permute-start.73 = (bf16[1,64,2176]{2,1,0:T(8,128)(2,1)S(1)}, bf16[1,64,2176]{2,1,0:T(8,128)(2,1)S(1)}, u32[]{:S(2)}, u32[]{:S(2)}) collective-permute-start(bf16[1,64,2176]{2,1,0:T(8,128)(2,1)S(1)} %copy-done.64), channel_id=1, source_target_pairs={{0,16},{4,20},{8,24},{12,28},{16,0},{20,4},{24,8},{28,12},{1,17},{... | collective-permute-start | bytes 835592 | tf_op jit(solution)/shard_map/ppermute | solution.py:437
  510.0 9.0 %collective-permute-start.74 = (bf16[32,2176]{1,0:T(8,128)(2,1)S(1)}, bf16[32,2176]{1,0:T(8,128)(2,1)S(1)}, u32[]{:S(2)}, u32[]{:S(2)}) collective-permute-start(bf16[32,2176]{1,0:T(8,128)(2,1)S(1)} %fusion.36), channel_id=1, source_target_pairs={{0,1},{1,0},{2,3},{3,2},{4,5},{5,4},{6,7},{7,6},{8,9},{9,8},{10,11... | collective-permute-start | bytes 417800 | tf_op jit(solution)/shard_map/ppermute | solution.py:437
  (106 other events, 703.1 us)

commit v6 on v5

--- a/solution.py
+++ b/solution.py
@@ -380,7 +380,7 @@
         return total + xs_ref[at, :] * drive_ref[at, :]
 
     last = pl.ds(3 * ndim * SUB, SUB)
-    sums_ref[last, :] = lax.fori_loop(0, rows, skip_step, sums_ref[last, :], unroll=8)
+    sums_ref[last, :] = lax.fori_loop(0, rows, skip_step, sums_ref[last, :], unroll=32)
 
 
 def back_norm_kernel(*refs):
@@ -1215,6 +1215,10 @@
     def loose(*groups):
         return [(array, None, None) for group in groups for array in group.arrays]
 
+    grad_low = cotangent[0]
+    part = width // 2
+    cot_own = lax.dynamic_slice_in_dim(grad_low, core * part, part, axis=1)
+    cot_oth = other_core(tie(lax.dynamic_slice_in_dim(grad_low, (1 - core) * part, part, axis=1), mixed))
     shared, queries, keys, log_total, value_pre, values, gate_pre, attended, gated = grid_call(
         functools.partial(attention_kernel, weight1, tile),
         [still((rows, z_width), f32), still((rows, z_width), bf16), still((rows, z_width), bf16), still((rows, 1), f32)]
@@ -1223,7 +1227,7 @@
         + loose(weight1),
         weight1.tiles, me,
         scratch=[pltpu.VMEM(w1_shape, bf16), pltpu.VMEM((rows, rows), bf16), pltpu.SemaphoreType.DMA((2,))],
-        name="attention", micros=15, after=third_gate + third_up + (norm_other,),
+        name="attention", micros=15, after=third_gate + third_up + (norm_other, cot_oth),
     )
     middle, ffn_in, inverse = kernel_call(
         functools.partial(project_kernel, weight2),
@@ -1241,10 +1245,6 @@
         getter.step((ffn_in,))
     weight4 = Weight(Part(get_down, 0, width, w_down.shape[0]))
     weight3 = Weight(Part(get_gate, 0, hidden_width, short), Part(get_up, 0, hidden_width, short, 0, hidden_width))
-    grad_low = cotangent[0]
-    part = width // 2
-    cot_own = lax.dynamic_slice_in_dim(grad_low, core * part, part, axis=1)
-    cot_oth = other_core(tie(lax.dynamic_slice_in_dim(grad_low, (1 - core) * part, part, axis=1), mixed))
     gated_other, mix_other = other_core(gated), other_core(sent_mix)
     half = hidden_width // 2
     pair = ((rows, hidden_width), bf16, (rows, hidden_width), lambda g, me: (0, 0))
@@ -1254,7 +1254,7 @@
         [whole(ffn_in), whole(grad_low)] + [(array, None, None) for array in weight3.arrays + weight4.arrays],
         2, me,
         scratch=[pltpu.VMEM(w3_shape, bf16), pltpu.VMEM(w4_shape, bf16), pltpu.SemaphoreType.DMA((2, 3))],
-        name="hidden", micros=15, after=(cot_oth, gated_other, mix_other),
+        name="hidden", micros=15, after=(gated_other, mix_other),
     )
     ffn_other = other_core(ffn_in)
     (output,) = kernel_call(
@@ -1377,7 +1377,6 @@
     (input_grad,) = kernel_call(
         input_kernel, [((rows, width), f32)],
         [dn, suffix, back_carry, tokens[0], valid_col, seg_col, prefix, carry, grad_middle], name="input", micros=6,
-        after=last.step(back_carry),
     )
     total = sum_over(sum_over(own_pack, "core"), "chip")
     mine = lax.dynamic_index_in_dim(total[4 * ndim + 2 :].reshape(-1)[:size].reshape(dp_count, -1), dp_index, 0, keepdims=False)

time: 528 us -> 526 us (level)
  no operation moved by 1% of the time
where the time goes in v6:
time: 526 us; the launch traced here: 520 us
  Pallas kernels  233 us (44%)
  other arithmetic  89.9 us (17%)
  waiting for transfers between devices  87.9 us (17%)
  starting transfers between devices  69.6 us (13%)
  local copies, waits for them, and re-layouts  30.4 us (6%)
  between operations  8.56 us (2%)
    pallas_call x14, Pallas kernels, kernel_call(): pl.pallas_call(run, out_shape=tuple((jax.ShapeDtypeStruct(shape, dtype) f...  136 us
    pallas_call x9, Pallas kernels, grid_call(): pl.pallas_call(run, out_shape=tuple((jax.ShapeDtypeStruct(shape, dtype) f...  90.8 us
    ppermute x80, waiting for transfers between devices, swap(): return lax.ppermute(value, axis, [(i, i ^ bit) for i in range(count)])  87.9 us
    ppermute x80, starting transfers between devices, swap(): return lax.ppermute(value, axis, [(i, i ^ bit) for i in range(count)])  69.6 us
    add x16, other arithmetic, add_low(): return left + right + zero  32.8 us
    concatenate x15, other arithmetic, step(): self.arrays = [jnp.concatenate([mine[0], others[0]], axis=0)]  20.4 us
    unnamed x187, local copies, waits for them, and re-layouts  17.2 us
  transfers between devices with their start and end apart: 80, of which 29 were waited for; matrix products, arithmetic and copies ran while one was open for 19% of the time, Pallas kernels for 41%

profile of v6, /device:TPU:0, one launch (start us, length us, event | category | flops | bytes accessed | tf_op | source)
XLA Modules:
  0.0 519.6 jit_solution(18298156182884171053)
XLA Ops:
  5.2 3.7 collective-permute-start.3
  13.4 4.4 stats.1
  25.0 2.8 collective-permute-done.4
  30.0 3.2 collective-permute-done.5
  33.2 2.4 collective-permute-start.6
  44.6 12.1 %norm.1 = (bf16[512,1024]{1,0:T(8,128)(2,1)}, f32[4096,128]{1,0:T(8,128)}, f32[256,128]{1,0:T(8,128)}) custom-call(bf16[512,1024]{1,0:T(8,128)(2,1)} %bitcast.198, f32[512,1]{1,0:T(8,128)} %copy.85.refs_1_.refs_3_.refs_6_.refs_4_, s32[512,1]{1,0:T(8,128)} %copy.86.refs_2_.refs_3_.refs_6_.refs_7_.refs_5_, ...), custom_call_target="tpu_custom_call" | custom-call | flops 1300000000 | bytes 3900000 | tf_op jit(solution)/shard_map/norm/pallas_call | solution.py:75
  62.8 3.2 collective-permute-done.10
  72.1 2.6 collective-permute-start.17
  78.4 4.7 collective-permute-done.16
  85.6 2.4 collective-permute-done.17
  88.7 2.6 collective-permute-done.13
  95.9 2.6 collective-permute-start.20
  98.5 2.0 collective-permute-start.18
  100.5 6.4 %collective-permute-done.19 = bf16[2,32,2560]{2,1,0:T(8,128)(2,1)} collective-permute-done((bf16[2,32,2560]{2,1,0:T(8,128)(2,1)}, bf16[2,32,2560]{2,1,0:T(8,128)(2,1)}, u32[]{:S(2)}, u32[]{:S(2)}) %collective-permute-start.19) | collective-permute-done | bytes 327712 | tf_op jit(solution)/shard_map/ppermute | solution.py:437
  106.9 2.0 pad_maximum_fusion.9.refs_7_.refs_0_.refs_2_
  108.9 3.1 collective-permute-done.18
  113.4 14.7 %mix.1 = (f32[4096,128]{1,0:T(8,128)}, bf16[512,1024]{1,0:T(8,128)(2,1)}, f32[16,256,128]{2,1,0:T(8,128)}) custom-call(f32[4096,128]{1,0:T(8,128)} %get-tuple-element.89.refs_0_, f32[256,128]{1,0:T(8,128)} %bitcast.203, f32[128,128]{1,0:T(8,128)} %bitcast.218, f32[128,128]{1,0:T(8,128)} %bitcast.211, f32[128,128]{1,0:T(8,128)} %bitcast.224, ...), custom_call_target="tpu_custom_call" | custom-call | flops 1600000000 | bytes 4800000 | tf_op jit(solution)/shard_map/mix/pallas_call | solution.py:75
  128.8 2.0 collective-permute-done.23.refs_3_.refs_14_.refs_10_.refs_20_.refs_9_
  139.3 2.5 pad_maximum_fusion.4.refs_0_
  142.3 2.5 collective-permute-done.27
  145.6 2.3 pad_maximum_fusion.3.refs_18_.refs_0_.refs_2_
  147.9 2.3 pad_maximum_fusion.2.refs_17_.refs_0_.refs_1_
  156.8 13.3 %attention.1 = (f32[512,256]{1,0:T(8,128)}, bf16[512,256]{1,0:T(8,128)(2,1)}, bf16[512,256]{1,0:T(8,128)(2,1)}, f32[512,1]{1,0:T(8,128)}, bf16[512,2048]{1,0:T(8...) custom-call(s32[2]{0:T(128)} %pad_add_fusion.refs_0_, ...), custom_call_target="tpu_custom_call" | custom-call | flops 1500000000 | bytes 4500000 | tf_op jit(solution)/shard_map/attention/pallas_call | solution.py:102
  170.2 7.9 %project.1 = (f32[512,1024]{1,0:T(8,128)}, bf16[512,1024]{1,0:T(8,128)(2,1)}, f32[512,1]{1,0:T(8,128)}) custom-call(s32[2]{0:T(128)} %pad_add_fusion.refs_0_, bf16[512,2048]{1,0:T(8,128)(2,1)} %get-tuple-element.93.refs_1_, bf16[512,1024]{1,0:T(8,128)(2,1)} %bitcast.199, f32[512,1]{1,0:T(8,128)} %copy.85.refs_1_.refs_3_.refs_6_.refs_4_, ...), custom_call_target="tpu_custom_call" | custom-call | flops 600000000 | bytes 1800000 | tf_op jit(solution)/shard_map/project/pallas_call | solution.py:75
  178.1 3.7 collective-permute-done.37.refs_0_
  183.9 3.2 collective-permute-done.30.refs_0_
  190.0 7.1 %collective-permute-done.35.refs_10_.refs_14_ = bf16[8,32,2560]{2,1,0:T(8,128)(2,1)} collective-permute-done((bf16[8,32,2560]{2,1,0:T(8,128)(2,1)}, bf16[8,32,2560]{2,1,0:T(8,128)(2,1)}, u32[]{:S(2)}, u32[]{:S(2)}) %collective-permute-start.35) | collective-permute-done | bytes 1310752 | tf_op jit(solution)/shard_map/ppermute | solution.py:437
  199.7 19.0 %hidden.1 = (bf16[512,2560]{1,0:T(8,128)(2,1)}, bf16[512,2560]{1,0:T(8,128)(2,1)}, bf16[512,2560]{1,0:T(8,128)(2,1)}) custom-call(s32[2]{0:T(128)} %pad_add_fusion.refs_0_, bf16[512,1024]{1,0:T(8,128)(2,1)} %get-tuple-element.94.refs_1_, bf16[512,1024]{1,0:T(8,128)(2,1)} %bitcast.195, bf16[8,32,2560]{2,1,0:T(8,128)(2,1)} %tie.55.refs_3_.refs_7_, ...), custom_call_target="tpu_custom_call" | custom-call | flops 1500000000 | bytes 4500000 | tf_op jit(solution)/shard_map/hidden/pallas_call | solution.py:102
  219.5 8.2 %out.1.refs_5_ = bf16[512,1024]{1,0:T(8,128)(2,1)} custom-call(s32[2]{0:T(128)} %pad_add_fusion.refs_0_, bf16[512,2560]{1,0:T(8,128)(2,1)} %get-tuple-element.95.refs_1_, f32[512,1024]{1,0:T(8,128)} %get-tuple-element.96.refs_2_.refs_3_, bf16[8,80,1024]{2,1,0:T(8,128)(2,1)} %tie.61.refs_11_.refs_3_, bf16[8,80,1024]{2,1,0:T(8,128)(2,1)} %tie.62.refs_12_.refs_4_, ...), custom_call_target="tpu_custom_call" | custom-call | flops 700000000 | bytes 2100000 | tf_op jit(solution)/shard_map/out/pallas_call | solution.py:75
  227.7 7.5 %grad_down.1 = (bf16[8,160,512]{2,1,0:T(8,128)(2,1)}, bf16[8,160,512]{2,1,0:T(8,128)(2,1)}) custom-call(s32[2]{0:T(128)} %pad_add_fusion.refs_0_, bf16[512,2560]{1,0:T(8,128)(2,1)} %get-tuple-element.95.refs_1_, bf16[512,2560]{1,0:T(8,128)(2,1)} %collective-permute-done.44.refs_2_, bf16[512,512]{1,0:T(8,128)(2,1)} %get-tuple-element.191.refs_3_, ...), custom_call_target="tpu_custom_call" | custom-call | flops 600000000 | bytes 1800000 | tf_op jit(solution)/shard_map/grad_down/pallas_call | solution.py:102
  237.8 7.0 %grad_gate.1 = (bf16[8,64,1280]{2,1,0:T(8,128)(2,1)}, bf16[8,64,1280]{2,1,0:T(8,128)(2,1)}) custom-call(s32[2]{0:T(128)} %pad_add_fusion.refs_0_, bf16[512,1024]{1,0:T(8,128)(2,1)} %get-tuple-element.94.refs_1_, bf16[512,1024]{1,0:T(8,128)(2,1)} %collective-permute-done.42.refs_2_, bf16[512,2560]{1,0:T(8,128)(2,1)} %get-tuple-element.97.refs_3_.refs_1_, ...), custom_call_target="tpu_custom_call" | custom-call | flops 600000000 | bytes 1800000 | tf_op jit(solution)/shard_map/grad_gate/pallas_call | solution.py:102
  246.4 7.2 %grad_up.1 = (bf16[8,64,1280]{2,1,0:T(8,128)(2,1)}, bf16[8,64,1280]{2,1,0:T(8,128)(2,1)}) custom-call(s32[2]{0:T(128)} %pad_add_fusion.refs_0_, bf16[512,1024]{1,0:T(8,128)(2,1)} %get-tuple-element.94.refs_1_, bf16[512,1024]{1,0:T(8,128)(2,1)} %collective-permute-done.42.refs_2_, bf16[512,2560]{1,0:T(8,128)(2,1)} %get-tuple-element.97.refs_3_.refs_1_, ...), custom_call_target="tpu_custom_call" | custom-call | flops 600000000 | bytes 1800000 | tf_op jit(solution)/shard_map/grad_up/pallas_call | solution.py:102
  253.6 14.9 %ffn_back.1 = (f32[512,1024]{1,0:T(8,128)}, bf16[512,512]{1,0:T(8,128)(2,1)}, bf16[512,512]{1,0:T(8,128)(2,1)}, bf16[512,1024]{1,0:T(8,128)(2,1)}, f32[1,1024]{1,0:T(1,128)}) custom-call(s32[2]{0:T(128)} %pad_add_fusion.refs_0_, bf16[512,2560]{1,0:T(8,128)(2,1)} %get-tuple-element.97.refs_3_.refs_1_, bf16[512,2560]{1,0:T(8,128)(2,1)} %get-tuple-element.98.refs_2_, ...), custom_call_target="tpu_custom_call" | custom-call | flops 1700000000 | bytes 5100000 | tf_op jit(solution)/shard_map/ffn_back/pallas_call | solution.py:75
  273.7 2.9 fusion.2
  278.2 6.9 %grad_h.1 = (bf16[8,128,512]{2,1,0:T(8,128)(2,1)}, bf16[8,128,512]{2,1,0:T(8,128)(2,1)}) custom-call(s32[2]{0:T(128)} %pad_add_fusion.refs_0_, bf16[512,2048]{1,0:T(8,128)(2,1)} %get-tuple-element.93.refs_1_, bf16[512,2048]{1,0:T(8,128)(2,1)} %collective-permute-done.40.refs_15_.refs_2_, bf16[512,512]{1,0:T(8,128)(2,1)} %get-tuple-element.112.refs_1_.refs_3_, ...), custom_call_target="tpu_custom_call" | custom-call | flops 600000000 | bytes 1800000 | tf_op jit(solution)/shard_map/grad_h/pallas_call | solution.py:102
  285.6 1.9 fusion.1
  287.5 16.6 %attention_back.1 = (bf16[512,2048]{1,0:T(8,128)(2,1)}, bf16[512,2048]{1,0:T(8,128)(2,1)}, bf16[512,1024]{1,0:T(8,128)(2,1)}, bf16[512,1024]{1,0:T(8,128)(2,1)},...) custom-call(s32[2]{0:T(128)} %pad_add_fusion.refs_0_, ...), custom_call_target="tpu_custom_call" | custom-call | flops 1900000000 | bytes 5700000 | tf_op jit(solution)/shard_map/attention_back/pallas_call | solution.py:102
  307.3 3.2 fusion
  314.8 10.6 %sent_back.1 = (bf16[512,1024]{1,0:T(8,128)(2,1)}, bf16[512,1024]{1,0:T(8,128)(2,1)}) custom-call(s32[2]{0:T(128)} %pad_add_fusion.refs_0_, bf16[512,2048]{1,0:T(8,128)(2,1)} %get-tuple-element.117.refs_1_, bf16[512,2048]{1,0:T(8,128)(2,1)} %get-tuple-element.118.refs_2_, bf16[512,256]{1,0:T(8,128)(2,1)} %get-tuple-element.119.refs_3_, ...), custom_call_target="tpu_custom_call" | custom-call | flops 1100000000 | bytes 3300000 | tf_op jit(solution)/shard_map/sent_back/pallas_call | solution.py:75
  326.6 2.2 fusion.34.refs_5_
  328.8 3.7 collective-permute-done.50
  332.9 2.8 fusion.10
  335.7 11.9 %back_ends.1 = (f32[4096,128]{1,0:T(8,128)}, f32[256,128]{1,0:T(8,128)}) custom-call(bf16[512,1024]{1,0:T(8,128)(2,1)} %get-tuple-element.122.refs_1_.refs_0_, f32[4096,128]{1,0:T(8,128)} %get-tuple-element.92.refs_1_, f32[128,128]{1,0:T(8,128)} %bitcast.219, f32[128,128]{1,0:T(8,128)} %bitcast.212, bf16[4,128,512]{2,1,0:T(8,128)(2,1)} %get-tuple-element.178.refs_4_, ...), custom_call_target="tpu_custom_call" | custom-call | flops 1200000000 | bytes 3600000 | tf_op jit(solution)/shard_map/back_ends/pallas_call | solution.py:75
  351.7 1.9 fusion.16
  358.0 6.3 %grad_v.1 = (bf16[8,64,1024]{2,1,0:T(8,128)(2,1)}, bf16[8,64,1024]{2,1,0:T(8,128)(2,1)}) custom-call(s32[2]{0:T(128)} %pad_add_fusion.refs_0_, bf16[512,1024]{1,0:T(8,128)(2,1)} %get-tuple-element.88.refs_1_, bf16[512,1024]{1,0:T(8,128)(2,1)} %collective-permute-done.28.refs_19_.refs_2_, bf16[512,1024]{1,0:T(8,128)(2,1)} %get-tuple-element.127.refs_3_, ...), custom_call_target="tpu_custom_call" | custom-call | flops 600000000 | bytes 1800000 | tf_op jit(solution)/shard_map/grad_v/pallas_call | solution.py:102
  365.4 2.3 add_add_fusion.1.refs_7_
  367.7 7.0 %grad_r.1 = (bf16[8,64,1152]{2,1,0:T(8,128)(2,1)}, bf16[8,64,1152]{2,1,0:T(8,128)(2,1)}) custom-call(s32[2]{0:T(128)} %pad_add_fusion.refs_0_, bf16[512,1024]{1,0:T(8,128)(2,1)} %get-tuple-element.91.refs_2_.refs_1_, bf16[512,1024]{1,0:T(8,128)(2,1)} %collective-permute-done.41.refs_16_.refs_2_, bf16[512,1152]{1,0:T(8,128)(2,1)} %get-tuple-element.130.refs_3_, ...), custom_call_target="tpu_custom_call" | custom-call | flops 600000000 | bytes 1800000 | tf_op jit(solution)/shard_map/grad_r/pallas_call | solution.py:102
  378.0 3.2 collective-permute-done.55
  385.6 6.5 %collective-permute-done.59 = f32[32,8,128]{2,1,0:T(8,128)S(1)} collective-permute-done((f32[32,8,128]{2,1,0:T(8,128)}, f32[32,8,128]{2,1,0:T(8,128)S(1)}, u32[]{:S(2)}, u32[]{:S(2)}) %collective-permute-start.59) | collective-permute-done | bytes 131104 | tf_op jit(solution)/shard_map/ppermute | solution.py:437
  392.9 2.4 fusion.30
  397.0 2.1 collective-permute-start.65
  399.8 9.7 %back.4 = (f32[1024,128]{1,0:T(8,128)}, f32[256,128]{1,0:T(8,128)}, f32[392,128]{1,0:T(8,128)}) custom-call(f32[4096,128]{1,0:T(8,128)} %get-tuple-element.89.refs_0_, f32[4096,128]{1,0:T(8,128)} %get-tuple-element.124.refs_1_, f32[16,256,128]{2,1,0:T(8,128)} %get-tuple-element.125.refs_2_, f32[256,128]{1,0:T(8,128)} %maximum_bitcast_fusion.2.refs_3_, ...), custom_call_target="tpu_custom_call" | custom-call | flops 1000000000 | bytes 3000000 | tf_op jit(solution)/shard_map/back/pallas_call | solution.py:75
  415.3 9.8 %back.5 = (f32[1024,128]{1,0:T(8,128)}, f32[256,128]{1,0:T(8,128)}, f32[392,128]{1,0:T(8,128)}) custom-call(f32[4096,128]{1,0:T(8,128)} %get-tuple-element.89.refs_0_, f32[4096,128]{1,0:T(8,128)} %get-tuple-element.124.refs_1_, f32[16,256,128]{2,1,0:T(8,128)} %get-tuple-element.125.refs_2_, f32[256,128]{1,0:T(8,128)} %get-tuple-element.132.refs_3_, ...), custom_call_target="tpu_custom_call" | custom-call | flops 1000000000 | bytes 3000000 | tf_op jit(solution)/shard_map/back/pallas_call | solution.py:75
  429.1 2.1 fusion.6
  432.1 9.6 %back.6 = (f32[1024,128]{1,0:T(8,128)}, f32[256,128]{1,0:T(8,128)}, f32[392,128]{1,0:T(8,128)}) custom-call(f32[4096,128]{1,0:T(8,128)} %get-tuple-element.89.refs_0_, f32[4096,128]{1,0:T(8,128)} %get-tuple-element.124.refs_1_, f32[16,256,128]{2,1,0:T(8,128)} %get-tuple-element.125.refs_2_, f32[256,128]{1,0:T(8,128)} %get-tuple-element.136.refs_3_, ...), custom_call_target="tpu_custom_call" | custom-call | flops 1000000000 | bytes 3000000 | tf_op jit(solution)/shard_map/back/pallas_call | solution.py:75
  445.3 9.7 %back.7 = (f32[1024,128]{1,0:T(8,128)}, f32[256,128]{1,0:T(8,128)}, f32[392,128]{1,0:T(8,128)}) custom-call(f32[4096,128]{1,0:T(8,128)} %get-tuple-element.89.refs_0_, f32[4096,128]{1,0:T(8,128)} %get-tuple-element.124.refs_1_, f32[16,256,128]{2,1,0:T(8,128)} %get-tuple-element.125.refs_2_, f32[256,128]{1,0:T(8,128)} %get-tuple-element.140.refs_3_, ...), custom_call_target="tpu_custom_call" | custom-call | flops 1000000000 | bytes 3000000 | tf_op jit(solution)/shard_map/back/pallas_call | solution.py:75
  464.2 2.1 collective-permute-start.69
  466.3 7.0 %back_norm.1 = (f32[512,1024]{1,0:T(8,128)}, f32[1,1024]{1,0:T(1,128)}, f32[512,128]{1,0:T(8,128)}, f32[16,128]{1,0:T(8,128)}) custom-call(f32[1024,128]{1,0:T(8,128)} %get-tuple-element.143.refs_1_.refs_0_, f32[1024,128]{1,0:T(8,128)} %get-tuple-element.142.refs_1_, f32[1024,128]{1,0:T(8,128)} %get-tuple-element.139.refs_1_.refs_2_, ...), custom_call_target="tpu_custom_call" | custom-call | flops 600000000 | bytes 1800000 | tf_op jit(solution)/shard_map/back_norm/pallas_call | solution.py:75
  474.7 4.5 collective-permute-done.69
  483.3 3.4 collective-permute-done.70
  491.3 3.0 collective-permute-start.72
  495.1 8.0 %collective-permute-done.72 = f32[84,128]{1,0:T(8,128)S(1)} collective-permute-done((f32[84,128]{1,0:T(8,128)S(1)}, f32[84,128]{1,0:T(8,128)S(1)}, u32[]{:S(2)}, u32[]{:S(2)}) %collective-permute-start.72) | collective-permute-done | bytes 43040 | tf_op jit(solution)/shard_map/ppermute | solution.py:437
  503.8 5.9 %input.1 = f32[512,1024]{1,0:T(8,128)} custom-call(f32[512,1024]{1,0:T(8,128)} %get-tuple-element.145.refs_0_, f32[512,128]{1,0:T(8,128)} %get-tuple-element.146.refs_1_, f32[1,128]{1,0:T(1,128)} %fusion.53.refs_2_, bf16[512,1024]{1,0:T(8,128)(2,1)} %bitcast.201, f32[512,1]{1,0:T(8,128)} %copy.85.refs_1_.refs_3_.refs_6_.refs_4_, ...), custom_call_target="tpu_custom_call" | custom-call | flops 600000000 | bytes 1800000 | tf_op jit(solution)/shard_map/input/pallas_call | solution.py:75
  511.1 3.4 collective-permute-done.79
  (511 shorter events, 153.1 us)
Async XLA Ops:
  2.8 8.8 %collective-permute-start = (f32[1,1,56]{2,1,0:T(1,128)S(1)}, f32[1,1,56]{2,1,0:T(1,128)S(1)}, u32[]{:S(2)}, u32[]{:S(2)}) collective-permute-start(f32[1,1,56]{2,1,0:T(1,128)S(1)} %maximum_convert_fusion), channel_id=1, source_target_pairs={{0,1},{1,0},{2,3},{3,2},{4,5},{5,4},{6,7},{7,6},{8,9},{9,8},{10,11... | collective-permute-start | bytes 680 | tf_op jit(solution)/shard_map/ppermute | solution.py:437
  5.2 19.0 %collective-permute-start.3 = (bf16[1,32,3072]{2,1,0:T(8,128)(2,1)S(1)}, bf16[1,32,3072]{2,1,0:T(8,128)(2,1)S(1)}, u32[]{:S(2)}, u32[]{:S(2)}) collective-permute-start(bf16[1,32,3072]{2,1,0:T(8,128)(2,1)S(1)} %maximum_bitcast_fusion.1), channel_id=1, source_target_pairs={{0,16},{4,20},{8,24},{12,28},{16,0},{20,4},{24,8},{28,12},{1,17},{... | collective-permute-start | bytes 589832 | tf_op jit(solution)/shard_map/ppermute | solution.py:437
  9.0 18.8 %collective-permute-start.4 = (bf16[1,32,3328]{2,1,0:T(8,128)(2,1)S(1)}, bf16[1,32,3328]{2,1,0:T(8,128)(2,1)S(1)}, u32[]{:S(2)}, u32[]{:S(2)}) collective-permute-start(bf16[1,32,3328]{2,1,0:T(8,128)(2,1)S(1)} %maximum_bitcast_fusion), channel_id=1, source_target_pairs={{0,16},{4,20},{8,24},{12,28},{16,0},{20,4},{24,8},{28,12},{1,17},{... | collective-permute-start | bytes 638984 | tf_op jit(solution)/shard_map/ppermute | solution.py:437
  20.3 19.2 %collective-permute-start.7 = (bf16[1,80,1024]{2,1,0:T(8,128)(2,1)S(1)}, bf16[1,80,1024]{2,1,0:T(8,128)(2,1)S(1)}, u32[]{:S(2)}, u32[]{:S(2)}) collective-permute-start(bf16[1,80,1024]{2,1,0:T(8,128)(2,1)S(1)} %convert_bitcast_fusion.2), channel_id=1, source_target_pairs={{0,2},{2,0},{1,3},{3,1},{4,6},{6,4},{5,7},{7,5},{8,10},{10,8},{9,1... | collective-permute-start | bytes 491528 | tf_op jit(solution)/shard_map/ppermute | solution.py:437
  33.2 9.1 %collective-permute-start.6 = (f32[288,128]{1,0:T(8,128)S(1)}, f32[288,128]{1,0:T(8,128)S(1)}, u32[]{:S(2)}, u32[]{:S(2)}) collective-permute-start(f32[288,128]{1,0:T(8,128)S(1)} %pad_maximum_fusion.27), channel_id=1, source_target_pairs={{0,16},{4,20},{8,24},{12,28},{16,0},{20,4},{24,8},{28,12},{1,17},{... | collective-permute-start | bytes 442376 | tf_op jit(solution)/shard_map/ppermute | solution.py:437
  40.3 18.0 %collective-permute-start.8 = (bf16[2,32,3072]{2,1,0:T(8,128)(2,1)S(1)}, bf16[2,32,3072]{2,1,0:T(8,128)(2,1)}, u32[]{:S(2)}, u32[]{:S(2)}) collective-permute-start(bf16[2,32,3072]{2,1,0:T(8,128)(2,1)S(1)} %copy-done.31), channel_id=1, source_target_pairs={{0,8},{4,12},{8,0},{12,4},{16,24},{20,28},{24,16},{28,20},{1,9},{5... | collective-permute-start | bytes 1179656 | tf_op jit(solution)/shard_map/ppermute | solution.py:437
  42.1 18.5 %collective-permute-start.9 = (bf16[2,32,3328]{2,1,0:T(8,128)(2,1)S(1)}, bf16[2,32,3328]{2,1,0:T(8,128)(2,1)}, u32[]{:S(2)}, u32[]{:S(2)}) collective-permute-start(bf16[2,32,3328]{2,1,0:T(8,128)(2,1)S(1)} %copy-done.54), channel_id=1, source_target_pairs={{0,8},{4,12},{8,0},{12,4},{16,24},{20,28},{24,16},{28,20},{1,9},{5... | collective-permute-start | bytes 1277960 | tf_op jit(solution)/shard_map/ppermute | solution.py:437
  56.7 9.3 %collective-permute-start.10 = (bf16[2,80,1024]{2,1,0:T(8,128)(2,1)}, bf16[2,80,1024]{2,1,0:T(8,128)(2,1)}, u32[]{:S(2)}, u32[]{:S(2)}) collective-permute-start(bf16[2,80,1024]{2,1,0:T(8,128)(2,1)} %tie.40), channel_id=1, source_target_pairs={{0,4},{4,0},{8,12},{12,8},{16,20},{20,16},{24,28},{28,24},{1,5},{5... | collective-permute-start | bytes 983048 | tf_op jit(solution)/shard_map/ppermute | solution.py:437
  69.5 13.6 %collective-permute-start.16 = (bf16[1,32,2560]{2,1,0:T(8,128)(2,1)S(1)}, bf16[1,32,2560]{2,1,0:T(8,128)(2,1)S(1)}, u32[]{:S(2)}, u32[]{:S(2)}) collective-permute-start(bf16[1,32,2560]{2,1,0:T(8,128)(2,1)S(1)} %copy-done.55), channel_id=1, source_target_pairs={{0,16},{4,20},{8,24},{12,28},{16,0},{20,4},{24,8},{28,12},{1,17},{... | collective-permute-start | bytes 491528 | tf_op jit(solution)/shard_map/ppermute | solution.py:437
  69.5 22.5 %collective-permute-start.14 = (bf16[4,32,3072]{2,1,0:T(8,128)(2,1)S(1)}, bf16[4,32,3072]{2,1,0:T(8,128)(2,1)S(1)}, u32[]{:S(2)}, u32[]{:S(2)}) collective-permute-start(bf16[4,32,3072]{2,1,0:T(8,128)(2,1)S(1)} %copy-done.21), channel_id=1, source_target_pairs={{0,4},{4,0},{8,12},{12,8},{16,20},{20,16},{24,28},{28,24},{1,5},{5... | collective-permute-start | bytes 2359304 | tf_op jit(solution)/shard_map/ppermute | solution.py:437
  70.6 22.7 %collective-permute-start.15 = (bf16[4,32,3328]{2,1,0:T(8,128)(2,1)S(1)}, bf16[4,32,3328]{2,1,0:T(8,128)(2,1)S(1)}, u32[]{:S(2)}, u32[]{:S(2)}) collective-permute-start(bf16[4,32,3328]{2,1,0:T(8,128)(2,1)S(1)} %copy-done.20), channel_id=1, source_target_pairs={{0,2},{2,0},{1,3},{3,1},{4,6},{6,4},{5,7},{7,5},{8,10},{10,8},{9,1... | collective-permute-start | bytes 2555912 | tf_op jit(solution)/shard_map/ppermute | solution.py:437
  72.1 15.8 %collective-permute-start.17 = (bf16[1,32,2560]{2,1,0:T(8,128)(2,1)S(1)}, bf16[1,32,2560]{2,1,0:T(8,128)(2,1)S(1)}, u32[]{:S(2)}, u32[]{:S(2)}) collective-permute-start(bf16[1,32,2560]{2,1,0:T(8,128)(2,1)S(1)} %copy-done.56), channel_id=1, source_target_pairs={{0,16},{4,20},{8,24},{12,28},{16,0},{20,4},{24,8},{28,12},{1,17},{... | collective-permute-start | bytes 491528 | tf_op jit(solution)/shard_map/ppermute | solution.py:437
  94.7 36.0 %collective-permute-start.23 = (bf16[8,32,3328]{2,1,0:T(8,128)(2,1)}, bf16[8,32,3328]{2,1,0:T(8,128)(2,1)S(1)}, u32[]{:S(2)}, u32[]{:S(2)}) collective-permute-start(bf16[8,32,3328]{2,1,0:T(8,128)(2,1)} %tie.50.refs_13_.refs_9_.refs_19_.refs_8_), channel_id=1, source_target_pairs={{0,4},{4,0},{8,12},{12,8},{16,20},{20,16},{24,28},{28,24},{1,5},{5... | collective-permute-start | bytes 5111816 | tf_op jit(solution)/shard_map/ppermute | solution.py:437
  95.9 32.9 %collective-permute-start.20 = (bf16[8,32,3072]{2,1,0:T(8,128)(2,1)}, bf16[8,32,3072]{2,1,0:T(8,128)(2,1)S(1)}, u32[]{:S(2)}, u32[]{:S(2)}) collective-permute-start(bf16[8,32,3072]{2,1,0:T(8,128)(2,1)} %tie.49.refs_9_.refs_5_.refs_15_.refs_4_), channel_id=1, source_target_pairs={{0,2},{2,0},{1,3},{3,1},{4,6},{6,4},{5,7},{7,5},{8,10},{10,8},{9,1... | collective-permute-start | bytes 4718600 | tf_op jit(solution)/shard_map/ppermute | solution.py:437
  98.5 8.4 %collective-permute-start.19 = (bf16[2,32,2560]{2,1,0:T(8,128)(2,1)}, bf16[2,32,2560]{2,1,0:T(8,128)(2,1)}, u32[]{:S(2)}, u32[]{:S(2)}) collective-permute-start(bf16[2,32,2560]{2,1,0:T(8,128)(2,1)} %tie.48), channel_id=1, source_target_pairs={{0,8},{4,12},{8,0},{12,4},{16,24},{20,28},{24,16},{28,20},{1,9},{5... | collective-permute-start | bytes 983048 | tf_op jit(solution)/shard_map/ppermute | solution.py:437
  98.5 13.5 %collective-permute-start.18 = (bf16[2,32,2560]{2,1,0:T(8,128)(2,1)}, bf16[2,32,2560]{2,1,0:T(8,128)(2,1)S(1)}, u32[]{:S(2)}, u32[]{:S(2)}) collective-permute-start(bf16[2,32,2560]{2,1,0:T(8,128)(2,1)} %tie.47), channel_id=1, source_target_pairs={{0,8},{4,12},{8,0},{12,4},{16,24},{20,28},{24,16},{28,20},{1,9},{5... | collective-permute-start | bytes 983048 | tf_op jit(solution)/shard_map/ppermute | solution.py:437
  112.9 25.0 %collective-permute-start.36 = (bf16[4,80,1024]{2,1,0:T(8,128)(2,1)}, bf16[4,80,1024]{2,1,0:T(8,128)(2,1)}, u32[]{:S(2)}, u32[]{:S(2)}) collective-permute-start(bf16[4,80,1024]{2,1,0:T(8,128)(2,1)} %tie.59), channel_id=1, source_target_pairs={{0,16},{4,20},{8,24},{12,28},{16,0},{20,4},{24,8},{28,12},{1,17},{... | collective-permute-start | bytes 1966088 | tf_op jit(solution)/shard_map/ppermute | solution.py:437
  131.9 12.9 %collective-permute-start.27 = (bf16[4,32,2560]{2,1,0:T(8,128)(2,1)}, bf16[4,32,2560]{2,1,0:T(8,128)(2,1)}, u32[]{:S(2)}, u32[]{:S(2)}) collective-permute-start(bf16[4,32,2560]{2,1,0:T(8,128)(2,1)} %tie.52), channel_id=1, source_target_pairs={{0,2},{2,0},{1,3},{3,1},{4,6},{6,4},{5,7},{7,5},{8,10},{10,8},{9,1... | collective-permute-start | bytes 1966088 | tf_op jit(solution)/shard_map/ppermute | solution.py:437
  133.5 12.2 %collective-permute-start.26 = (bf16[4,32,2560]{2,1,0:T(8,128)(2,1)}, bf16[4,32,2560]{2,1,0:T(8,128)(2,1)}, u32[]{:S(2)}, u32[]{:S(2)}) collective-permute-start(bf16[4,32,2560]{2,1,0:T(8,128)(2,1)} %tie.51), channel_id=1, source_target_pairs={{0,4},{4,0},{8,12},{12,8},{16,20},{20,16},{24,28},{28,24},{1,5},{5... | collective-permute-start | bytes 1966088 | tf_op jit(solution)/shard_map/ppermute | solution.py:437
  137.9 12.4 %collective-permute-start.28 = (bf16[512,1024]{1,0:T(8,128)(2,1)}, bf16[512,1024]{1,0:T(8,128)(2,1)}, u32[]{:S(2)}, u32[]{:S(2)}) collective-permute-start(bf16[512,1024]{1,0:T(8,128)(2,1)} %tie.53), channel_id=1, source_target_pairs={{0,1},{1,0},{2,3},{3,2},{4,5},{5,4},{6,7},{7,6},{8,9},{9,8},{10,11... | collective-permute-start | bytes 3145736 | tf_op jit(solution)/shard_map/ppermute | solution.py:437
  139.3 12.4 %collective-permute-start.21 = (bf16[8,32,3072]{2,1,0:T(8,128)(2,1)S(1)}, bf16[8,32,3072]{2,1,0:T(8,128)(2,1)}, u32[]{:S(2)}, u32[]{:S(2)}) collective-permute-start(bf16[8,32,3072]{2,1,0:T(8,128)(2,1)S(1)} %copy-done.2), channel_id=1, source_target_pairs={{0,1},{1,0},{2,3},{3,2},{4,5},{5,4},{6,7},{7,6},{8,9},{9,8},{10,11... | collective-permute-start | bytes 4718600 | tf_op jit(solution)/shard_map/ppermute | solution.py:437
  141.7 14.5 %collective-permute-start.24 = (bf16[8,32,3328]{2,1,0:T(8,128)(2,1)S(1)}, bf16[8,32,3328]{2,1,0:T(8,128)(2,1)}, u32[]{:S(2)}, u32[]{:S(2)}) collective-permute-start(bf16[8,32,3328]{2,1,0:T(8,128)(2,1)S(1)} %copy-done.1), channel_id=1, source_target_pairs={{0,1},{1,0},{2,3},{3,2},{4,5},{5,4},{6,7},{7,6},{8,9},{9,8},{10,11... | collective-permute-start | bytes 5111816 | tf_op jit(solution)/shard_map/ppermute | solution.py:437
  144.8 12.1 %collective-permute-start.22 = (bf16[8,32,3072]{2,1,0:T(8,128)(2,1)}, bf16[8,32,3072]{2,1,0:T(8,128)(2,1)}, u32[]{:S(2)}, u32[]{:S(2)}) collective-permute-start(bf16[8,32,3072]{2,1,0:T(8,128)(2,1)} %copy-done.4), channel_id=1, source_target_pairs={{0,1},{1,0},{2,3},{3,2},{4,5},{5,4},{6,7},{7,6},{8,9},{9,8},{10,11... | collective-permute-start | bytes 4718600 | tf_op jit(solution)/shard_map/ppermute | solution.py:437
  145.6 11.2 %collective-permute-start.25 = (bf16[8,32,3328]{2,1,0:T(8,128)(2,1)}, bf16[8,32,3328]{2,1,0:T(8,128)(2,1)}, u32[]{:S(2)}, u32[]{:S(2)}) collective-permute-start(bf16[8,32,3328]{2,1,0:T(8,128)(2,1)} %copy-done.3), channel_id=1, source_target_pairs={{0,1},{1,0},{2,3},{3,2},{4,5},{5,4},{6,7},{7,6},{8,9},{9,8},{10,11... | collective-permute-start | bytes 5111816 | tf_op jit(solution)/shard_map/ppermute | solution.py:437
  150.2 31.5 %collective-permute-start.37 = (bf16[8,80,1024]{2,1,0:T(8,128)(2,1)}, bf16[8,80,1024]{2,1,0:T(8,128)(2,1)}, u32[]{:S(2)}, u32[]{:S(2)}) collective-permute-start(bf16[8,80,1024]{2,1,0:T(8,128)(2,1)} %tie.60.refs_0_), channel_id=1, source_target_pairs={{0,8},{4,12},{8,0},{12,4},{16,24},{20,28},{24,16},{28,20},{1,9},{5... | collective-permute-start | bytes 3932168 | tf_op jit(solution)/shard_map/ppermute | solution.py:437
  151.7 31.1 %collective-permute-start.33 = (bf16[8,32,2560]{2,1,0:T(8,128)(2,1)}, bf16[8,32,2560]{2,1,0:T(8,128)(2,1)S(1)}, u32[]{:S(2)}, u32[]{:S(2)}) collective-permute-start(bf16[8,32,2560]{2,1,0:T(8,128)(2,1)} %pad_maximum_fusion.3.refs_18_.refs_0_.refs_2_), channel_id=1, source_target_pairs={{0,4},{4,0},{8,12},{12,8},{16,20},{20,16},{24,28},{28,24},{1,5},{5... | collective-permute-start | bytes 3932168 | tf_op jit(solution)/shard_map/ppermute | solution.py:437
  156.2 30.8 %collective-permute-start.30 = (bf16[8,32,2560]{2,1,0:T(8,128)(2,1)}, bf16[8,32,2560]{2,1,0:T(8,128)(2,1)S(1)}, u32[]{:S(2)}, u32[]{:S(2)}) collective-permute-start(bf16[8,32,2560]{2,1,0:T(8,128)(2,1)} %pad_maximum_fusion.2.refs_17_.refs_0_.refs_1_), channel_id=1, source_target_pairs={{0,2},{2,0},{1,3},{3,1},{4,6},{6,4},{5,7},{7,5},{8,10},{10,8},{9,1... | collective-permute-start | bytes 3932168 | tf_op jit(solution)/shard_map/ppermute | solution.py:437
  181.8 8.2 %collective-permute-start.38 = (bf16[8,80,1024]{2,1,0:T(8,128)(2,1)}, bf16[8,80,1024]{2,1,0:T(8,128)(2,1)}, u32[]{:S(2)}, u32[]{:S(2)}) collective-permute-start(bf16[8,80,1024]{2,1,0:T(8,128)(2,1)} %tie.61.refs_11_.refs_3_), channel_id=1, source_target_pairs={{0,1},{1,0},{2,3},{3,2},{4,5},{5,4},{6,7},{7,6},{8,9},{9,8},{10,11... | collective-permute-start | bytes 3932168 | tf_op jit(solution)/shard_map/ppermute | solution.py:437
  182.8 15.9 %collective-permute-start.40 = (bf16[512,2048]{1,0:T(8,128)(2,1)}, bf16[512,2048]{1,0:T(8,128)(2,1)}, u32[]{:S(2)}, u32[]{:S(2)}) collective-permute-start(bf16[512,2048]{1,0:T(8,128)(2,1)} %get-tuple-element.93.refs_1_), channel_id=1, source_target_pairs={{0,1},{1,0},{2,3},{3,2},{4,5},{5,4},{6,7},{7,6},{8,9},{9,8},{10,11... | collective-permute-start | bytes 6291464 | tf_op jit(solution)/shard_map/ppermute | solution.py:437
  187.0 10.1 %collective-permute-start.35 = (bf16[8,32,2560]{2,1,0:T(8,128)(2,1)}, bf16[8,32,2560]{2,1,0:T(8,128)(2,1)}, u32[]{:S(2)}, u32[]{:S(2)}) collective-permute-start(bf16[8,32,2560]{2,1,0:T(8,128)(2,1)} %tie.58.refs_8_.refs_12_), channel_id=1, source_target_pairs={{0,1},{1,0},{2,3},{3,2},{4,5},{5,4},{6,7},{7,6},{8,9},{9,8},{10,11... | collective-permute-start | bytes 3932168 | tf_op jit(solution)/shard_map/ppermute | solution.py:437
  189.4 7.7 %collective-permute-start.34 = (bf16[8,32,2560]{2,1,0:T(8,128)(2,1)S(1)}, bf16[8,32,2560]{2,1,0:T(8,128)(2,1)S(1)}, u32[]{:S(2)}, u32[]{:S(2)}) collective-permute-start(bf16[8,32,2560]{2,1,0:T(8,128)(2,1)S(1)} %copy-done.6), channel_id=1, source_target_pairs={{0,1},{1,0},{2,3},{3,2},{4,5},{5,4},{6,7},{7,6},{8,9},{9,8},{10,11... | collective-permute-start | bytes 3932168 | tf_op jit(solution)/shard_map/ppermute | solution.py:437
  189.4 7.7 %collective-permute-start.32 = (bf16[8,32,2560]{2,1,0:T(8,128)(2,1)}, bf16[8,32,2560]{2,1,0:T(8,128)(2,1)S(1)}, u32[]{:S(2)}, u32[]{:S(2)}) collective-permute-start(bf16[8,32,2560]{2,1,0:T(8,128)(2,1)} %tie.56.refs_4_.refs_8_), channel_id=1, source_target_pairs={{0,1},{1,0},{2,3},{3,2},{4,5},{5,4},{6,7},{7,6},{8,9},{9,8},{10,11... | collective-permute-start | bytes 3932168 | tf_op jit(solution)/shard_map/ppermute | solution.py:437
  190.0 8.7 %collective-permute-start.31 = (bf16[8,32,2560]{2,1,0:T(8,128)(2,1)S(1)}, bf16[8,32,2560]{2,1,0:T(8,128)(2,1)S(1)}, u32[]{:S(2)}, u32[]{:S(2)}) collective-permute-start(bf16[8,32,2560]{2,1,0:T(8,128)(2,1)S(1)} %copy-done.5), channel_id=1, source_target_pairs={{0,1},{1,0},{2,3},{3,2},{4,5},{5,4},{6,7},{7,6},{8,9},{9,8},{10,11... | collective-permute-start | bytes 3932168 | tf_op jit(solution)/shard_map/ppermute | solution.py:437
  218.8 8.9 %collective-permute-start.44 = (bf16[512,2560]{1,0:T(8,128)(2,1)}, bf16[512,2560]{1,0:T(8,128)(2,1)}, u32[]{:S(2)}, u32[]{:S(2)}) collective-permute-start(bf16[512,2560]{1,0:T(8,128)(2,1)} %get-tuple-element.95.refs_1_), channel_id=1, source_target_pairs={{0,1},{1,0},{2,3},{3,2},{4,5},{5,4},{6,7},{7,6},{8,9},{9,8},{10,11... | collective-permute-start | bytes 7864328 | tf_op jit(solution)/shard_map/ppermute | solution.py:437
  219.0 17.2 %collective-permute-start.43 = (bf16[512,2560]{1,0:T(8,128)(2,1)}, bf16[512,2560]{1,0:T(8,128)(2,1)S(1)}, u32[]{:S(2)}, u32[]{:S(2)}) collective-permute-start(bf16[512,2560]{1,0:T(8,128)(2,1)} %get-tuple-element.98.refs_2_), channel_id=1, source_target_pairs={{0,1},{1,0},{2,3},{3,2},{4,5},{5,4},{6,7},{7,6},{8,9},{9,8},{10,11... | collective-permute-start | bytes 7864328 | tf_op jit(solution)/shard_map/ppermute | solution.py:437
  219.4 16.8 %collective-permute-start.42 = (bf16[512,1024]{1,0:T(8,128)(2,1)S(1)}, bf16[512,1024]{1,0:T(8,128)(2,1)}, u32[]{:S(2)}, u32[]{:S(2)}) collective-permute-start(bf16[512,1024]{1,0:T(8,128)(2,1)S(1)} %copy-done), channel_id=1, source_target_pairs={{0,1},{1,0},{2,3},{3,2},{4,5},{5,4},{6,7},{7,6},{8,9},{9,8},{10,11... | collective-permute-start | bytes 3145736 | tf_op jit(solution)/shard_map/ppermute | solution.py:437
  235.2 38.5 %collective-permute-start.46 = (bf16[8,160,512]{2,1,0:T(8,128)(2,1)}, bf16[8,160,512]{2,1,0:T(8,128)(2,1)}, u32[]{:S(2)}, u32[]{:S(2)}) collective-permute-start(bf16[8,160,512]{2,1,0:T(8,128)(2,1)} %get-tuple-element.114), channel_id=1, source_target_pairs={{0,2},{2,0},{1,3},{3,1},{4,6},{6,4},{5,7},{7,5},{8,10},{10,8},{9,1... | collective-permute-start | bytes 3932168 | tf_op jit(solution)/shard_map/ppermute | solution.py:437
  244.8 40.8 %collective-permute-start.47 = (bf16[8,64,1280]{2,1,0:T(8,128)(2,1)}, bf16[8,64,1280]{2,1,0:T(8,128)(2,1)S(1)}, u32[]{:S(2)}, u32[]{:S(2)}) collective-permute-start(bf16[8,64,1280]{2,1,0:T(8,128)(2,1)} %get-tuple-element.116), channel_id=1, source_target_pairs={{0,4},{4,0},{8,12},{12,8},{16,20},{20,16},{24,28},{28,24},{1,5},{5... | collective-permute-start | bytes 3932168 | tf_op jit(solution)/shard_map/ppermute | solution.py:437
  268.5 9.6 %collective-permute-start.45 = (bf16[512,512]{1,0:T(8,128)(2,1)}, bf16[512,512]{1,0:T(8,128)(2,1)}, u32[]{:S(2)}, u32[]{:S(2)}) collective-permute-start(bf16[512,512]{1,0:T(8,128)(2,1)} %get-tuple-element.113), channel_id=1, source_target_pairs={{0,1},{1,0},{2,3},{3,2},{4,5},{5,4},{6,7},{7,6},{8,9},{9,8},{10,11... | collective-permute-start | bytes 1572872 | tf_op jit(solution)/shard_map/ppermute | solution.py:437
  268.6 38.7 %collective-permute-start.48 = (bf16[8,64,1280]{2,1,0:T(8,128)(2,1)}, bf16[8,64,1280]{2,1,0:T(8,128)(2,1)}, u32[]{:S(2)}, u32[]{:S(2)}) collective-permute-start(bf16[8,64,1280]{2,1,0:T(8,128)(2,1)} %get-tuple-element.120), channel_id=1, source_target_pairs={{0,2},{2,0},{1,3},{3,1},{4,6},{6,4},{5,7},{7,5},{8,10},{10,8},{9,1... | collective-permute-start | bytes 3932168 | tf_op jit(solution)/shard_map/ppermute | solution.py:437
  276.7 34.7 %collective-permute-start.49 = (bf16[4,160,512]{2,1,0:T(8,128)(2,1)S(1)}, bf16[4,160,512]{2,1,0:T(8,128)(2,1)}, u32[]{:S(2)}, u32[]{:S(2)}) collective-permute-start(bf16[4,160,512]{2,1,0:T(8,128)(2,1)S(1)} %get-tuple-element.172.refs_5_), channel_id=1, source_target_pairs={{0,4},{4,0},{8,12},{12,8},{16,20},{20,16},{24,28},{28,24},{1,5},{5... | collective-permute-start | bytes 1966088 | tf_op jit(solution)/shard_map/ppermute | solution.py:437
  304.6 51.2 %collective-permute-start.53 = (bf16[512,1024]{1,0:T(8,128)(2,1)}, bf16[512,1024]{1,0:T(8,128)(2,1)}, u32[]{:S(2)}, u32[]{:S(2)}) collective-permute-start(bf16[512,1024]{1,0:T(8,128)(2,1)} %get-tuple-element.121.refs_1_), channel_id=1, source_target_pairs={{0,1},{1,0},{2,3},{3,2},{4,5},{5,4},{6,7},{7,6},{8,9},{9,8},{10,11... | collective-permute-start | bytes 3145736 | tf_op jit(solution)/shard_map/ppermute | solution.py:437
  304.7 43.5 %collective-permute-start.56 = (bf16[4,64,1280]{2,1,0:T(8,128)(2,1)S(1)}, bf16[4,64,1280]{2,1,0:T(8,128)(2,1)}, u32[]{:S(2)}, u32[]{:S(2)}) collective-permute-start(bf16[4,64,1280]{2,1,0:T(8,128)(2,1)S(1)} %copy-done.44), channel_id=1, source_target_pairs={{0,2},{2,0},{1,3},{3,1},{4,6},{6,4},{5,7},{7,5},{8,10},{10,8},{9,1... | collective-permute-start | bytes 1966088 | tf_op jit(solution)/shard_map/ppermute | solution.py:437
  306.2 26.3 %collective-permute-start.50 = (bf16[8,128,512]{2,1,0:T(8,128)(2,1)}, bf16[8,128,512]{2,1,0:T(8,128)(2,1)}, u32[]{:S(2)}, u32[]{:S(2)}) collective-permute-start(bf16[8,128,512]{2,1,0:T(8,128)(2,1)} %get-tuple-element.123), channel_id=1, source_target_pairs={{0,4},{4,0},{8,12},{12,8},{16,20},{20,16},{24,28},{28,24},{1,5},{5... | collective-permute-start | bytes 3145736 | tf_op jit(solution)/shard_map/ppermute | solution.py:437
  310.5 41.2 %collective-permute-start.57 = (bf16[4,64,1280]{2,1,0:T(8,128)(2,1)}, bf16[4,64,1280]{2,1,0:T(8,128)(2,1)}, u32[]{:S(2)}, u32[]{:S(2)}) collective-permute-start(bf16[4,64,1280]{2,1,0:T(8,128)(2,1)} %get-tuple-element.170.refs_12_), channel_id=1, source_target_pairs={{0,4},{4,0},{8,12},{12,8},{16,20},{20,16},{24,28},{28,24},{1,5},{5... | collective-permute-start | bytes 1966088 | tf_op jit(solution)/shard_map/ppermute | solution.py:437
  313.2 12.7 %collective-permute-start.51 = (bf16[2,160,512]{2,1,0:T(8,128)(2,1)S(1)}, bf16[2,160,512]{2,1,0:T(8,128)(2,1)S(1)}, u32[]{:S(2)}, u32[]{:S(2)}) collective-permute-start(bf16[2,160,512]{2,1,0:T(8,128)(2,1)S(1)} %get-tuple-element.184.refs_13_), channel_id=1, source_target_pairs={{0,8},{4,12},{8,0},{12,4},{16,24},{20,28},{24,16},{28,20},{1,9},{5... | collective-permute-start | bytes 983048 | tf_op jit(solution)/shard_map/ppermute | solution.py:437
  326.6 30.3 %collective-permute-start.54 = (bf16[512,1152]{1,0:T(8,128)(2,1)}, bf16[512,1152]{1,0:T(8,128)(2,1)S(1)}, u32[]{:S(2)}, u32[]{:S(2)}) collective-permute-start(bf16[512,1152]{1,0:T(8,128)(2,1)} %get-tuple-element.128), channel_id=1, source_target_pairs={{0,1},{1,0},{2,3},{3,2},{4,5},{5,4},{6,7},{7,6},{8,9},{9,8},{10,11... | collective-permute-start | bytes 3538952 | tf_op jit(solution)/shard_map/ppermute | solution.py:437
  332.5 32.9 %collective-permute-start.58 = (bf16[1,160,512]{2,1,0:T(8,128)(2,1)}, bf16[1,160,512]{2,1,0:T(8,128)(2,1)}, u32[]{:S(2)}, u32[]{:S(2)}) collective-permute-start(bf16[1,160,512]{2,1,0:T(8,128)(2,1)} %fusion.34.refs_5_), channel_id=1, source_target_pairs={{0,16},{4,20},{8,24},{12,28},{16,0},{20,4},{24,8},{28,12},{1,17},{... | collective-permute-start | bytes 491528 | tf_op jit(solution)/shard_map/ppermute | solution.py:437
  348.2 44.7 %collective-permute-start.60 = (bf16[4,128,512]{2,1,0:T(8,128)(2,1)}, bf16[4,128,512]{2,1,0:T(8,128)(2,1)}, u32[]{:S(2)}, u32[]{:S(2)}) collective-permute-start(bf16[4,128,512]{2,1,0:T(8,128)(2,1)} %get-tuple-element.178.refs_4_), channel_id=1, source_target_pairs={{0,2},{2,0},{1,3},{3,1},{4,6},{6,4},{5,7},{7,5},{8,10},{10,8},{9,1... | collective-permute-start | bytes 1572872 | tf_op jit(solution)/shard_map/ppermute | solution.py:437
  354.5 40.8 %collective-permute-start.61 = (bf16[2,64,2560]{2,1,0:T(8,128)(2,1)}, bf16[2,64,2560]{2,1,0:T(8,128)(2,1)}, u32[]{:S(2)}, u32[]{:S(2)}) collective-permute-start(bf16[2,64,2560]{2,1,0:T(8,128)(2,1)} %pad_maximum_fusion.10.refs_6_), channel_id=1, source_target_pairs={{0,8},{4,12},{8,0},{12,4},{16,24},{20,28},{24,16},{28,20},{1,9},{5... | collective-permute-start | bytes 1966088 | tf_op jit(solution)/shard_map/ppermute | solution.py:437
  355.8 19.4 %collective-permute-start.52 = (f32[32,8,128]{2,1,0:T(8,128)S(1)}, f32[32,8,128]{2,1,0:T(8,128)S(1)}, u32[]{:S(2)}, u32[]{:S(2)}) collective-permute-start(f32[32,8,128]{2,1,0:T(8,128)S(1)} %bitcast.231), channel_id=1, source_target_pairs={{0,4},{4,0},{8,12},{12,8},{16,20},{20,16},{24,28},{28,24},{1,5},{5... | collective-permute-start | bytes 393224 | tf_op jit(solution)/shard_map/ppermute | solution.py:437
  376.8 35.8 %collective-permute-start.62 = (bf16[8,64,1024]{2,1,0:T(8,128)(2,1)}, bf16[8,64,1024]{2,1,0:T(8,128)(2,1)S(1)}, u32[]{:S(2)}, u32[]{:S(2)}) collective-permute-start(bf16[8,64,1024]{2,1,0:T(8,128)(2,1)} %get-tuple-element.134), channel_id=1, source_target_pairs={{0,2},{2,0},{1,3},{3,1},{4,6},{6,4},{5,7},{7,5},{8,10},{10,8},{9,1... | collective-permute-start | bytes 3145736 | tf_op jit(solution)/shard_map/ppermute | solution.py:437
  377.0 52.1 %collective-permute-start.64 = (bf16[8,64,1152]{2,1,0:T(8,128)(2,1)}, bf16[8,64,1152]{2,1,0:T(8,128)(2,1)}, u32[]{:S(2)}, u32[]{:S(2)}) collective-permute-start(bf16[8,64,1152]{2,1,0:T(8,128)(2,1)} %get-tuple-element.138), channel_id=1, source_target_pairs={{0,4},{4,0},{8,12},{12,8},{16,20},{20,16},{24,28},{28,24},{1,5},{5... | collective-permute-start | bytes 3538952 | tf_op jit(solution)/shard_map/ppermute | solution.py:437
  382.6 9.5 %collective-permute-start.59 = (f32[32,8,128]{2,1,0:T(8,128)}, f32[32,8,128]{2,1,0:T(8,128)S(1)}, u32[]{:S(2)}, u32[]{:S(2)}) collective-permute-start(f32[32,8,128]{2,1,0:T(8,128)} %tie.70), channel_id=1, source_target_pairs={{0,16},{4,20},{8,24},{12,28},{16,0},{20,4},{24,8},{28,12},{1,17},{... | collective-permute-start | bytes 393224 | tf_op jit(solution)/shard_map/ppermute | solution.py:437
  395.3 14.7 %collective-permute-start.63 = (bf16[2,128,512]{2,1,0:T(8,128)(2,1)}, bf16[2,128,512]{2,1,0:T(8,128)(2,1)}, u32[]{:S(2)}, u32[]{:S(2)}) collective-permute-start(bf16[2,128,512]{2,1,0:T(8,128)(2,1)} %get-tuple-element.190.refs_9_), channel_id=1, source_target_pairs={{0,8},{4,12},{8,0},{12,4},{16,24},{20,28},{24,16},{28,20},{1,9},{5... | collective-permute-start | bytes 786440 | tf_op jit(solution)/shard_map/ppermute | solution.py:437
  397.0 29.4 %collective-permute-start.65 = (bf16[1,64,2560]{2,1,0:T(8,128)(2,1)S(1)}, bf16[1,64,2560]{2,1,0:T(8,128)(2,1)}, u32[]{:S(2)}, u32[]{:S(2)}) collective-permute-start(bf16[1,64,2560]{2,1,0:T(8,128)(2,1)S(1)} %fusion.14.refs_10_), channel_id=1, source_target_pairs={{0,16},{4,20},{8,24},{12,28},{16,0},{20,4},{24,8},{28,12},{1,17},{... | collective-permute-start | bytes 983048 | tf_op jit(solution)/shard_map/ppermute | solution.py:437
  411.7 31.2 %collective-permute-start.66 = (bf16[1,128,512]{2,1,0:T(8,128)(2,1)S(1)}, bf16[1,128,512]{2,1,0:T(8,128)(2,1)}, u32[]{:S(2)}, u32[]{:S(2)}) collective-permute-start(bf16[1,128,512]{2,1,0:T(8,128)(2,1)S(1)} %fusion.38.refs_10_), channel_id=1, source_target_pairs={{0,16},{4,20},{8,24},{12,28},{16,0},{20,4},{24,8},{28,12},{1,17},{... | collective-permute-start | bytes 393224 | tf_op jit(solution)/shard_map/ppermute | solution.py:437
  414.3 46.5 %collective-permute-start.67 = (bf16[4,64,1024]{2,1,0:T(8,128)(2,1)}, bf16[4,64,1024]{2,1,0:T(8,128)(2,1)}, u32[]{:S(2)}, u32[]{:S(2)}) collective-permute-start(bf16[4,64,1024]{2,1,0:T(8,128)(2,1)} %get-tuple-element.176.refs_9_), channel_id=1, source_target_pairs={{0,4},{4,0},{8,12},{12,8},{16,20},{20,16},{24,28},{28,24},{1,5},{5... | collective-permute-start | bytes 1572872 | tf_op jit(solution)/shard_map/ppermute | solution.py:437
  429.0 29.3 %collective-permute-start.76 = (bf16[32,2560]{1,0:T(8,128)(2,1)}, bf16[32,2560]{1,0:T(8,128)(2,1)}, u32[]{:S(2)}, u32[]{:S(2)}) collective-permute-start(bf16[32,2560]{1,0:T(8,128)(2,1)} %fusion.32), channel_id=1, source_target_pairs={{0,1},{1,0},{2,3},{3,2},{4,5},{5,4},{6,7},{7,6},{8,9},{9,8},{10,11... | collective-permute-start | bytes 491528 | tf_op jit(solution)/shard_map/ppermute | solution.py:437
  431.2 31.2 %collective-permute-start.68 = (bf16[4,64,1152]{2,1,0:T(8,128)(2,1)S(1)}, bf16[4,64,1152]{2,1,0:T(8,128)(2,1)}, u32[]{:S(2)}, u32[]{:S(2)}) collective-permute-start(bf16[4,64,1152]{2,1,0:T(8,128)(2,1)S(1)} %get-tuple-element.174.refs_9_), channel_id=1, source_target_pairs={{0,2},{2,0},{1,3},{3,1},{4,6},{6,4},{5,7},{7,5},{8,10},{10,8},{9,1... | collective-permute-start | bytes 1769480 | tf_op jit(solution)/shard_map/ppermute | solution.py:437
  457.7 30.8 %collective-permute-start.75 = (bf16[64,512]{1,0:T(8,128)(2,1)}, bf16[64,512]{1,0:T(8,128)(2,1)}, u32[]{:S(2)}, u32[]{:S(2)}) collective-permute-start(bf16[64,512]{1,0:T(8,128)(2,1)} %fusion.41), channel_id=1, source_target_pairs={{0,1},{1,0},{2,3},{3,2},{4,5},{5,4},{6,7},{7,6},{8,9},{9,8},{10,11... | collective-permute-start | bytes 196616 | tf_op jit(solution)/shard_map/ppermute | solution.py:437
  464.2 14.9 %collective-permute-start.69 = (bf16[2,64,2176]{2,1,0:T(8,128)(2,1)S(1)}, bf16[2,64,2176]{2,1,0:T(8,128)(2,1)S(1)}, u32[]{:S(2)}, u32[]{:S(2)}) collective-permute-start(bf16[2,64,2176]{2,1,0:T(8,128)(2,1)S(1)} %pad_maximum_fusion.11.refs_12_), channel_id=1, source_target_pairs={{0,8},{4,12},{8,0},{12,4},{16,24},{20,28},{24,16},{28,20},{1,9},{5... | collective-permute-start | bytes 1671176 | tf_op jit(solution)/shard_map/ppermute | solution.py:437
  491.3 11.8 %collective-permute-start.72 = (f32[84,128]{1,0:T(8,128)S(1)}, f32[84,128]{1,0:T(8,128)S(1)}, u32[]{:S(2)}, u32[]{:S(2)}) collective-permute-start(f32[84,128]{1,0:T(8,128)S(1)} %pad_maximum_fusion.38), channel_id=1, source_target_pairs={{0,16},{4,20},{8,24},{12,28},{16,0},{20,4},{24,8},{28,12},{1,17},{... | collective-permute-start | bytes 129032 | tf_op jit(solution)/shard_map/ppermute | solution.py:437
  495.1 14.6 %collective-permute-start.73 = (bf16[1,64,2176]{2,1,0:T(8,128)(2,1)S(1)}, bf16[1,64,2176]{2,1,0:T(8,128)(2,1)S(1)}, u32[]{:S(2)}, u32[]{:S(2)}) collective-permute-start(bf16[1,64,2176]{2,1,0:T(8,128)(2,1)S(1)} %copy-done.64), channel_id=1, source_target_pairs={{0,16},{4,20},{8,24},{12,28},{16,0},{20,4},{24,8},{28,12},{1,17},{... | collective-permute-start | bytes 835592 | tf_op jit(solution)/shard_map/ppermute | solution.py:437
  (106 other events, 683.7 us)
